TPU v7x, 32 devices: a whole 2x2x4 slice. The times are simulated.
32 devices in a mesh: ctx: 4 (over y, x), ch: 8 (over z, core).
Axes of the slice: x: 2, y: 2, z: 4, core: 2. Of those that a mesh axis runs over, the one named last changes fastest.
Arguments:
- qkv: bfloat16 [3, 512, 4096], P(None, 'ch', 'ctx'), may hold values from -6 to 6
- short_taps: float32 [3, 512, 7], P(None, 'ch'), may hold values from -2 to 2
- long_filter: float32 [512, 4096], P('ch', 'ctx'), may hold values from -0.09375 to 0.09375
- skip_gain: float32 [512], P('ch'), may hold values from -4 to 4
- out_weight: bfloat16 [8192, 512], P('ch'), may hold values from -0.25 to 0.25
Outputs:
- projected: bfloat16 [8192, 4096], P('ch', 'ctx')
All inputs are finite; a program needn't handle non-finite values.
Results may differ from a plain program's by a relative error of at most 0.0049.
Values may be sent and summed in bfloat16 or wider, within the bound.
No kernel may reach another device: no remote copies, remote signals or barrier semaphores. Data moves between devices by JAX's collectives and lax.ppermute only.
A program may use at most 64 MiB of HBM per device.

v0:
```python
import math

import jax
import jax.numpy as jnp
from jax import lax
from jax.sharding import PartitionSpec as P

exact_mode = lax.Precision.HIGHEST


def from_behind(block, axis, distance):
    devices = range(lax.axis_size(axis))
    route = [(i - distance, i) for i in devices if i - distance in devices]
    return lax.ppermute(block, axis, route)


def contract(pattern, operand, table):
    return jnp.einsum(
        pattern, operand, table, precision=exact_mode, preferred_element_type=jnp.float32
    )


def angle_table(row_index, col_index, period):
    product = row_index[:, None] * col_index[None, :] % period
    return product.astype(jnp.float32) * (2.0 * math.pi / period)


def short_conv(extended, short_taps, length):
    tap_count = short_taps.shape[2]
    result = jnp.zeros(extended.shape[:2] + (length,), jnp.float32)
    for offset in range(tap_count):
        begin_at = tap_count - 1 - offset
        result = (
            result
            + short_taps[:, :, offset : offset + 1] * extended[:, :, begin_at : begin_at + length]
        )
    return result


def spread(stacked):
    return lax.all_to_all(stacked, "ctx", split_axis=2, concat_axis=1, tiled=True)


def collect(stacked):
    return lax.all_to_all(stacked, "ctx", split_axis=1, concat_axis=2, tiled=True)


def local_forward(real_part, imag_part, radix):
    groups, pair_count, length = real_part.shape
    inner_len = length // radix
    split_shape = (groups, pair_count, radix, inner_len)
    real_part = real_part.reshape(split_shape)
    imag_part = imag_part.reshape(split_shape)
    first_angle = angle_table(
        jnp.arange(radix, dtype=jnp.int32), jnp.arange(radix, dtype=jnp.int32), radix
    )
    cos_first = jnp.cos(first_angle)
    sin_first = jnp.sin(first_angle)
    section_real = contract("gars,rk->gaks", real_part, cos_first) + contract(
        "gars,rk->gaks", imag_part, sin_first
    )
    section_imag = contract("gars,rk->gaks", imag_part, cos_first) - contract(
        "gars,rk->gaks", real_part, sin_first
    )
    twist_angle = angle_table(
        jnp.arange(radix, dtype=jnp.int32), jnp.arange(inner_len, dtype=jnp.int32), length
    )
    cos_twist = jnp.cos(twist_angle)
    sin_twist = jnp.sin(twist_angle)
    turned_real = section_real * cos_twist + section_imag * sin_twist
    turned_imag = section_imag * cos_twist - section_real * sin_twist
    second_angle = angle_table(
        jnp.arange(inner_len, dtype=jnp.int32), jnp.arange(inner_len, dtype=jnp.int32), inner_len
    )
    cos_second = jnp.cos(second_angle)
    sin_second = jnp.sin(second_angle)
    out_real = contract("gaks,sb->gabk", turned_real, cos_second) + contract(
        "gaks,sb->gabk", turned_imag, sin_second
    )
    out_imag = contract("gaks,sb->gabk", turned_imag, cos_second) - contract(
        "gaks,sb->gabk", turned_real, sin_second
    )
    return (
        out_real.reshape(groups, pair_count, length),
        out_imag.reshape(groups, pair_count, length),
    )


def local_inverse(real_part, imag_part, radix):
    groups, pair_count, length = real_part.shape
    inner_len = length // radix
    split_shape = (groups, pair_count, inner_len, radix)
    real_part = real_part.reshape(split_shape)
    imag_part = imag_part.reshape(split_shape)
    second_angle = angle_table(
        jnp.arange(inner_len, dtype=jnp.int32), jnp.arange(inner_len, dtype=jnp.int32), inner_len
    )
    cos_second = jnp.cos(second_angle)
    sin_second = jnp.sin(second_angle)
    section_real = contract("gabk,sb->gaks", real_part, cos_second) - contract(
        "gabk,sb->gaks", imag_part, sin_second
    )
    section_imag = contract("gabk,sb->gaks", imag_part, cos_second) + contract(
        "gabk,sb->gaks", real_part, sin_second
    )
    twist_angle = angle_table(
        jnp.arange(radix, dtype=jnp.int32), jnp.arange(inner_len, dtype=jnp.int32), length
    )
    cos_twist = jnp.cos(twist_angle)
    sin_twist = jnp.sin(twist_angle)
    turned_real = section_real * cos_twist - section_imag * sin_twist
    turned_imag = section_imag * cos_twist + section_real * sin_twist
    first_angle = angle_table(
        jnp.arange(radix, dtype=jnp.int32), jnp.arange(radix, dtype=jnp.int32), radix
    )
    cos_first = jnp.cos(first_angle)
    sin_first = jnp.sin(first_angle)
    out_real = contract("gaks,rk->gars", turned_real, cos_first) - contract(
        "gaks,rk->gars", turned_imag, sin_first
    )
    out_imag = contract("gaks,rk->gars", turned_imag, cos_first) + contract(
        "gaks,rk->gars", turned_real, sin_first
    )
    return (
        out_real.reshape(groups, pair_count, length),
        out_imag.reshape(groups, pair_count, length),
    )


def distributed(product, long_filter):
    nodes = lax.axis_size("ctx")
    place = lax.axis_index("ctx")
    chan_dev = product.shape[0]
    block = product.shape[1]
    piece_len = block // nodes
    total_len = 2 * nodes * block
    radix = 1 << (block.bit_length() - 1) // 2
    signals = jnp.concatenate([product, long_filter], axis=0)[:, None, :]
    columns = spread(signals)
    head_angle = angle_table(
        jnp.arange(2 * nodes, dtype=jnp.int32), jnp.arange(nodes, dtype=jnp.int32), 2 * nodes
    )
    head_cos = jnp.cos(head_angle)
    head_sin = jnp.sin(head_angle)
    head_real = contract("gnm,kn->gkm", columns, head_cos)
    head_imag = -contract("gnm,kn->gkm", columns, head_sin)
    local_pos = place * piece_len + jnp.arange(piece_len, dtype=jnp.int32)
    mid_angle = angle_table(jnp.arange(2 * nodes, dtype=jnp.int32), local_pos, total_len)
    mid_cos = jnp.cos(mid_angle)
    mid_sin = jnp.sin(mid_angle)
    turned_real = head_real * mid_cos + head_imag * mid_sin
    turned_imag = head_imag * mid_cos - head_real * mid_sin
    rows = collect(jnp.concatenate([turned_real, turned_imag], axis=0))
    spec_real, spec_imag = local_forward(rows[: 2 * chan_dev], rows[2 * chan_dev :], radix)
    ordered = spread(jnp.concatenate([spec_real, spec_imag], axis=0))
    sig_real = ordered[:chan_dev]
    fil_real = ordered[chan_dev : 2 * chan_dev]
    sig_imag = ordered[2 * chan_dev : 3 * chan_dev]
    fil_imag = ordered[3 * chan_dev :]
    sorted_real = sig_real * fil_real - sig_imag * fil_imag
    sorted_imag = sig_real * fil_imag + sig_imag * fil_real
    restored = collect(jnp.concatenate([sorted_real, sorted_imag], axis=0))
    prod_real = restored[:chan_dev]
    prod_imag = restored[chan_dev:]
    back_real, back_imag = local_inverse(prod_real, prod_imag, radix)
    pair_freq = 2 * place + jnp.arange(2, dtype=jnp.int32)
    tail_angle = angle_table(pair_freq, jnp.arange(block, dtype=jnp.int32), total_len)
    tail_cos = jnp.cos(tail_angle)
    tail_sin = jnp.sin(tail_angle)
    unturned_real = back_real * tail_cos - back_imag * tail_sin
    unturned_imag = back_imag * tail_cos + back_real * tail_sin
    gathered_freq = spread(jnp.concatenate([unturned_real, unturned_imag], axis=0))
    final_real = gathered_freq[:chan_dev]
    final_imag = gathered_freq[chan_dev:]
    convolved = (
        contract("gkm,kn->gnm", final_real, head_cos)
        - contract("gkm,kn->gnm", final_imag, head_sin)
    ) / total_len
    return collect(convolved).reshape(chan_dev, block)


def local(qkv, short_taps, long_filter, skip_gain, out_weight):
    block = qkv.shape[2]
    rim_len = short_taps.shape[2] - 1
    history = from_behind(qkv[:, :, block - rim_len :], "ctx", 1)
    extended = jnp.concatenate([history, qkv], axis=2).astype(jnp.float32)
    featured = short_conv(extended, short_taps, block)
    query = featured[0]
    product = featured[1] * featured[2]
    blocks = distributed(product, long_filter)
    mixed = blocks + skip_gain[:, None] * product
    gated = (query * mixed).astype(jnp.bfloat16)
    summed = jnp.dot(
        out_weight,
        lax.all_gather(gated, "ch", axis=0, tiled=True),
        preferred_element_type=jnp.float32,
    )
    return summed.astype(jnp.bfloat16)


def solution(mesh):
    placed = (P(None, "ch", "ctx"), P(None, "ch", None), P("ch", "ctx"), P("ch"), P("ch", None))
    return jax.shard_map(
        local, mesh=mesh, in_specs=placed, out_specs=P("ch", "ctx"), check_vma=False
    )
```

profile of v0, /device:TPU:0, one launch (start us, length us, event | category | flops | bytes accessed | tf_op | source)
XLA Modules:
  0.0 251.8 jit_solution(3550119160904177395)
XLA Ops:
  6.5 1.5 copy.149
  8.0 4.8 %collective-permute-start = (bf16[3,64,6]{1,2,0:T(8,128)(2,1)S(1)}, bf16[3,64,6]{1,2,0:T(8,128)(2,1)S(1)}, u32[]{:S(2)}, u32[]{:S(2)}) collective-permute-start(bf16[3,64,6]{1,2,0:T(8,128)(2,1)S(1)} %slice.128), channel_id=1, source_target_pairs={{0,8},{8,16},{16,24},{1,9},{9,17},{17,25},{2,10},{10,18},{18,26},{... | collective-permute-start | bytes 6920 | tf_op jit(solution)/shard_map/ppermute | solution.py:14
  15.3 1.3 fusion
  17.6 3.6 %all-to-all-start = ((f32[128,1,1024]{0,1,2:T(1,128)}), f32[128,1,1024]{0,1,2:T(1,128)S(1)}, u32[]{:S(2)}, u32[]{:S(2)}) async-start(f32[128,1,1024]{0,1,2:T(1,128)} %bitcast.7), calls=%async_computation | async-start | bytes 1048576 | tf_op jit(solution)/shard_map/all_to_all | solution.py:41
  21.3 7.7 %all-to-all-done = f32[128,1,1024]{0,1,2:T(1,128)S(1)} async-done(((f32[128,1,1024]{0,1,2:T(1,128)}), f32[128,1,1024]{0,1,2:T(1,128)S(1)}, u32[]{:S(2)}, u32[]{:S(2)}) %all-to-all-start) | async-done | bytes 524320 | tf_op jit(solution)/shard_map/all_to_all | solution.py:41
  29.9 1.3 copy.209
  32.4 1.4 add_bitcast_fusion.1
  34.0 2.0 copy.153
  36.0 4.9 %all-to-all-start.1 = ((f32[256,8,256]{2,0,1:T(8,128)}), f32[256,8,256]{2,0,1:T(8,128)}, u32[]{:S(2)}, u32[]{:S(2)}) async-start(f32[256,8,256]{2,0,1:T(8,128)} %copy.153), calls=%async_computation.1 | async-start | bytes 4194304 | tf_op jit(solution)/shard_map/all_to_all | solution.py:45
  41.0 23.2 %all-to-all-done.1 = f32[256,8,256]{2,0,1:T(8,128)} async-done(((f32[256,8,256]{2,0,1:T(8,128)}), f32[256,8,256]{2,0,1:T(8,128)}, u32[]{:S(2)}, u32[]{:S(2)}) %all-to-all-start.1) | async-done | bytes 2097184 | tf_op jit(solution)/shard_map/all_to_all | solution.py:45
  64.3 3.1 %fusion.196 = (f32[128,2,4,256]{3,0,1,2:T(8,128)}, f32[128,2,4,256]{3,0,1,2:T(8,128)}) fusion(f32[256,2,4,256]{3,0,1,2:T(8,128)} %bitcast.13), kind=kLoop, calls=%fused_computation.239 | loop fusion | bytes 4194304 | tf_op jit(solution)/shard_map/slice | solution.py:154
  67.3 2.5 %copy.157 = f32[128,2,4,256]{0,3,2,1:T(8,128)} copy(f32[128,2,4,256]{3,0,1,2:T(8,128)} %get-tuple-element.15) | data formatting | bytes 2097152 | tf_op jit(solution)/shard_map/slice | solution.py:154
  69.9 3.8 %fusion.32 = f32[32,128,2,32]{1,0,3,2:T(8,128)} fusion(f32[128,2,32,32]{0,3,2,1:T(8,128)} %bitcast.152), kind=kOutput, calls=%fused_computation.66 | convolution fusion | flops 100677632 | bytes 2097152 | tf_op jit(solution)/shard_map/gars,rk->gaks/dot_general | solution.py:18
  73.7 2.5 %copy.154 = f32[128,2,4,256]{0,3,2,1:T(8,128)} copy(f32[128,2,4,256]{3,0,1,2:T(8,128)} %get-tuple-element.16) | data formatting | bytes 2097152 | tf_op jit(solution)/shard_map/slice | solution.py:154
  76.2 3.0 %fusion.36 = f32[32,128,2,32]{1,0,3,2:T(8,128)S(1)} fusion(f32[128,2,32,32]{0,3,2,1:T(8,128)} %bitcast.154), kind=kOutput, calls=%fused_computation.70 | convolution fusion | flops 100677632 | bytes 2097152 | tf_op jit(solution)/shard_map/gars,rk->gaks/dot_general | solution.py:18
  79.2 1.7 convolution_subtract_fusion.3
  80.9 2.1 add_bitcast_fusion
  83.0 1.6 fusion.30
  84.7 1.6 fusion.26
  86.3 14.5 %fusion.9 = f32[128,2,32,32]{0,2,3,1:T(8,128)S(1)} fusion(f32[32,128,2,32]{1,0,3,2:T(8,128)S(1)} %fusion.30, f32[128,2,32,32]{0,2,3,1:T(8,128)S(1)} %get-tuple-element.8), kind=kOutput, calls=%fused_computation.25 | convolution fusion | flops 100939776 | bytes 3145728 | tf_op jit(solution)/shard_map/gaks,sb->gabk/dot_general | solution.py:18
  101.4 1.6 fusion.8
  103.9 1.6 copy.176
  105.5 27.3 %all_to_all.81 = f32[256,2,1024]{0,1,2:T(2,128)S(1)} all-to-all(f32[256,2,1024]{0,1,2:T(2,128)S(1)} %copy.176), channel_id=1, replica_groups=mesh['ctx'=4,'ch'=8] {'ctx'}, dimensions={2} | all-to-all | bytes 4194304 | tf_op jit(solution)/shard_map/all_to_all | solution.py:41
  132.9 1.9 multiply_subtract_fusion.1
  134.9 1.5 copy.178
  136.4 2.4 copy.179
  138.8 2.1 pad_maximum_fusion.2
  140.9 4.2 %all-to-all-start.3 = ((f32[128,8,256]{2,0,1:T(8,128)}), f32[128,8,256]{2,0,1:T(8,128)}, u32[]{:S(2)}, u32[]{:S(2)}) async-start(f32[128,8,256]{2,0,1:T(8,128)} %pad_maximum_fusion.2), calls=%async_computation.3 | async-start | bytes 2097152 | tf_op jit(solution)/shard_map/all_to_all | solution.py:45
  145.4 11.5 %all-to-all-done.3 = f32[128,8,256]{2,0,1:T(8,128)} async-done(((f32[128,8,256]{2,0,1:T(8,128)}), f32[128,8,256]{2,0,1:T(8,128)}, u32[]{:S(2)}, u32[]{:S(2)}) %all-to-all-start.3) | async-done | bytes 1048608 | tf_op jit(solution)/shard_map/all_to_all | solution.py:45
  157.0 2.5 %copy.180 = f32[128,4,2,256]{0,3,1,2:T(8,128)} copy(f32[128,4,2,256]{3,0,2,1:T(8,128)} %bitcast.34) | data formatting | bytes 2097152 | tf_op jit(solution)/shard_map/all_to_all | solution.py:45
  159.5 1.9 fusion.198
  161.4 1.7 fusion.24
  163.1 1.7 fusion.20
  164.8 1.8 convolution_subtract_fusion.1
  166.6 2.2 multiply_subtract_fusion
  168.7 1.6 fusion.18
  170.3 1.6 fusion.14
  171.9 1.8 fusion.7
  174.4 1.6 fusion.6
  178.7 16.7 %all_to_all.82 = f32[128,2,1024]{0,1,2:T(2,128)} all-to-all(f32[128,2,1024]{0,1,2:T(2,128)S(1)} %copy.191), channel_id=1, replica_groups=mesh['ctx'=4,'ch'=8] {'ctx'}, dimensions={2} | all-to-all | bytes 2097152 | tf_op jit(solution)/shard_map/all_to_all | solution.py:41
  195.4 3.6 %copy.192 = f32[128,2,4,256]{3,1,2,0:T(2,128)} copy(f32[128,2,4,256]{0,1,3,2:T(2,128)} %bitcast.162) | data formatting | bytes 2097152 | tf_op jit(solution)/shard_map/all_to_all | solution.py:41
  199.0 2.5 %fusion.197 = (f32[64,4,2,256]{3,2,1,0:T(2,128)}, f32[64,4,2,256]{3,2,1,0:T(2,128)}) fusion(f32[128,4,2,256]{3,2,1,0:T(2,128)} %bitcast.161), kind=kLoop, calls=%fused_computation.240 | loop fusion | bytes 2097152 | tf_op jit(solution)/shard_map/slice | solution.py:174
  201.5 1.4 slice.125
  203.6 1.4 slice.127
  205.7 8.1 %all_to_all.83 = f32[64,4,256]{2,0,1:T(8,128)S(1)} all-to-all(f32[64,4,256]{2,0,1:T(8,128)S(1)} %copy.193), channel_id=1, replica_groups=mesh['ctx'=4,'ch'=8] {'ctx'}, dimensions={1} | all-to-all | bytes 524288 | tf_op jit(solution)/shard_map/all_to_all | solution.py:45
  214.9 22.0 %all-gather.2.cloned.1.call-done = bf16[512,1024]{1,0:T(8,128)(2,1)} async-done(((bf16[64,1024]{1,0:T(8,128)(2,1)}), bf16[512,1024]{1,0:T(8,128)(2,1)}) %all-gather.2.cloned.1.call-update) | async-done | bytes 1048592 | tf_op jit(solution)/shard_map/all_gather | solution.py:195
  236.9 3.9 %convert_bitcast_fusion = bf16[1024,1024]{0,1:T(8,128)(2,1)} fusion(bf16[512,1024]{1,0:T(8,128)(2,1)} %all-gather.2.cloned.1.call-done, bf16[1024,512]{1,0:T(8,128)(2,1)S(1)} %copy-done), kind=kOutput, calls=%fused_computation.2 | convolution fusion | flops 1074790400 | bytes 4194304 | tf_op jit(solution)/shard_map/dot_general | solution.py:193
  240.8 3.9 %copy.196 = bf16[1024,1024]{1,0:T(8,128)(2,1)} copy(bf16[1024,1024]{0,1:T(8,128)(2,1)} %convert_bitcast_fusion) | data formatting | bytes 4194304 | tf_op jit(solution)/shard_map/convert_element_type | solution.py:198
  (49 shorter events, 13.3 us)
Async XLA Ops:
  6.5 230.3 %copy-start = (bf16[1024,512]{1,0:T(8,128)(2,1)S(1)}, bf16[1024,512]{1,0:T(8,128)(2,1)}, u32[]{:S(2)}) copy-start(bf16[1024,512]{1,0:T(8,128)(2,1)} %param.9) | copy-start | bytes 3145732
  8.0 7.0 %collective-permute-start = (bf16[3,64,6]{1,2,0:T(8,128)(2,1)S(1)}, bf16[3,64,6]{1,2,0:T(8,128)(2,1)S(1)}, u32[]{:S(2)}, u32[]{:S(2)}) collective-permute-start(bf16[3,64,6]{1,2,0:T(8,128)(2,1)S(1)} %slice.128), channel_id=1, source_target_pairs={{0,8},{8,16},{16,24},{1,9},{9,17},{17,25},{2,10},{10,18},{18,26},{... | collective-permute-start | bytes 6920 | tf_op jit(solution)/shard_map/ppermute | solution.py:14
  17.6 11.5 %all-to-all-start = ((f32[128,1,1024]{0,1,2:T(1,128)}), f32[128,1,1024]{0,1,2:T(1,128)S(1)}, u32[]{:S(2)}, u32[]{:S(2)}) async-start(f32[128,1,1024]{0,1,2:T(1,128)} %bitcast.7), calls=%async_computation | async-start | bytes 1048576 | tf_op jit(solution)/shard_map/all_to_all | solution.py:41
  29.1 0.8 copy-start.4
  36.0 28.3 %all-to-all-start.1 = ((f32[256,8,256]{2,0,1:T(8,128)}), f32[256,8,256]{2,0,1:T(8,128)}, u32[]{:S(2)}, u32[]{:S(2)}) async-start(f32[256,8,256]{2,0,1:T(8,128)} %copy.153), calls=%async_computation.1 | async-start | bytes 4194304 | tf_op jit(solution)/shard_map/all_to_all | solution.py:45
  76.2 3.0 %copy-start.2 = (f32[128,2,4,256]{0,3,2,1:T(8,128)S(1)}, f32[128,2,4,256]{0,3,2,1:T(8,128)}, u32[]{:S(2)}) copy-start(f32[128,2,4,256]{0,3,2,1:T(8,128)} %copy.154) | copy-start | bytes 3145732
  76.2 3.0 %copy-start.3 = (f32[32,128,2,32]{1,0,3,2:T(8,128)S(1)}, f32[32,128,2,32]{1,0,3,2:T(8,128)}, u32[]{:S(2)}) copy-start(f32[32,128,2,32]{1,0,3,2:T(8,128)} %fusion.32) | copy-start | bytes 3145732
  79.2 1.7 copy-start.1
  140.9 16.0 %all-to-all-start.3 = ((f32[128,8,256]{2,0,1:T(8,128)}), f32[128,8,256]{2,0,1:T(8,128)}, u32[]{:S(2)}, u32[]{:S(2)}) async-start(f32[128,8,256]{2,0,1:T(8,128)} %pad_maximum_fusion.2), calls=%async_computation.3 | async-start | bytes 2097152 | tf_op jit(solution)/shard_map/all_to_all | solution.py:45
  145.2 91.7 %all-gather.2.cloned.1.call-start = ((), (), s32[]{:S(2)}) async-start(), calls=%async_computation.6 | async-start | bytes 1179648 | tf_op jit(solution)/shard_map/all_gather | solution.py:195
  205.0 9.0 %copy-start.5 = (f32[64]{0:T(128)S(1)}, f32[64]{0:T(128)}, u32[]{:S(2)}) copy-start(f32[64]{0:T(128)} %param.8) | copy-start | bytes 772
Sparse Core Ops, SparseCore 0:
  215.0 21.8 all-gather.1
where the time goes:
time: 252 us
  waiting for transfers between devices  64.5 us (26%)
  blocking collectives  52.1 us (21%)
  matrix products  51.7 us (21%)
  local copies, waits for them, and re-layouts  43.2 us (17%)
  starting transfers between devices  17.6 us (7%)
  between operations  14.1 us (6%)
  other arithmetic  8.54 us (3%)
    dot_general x20, matrix products, contract(): jnp.einsum(pattern, operand, table, precision=exact_mode, preferred_eleme...  47.8 us
    all_to_all x2, blocking collectives, spread(): lax.all_to_all(stacked, 'ctx', split_axis=2, concat_axis=1, tiled=True)  44 us
    all_to_all x2, waiting for transfers between devices, collect(): lax.all_to_all(stacked, 'ctx', split_axis=1, concat_axis=2, tiled=True)  34.7 us
    all_gather x1, waiting for transfers between devices, local(): lax.all_gather(gated, 'ch', axis=0, tiled=True)  22 us
    all_to_all x2, starting transfers between devices, collect(): lax.all_to_all(stacked, 'ctx', split_axis=1, concat_axis=2, tiled=True)  9.1 us
    all_to_all x1, blocking collectives, collect(): lax.all_to_all(stacked, 'ctx', split_axis=1, concat_axis=2, tiled=True)  8.11 us
    all_to_all x1, waiting for transfers between devices, spread(): lax.all_to_all(stacked, 'ctx', split_axis=2, concat_axis=1, tiled=True)  7.75 us
    slice x2, local copies, waits for them, and re-layouts, distributed(): rows[2 * chan_dev:]  5.6 us
  transfers between devices with their start and end apart: 5, of which 4 were waited for; matrix products, arithmetic and copies ran while one was open for 1% of the time, Pallas kernels for 0%

commit v1 on v0

v1 whole, which is shorter than its diff:
```python
import math

import numpy as np

import jax
import jax.numpy as jnp
from jax import lax
from jax.experimental import pallas as pl
from jax.experimental.pallas import tpu as pltpu
from jax.sharding import PartitionSpec as P

LANES = 128
PAD = 8


def split_table(table):
    high = table.astype(jnp.bfloat16)
    low = (table - high.astype(np.float64)).astype(jnp.bfloat16)
    return high, low


def dft_tables(rows):
    total = 2 * rows * LANES
    block = np.arange(rows, dtype=np.float64)
    freq = np.arange(rows, dtype=np.float64) + 0.5
    lane = np.arange(LANES, dtype=np.float64)
    head = 2.0 * math.pi * np.outer(freq, block) / (2 * rows)
    head_high, head_low = split_table(np.concatenate([np.cos(head), -np.sin(head)], axis=0))
    first = np.concatenate([head_high, head_high, head_low], axis=1)
    turn = 2.0 * math.pi * np.outer(freq, lane) / total
    twist = np.concatenate([np.cos(turn), np.sin(turn)], axis=1).astype(np.float32)
    inner = 2.0 * math.pi * np.outer(lane, lane) / LANES
    square = np.block([[np.cos(inner), -np.sin(inner)], [np.sin(inner), np.cos(inner)]])
    second = np.concatenate(split_table(square), axis=1)
    tail = head.T
    tail_high, tail_low = split_table(
        (2.0 / total) * np.concatenate([np.cos(tail), np.sin(tail)], axis=1)
    )
    last = np.concatenate([tail_high, tail_high, tail_low], axis=1)
    return first, twist, second, last


def halves(value):
    high = value.astype(jnp.bfloat16)
    low = (value - high.astype(jnp.float32)).astype(jnp.bfloat16)
    return high, low


def dot(left, right):
    return jnp.dot(left, right, preferred_element_type=jnp.float32)


def long_kernel(
    nodes, chans, per_node, taps_ref, skip_ref, first_ref, twist_ref, second_ref, last_ref, *refs
):
    pieces = refs[:nodes]
    outs = refs[nodes : 2 * nodes]
    raw, query, prod, mid, spec, unturned, final = refs[2 * nodes :]
    rows = nodes * per_node
    pitch = rows + PAD
    place = lax.axis_index("ctx")
    base = place * chans
    tap_count = taps_ref.shape[2]

    for stream in range(4):
        raw[stream, pl.ds(PAD - 1, chans, stride=pitch), :] = jnp.zeros((chans, LANES), jnp.float32)
    for mask in range(nodes):
        start = (place ^ mask) * per_node + PAD
        for stream in range(4):
            for tile in range(per_node):
                raw[stream, pl.ds(start + tile, chans, stride=pitch), :] = pieces[mask][
                    stream, :, tile * LANES : (tile + 1) * LANES
                ].astype(jnp.float32)

    lane = lax.broadcasted_iota(jnp.int32, (rows, LANES), 1)

    def featured(stream, chan):
        begin = chan * pitch + PAD
        now = raw[stream, begin : begin + rows, :]
        before = raw[stream, begin - 1 : begin - 1 + rows, :]
        total = taps_ref[stream, base + chan, 0] * now
        for shift in range(1, tap_count):
            mixed = jnp.where(lane >= LANES - shift, before, now)
            total = total + taps_ref[stream, base + chan, shift] * pltpu.roll(mixed, shift, 1)
        return total

    cos_twist = twist_ref[:, :LANES]
    sin_twist = twist_ref[:, LANES:]
    zero = jnp.zeros((rows, LANES), jnp.bfloat16)
    for chan in range(chans):
        query[chan * rows : (chan + 1) * rows, :] = featured(0, chan)
        product = featured(1, chan) * featured(2, chan)
        prod[chan * rows : (chan + 1) * rows, :] = product
        high, low = halves(product)
        begin = chan * pitch + PAD
        filt = raw[3, begin : begin + rows, :].astype(jnp.bfloat16)
        operand = jnp.concatenate(
            [
                jnp.concatenate([high, filt], axis=1),
                jnp.concatenate([low, zero], axis=1),
                jnp.concatenate([high, filt], axis=1),
            ],
            axis=0,
        )
        section = dot(first_ref[...], operand)
        for part in range(2):
            real = section[:rows, part * LANES : (part + 1) * LANES]
            imag = section[rows:, part * LANES : (part + 1) * LANES]
            turned = jnp.concatenate(
                [
                    real * cos_twist + imag * sin_twist,
                    imag * cos_twist - real * sin_twist,
                ],
                axis=1,
            )
            high, low = halves(turned)
            at = (part * chans + chan) * rows
            mid[0, at : at + rows, :] = high
            mid[1, at : at + rows, :] = low

    def inner(high, low):
        table_high = second_ref[:, : 2 * LANES]
        table_low = second_ref[:, 2 * LANES :]
        return dot(high, table_high) + dot(low, table_high) + dot(high, table_low)

    spec[...] = inner(mid[0], mid[1])
    for chan in range(chans):
        sig = spec[chan * rows : (chan + 1) * rows, :]
        fil = spec[(chans + chan) * rows : (chans + chan + 1) * rows, :]
        sig_real, sig_imag = sig[:, :LANES], sig[:, LANES:]
        fil_real, fil_imag = fil[:, :LANES], fil[:, LANES:]
        joined = jnp.concatenate(
            [
                sig_real * fil_real - sig_imag * fil_imag,
                -(sig_real * fil_imag + sig_imag * fil_real),
            ],
            axis=1,
        )
        high, low = halves(joined)
        mid[0, chan * rows : (chan + 1) * rows, :] = high
        mid[1, chan * rows : (chan + 1) * rows, :] = low
    half = chans * rows
    unturned[...] = inner(mid[0, :half, :], mid[1, :half, :])
    for chan in range(chans):
        back = unturned[chan * rows : (chan + 1) * rows, :]
        real, imag = back[:, :LANES], back[:, LANES:]
        turned = jnp.concatenate(
            [real * cos_twist + imag * sin_twist, imag * cos_twist - real * sin_twist], axis=0
        )
        high, low = halves(turned)
        convolved = dot(last_ref[...], jnp.concatenate([high, low, high], axis=0))
        span = slice(chan * rows, (chan + 1) * rows)
        mixed = convolved + skip_ref[base + chan] * prod[span, :]
        final[span, :] = query[span, :] * mixed
    for mask in range(nodes):
        start = (place ^ mask) * per_node
        for tile in range(per_node):
            outs[mask][:, tile * LANES : (tile + 1) * LANES] = final[
                pl.ds(start + tile, chans, stride=rows), :
            ].astype(jnp.bfloat16)


def long_mix(pieces, short_taps, skip_gain):
    nodes = len(pieces)
    _, chans, block = pieces[0].shape
    per_node = block // LANES
    rows = nodes * per_node
    first, twist, second, last = dft_tables(rows)
    whole = pl.BlockSpec(memory_space=pltpu.VMEM)
    scalars = pl.BlockSpec(memory_space=pltpu.SMEM)
    return pl.pallas_call(
        lambda *refs: long_kernel(nodes, chans, per_node, *refs),
        out_shape=[jax.ShapeDtypeStruct((chans, block), jnp.bfloat16)] * nodes,
        in_specs=[scalars, scalars] + [whole] * (4 + nodes),
        out_specs=[whole] * nodes,
        scratch_shapes=[
            pltpu.VMEM((4, chans * (rows + PAD), LANES), jnp.float32),
            pltpu.VMEM((chans * rows, LANES), jnp.float32),
            pltpu.VMEM((chans * rows, LANES), jnp.float32),
            pltpu.VMEM((2, 2 * chans * rows, 2 * LANES), jnp.bfloat16),
            pltpu.VMEM((2 * chans * rows, 2 * LANES), jnp.float32),
            pltpu.VMEM((chans * rows, 2 * LANES), jnp.float32),
            pltpu.VMEM((chans * rows, LANES), jnp.float32),
        ],
        compiler_params=pltpu.CompilerParams(vmem_limit_bytes=40 << 20),
        name="long_mix",
    )(short_taps, skip_gain, first, twist, second, last, *pieces)


def project_kernel(nodes, stacks, weight_ref, *refs):
    blocks = refs[: 2 * stacks]
    out_ref, gathered = refs[2 * stacks :]
    place = lax.axis_index("ctx")
    spot = lax.axis_index("ch")
    chans = blocks[0].shape[1]

    @pl.when(pl.program_id(0) == 0)
    def _():
        for index in range(2 * stacks):
            core, depth = index // stacks, index % stacks
            owner = spot ^ (2 * depth + core)
            for mask in range(nodes):
                row = (owner * nodes + (place ^ mask)) * chans
                gathered[pl.ds(pl.multiple_of(row, chans), chans), :] = blocks[index][mask]

    out_ref[...] = dot(weight_ref[...], gathered[...]).astype(jnp.bfloat16)


def project(blocks, out_weight, tile):
    nodes, _, block = blocks[0].shape
    features, channels = out_weight.shape
    whole = pl.BlockSpec(memory_space=pltpu.VMEM)
    return pl.pallas_call(
        lambda *refs: project_kernel(nodes, len(blocks) // 2, *refs),
        grid=(features // tile,),
        out_shape=jax.ShapeDtypeStruct((features, block), jnp.bfloat16),
        in_specs=[pl.BlockSpec((tile, channels), lambda i: (i, 0))] + [whole] * len(blocks),
        out_specs=pl.BlockSpec((tile, block), lambda i: (i, 0)),
        scratch_shapes=[pltpu.VMEM((channels, block), jnp.bfloat16)],
        compiler_params=pltpu.CompilerParams(vmem_limit_bytes=40 << 20),
        name="project",
    )(out_weight, *blocks)


def project_plain(blocks, out_weight):
    nodes, chans, block = blocks[0].shape
    stacks = len(blocks) // 2
    place = lax.axis_index("ctx")
    spot = lax.axis_index("ch")
    found = jnp.stack(blocks).reshape(2, stacks, nodes, chans, block)
    index = jnp.arange(2 * stacks, dtype=jnp.int32) ^ spot
    found = found[index % 2, index // 2]
    found = found[:, jnp.arange(nodes, dtype=jnp.int32) ^ place]
    summed = jnp.dot(
        out_weight, found.reshape(-1, block), preferred_element_type=jnp.float32
    )
    return summed.astype(jnp.bfloat16)


def local(qkv, short_taps, long_filter, skip_gain, out_weight):
    nodes = lax.axis_size("ctx")
    spread = lax.axis_size("ch")
    stacks = spread // 2
    place = lax.axis_index("ctx")
    streams, chan_dev, block = qkv.shape
    chans = chan_dev // nodes

    by_node = qkv.reshape(streams, nodes, chans, block)
    filters = long_filter.reshape(nodes, chans, block)
    pieces = []
    for mask in range(nodes):
        target = place ^ mask
        piece = jnp.concatenate(
            [
                lax.dynamic_index_in_dim(by_node, target, 1, False),
                lax.dynamic_index_in_dim(filters, target, 0, True).astype(jnp.bfloat16),
            ],
            axis=0,
        )
        if mask:
            piece = lax.ppermute(piece, "ctx", [(i, i ^ mask) for i in range(nodes)])
        pieces.append(piece)

    gated = long_mix(pieces, short_taps, skip_gain)

    mine = [gated[0]] + [
        lax.ppermute(gated[mask], "ctx", [(i, i ^ mask) for i in range(nodes)])
        for mask in range(1, nodes)
    ]
    mine = jnp.stack(mine)
    column = [mine] + [
        lax.ppermute(mine, "ch", [(i, i ^ (2 * depth)) for i in range(spread)])
        for depth in range(1, stacks)
    ]
    other = [lax.ppermute(part, "ch", [(i, i ^ 1) for i in range(spread)]) for part in column]
    if chans % 16:
        return project_plain(column + other, out_weight)
    return project(column + other, out_weight, 256)


def solution(mesh):
    placed = (P(None, "ch", "ctx"), P(None, "ch", None), P("ch", "ctx"), P("ch"), P("ch", None))
    return jax.shard_map(
        local, mesh=mesh, in_specs=placed, out_specs=P("ch", "ctx"), check_vma=False
    )
```

time: 252 us -> 41.8 us (0.17)
  blocking collectives: 52.1 us -> 0 us
  matrix products: 51.7 us -> 0 us
  waiting for transfers between devices: 64.5 us -> 17 us
  local copies, waits for them, and re-layouts: 43.2 us -> 2.97 us
  between operations: 14.1 us -> 0.13 us
  other arithmetic: 8.54 us -> 0.08 us
  Pallas kernels: 0 us -> 8.23 us
  starting transfers between devices: 17.6 us -> 13.2 us
    all_to_all x3 -> x0, blocking collectives: 52.1 us -> none  [the longest x2 44 us: spread(): lax.all_to_all(stacked, 'ctx', split_axis=2, concat_axis=1, tiled=True)]
    dot_general x21 -> x0, matrix products: 51.7 us -> none  [the longest x20 47.8 us: contract(): jnp.einsum(pattern, operand, table, precision=exact_mode, preferred_eleme...]
    all_to_all x3 -> x0, waiting for transfers between devices: 42.5 us -> none  [the longest x2 34.7 us: collect(): lax.all_to_all(stacked, 'ctx', split_axis=1, concat_axis=2, tiled=True)]
    all_gather x1 -> x0, waiting for transfers between devices: 22 us -> none  [local(): lax.all_gather(gated, 'ch', axis=0, tiled=True)]
    ppermute x1 -> x13, waiting for transfers between devices: 0.01 us -> 17 us  [the longest x3 7.3 us: local(): lax.ppermute(mine, 'ch', [(i, i ^ 2 * depth) for i in range(spread)])]
    slice x9 -> x0, local copies, waits for them, and re-layouts: 16.3 us -> none  [the longest x2 5.6 us: distributed(): rows[2 * chan_dev:]]
    all_to_all x3 -> x0, starting transfers between devices: 12.7 us -> none  [the longest x2 9.1 us: collect(): lax.all_to_all(stacked, 'ctx', split_axis=1, concat_axis=2, tiled=True)]
    ppermute x1 -> x13, starting transfers between devices: 4.84 us -> 13.2 us  [the longest x3 4.67 us: local(): piece = lax.ppermute(piece, 'ctx', [(i, i ^ mask) for i in range(nodes)])]
  transfers between devices with their start and end apart: 5 -> 13, of which waited for: 4 -> 9; matrix products, arithmetic and copies ran while one was open for 1% -> 2% of each run, Pallas kernels for 0% -> 0%
where the time goes in v1:
time: 41.8 us; the launch traced here: 41.6 us
  waiting for transfers between devices  17 us (41%)
  starting transfers between devices  13.2 us (32%)
  Pallas kernels  8.23 us (20%)
  local copies, waits for them, and re-layouts  2.97 us (7%)
    ppermute x3, waiting for transfers between devices, local(): lax.ppermute(mine, 'ch', [(i, i ^ 2 * depth) for i in range(spread)])  7.3 us
    ppermute x3, waiting for transfers between devices, local(): piece = lax.ppermute(piece, 'ctx', [(i, i ^ mask) for i in range(nodes)])  5.33 us
    pallas_call x1, Pallas kernels, long_mix(): pl.pallas_call(lambda *refs: long_kernel(nodes, chans, per_node, *refs),...  5.19 us
    ppermute x3, starting transfers between devices, local(): piece = lax.ppermute(piece, 'ctx', [(i, i ^ mask) for i in range(nodes)])  4.67 us
    ppermute x3, starting transfers between devices, local(): lax.ppermute(mine, 'ch', [(i, i ^ 2 * depth) for i in range(spread)])  4.45 us
    ppermute x3, starting transfers between devices, local(): lax.ppermute(gated[mask], 'ctx', [(i, i ^ mask) for i in range(nodes)])  3.55 us
    ppermute x3, waiting for transfers between devices, local(): lax.ppermute(gated[mask], 'ctx', [(i, i ^ mask) for i in range(nodes)])  3.37 us
    pallas_call x1, Pallas kernels, project(): pl.pallas_call(lambda *refs: project_kernel(nodes, len(blocks) // 2, *ref...  3.04 us
  transfers between devices with their start and end apart: 13, of which 9 were waited for; matrix products, arithmetic and copies ran while one was open for 2% of the time, Pallas kernels for 0%

profile of v1, /device:TPU:0, one launch (start us, length us, event | category | flops | bytes accessed | tf_op | source)
XLA Modules:
  0.0 41.6 jit_solution(748485688459026490)
XLA Ops:
  0.0 0.0 copy-start.3
  0.0 0.0 copy-start.1
  0.0 0.0 copy-start.2
  0.0 0.0 copy-start.4
  0.0 0.0 copy-start.5
  0.0 0.0 copy-start
  0.0 1.1 %dynamic-slice_convert_fusion = (bf16[1,16,1024]{2,1,0:T(8,128)(2,1)S(1)}, bf16[1,16,1024]{2,1,0:T(8,128)(2,1)S(1)}, bf16[1,16,1024]{2,1,0:T(8,128)(2,1)S(1)}, bf16[1,16,1024]{2,1,0:T(8,128)(2,1)S(1)}) fusion(f32[4,16,1024]{2,1,0:T(8,128)} %bitcast.24, s32[]{:T(128)S(6)} %select_n.21, s32[]{:T(128)S(6)} %select_n.20, s32[]{:T(128)S(6)} %select_n.19, ...), kind=kLoop, calls=%fused_computation.9 | loop fusion | bytes 262160 | tf_op jit(solution)/shard_map/convert_element_type | solution.py:256
  1.1 1.1 %dynamic-slice_bitcast_fusion = (bf16[3,16,1024]{2,1,0:T(8,128)(2,1)S(1)}, bf16[3,16,1024]{2,1,0:T(8,128)(2,1)S(1)}, bf16[3,16,1024]{2,1,0:T(8,128)(2,1)S(1)}, bf16[3,16,1024]{2,1,0:T(8,128)(2,1)S(1)}) fusion(bf16[3,4,16,1024]{3,2,1,0:T(8,128)(2,1)} %bitcast.23, s32[]{:T(128)S(6)} %select_n.21, s32[]{:T(128)S(6)} %select_n.20, s32[]{:T(128)S(6)} %select_n.19, ...), kind=kLoop, calls=%fused_computation.5 | loop fusion | bytes 786448 | tf_op jit(solution)/shard_map/jit(dynamic_index_in_dim)/squeeze | solution.py:255
  2.2 3.0 %collective-permute-start = (bf16[4,16,1024]{2,1,0:T(8,128)(2,1)S(1)}, bf16[4,16,1024]{2,1,0:T(8,128)(2,1)S(1)}, u32[]{:S(2)}, u32[]{:S(2)}) collective-permute-start(bf16[4,16,1024]{2,1,0:T(8,128)(2,1)S(1)} %pad_maximum_fusion.1), channel_id=1, source_target_pairs={{0,8},{8,0},{16,24},{24,16},{1,9},{9,1},{17,25},{25,17},{2,10},{10... | collective-permute-start | bytes 393224 | tf_op jit(solution)/shard_map/ppermute | solution.py:261
  5.2 1.6 %collective-permute-start.1 = (bf16[4,16,1024]{2,1,0:T(8,128)(2,1)S(1)}, bf16[4,16,1024]{2,1,0:T(8,128)(2,1)S(1)}, u32[]{:S(2)}, u32[]{:S(2)}) collective-permute-start(bf16[4,16,1024]{2,1,0:T(8,128)(2,1)S(1)} %pad_maximum_fusion.2), channel_id=1, source_target_pairs={{0,16},{8,24},{16,0},{24,8},{1,17},{9,25},{17,1},{25,9},{2,18},{10... | collective-permute-start | bytes 393224 | tf_op jit(solution)/shard_map/ppermute | solution.py:261
  6.9 0.1 collective-permute-start.2
  6.9 0.8 %copy.14.refs_0_ = f32[3,64,7]{2,1,0:T(8,128)S(1)} copy(f32[3,64,7]{1,2,0:T(8,128)} %param.10) | data formatting | bytes 10752 | tf_op args[1]
  7.8 1.4 %collective-permute-done.refs_7_ = bf16[4,16,1024]{2,1,0:T(8,128)(2,1)S(1)} collective-permute-done((bf16[4,16,1024]{2,1,0:T(8,128)(2,1)S(1)}, bf16[4,16,1024]{2,1,0:T(8,128)(2,1)S(1)}, u32[]{:S(2)}, u32[]{:S(2)}) %collective-permute-start) | collective-permute-done | bytes 131104 | tf_op jit(solution)/shard_map/ppermute | solution.py:261
  9.1 4.0 %collective-permute-done.1.refs_8_ = bf16[4,16,1024]{2,1,0:T(8,128)(2,1)S(1)} collective-permute-done((bf16[4,16,1024]{2,1,0:T(8,128)(2,1)S(1)}, bf16[4,16,1024]{2,1,0:T(8,128)(2,1)S(1)}, u32[]{:S(2)}, u32[]{:S(2)}) %collective-permute-start.1) | collective-permute-done | bytes 131104 | tf_op jit(solution)/shard_map/ppermute | solution.py:261
  13.1 0.0 collective-permute-done.2.refs_9_
  13.1 0.0 copy-done.3
  13.1 0.0 copy-done.1
  13.1 0.0 copy-done.2
  13.1 0.0 copy-done.4
  13.1 0.0 copy-done.5
  13.1 5.2 %long_mix.1 = (bf16[16,1024]{1,0:T(8,128)(2,1)S(1)}, bf16[16,1024]{1,0:T(8,128)(2,1)S(1)}, bf16[16,1024]{1,0:T(8,128)(2,1)S(1)}, bf16[16,1024]{1,0:T(8,128)(2,1)S(1)}) custom-call(f32[3,64,7]{2,1,0:T(8,128)S(1)} %copy.14.refs_0_, f32[64]{0:T(128)S(1)} %copy-done.5, bf16[64,96]{1,0:T(8,128)(2,1)S(1)} %copy-done.4, f32[32,256]{1,0:T(8,128)S(1)} %copy-done.2, ...), custom_call_target="tpu_custom_call" | custom-call | tf_op jit(solution)/shard_map/long_mix/pallas_call | solution.py:171
  18.3 1.2 %collective-permute-start.3 = (bf16[16,1024]{1,0:T(8,128)(2,1)S(1)}, bf16[16,1024]{1,0:T(8,128)(2,1)S(1)}, u32[]{:S(2)}, u32[]{:S(2)}) collective-permute-start(bf16[16,1024]{1,0:T(8,128)(2,1)S(1)} %get-tuple-element.10), channel_id=1, source_target_pairs={{0,8},{8,0},{16,24},{24,16},{1,9},{9,1},{17,25},{25,17},{2,10},{10... | collective-permute-start | bytes 98312 | tf_op jit(solution)/shard_map/ppermute | solution.py:267
  19.5 0.9 %collective-permute-start.4 = (bf16[16,1024]{1,0:T(8,128)(2,1)S(1)}, bf16[16,1024]{1,0:T(8,128)(2,1)S(1)}, u32[]{:S(2)}, u32[]{:S(2)}) collective-permute-start(bf16[16,1024]{1,0:T(8,128)(2,1)S(1)} %get-tuple-element.11), channel_id=1, source_target_pairs={{0,16},{8,24},{16,0},{24,8},{1,17},{9,25},{17,1},{25,9},{2,18},{10... | collective-permute-start | bytes 98312 | tf_op jit(solution)/shard_map/ppermute | solution.py:267
  20.4 1.4 %collective-permute-start.5 = (bf16[16,1024]{1,0:T(8,128)(2,1)S(1)}, bf16[16,1024]{1,0:T(8,128)(2,1)S(1)}, u32[]{:S(2)}, u32[]{:S(2)}) collective-permute-start(bf16[16,1024]{1,0:T(8,128)(2,1)S(1)} %get-tuple-element.12), channel_id=1, source_target_pairs={{0,24},{8,16},{16,8},{24,0},{1,25},{9,17},{17,9},{25,1},{2,26},{10... | collective-permute-start | bytes 98312 | tf_op jit(solution)/shard_map/ppermute | solution.py:267
  21.9 0.7 %collective-permute-done.3 = bf16[16,1024]{1,0:T(8,128)(2,1)S(1)} collective-permute-done((bf16[16,1024]{1,0:T(8,128)(2,1)S(1)}, bf16[16,1024]{1,0:T(8,128)(2,1)S(1)}, u32[]{:S(2)}, u32[]{:S(2)}) %collective-permute-start.3) | collective-permute-done | bytes 32800 | tf_op jit(solution)/shard_map/ppermute | solution.py:267
  22.6 0.8 %collective-permute-done.4 = bf16[16,1024]{1,0:T(8,128)(2,1)S(1)} collective-permute-done((bf16[16,1024]{1,0:T(8,128)(2,1)S(1)}, bf16[16,1024]{1,0:T(8,128)(2,1)S(1)}, u32[]{:S(2)}, u32[]{:S(2)}) %collective-permute-start.4) | collective-permute-done | bytes 32800 | tf_op jit(solution)/shard_map/ppermute | solution.py:267
  23.4 1.8 %collective-permute-done.5 = bf16[16,1024]{1,0:T(8,128)(2,1)S(1)} collective-permute-done((bf16[16,1024]{1,0:T(8,128)(2,1)S(1)}, bf16[16,1024]{1,0:T(8,128)(2,1)S(1)}, u32[]{:S(2)}, u32[]{:S(2)}) %collective-permute-start.5) | collective-permute-done | bytes 32800 | tf_op jit(solution)/shard_map/ppermute | solution.py:267
  25.3 3.7 %collective-permute-start.8 = (bf16[4,16,1024]{2,1,0:T(8,128)(2,1)S(1)}, bf16[4,16,1024]{2,1,0:T(8,128)(2,1)S(1)}, u32[]{:S(2)}, u32[]{:S(2)}) collective-permute-start(bf16[4,16,1024]{2,1,0:T(8,128)(2,1)S(1)} %pad_maximum_fusion.4.refs_1_), channel_id=1, source_target_pairs={{0,6},{1,7},{2,4},{3,5},{4,2},{5,3},{6,0},{7,1},{8,14},{9,15},{10,... | collective-permute-start | bytes 393224 | tf_op jit(solution)/shard_map/ppermute | solution.py:272
  28.9 0.0 collective-permute-start.7
  29.0 0.8 %collective-permute-start.6 = (bf16[4,16,1024]{2,1,0:T(8,128)(2,1)S(1)}, bf16[4,16,1024]{2,1,0:T(8,128)(2,1)S(1)}, u32[]{:S(2)}, u32[]{:S(2)}) collective-permute-start(bf16[4,16,1024]{2,1,0:T(8,128)(2,1)S(1)} %pad_maximum_fusion.4.refs_1_), channel_id=1, source_target_pairs={{0,2},{1,3},{2,0},{3,1},{4,6},{5,7},{6,4},{7,5},{8,10},{9,11},{10,... | collective-permute-start | bytes 393224 | tf_op jit(solution)/shard_map/ppermute | solution.py:272
  29.7 0.0 collective-permute-start.9
  29.7 3.3 %collective-permute-done.8.refs_4_ = bf16[4,16,1024]{2,1,0:T(8,128)(2,1)S(1)} collective-permute-done((bf16[4,16,1024]{2,1,0:T(8,128)(2,1)S(1)}, bf16[4,16,1024]{2,1,0:T(8,128)(2,1)S(1)}, u32[]{:S(2)}, u32[]{:S(2)}) %collective-permute-start.8) | collective-permute-done | bytes 131104 | tf_op jit(solution)/shard_map/ppermute | solution.py:272
  33.0 0.0 collective-permute-start.12
  33.0 4.0 %collective-permute-done.7.refs_3_ = bf16[4,16,1024]{2,1,0:T(8,128)(2,1)S(1)} collective-permute-done((bf16[4,16,1024]{2,1,0:T(8,128)(2,1)S(1)}, bf16[4,16,1024]{2,1,0:T(8,128)(2,1)S(1)}, u32[]{:S(2)}, u32[]{:S(2)}) %collective-permute-start.7) | collective-permute-done | bytes 131104 | tf_op jit(solution)/shard_map/ppermute | solution.py:272
  37.0 0.0 collective-permute-start.11
  37.0 0.0 collective-permute-done.6.refs_2_
  37.0 0.5 %collective-permute-start.10 = (bf16[4,16,1024]{2,1,0:T(8,128)(2,1)S(1)}, bf16[4,16,1024]{2,1,0:T(8,128)(2,1)S(1)}, u32[]{:S(2)}, u32[]{:S(2)}) collective-permute-start(bf16[4,16,1024]{2,1,0:T(8,128)(2,1)S(1)} %collective-permute-done.6.refs_2_), channel_id=1, source_target_pairs={{0,1},{1,0},{2,3},{3,2},{4,5},{5,4},{6,7},{7,6},{8,9},{9,8},{10,11... | collective-permute-start | bytes 393224 | tf_op jit(solution)/shard_map/ppermute | solution.py:275
  37.5 0.0 collective-permute-done.9.refs_5_
  37.6 0.0 collective-permute-done.12.refs_8_
  37.6 0.8 %collective-permute-done.11.refs_7_ = bf16[4,16,1024]{2,1,0:T(8,128)(2,1)S(1)} collective-permute-done((bf16[4,16,1024]{2,1,0:T(8,128)(2,1)S(1)}, bf16[4,16,1024]{2,1,0:T(8,128)(2,1)S(1)}, u32[]{:S(2)}, u32[]{:S(2)}) %collective-permute-start.11) | collective-permute-done | bytes 131104 | tf_op jit(solution)/shard_map/ppermute | solution.py:275
  38.4 0.2 collective-permute-done.10.refs_6_
  38.6 0.0 copy-done
  38.6 3.0 %project.1 = bf16[1024,1024]{1,0:T(8,128)(2,1)} custom-call(bf16[1024,512]{1,0:T(8,128)(2,1)S(1)} %copy-done, bf16[4,16,1024]{2,1,0:T(8,128)(2,1)S(1)} %pad_maximum_fusion.4.refs_1_, bf16[4,16,1024]{2,1,0:T(8,128)(2,1)S(1)} %collective-permute-done.6.refs_2_, bf16[4,16,1024]{2,1,0:T(8,128)(2,1)S(1)} %collective-permute-done.7.refs_3_, ...), custom_call_target="tpu_custom_call" | custom-call | tf_op jit(solution)/shard_map/project/pallas_call | solution.py:213
  (5 shorter events, 0.1 us)
Async XLA Ops:
  0.0 13.1 %copy-start.3 = (bf16[32,192]{1,0:T(8,128)(2,1)S(1)}, bf16[32,192]{1,0:T(8,128)(2,1)}, u32[]{:S(2)}) copy-start(bf16[32,192]{1,0:T(8,128)(2,1)} %constant.44.clone.refs_5_) | copy-start | bytes 36868
  0.0 13.1 %copy-start.1 = (bf16[256,512]{1,0:T(8,128)(2,1)S(1)}, bf16[256,512]{1,0:T(8,128)(2,1)}, u32[]{:S(2)}) copy-start(bf16[256,512]{1,0:T(8,128)(2,1)} %constant.43.clone.refs_4_) | copy-start | bytes 786436
  0.0 13.1 %copy-start.2 = (f32[32,256]{1,0:T(8,128)S(1)}, f32[32,256]{1,0:T(8,128)}, u32[]{:S(2)}) copy-start(f32[32,256]{1,0:T(8,128)} %constant.42.clone.refs_3_) | copy-start | bytes 98308
  0.0 13.1 %copy-start.4 = (bf16[64,96]{1,0:T(8,128)(2,1)S(1)}, bf16[64,96]{1,0:T(8,128)(2,1)}, u32[]{:S(2)}) copy-start(bf16[64,96]{1,0:T(8,128)(2,1)} %constant.41.clone.refs_2_) | copy-start | bytes 36868
  0.0 13.1 %copy-start.5 = (f32[64]{0:T(128)S(1)}, f32[64]{0:T(128)}, u32[]{:S(2)}) copy-start(f32[64]{0:T(128)} %refs_1_.1) | copy-start | bytes 772
  0.0 38.6 %copy-start = (bf16[1024,512]{1,0:T(8,128)(2,1)S(1)}, bf16[1024,512]{1,0:T(8,128)(2,1)}, u32[]{:S(2)}) copy-start(bf16[1024,512]{1,0:T(8,128)(2,1)} %refs_0_.2) | copy-start | bytes 3145732
  2.2 6.9 %collective-permute-start = (bf16[4,16,1024]{2,1,0:T(8,128)(2,1)S(1)}, bf16[4,16,1024]{2,1,0:T(8,128)(2,1)S(1)}, u32[]{:S(2)}, u32[]{:S(2)}) collective-permute-start(bf16[4,16,1024]{2,1,0:T(8,128)(2,1)S(1)} %pad_maximum_fusion.1), channel_id=1, source_target_pairs={{0,8},{8,0},{16,24},{24,16},{1,9},{9,1},{17,25},{25,17},{2,10},{10... | collective-permute-start | bytes 393224 | tf_op jit(solution)/shard_map/ppermute | solution.py:261
  5.2 7.8 %collective-permute-start.1 = (bf16[4,16,1024]{2,1,0:T(8,128)(2,1)S(1)}, bf16[4,16,1024]{2,1,0:T(8,128)(2,1)S(1)}, u32[]{:S(2)}, u32[]{:S(2)}) collective-permute-start(bf16[4,16,1024]{2,1,0:T(8,128)(2,1)S(1)} %pad_maximum_fusion.2), channel_id=1, source_target_pairs={{0,16},{8,24},{16,0},{24,8},{1,17},{9,25},{17,1},{25,9},{2,18},{10... | collective-permute-start | bytes 393224 | tf_op jit(solution)/shard_map/ppermute | solution.py:261
  6.9 6.2 %collective-permute-start.2 = (bf16[4,16,1024]{2,1,0:T(8,128)(2,1)S(1)}, bf16[4,16,1024]{2,1,0:T(8,128)(2,1)S(1)}, u32[]{:S(2)}, u32[]{:S(2)}) collective-permute-start(bf16[4,16,1024]{2,1,0:T(8,128)(2,1)S(1)} %pad_maximum_fusion.3), channel_id=1, source_target_pairs={{0,24},{8,16},{16,8},{24,0},{1,25},{9,17},{17,9},{25,1},{2,26},{10... | collective-permute-start | bytes 393224 | tf_op jit(solution)/shard_map/ppermute | solution.py:261
  18.3 4.3 %collective-permute-start.3 = (bf16[16,1024]{1,0:T(8,128)(2,1)S(1)}, bf16[16,1024]{1,0:T(8,128)(2,1)S(1)}, u32[]{:S(2)}, u32[]{:S(2)}) collective-permute-start(bf16[16,1024]{1,0:T(8,128)(2,1)S(1)} %get-tuple-element.10), channel_id=1, source_target_pairs={{0,8},{8,0},{16,24},{24,16},{1,9},{9,1},{17,25},{25,17},{2,10},{10... | collective-permute-start | bytes 98312 | tf_op jit(solution)/shard_map/ppermute | solution.py:267
  19.5 3.9 %collective-permute-start.4 = (bf16[16,1024]{1,0:T(8,128)(2,1)S(1)}, bf16[16,1024]{1,0:T(8,128)(2,1)S(1)}, u32[]{:S(2)}, u32[]{:S(2)}) collective-permute-start(bf16[16,1024]{1,0:T(8,128)(2,1)S(1)} %get-tuple-element.11), channel_id=1, source_target_pairs={{0,16},{8,24},{16,0},{24,8},{1,17},{9,25},{17,1},{25,9},{2,18},{10... | collective-permute-start | bytes 98312 | tf_op jit(solution)/shard_map/ppermute | solution.py:267
  20.4 4.8 %collective-permute-start.5 = (bf16[16,1024]{1,0:T(8,128)(2,1)S(1)}, bf16[16,1024]{1,0:T(8,128)(2,1)S(1)}, u32[]{:S(2)}, u32[]{:S(2)}) collective-permute-start(bf16[16,1024]{1,0:T(8,128)(2,1)S(1)} %get-tuple-element.12), channel_id=1, source_target_pairs={{0,24},{8,16},{16,8},{24,0},{1,25},{9,17},{17,9},{25,1},{2,26},{10... | collective-permute-start | bytes 98312 | tf_op jit(solution)/shard_map/ppermute | solution.py:267
  25.3 7.8 %collective-permute-start.8 = (bf16[4,16,1024]{2,1,0:T(8,128)(2,1)S(1)}, bf16[4,16,1024]{2,1,0:T(8,128)(2,1)S(1)}, u32[]{:S(2)}, u32[]{:S(2)}) collective-permute-start(bf16[4,16,1024]{2,1,0:T(8,128)(2,1)S(1)} %pad_maximum_fusion.4.refs_1_), channel_id=1, source_target_pairs={{0,6},{1,7},{2,4},{3,5},{4,2},{5,3},{6,0},{7,1},{8,14},{9,15},{10,... | collective-permute-start | bytes 393224 | tf_op jit(solution)/shard_map/ppermute | solution.py:272
  28.9 8.1 %collective-permute-start.7 = (bf16[4,16,1024]{2,1,0:T(8,128)(2,1)S(1)}, bf16[4,16,1024]{2,1,0:T(8,128)(2,1)S(1)}, u32[]{:S(2)}, u32[]{:S(2)}) collective-permute-start(bf16[4,16,1024]{2,1,0:T(8,128)(2,1)S(1)} %pad_maximum_fusion.4.refs_1_), channel_id=1, source_target_pairs={{0,4},{1,5},{2,6},{3,7},{4,0},{5,1},{6,2},{7,3},{8,12},{9,13},{10,... | collective-permute-start | bytes 393224 | tf_op jit(solution)/shard_map/ppermute | solution.py:272
  29.0 8.1 %collective-permute-start.6 = (bf16[4,16,1024]{2,1,0:T(8,128)(2,1)S(1)}, bf16[4,16,1024]{2,1,0:T(8,128)(2,1)S(1)}, u32[]{:S(2)}, u32[]{:S(2)}) collective-permute-start(bf16[4,16,1024]{2,1,0:T(8,128)(2,1)S(1)} %pad_maximum_fusion.4.refs_1_), channel_id=1, source_target_pairs={{0,2},{1,3},{2,0},{3,1},{4,6},{5,7},{6,4},{7,5},{8,10},{9,11},{10,... | collective-permute-start | bytes 393224 | tf_op jit(solution)/shard_map/ppermute | solution.py:272
  29.7 7.8 %collective-permute-start.9 = (bf16[4,16,1024]{2,1,0:T(8,128)(2,1)S(1)}, bf16[4,16,1024]{2,1,0:T(8,128)(2,1)S(1)}, u32[]{:S(2)}, u32[]{:S(2)}) collective-permute-start(bf16[4,16,1024]{2,1,0:T(8,128)(2,1)S(1)} %pad_maximum_fusion.4.refs_1_), channel_id=1, source_target_pairs={{0,1},{1,0},{2,3},{3,2},{4,5},{5,4},{6,7},{7,6},{8,9},{9,8},{10,11... | collective-permute-start | bytes 393224 | tf_op jit(solution)/shard_map/ppermute | solution.py:275
  33.0 4.5 %collective-permute-start.12 = (bf16[4,16,1024]{2,1,0:T(8,128)(2,1)S(1)}, bf16[4,16,1024]{2,1,0:T(8,128)(2,1)S(1)}, u32[]{:S(2)}, u32[]{:S(2)}) collective-permute-start(bf16[4,16,1024]{2,1,0:T(8,128)(2,1)S(1)} %collective-permute-done.8.refs_4_), channel_id=1, source_target_pairs={{0,1},{1,0},{2,3},{3,2},{4,5},{5,4},{6,7},{7,6},{8,9},{9,8},{10,11... | collective-permute-start | bytes 393224 | tf_op jit(solution)/shard_map/ppermute | solution.py:275
  37.0 1.3 %collective-permute-start.11 = (bf16[4,16,1024]{2,1,0:T(8,128)(2,1)S(1)}, bf16[4,16,1024]{2,1,0:T(8,128)(2,1)S(1)}, u32[]{:S(2)}, u32[]{:S(2)}) collective-permute-start(bf16[4,16,1024]{2,1,0:T(8,128)(2,1)S(1)} %collective-permute-done.7.refs_3_), channel_id=1, source_target_pairs={{0,1},{1,0},{2,3},{3,2},{4,5},{5,4},{6,7},{7,6},{8,9},{9,8},{10,11... | collective-permute-start | bytes 393224 | tf_op jit(solution)/shard_map/ppermute | solution.py:275
  37.0 1.5 %collective-permute-start.10 = (bf16[4,16,1024]{2,1,0:T(8,128)(2,1)S(1)}, bf16[4,16,1024]{2,1,0:T(8,128)(2,1)S(1)}, u32[]{:S(2)}, u32[]{:S(2)}) collective-permute-start(bf16[4,16,1024]{2,1,0:T(8,128)(2,1)S(1)} %collective-permute-done.6.refs_2_), channel_id=1, source_target_pairs={{0,1},{1,0},{2,3},{3,2},{4,5},{5,4},{6,7},{7,6},{8,9},{9,8},{10,11... | collective-permute-start | bytes 393224 | tf_op jit(solution)/shard_map/ppermute | solution.py:275

commit v2 on v1

v2 whole, which is shorter than its diff:
```python
import math

import numpy as np

import jax
import jax.numpy as jnp
from jax import lax
from jax.experimental import pallas as pl
from jax.experimental.pallas import tpu as pltpu
from jax.sharding import PartitionSpec as P

LANES = 128
PAD = 8
LANE_V = 16
LANE_Q = 32


def split_table(table):
    high = table.astype(jnp.bfloat16)
    low = (table - high.astype(np.float64)).astype(jnp.bfloat16)
    return high, low


def dft_tables(rows):
    total = 2 * rows * LANES
    block = np.arange(rows, dtype=np.float64)
    freq = np.arange(rows, dtype=np.float64) + 0.5
    lane = np.arange(LANES, dtype=np.float64)
    head = 2.0 * math.pi * np.outer(freq, block) / (2 * rows)
    first = np.concatenate(
        split_table(np.concatenate([np.cos(head), -np.sin(head)], axis=0)), axis=1
    )
    turn = 2.0 * math.pi * np.outer(freq, lane) / total
    twist = np.concatenate([np.cos(turn), np.sin(turn)], axis=1).astype(np.float32)
    inner = 2.0 * math.pi * np.outer(lane, lane) / LANES
    square = np.block([[np.cos(inner), -np.sin(inner)], [np.sin(inner), np.cos(inner)]])
    second = np.concatenate(split_table(square), axis=1)
    tail = head.T
    tail_high, tail_low = split_table(
        (2.0 / total) * np.concatenate([np.cos(tail), np.sin(tail)], axis=1)
    )
    last = np.concatenate([tail_high, tail_high, tail_low], axis=1)
    return first, twist, second, last


def halves(value):
    high = value.astype(jnp.bfloat16)
    low = (value - high.astype(jnp.float32)).astype(jnp.bfloat16)
    return high, low


def dot(left, right):
    return jnp.dot(left, right, preferred_element_type=jnp.float32)


def rolled_taps(values, taps):
    total = taps[:, :1] * values
    for shift in range(1, taps.shape[1]):
        total = total + taps[:, shift : shift + 1] * pltpu.roll(values, shift, 1)
    return total


def in_hbm(*arrays):
    return [pltpu.with_memory_space_constraint(array, pltpu.HBM) for array in arrays]


def tables_kernel(count, *refs):
    sources, skip_ref = refs[:count], refs[count]
    outs, column_ref = refs[count + 2 : 2 * count + 2], refs[2 * count + 2]
    skips, sems = refs[2 * count + 3 :]
    moves = [
        pltpu.make_async_copy(source, out, sems.at[index])
        for index, (source, out) in enumerate(zip(sources, outs))
    ]
    moves.append(pltpu.make_async_copy(skip_ref, skips, sems.at[count]))
    for move in moves:
        move.start()
    moves[count].wait()
    column_ref[...] = jnp.broadcast_to(skips[...].reshape(1, -1), (8, skips.shape[0])).T
    for move in moves[:count]:
        move.wait()


def near_tables(rows, skip_gain, after):
    tables = dft_tables(rows)
    count = len(tables)
    far = pl.BlockSpec(memory_space=pltpu.HBM)
    near = pl.BlockSpec(memory_space=pltpu.VMEM)
    return pl.pallas_call(
        lambda *refs: tables_kernel(count, *refs),
        out_shape=[jax.ShapeDtypeStruct(table.shape, table.dtype) for table in tables]
        + [jax.ShapeDtypeStruct((skip_gain.shape[0], 8), jnp.float32)],
        in_specs=[far] * (count + 1) + [near],
        out_specs=[near] * (count + 1),
        scratch_shapes=[
            pltpu.VMEM(skip_gain.shape, jnp.float32),
            pltpu.SemaphoreType.DMA((count + 1,)),
        ],
        compiler_params=pltpu.CompilerParams(vmem_limit_bytes=16 << 20),
        name="near_tables",
    )(*in_hbm(*[jnp.asarray(table) for table in tables], skip_gain), after)


def pack_kernel(nodes, chans, qkv_ref, filter_ref, flat_ref, *refs):
    outs = refs[:nodes]
    query_ref, taps_ref = refs[nodes : nodes + 2]
    filters, streams, flat, sems = refs[nodes + 2 :]
    place = lax.axis_index("ctx")
    block = qkv_ref.shape[2]
    rim = taps_ref.shape[2] - 1
    moves = [
        pltpu.make_async_copy(flat_ref, flat, sems.at[3]),
        pltpu.make_async_copy(qkv_ref.at[pl.ds(1, 2)], streams, sems.at[0]),
        pltpu.make_async_copy(qkv_ref.at[0], query_ref, sems.at[1]),
        pltpu.make_async_copy(filter_ref, filters, sems.at[2]),
    ]
    for move in moves:
        move.start()
    lane = lax.broadcasted_iota(jnp.int32, (chans, LANES), 1)

    def place_at(tile, source, target, size, under):
        moved = pltpu.roll(tile, (target - source) % LANES, 1)
        return jnp.where((lane >= target) & (lane < target + size), moved, under)

    moves[0].wait()
    for stream in range(3):
        taps_ref[stream] = flat[stream].T
    moves[1].wait()
    for mask in range(nodes):
        rows = pl.ds(pl.multiple_of((place ^ mask) * chans, chans), chans)
        edge = jnp.zeros((chans, LANES), jnp.float32)
        product = None
        for stream in range(2):
            values = streams[stream, rows, :].astype(jnp.float32)
            at = stream * LANE_V
            edge = place_at(values[:, block - LANES :], LANES - rim, at, rim, edge)
            edge = place_at(values[:, :LANES], 0, at + rim, rim, edge)
            featured = rolled_taps(values, taps_ref[1 + stream, rows, :])
            product = featured if product is None else product * featured
        outs[mask][:, :block] = product.astype(jnp.bfloat16)
        outs[mask][:, 2 * block :] = edge.astype(jnp.bfloat16)
    moves[2].wait()
    queries = jnp.zeros((chans, LANES), jnp.float32)
    for share in range(nodes):
        tile = query_ref[share * chans : (share + 1) * chans, block - LANES :]
        queries = place_at(
            tile.astype(jnp.float32), LANES - rim, LANE_Q + share * rim, rim, queries
        )
    for mask in range(nodes):
        edge = outs[mask][:, 2 * block :].astype(jnp.float32)
        outs[mask][:, 2 * block :] = jnp.where(lane >= LANE_Q, queries, edge).astype(jnp.bfloat16)
    moves[3].wait()
    for mask in range(nodes):
        rows = pl.ds(pl.multiple_of((place ^ mask) * chans, chans), chans)
        outs[mask][:, block : 2 * block] = filters[rows, :].astype(jnp.bfloat16)


def pack(qkv, long_filter, short_taps, nodes, chans):
    _, every, block = qkv.shape
    far = pl.BlockSpec(memory_space=pltpu.HBM)
    near = pl.BlockSpec(memory_space=pltpu.VMEM)
    flat = jnp.swapaxes(short_taps, 1, 2)
    *pieces, query, taps = pl.pallas_call(
        lambda *refs: pack_kernel(nodes, chans, *refs),
        out_shape=[jax.ShapeDtypeStruct((chans, 2 * block + LANES), jnp.bfloat16)] * nodes
        + [
            jax.ShapeDtypeStruct((every, block), jnp.bfloat16),
            jax.ShapeDtypeStruct(short_taps.shape, jnp.float32),
        ],
        in_specs=[far] * 3,
        out_specs=[near] * (nodes + 2),
        scratch_shapes=[
            pltpu.VMEM((every, block), jnp.float32),
            pltpu.VMEM((2, every, block), jnp.bfloat16),
            pltpu.VMEM(flat.shape, jnp.float32),
            pltpu.SemaphoreType.DMA((4,)),
        ],
        compiler_params=pltpu.CompilerParams(vmem_limit_bytes=16 << 20),
        name="pack",
    )(*in_hbm(qkv, long_filter, flat))
    return pieces, query, taps


def query_kernel(nodes, query_ref, taps_ref, *refs):
    pieces = refs[:nodes]
    out_ref = refs[nodes]
    place = lax.axis_index("ctx")
    _, chans, block = out_ref.shape
    rim = taps_ref.shape[2] - 1
    lane = lax.broadcasted_iota(jnp.int32, (chans, LANES), 1)
    edge = jnp.zeros((chans, LANES), jnp.float32)
    for mask in range(1, nodes):
        before = (place ^ mask) == place - 1
        found = pieces[mask][:, pieces[mask].shape[1] - LANES :].astype(jnp.float32)
        edge = jnp.where(before, found, edge)
    for mask in range(nodes):
        share = place ^ mask
        rows = pl.ds(pl.multiple_of(share * chans, chans), chans)
        taps = taps_ref[0, rows, :]
        values = query_ref[rows, :].astype(jnp.float32)
        history = pltpu.roll(edge, LANES - LANE_Q - (share + 1) * rim, 1)
        first = taps[:, :1] * values[:, :LANES]
        for shift in range(1, rim + 1):
            joined = jnp.where(lane >= LANES - shift, history, values[:, :LANES])
            first = first + taps[:, shift : shift + 1] * pltpu.roll(joined, shift, 1)
        out_ref[mask] = rolled_taps(values, taps)
        out_ref[mask, :, :LANES] = first


def query_features(query, short_taps, pieces, nodes, chans):
    near = pl.BlockSpec(memory_space=pltpu.VMEM)
    return pl.pallas_call(
        lambda *refs: query_kernel(nodes, *refs),
        out_shape=jax.ShapeDtypeStruct((nodes, chans, query.shape[1]), jnp.float32),
        in_specs=[near] * (2 + nodes),
        out_specs=near,
        compiler_params=pltpu.CompilerParams(vmem_limit_bytes=16 << 20),
        name="query_features",
    )(query, short_taps, *pieces)


def long_kernel(
    nodes, chans, per_node, repair, taps_ref, first_ref, twist_ref, second_ref, last_ref, skip_ref, *refs
):
    pieces = refs[:nodes]
    outs = refs[nodes : 2 * nodes]
    raw, edges, mid, spec, unturned, final = refs[2 * nodes :]
    rows = nodes * per_node
    pitch = rows + PAD
    place = lax.axis_index("ctx")
    base = place * chans
    block = per_node * LANES

    for mask in range(nodes):
        start = (place ^ mask) * per_node
        for part in range(2):
            for tile in range(per_node):
                at = part * block + tile * LANES
                raw[part, pl.ds(start + tile, chans, stride=pitch), :] = pieces[mask][
                    :, at : at + LANES
                ].astype(jnp.float32)
        if repair:
            edges[(place ^ mask) + 1] = pieces[mask][:, 2 * block :].astype(jnp.float32)
    if repair:
        rim = taps_ref.shape[2] - 1
        lane = lax.broadcasted_iota(jnp.int32, (chans, LANES), 1)
        own = pl.ds(pl.multiple_of(base, chans), chans)
        edges[0] = jnp.zeros((chans, LANES), jnp.float32)
        for node in range(nodes):
            before, now = edges[node], edges[node + 1]
            product = None
            for stream in range(2):
                back = (LANES - stream * LANE_V) % LANES
                joined = jnp.where(lane < stream * LANE_V + rim, before, now)
                if back:
                    joined = pltpu.roll(joined, back, 1)
                featured = rolled_taps(joined, taps_ref[1 + stream, own, :])
                product = featured if product is None else product * featured
            product = pltpu.roll(product, LANES - rim, 1).astype(jnp.bfloat16).astype(jnp.float32)
            spot = pl.ds(node * per_node, chans, stride=pitch)
            raw[0, spot, :] = jnp.where(lane < rim, product, raw[0, spot, :])

    cos_twist = twist_ref[:, :LANES]
    sin_twist = twist_ref[:, LANES:]
    for chan in range(chans):
        span = slice(chan * pitch, chan * pitch + rows)
        both = jnp.concatenate([raw[0, span, :], raw[1, span, :]], axis=1).astype(jnp.bfloat16)
        section = dot(first_ref[...], jnp.concatenate([both, both], axis=0))
        for part in range(2):
            real = section[:rows, part * LANES : (part + 1) * LANES]
            imag = section[rows:, part * LANES : (part + 1) * LANES]
            turned = jnp.concatenate(
                [
                    real * cos_twist + imag * sin_twist,
                    imag * cos_twist - real * sin_twist,
                ],
                axis=1,
            )
            high, low = halves(turned)
            at = (part * chans + chan) * rows
            mid[0, at : at + rows, :] = high
            mid[1, at : at + rows, :] = low

    def inner(high, low):
        table_high = second_ref[:, : 2 * LANES]
        table_low = second_ref[:, 2 * LANES :]
        return dot(high, table_high) + dot(low, table_high) + dot(high, table_low)

    spec[...] = inner(mid[0], mid[1])
    for chan in range(chans):
        sig = spec[chan * rows : (chan + 1) * rows, :]
        fil = spec[(chans + chan) * rows : (chans + chan + 1) * rows, :]
        sig_real, sig_imag = sig[:, :LANES], sig[:, LANES:]
        fil_real, fil_imag = fil[:, :LANES], fil[:, LANES:]
        joined = jnp.concatenate(
            [
                sig_real * fil_real - sig_imag * fil_imag,
                -(sig_real * fil_imag + sig_imag * fil_real),
            ],
            axis=1,
        )
        high, low = halves(joined)
        mid[0, chan * rows : (chan + 1) * rows, :] = high
        mid[1, chan * rows : (chan + 1) * rows, :] = low
    skips = skip_ref[pl.ds(pl.multiple_of(base, chans), chans), :]
    half = chans * rows
    unturned[...] = inner(mid[0, :half, :], mid[1, :half, :])
    for chan in range(chans):
        back = unturned[chan * rows : (chan + 1) * rows, :]
        real, imag = back[:, :LANES], back[:, LANES:]
        turned = jnp.concatenate(
            [real * cos_twist + imag * sin_twist, imag * cos_twist - real * sin_twist], axis=0
        )
        high, low = halves(turned)
        convolved = dot(last_ref[...], jnp.concatenate([high, low, high], axis=0))
        product = raw[0, chan * pitch : chan * pitch + rows, :]
        final[chan * rows : (chan + 1) * rows, :] = convolved + skips[chan : chan + 1, :1] * product
    for mask in range(nodes):
        start = (place ^ mask) * per_node
        for tile in range(per_node):
            outs[mask][:, tile * LANES : (tile + 1) * LANES] = final[
                pl.ds(start + tile, chans, stride=rows), :
            ].astype(jnp.bfloat16)


def long_mix(pieces, taps, tables, block):
    nodes = len(pieces)
    chans, width = pieces[0].shape
    per_node = block // LANES
    rows = nodes * per_node
    near = pl.BlockSpec(memory_space=pltpu.VMEM)
    return pl.pallas_call(
        lambda *refs: long_kernel(nodes, chans, per_node, width > 2 * block, *refs),
        out_shape=[jax.ShapeDtypeStruct((chans, block), jnp.bfloat16)] * nodes,
        in_specs=[near] * (1 + len(tables) + nodes),
        out_specs=[near] * nodes,
        scratch_shapes=[
            pltpu.VMEM((2, chans * (rows + PAD), LANES), jnp.float32),
            pltpu.VMEM((nodes + 1, chans, LANES), jnp.float32),
            pltpu.VMEM((2, 2 * chans * rows, 2 * LANES), jnp.bfloat16),
            pltpu.VMEM((2 * chans * rows, 2 * LANES), jnp.float32),
            pltpu.VMEM((chans * rows, 2 * LANES), jnp.float32),
            pltpu.VMEM((chans * rows, LANES), jnp.float32),
        ],
        compiler_params=pltpu.CompilerParams(vmem_limit_bytes=24 << 20),
        name="long_mix",
    )(taps, *tables, *pieces)


def project_kernel(nodes, weight_ref, *refs):
    stacks = (len(refs) - 4) // 2
    blocks = refs[: 2 * stacks]
    out_ref, gathered, held, sems = refs[2 * stacks :]
    place = lax.axis_index("ctx")
    spot = lax.axis_index("ch")
    chans = blocks[0].shape[1]
    for index in range(2 * stacks):
        owner = spot ^ (2 * (index % stacks) + index // stacks)
        for mask in range(nodes):
            row = (owner * nodes + (place ^ mask)) * chans
            gathered[pl.ds(pl.multiple_of(row, chans), chans), :] = blocks[index][mask]

    parts = held.shape[0]
    rows = held.shape[1]
    copies = []
    for part in range(parts):
        span = slice(part * rows, (part + 1) * rows)
        held[part] = dot(weight_ref[span, :], gathered[...]).astype(jnp.bfloat16)
        copies.append(
            pltpu.make_async_copy(held.at[part], out_ref.at[pl.ds(part * rows, rows), :], sems.at[part])
        )
        copies[-1].start()
    for copy in copies:
        copy.wait()


def project(blocks, out_weight, parts):
    nodes, _, block = blocks[0].shape
    features, channels = out_weight.shape
    whole = pl.BlockSpec(memory_space=pltpu.VMEM)
    return pl.pallas_call(
        lambda *refs: project_kernel(nodes, *refs),
        out_shape=jax.ShapeDtypeStruct((features, block), jnp.bfloat16),
        in_specs=[whole] * (1 + len(blocks)),
        out_specs=pl.BlockSpec(memory_space=pl.ANY),
        scratch_shapes=[
            pltpu.VMEM((channels, block), jnp.bfloat16),
            pltpu.VMEM((parts, features // parts, block), jnp.bfloat16),
            pltpu.SemaphoreType.DMA((parts,)),
        ],
        compiler_params=pltpu.CompilerParams(vmem_limit_bytes=16 << 20),
        name="project",
    )(out_weight, *blocks)


def project_plain(blocks, out_weight):
    nodes, chans, block = blocks[0].shape
    stacks = len(blocks) // 2
    place = lax.axis_index("ctx")
    spot = lax.axis_index("ch")
    found = jnp.stack(blocks).reshape(2, stacks, nodes, chans, block)
    index = jnp.arange(2 * stacks, dtype=jnp.int32) ^ spot
    found = found[index % 2, index // 2]
    found = found[:, jnp.arange(nodes, dtype=jnp.int32) ^ place]
    summed = jnp.dot(
        out_weight, found.reshape(-1, block), preferred_element_type=jnp.float32
    )
    return summed.astype(jnp.bfloat16)


def features_plain(qkv, short_taps):
    block = qkv.shape[2]
    tap_count = short_taps.shape[2]
    devices = lax.axis_size("ctx")
    route = [(i, i + 1) for i in range(devices - 1)]
    history = lax.ppermute(qkv[:, :, block - (tap_count - 1) :], "ctx", route)
    extended = jnp.concatenate([history, qkv], axis=2).astype(jnp.float32)
    result = jnp.zeros(qkv.shape, jnp.float32)
    for offset in range(tap_count):
        begin = tap_count - 1 - offset
        result = (
            result
            + short_taps[:, :, offset : offset + 1] * extended[:, :, begin : begin + block]
        )
    return result


def swapped(block, mask, axis):
    if mask == 0:
        return block
    return lax.ppermute(block, axis, [(i, i ^ mask) for i in range(lax.axis_size(axis))])


def local(qkv, short_taps, long_filter, skip_gain, out_weight):
    nodes = lax.axis_size("ctx")
    spread = lax.axis_size("ch")
    stacks = spread // 2
    place = lax.axis_index("ctx")
    _, every, block = qkv.shape
    chans = every // nodes
    fits = chans % 16 == 0

    if fits:
        pieces, query, taps = pack(qkv, long_filter, short_taps, nodes, chans)
    else:
        taps = short_taps
        query, key, value = features_plain(qkv, short_taps)
        both = jnp.concatenate([key * value, long_filter], axis=1).astype(jnp.bfloat16)
        both = both.reshape(nodes, chans, 2 * block)
        pieces = [lax.dynamic_index_in_dim(both, place ^ mask, 0, False) for mask in range(nodes)]
    pieces = [swapped(pieces[mask], mask, "ctx") for mask in range(nodes)]
    tables = near_tables(nodes * block // LANES, skip_gain, pieces[0])
    mixed = long_mix(pieces, taps, tables, block)

    if fits:
        tied = lax.optimization_barrier((pieces, mixed[0]))[0]
        featured = query_features(query, taps, tied, nodes, chans)
    else:
        featured = query.reshape(nodes, chans, block)[jnp.arange(nodes, dtype=jnp.int32) ^ place]
    mixed = jnp.stack([swapped(mixed[mask], mask, "ctx") for mask in range(nodes)])
    gated = (featured * mixed.astype(jnp.float32)).astype(jnp.bfloat16)

    column = [swapped(gated, 2 * depth, "ch") for depth in range(stacks)]
    blocks = column + [swapped(part, 1, "ch") for part in column]
    if fits:
        return project(blocks, out_weight, 4)
    return project_plain(blocks, out_weight)


def solution(mesh):
    placed = (P(None, "ch", "ctx"), P(None, "ch", None), P("ch", "ctx"), P("ch"), P("ch", None))
    return jax.shard_map(
        local, mesh=mesh, in_specs=placed, out_specs=P("ch", "ctx"), check_vma=False
    )
```

time: 41.8 us -> 36 us (0.86)
  local copies, waits for them, and re-layouts: 2.97 us -> 0.01 us
  waiting for transfers between devices: 17 us -> 14.4 us
    ppermute x13, waiting for transfers between devices: 17 us -> 14.4 us  [swapped(): lax.ppermute(block, axis, [(i, i ^ mask) for i in range(lax.axis_size(axi...]
    squeeze x1 -> x0, local copies, waits for them, and re-layouts: 1.08 us -> none  [local(): lax.dynamic_index_in_dim(by_node, target, 1, False)]
    convert_element_type x1 -> x0, local copies, waits for them, and re-layouts: 1.06 us -> none  [local(): lax.dynamic_index_in_dim(filters, target, 0, True).astype(jnp.bfloat16)]
    unnamed x13 -> x2, local copies, waits for them, and re-layouts: 0.84 us -> 0.01 us
    pallas_call x2 -> x5, Pallas kernels: 8.23 us -> 8.24 us  [the longest x1 2.54 us: long_mix(): pl.pallas_call(lambda *refs: long_kernel(nodes, chans, per_node, width >...]
  transfers between devices with their start and end apart: 13 -> 13, of which waited for: 9 -> 8; matrix products, arithmetic and copies ran while one was open for 2% -> 0% of each run, Pallas kernels for 0% -> 4%
where the time goes in v2:
time: 36 us; the launch traced here: 35.9 us
  waiting for transfers between devices  14.4 us (40%)
  starting transfers between devices  13.1 us (36%)
  Pallas kernels  8.24 us (23%)
    ppermute x13, waiting for transfers between devices, swapped(): lax.ppermute(block, axis, [(i, i ^ mask) for i in range(lax.axis_size(axi...  14.4 us
    ppermute x13, starting transfers between devices, swapped(): lax.ppermute(block, axis, [(i, i ^ mask) for i in range(lax.axis_size(axi...  13.1 us
    pallas_call x1, Pallas kernels, long_mix(): pl.pallas_call(lambda *refs: long_kernel(nodes, chans, per_node, width >...  2.54 us
    pallas_call x1, Pallas kernels, project(): pl.pallas_call(lambda *refs: project_kernel(nodes, *refs), out_shape=jax....  2.17 us
    pallas_call x1, Pallas kernels, pack(): pl.pallas_call(lambda *refs: pack_kernel(nodes, chans, *refs), out_shape=...  2.03 us
    pallas_call x1, Pallas kernels, near_tables(): pl.pallas_call(lambda *refs: tables_kernel(count, *refs), out_shape=[jax....  1.03 us
  transfers between devices with their start and end apart: 13, of which 8 were waited for; matrix products, arithmetic and copies ran while one was open for 0% of the time, Pallas kernels for 4%

profile of v2, /device:TPU:0, one launch (start us, length us, event | category | flops | bytes accessed | tf_op | source)
XLA Modules:
  0.0 35.9 jit_solution(2998760422337459268)
XLA Ops:
  0.0 0.0 copy-start
  0.0 2.0 %pack.1 = (bf16[16,2176]{1,0:T(8,128)(2,1)S(1)}, bf16[16,2176]{1,0:T(8,128)(2,1)S(1)}, bf16[16,2176]{1,0:T(8,128)(2,1)S(1)}, bf16[16,2176]{1,0:T(8,128)(2,1)S(1)...) custom-call(bf16[3,64,1024]{2,1,0:T(8,128)(2,1)} %refs_0_.3, f32[64,1024]{1,0:T(8,128)} %refs_1_.2, ...), custom_call_target="tpu_custom_call" | custom-call | tf_op jit(solution)/shard_map/pack/pallas_call | solution.py:163
  2.0 3.0 %collective-permute-start = (bf16[16,2176]{1,0:T(8,128)(2,1)S(1)}, bf16[16,2176]{1,0:T(8,128)(2,1)S(1)}, u32[]{:S(2)}, u32[]{:S(2)}) collective-permute-start(bf16[16,2176]{1,0:T(8,128)(2,1)S(1)} %get-tuple-element.27), channel_id=1, source_target_pairs={{0,8},{8,0},{16,24},{24,16},{1,9},{9,1},{17,25},{25,17},{2,10},{10... | collective-permute-start | bytes 208904 | tf_op jit(solution)/shard_map/ppermute | solution.py:431
  5.0 1.5 %collective-permute-start.1 = (bf16[16,2176]{1,0:T(8,128)(2,1)S(1)}, bf16[16,2176]{1,0:T(8,128)(2,1)S(1)}, u32[]{:S(2)}, u32[]{:S(2)}) collective-permute-start(bf16[16,2176]{1,0:T(8,128)(2,1)S(1)} %get-tuple-element.28), channel_id=1, source_target_pairs={{0,16},{8,24},{16,0},{24,8},{1,17},{9,25},{17,1},{25,9},{2,18},{10... | collective-permute-start | bytes 208904 | tf_op jit(solution)/shard_map/ppermute | solution.py:431
  6.6 0.0 collective-permute-start.2
  6.6 1.0 %near_tables.1 = (bf16[64,64]{1,0:T(8,128)(2,1)S(1)}, f32[32,256]{1,0:T(8,128)S(1)}, bf16[256,512]{1,0:T(8,128)(2,1)S(1)}, bf16[32,192]{1,0:T(8,128)(2,1)S(1)}, f32[64,8]{1,0:T(8,128)S(1)}) custom-call(bf16[64,64]{1,0:T(8,128)(2,1)} %constant.8.clone.refs_0_, f32[32,256]{1,0:T(8,128)} %constant.9.clone.refs_1_, bf16[256,512]{1,0:T(8,128)(2,1)} %constant.10.clone.refs_2_, ...), custom_call_target="tpu_custom_call" | custom-call | tf_op jit(solution)/shard_map/near_tables/pallas_call | solution.py:89
  7.6 0.0 collective-permute-done.refs_7_.refs_3_
  7.6 1.7 %collective-permute-done.1.refs_8_.refs_4_ = bf16[16,2176]{1,0:T(8,128)(2,1)S(1)} collective-permute-done((bf16[16,2176]{1,0:T(8,128)(2,1)S(1)}, bf16[16,2176]{1,0:T(8,128)(2,1)S(1)}, u32[]{:S(2)}, u32[]{:S(2)}) %collective-permute-start.1) | collective-permute-done | bytes 69664 | tf_op jit(solution)/shard_map/ppermute | solution.py:431
  9.4 2.4 %collective-permute-done.2.refs_9_.refs_5_ = bf16[16,2176]{1,0:T(8,128)(2,1)S(1)} collective-permute-done((bf16[16,2176]{1,0:T(8,128)(2,1)S(1)}, bf16[16,2176]{1,0:T(8,128)(2,1)S(1)}, u32[]{:S(2)}, u32[]{:S(2)}) %collective-permute-start.2) | collective-permute-done | bytes 69664 | tf_op jit(solution)/shard_map/ppermute | solution.py:431
  11.8 2.5 %long_mix.1 = (bf16[16,1024]{1,0:T(8,128)(2,1)S(1)}, bf16[16,1024]{1,0:T(8,128)(2,1)S(1)}, bf16[16,1024]{1,0:T(8,128)(2,1)S(1)}, bf16[16,1024]{1,0:T(8,128)(2,1)S(1)}) custom-call(f32[3,64,7]{2,1,0:T(8,128)S(1)} %get-tuple-element.25.refs_0_.refs_1_, bf16[64,64]{1,0:T(8,128)(2,1)S(1)} %get-tuple-element.30.refs_1_, f32[32,256]{1,0:T(8,128)S(1)} %get-tuple-element.31.refs_2_, ...), custom_call_target="tpu_custom_call" | custom-call | tf_op jit(solution)/shard_map/long_mix/pallas_call | solution.py:332
  14.3 0.6 %collective-permute-start.3 = (bf16[16,1024]{1,0:T(8,128)(2,1)S(1)}, bf16[16,1024]{1,0:T(8,128)(2,1)S(1)}, u32[]{:S(2)}, u32[]{:S(2)}) collective-permute-start(bf16[16,1024]{1,0:T(8,128)(2,1)S(1)} %get-tuple-element.40), channel_id=1, source_target_pairs={{0,8},{8,0},{16,24},{24,16},{1,9},{9,1},{17,25},{25,17},{2,10},{10... | collective-permute-start | bytes 98312 | tf_op jit(solution)/shard_map/ppermute | solution.py:431
  14.9 0.4 %collective-permute-start.4 = (bf16[16,1024]{1,0:T(8,128)(2,1)S(1)}, bf16[16,1024]{1,0:T(8,128)(2,1)S(1)}, u32[]{:S(2)}, u32[]{:S(2)}) collective-permute-start(bf16[16,1024]{1,0:T(8,128)(2,1)S(1)} %get-tuple-element.41), channel_id=1, source_target_pairs={{0,16},{8,24},{16,0},{24,8},{1,17},{9,25},{17,1},{25,9},{2,18},{10... | collective-permute-start | bytes 98312 | tf_op jit(solution)/shard_map/ppermute | solution.py:431
  15.3 2.6 %collective-permute-start.5 = (bf16[16,1024]{1,0:T(8,128)(2,1)S(1)}, bf16[16,1024]{1,0:T(8,128)(2,1)S(1)}, u32[]{:S(2)}, u32[]{:S(2)}) collective-permute-start(bf16[16,1024]{1,0:T(8,128)(2,1)S(1)} %get-tuple-element.42), channel_id=1, source_target_pairs={{0,24},{8,16},{16,8},{24,0},{1,25},{9,17},{17,9},{25,1},{2,26},{10... | collective-permute-start | bytes 98312 | tf_op jit(solution)/shard_map/ppermute | solution.py:431
  17.9 0.5 %query_features.1 = f32[4,16,1024]{2,1,0:T(8,128)S(1)} custom-call(bf16[64,1024]{1,0:T(8,128)(2,1)S(1)} %get-tuple-element.24.refs_0_, f32[3,64,7]{2,1,0:T(8,128)S(1)} %get-tuple-element.25.refs_0_.refs_1_, bf16[16,2176]{1,0:T(8,128)(2,1)S(1)} %get-tuple-element.36.refs_5_.refs_6_.refs_2_, bf16[16,2176]{1,0:T(8,128)(2,1)S(1)} %collective-permute-done.refs_7_.refs_3_, ...), custom_call_target="tpu_custom_call" | custom-call | tf_op jit(solution)/shard_map/query_features/pallas_call | solution.py:212
  18.4 0.0 collective-permute-done.3
  18.4 0.5 %collective-permute-done.4 = bf16[16,1024]{1,0:T(8,128)(2,1)S(1)} collective-permute-done((bf16[16,1024]{1,0:T(8,128)(2,1)S(1)}, bf16[16,1024]{1,0:T(8,128)(2,1)S(1)}, u32[]{:S(2)}, u32[]{:S(2)}) %collective-permute-start.4) | collective-permute-done | bytes 32800 | tf_op jit(solution)/shard_map/ppermute | solution.py:431
  18.8 1.3 %collective-permute-done.5 = bf16[16,1024]{1,0:T(8,128)(2,1)S(1)} collective-permute-done((bf16[16,1024]{1,0:T(8,128)(2,1)S(1)}, bf16[16,1024]{1,0:T(8,128)(2,1)S(1)}, u32[]{:S(2)}, u32[]{:S(2)}) %collective-permute-start.5) | collective-permute-done | bytes 32800 | tf_op jit(solution)/shard_map/ppermute | solution.py:431
  20.2 3.8 %collective-permute-start.8 = (bf16[4,16,1024]{2,1,0:T(8,128)(2,1)S(1)}, bf16[4,16,1024]{2,1,0:T(8,128)(2,1)S(1)}, u32[]{:S(2)}, u32[]{:S(2)}) collective-permute-start(bf16[4,16,1024]{2,1,0:T(8,128)(2,1)S(1)} %multiply_convert_fusion.refs_1_), channel_id=1, source_target_pairs={{0,6},{1,7},{2,4},{3,5},{4,2},{5,3},{6,0},{7,1},{8,14},{9,15},{10,... | collective-permute-start | bytes 393224 | tf_op jit(solution)/shard_map/ppermute | solution.py:431
  24.0 0.0 collective-permute-start.7
  24.0 0.6 %collective-permute-start.6 = (bf16[4,16,1024]{2,1,0:T(8,128)(2,1)S(1)}, bf16[4,16,1024]{2,1,0:T(8,128)(2,1)S(1)}, u32[]{:S(2)}, u32[]{:S(2)}) collective-permute-start(bf16[4,16,1024]{2,1,0:T(8,128)(2,1)S(1)} %multiply_convert_fusion.refs_1_), channel_id=1, source_target_pairs={{0,2},{1,3},{2,0},{3,1},{4,6},{5,7},{6,4},{7,5},{8,10},{9,11},{10,... | collective-permute-start | bytes 393224 | tf_op jit(solution)/shard_map/ppermute | solution.py:431
  24.6 0.0 collective-permute-start.9
  24.6 3.7 %collective-permute-done.8.refs_4_ = bf16[4,16,1024]{2,1,0:T(8,128)(2,1)S(1)} collective-permute-done((bf16[4,16,1024]{2,1,0:T(8,128)(2,1)S(1)}, bf16[4,16,1024]{2,1,0:T(8,128)(2,1)S(1)}, u32[]{:S(2)}, u32[]{:S(2)}) %collective-permute-start.8) | collective-permute-done | bytes 131104 | tf_op jit(solution)/shard_map/ppermute | solution.py:431
  28.3 0.0 collective-permute-start.12
  28.3 3.9 %collective-permute-done.7.refs_3_ = bf16[4,16,1024]{2,1,0:T(8,128)(2,1)S(1)} collective-permute-done((bf16[4,16,1024]{2,1,0:T(8,128)(2,1)S(1)}, bf16[4,16,1024]{2,1,0:T(8,128)(2,1)S(1)}, u32[]{:S(2)}, u32[]{:S(2)}) %collective-permute-start.7) | collective-permute-done | bytes 131104 | tf_op jit(solution)/shard_map/ppermute | solution.py:431
  32.2 0.0 collective-permute-start.11
  32.2 0.0 collective-permute-done.6.refs_2_
  32.2 0.5 %collective-permute-start.10 = (bf16[4,16,1024]{2,1,0:T(8,128)(2,1)S(1)}, bf16[4,16,1024]{2,1,0:T(8,128)(2,1)S(1)}, u32[]{:S(2)}, u32[]{:S(2)}) collective-permute-start(bf16[4,16,1024]{2,1,0:T(8,128)(2,1)S(1)} %collective-permute-done.6.refs_2_), channel_id=1, source_target_pairs={{0,1},{1,0},{2,3},{3,2},{4,5},{5,4},{6,7},{7,6},{8,9},{9,8},{10,11... | collective-permute-start | bytes 393224 | tf_op jit(solution)/shard_map/ppermute | solution.py:431
  32.7 0.0 collective-permute-done.9.refs_5_
  32.7 0.0 collective-permute-done.12.refs_8_
  32.7 0.8 %collective-permute-done.11.refs_7_ = bf16[4,16,1024]{2,1,0:T(8,128)(2,1)S(1)} collective-permute-done((bf16[4,16,1024]{2,1,0:T(8,128)(2,1)S(1)}, bf16[4,16,1024]{2,1,0:T(8,128)(2,1)S(1)}, u32[]{:S(2)}, u32[]{:S(2)}) %collective-permute-start.11) | collective-permute-done | bytes 131104 | tf_op jit(solution)/shard_map/ppermute | solution.py:431
  33.5 0.2 collective-permute-done.10.refs_6_
  33.7 0.0 copy-done
  33.7 2.2 %project.1 = bf16[1024,1024]{1,0:T(8,128)(2,1)} custom-call(bf16[1024,512]{1,0:T(8,128)(2,1)S(1)} %copy-done, bf16[4,16,1024]{2,1,0:T(8,128)(2,1)S(1)} %multiply_convert_fusion.refs_1_, bf16[4,16,1024]{2,1,0:T(8,128)(2,1)S(1)} %collective-permute-done.6.refs_2_, bf16[4,16,1024]{2,1,0:T(8,128)(2,1)S(1)} %collective-permute-done.7.refs_3_, ...), custom_call_target="tpu_custom_call" | custom-call | tf_op jit(solution)/shard_map/project/pallas_call | solution.py:381
  (1 shorter events, 0.0 us)
Async XLA Ops:
  0.0 33.7 %copy-start = (bf16[1024,512]{1,0:T(8,128)(2,1)S(1)}, bf16[1024,512]{1,0:T(8,128)(2,1)}, u32[]{:S(2)}) copy-start(bf16[1024,512]{1,0:T(8,128)(2,1)} %refs_0_.4) | copy-start | bytes 3145732
  2.0 5.6 %collective-permute-start = (bf16[16,2176]{1,0:T(8,128)(2,1)S(1)}, bf16[16,2176]{1,0:T(8,128)(2,1)S(1)}, u32[]{:S(2)}, u32[]{:S(2)}) collective-permute-start(bf16[16,2176]{1,0:T(8,128)(2,1)S(1)} %get-tuple-element.27), channel_id=1, source_target_pairs={{0,8},{8,0},{16,24},{24,16},{1,9},{9,1},{17,25},{25,17},{2,10},{10... | collective-permute-start | bytes 208904 | tf_op jit(solution)/shard_map/ppermute | solution.py:431
  5.0 4.3 %collective-permute-start.1 = (bf16[16,2176]{1,0:T(8,128)(2,1)S(1)}, bf16[16,2176]{1,0:T(8,128)(2,1)S(1)}, u32[]{:S(2)}, u32[]{:S(2)}) collective-permute-start(bf16[16,2176]{1,0:T(8,128)(2,1)S(1)} %get-tuple-element.28), channel_id=1, source_target_pairs={{0,16},{8,24},{16,0},{24,8},{1,17},{9,25},{17,1},{25,9},{2,18},{10... | collective-permute-start | bytes 208904 | tf_op jit(solution)/shard_map/ppermute | solution.py:431
  6.6 5.2 %collective-permute-start.2 = (bf16[16,2176]{1,0:T(8,128)(2,1)S(1)}, bf16[16,2176]{1,0:T(8,128)(2,1)S(1)}, u32[]{:S(2)}, u32[]{:S(2)}) collective-permute-start(bf16[16,2176]{1,0:T(8,128)(2,1)S(1)} %get-tuple-element.29), channel_id=1, source_target_pairs={{0,24},{8,16},{16,8},{24,0},{1,25},{9,17},{17,9},{25,1},{2,26},{10... | collective-permute-start | bytes 208904 | tf_op jit(solution)/shard_map/ppermute | solution.py:431
  14.3 4.0 %collective-permute-start.3 = (bf16[16,1024]{1,0:T(8,128)(2,1)S(1)}, bf16[16,1024]{1,0:T(8,128)(2,1)S(1)}, u32[]{:S(2)}, u32[]{:S(2)}) collective-permute-start(bf16[16,1024]{1,0:T(8,128)(2,1)S(1)} %get-tuple-element.40), channel_id=1, source_target_pairs={{0,8},{8,0},{16,24},{24,16},{1,9},{9,1},{17,25},{25,17},{2,10},{10... | collective-permute-start | bytes 98312 | tf_op jit(solution)/shard_map/ppermute | solution.py:431
  14.9 3.9 %collective-permute-start.4 = (bf16[16,1024]{1,0:T(8,128)(2,1)S(1)}, bf16[16,1024]{1,0:T(8,128)(2,1)S(1)}, u32[]{:S(2)}, u32[]{:S(2)}) collective-permute-start(bf16[16,1024]{1,0:T(8,128)(2,1)S(1)} %get-tuple-element.41), channel_id=1, source_target_pairs={{0,16},{8,24},{16,0},{24,8},{1,17},{9,25},{17,1},{25,9},{2,18},{10... | collective-permute-start | bytes 98312 | tf_op jit(solution)/shard_map/ppermute | solution.py:431
  15.3 4.8 %collective-permute-start.5 = (bf16[16,1024]{1,0:T(8,128)(2,1)S(1)}, bf16[16,1024]{1,0:T(8,128)(2,1)S(1)}, u32[]{:S(2)}, u32[]{:S(2)}) collective-permute-start(bf16[16,1024]{1,0:T(8,128)(2,1)S(1)} %get-tuple-element.42), channel_id=1, source_target_pairs={{0,24},{8,16},{16,8},{24,0},{1,25},{9,17},{17,9},{25,1},{2,26},{10... | collective-permute-start | bytes 98312 | tf_op jit(solution)/shard_map/ppermute | solution.py:431
  20.2 8.1 %collective-permute-start.8 = (bf16[4,16,1024]{2,1,0:T(8,128)(2,1)S(1)}, bf16[4,16,1024]{2,1,0:T(8,128)(2,1)S(1)}, u32[]{:S(2)}, u32[]{:S(2)}) collective-permute-start(bf16[4,16,1024]{2,1,0:T(8,128)(2,1)S(1)} %multiply_convert_fusion.refs_1_), channel_id=1, source_target_pairs={{0,6},{1,7},{2,4},{3,5},{4,2},{5,3},{6,0},{7,1},{8,14},{9,15},{10,... | collective-permute-start | bytes 393224 | tf_op jit(solution)/shard_map/ppermute | solution.py:431
  24.0 8.2 %collective-permute-start.7 = (bf16[4,16,1024]{2,1,0:T(8,128)(2,1)S(1)}, bf16[4,16,1024]{2,1,0:T(8,128)(2,1)S(1)}, u32[]{:S(2)}, u32[]{:S(2)}) collective-permute-start(bf16[4,16,1024]{2,1,0:T(8,128)(2,1)S(1)} %multiply_convert_fusion.refs_1_), channel_id=1, source_target_pairs={{0,4},{1,5},{2,6},{3,7},{4,0},{5,1},{6,2},{7,3},{8,12},{9,13},{10,... | collective-permute-start | bytes 393224 | tf_op jit(solution)/shard_map/ppermute | solution.py:431
  24.0 8.2 %collective-permute-start.6 = (bf16[4,16,1024]{2,1,0:T(8,128)(2,1)S(1)}, bf16[4,16,1024]{2,1,0:T(8,128)(2,1)S(1)}, u32[]{:S(2)}, u32[]{:S(2)}) collective-permute-start(bf16[4,16,1024]{2,1,0:T(8,128)(2,1)S(1)} %multiply_convert_fusion.refs_1_), channel_id=1, source_target_pairs={{0,2},{1,3},{2,0},{3,1},{4,6},{5,7},{6,4},{7,5},{8,10},{9,11},{10,... | collective-permute-start | bytes 393224 | tf_op jit(solution)/shard_map/ppermute | solution.py:431
  24.6 8.1 %collective-permute-start.9 = (bf16[4,16,1024]{2,1,0:T(8,128)(2,1)S(1)}, bf16[4,16,1024]{2,1,0:T(8,128)(2,1)S(1)}, u32[]{:S(2)}, u32[]{:S(2)}) collective-permute-start(bf16[4,16,1024]{2,1,0:T(8,128)(2,1)S(1)} %multiply_convert_fusion.refs_1_), channel_id=1, source_target_pairs={{0,1},{1,0},{2,3},{3,2},{4,5},{5,4},{6,7},{7,6},{8,9},{9,8},{10,11... | collective-permute-start | bytes 393224 | tf_op jit(solution)/shard_map/ppermute | solution.py:431
  28.3 4.4 %collective-permute-start.12 = (bf16[4,16,1024]{2,1,0:T(8,128)(2,1)S(1)}, bf16[4,16,1024]{2,1,0:T(8,128)(2,1)S(1)}, u32[]{:S(2)}, u32[]{:S(2)}) collective-permute-start(bf16[4,16,1024]{2,1,0:T(8,128)(2,1)S(1)} %collective-permute-done.8.refs_4_), channel_id=1, source_target_pairs={{0,1},{1,0},{2,3},{3,2},{4,5},{5,4},{6,7},{7,6},{8,9},{9,8},{10,11... | collective-permute-start | bytes 393224 | tf_op jit(solution)/shard_map/ppermute | solution.py:431
  32.2 1.3 %collective-permute-start.11 = (bf16[4,16,1024]{2,1,0:T(8,128)(2,1)S(1)}, bf16[4,16,1024]{2,1,0:T(8,128)(2,1)S(1)}, u32[]{:S(2)}, u32[]{:S(2)}) collective-permute-start(bf16[4,16,1024]{2,1,0:T(8,128)(2,1)S(1)} %collective-permute-done.7.refs_3_), channel_id=1, source_target_pairs={{0,1},{1,0},{2,3},{3,2},{4,5},{5,4},{6,7},{7,6},{8,9},{9,8},{10,11... | collective-permute-start | bytes 393224 | tf_op jit(solution)/shard_map/ppermute | solution.py:431
  32.2 1.5 %collective-permute-start.10 = (bf16[4,16,1024]{2,1,0:T(8,128)(2,1)S(1)}, bf16[4,16,1024]{2,1,0:T(8,128)(2,1)S(1)}, u32[]{:S(2)}, u32[]{:S(2)}) collective-permute-start(bf16[4,16,1024]{2,1,0:T(8,128)(2,1)S(1)} %collective-permute-done.6.refs_2_), channel_id=1, source_target_pairs={{0,1},{1,0},{2,3},{3,2},{4,5},{5,4},{6,7},{7,6},{8,9},{9,8},{10,11... | collective-permute-start | bytes 393224 | tf_op jit(solution)/shard_map/ppermute | solution.py:431

commit v3 on v2

--- a/solution.py
+++ b/solution.py
@@ -34,7 +34,8 @@
     twist = np.concatenate([np.cos(turn), np.sin(turn)], axis=1).astype(np.float32)
     inner = 2.0 * math.pi * np.outer(lane, lane) / LANES
     square = np.block([[np.cos(inner), -np.sin(inner)], [np.sin(inner), np.cos(inner)]])
-    second = np.concatenate(split_table(square), axis=1)
+    square_high, square_low = split_table(square)
+    second = np.concatenate([square_high, square_high, square_low], axis=0)
     tail = head.T
     tail_high, tail_low = split_table(
         (2.0 / total) * np.concatenate([np.cos(tail), np.sin(tail)], axis=1)
@@ -81,8 +82,8 @@
         move.wait()
 
 
-def near_tables(rows, skip_gain, after):
-    tables = dft_tables(rows)
+def near_tables(rows, skip_gain, out_weight, after):
+    tables = [out_weight] + [jnp.asarray(table) for table in dft_tables(rows)]
     count = len(tables)
     far = pl.BlockSpec(memory_space=pltpu.HBM)
     near = pl.BlockSpec(memory_space=pltpu.VMEM)
@@ -98,7 +99,7 @@
         ],
         compiler_params=pltpu.CompilerParams(vmem_limit_bytes=16 << 20),
         name="near_tables",
-    )(*in_hbm(*[jnp.asarray(table) for table in tables], skip_gain), after)
+    )(*in_hbm(*tables, skip_gain), after)
 
 
 def pack_kernel(nodes, chans, qkv_ref, filter_ref, flat_ref, *refs):
@@ -109,12 +110,21 @@
     block = qkv_ref.shape[2]
     rim = taps_ref.shape[2] - 1
     moves = [
-        pltpu.make_async_copy(flat_ref, flat, sems.at[3]),
-        pltpu.make_async_copy(qkv_ref.at[pl.ds(1, 2)], streams, sems.at[0]),
+        pltpu.make_async_copy(flat_ref, flat, sems.at[0]),
         pltpu.make_async_copy(qkv_ref.at[0], query_ref, sems.at[1]),
         pltpu.make_async_copy(filter_ref, filters, sems.at[2]),
     ]
-    for move in moves:
+    shares = [
+        pl.ds(pl.multiple_of((place ^ mask) * chans, chans), chans)
+        for mask in reversed(range(nodes))
+    ]
+    arrivals = [
+        pltpu.make_async_copy(
+            qkv_ref.at[pl.ds(1, 2), rows, :], streams.at[:, rows, :], sems.at[3 + index]
+        )
+        for index, rows in enumerate(shares)
+    ]
+    for move in moves[:1] + arrivals + moves[1:]:
         move.start()
     lane = lax.broadcasted_iota(jnp.int32, (chans, LANES), 1)
 
@@ -125,9 +135,9 @@
     moves[0].wait()
     for stream in range(3):
         taps_ref[stream] = flat[stream].T
-    moves[1].wait()
-    for mask in range(nodes):
-        rows = pl.ds(pl.multiple_of((place ^ mask) * chans, chans), chans)
+    for index, rows in enumerate(shares):
+        mask = nodes - 1 - index
+        arrivals[index].wait()
         edge = jnp.zeros((chans, LANES), jnp.float32)
         product = None
         for stream in range(2):
@@ -139,7 +149,7 @@
             product = featured if product is None else product * featured
         outs[mask][:, :block] = product.astype(jnp.bfloat16)
         outs[mask][:, 2 * block :] = edge.astype(jnp.bfloat16)
-    moves[2].wait()
+    moves[1].wait()
     queries = jnp.zeros((chans, LANES), jnp.float32)
     for share in range(nodes):
         tile = query_ref[share * chans : (share + 1) * chans, block - LANES :]
@@ -149,9 +159,9 @@
     for mask in range(nodes):
         edge = outs[mask][:, 2 * block :].astype(jnp.float32)
         outs[mask][:, 2 * block :] = jnp.where(lane >= LANE_Q, queries, edge).astype(jnp.bfloat16)
-    moves[3].wait()
-    for mask in range(nodes):
-        rows = pl.ds(pl.multiple_of((place ^ mask) * chans, chans), chans)
+    moves[2].wait()
+    for index, rows in enumerate(shares):
+        mask = nodes - 1 - index
         outs[mask][:, block : 2 * block] = filters[rows, :].astype(jnp.bfloat16)
 
 
@@ -173,7 +183,7 @@
             pltpu.VMEM((every, block), jnp.float32),
             pltpu.VMEM((2, every, block), jnp.bfloat16),
             pltpu.VMEM(flat.shape, jnp.float32),
-            pltpu.SemaphoreType.DMA((4,)),
+            pltpu.SemaphoreType.DMA((3 + nodes,)),
         ],
         compiler_params=pltpu.CompilerParams(vmem_limit_bytes=16 << 20),
         name="pack",
@@ -282,9 +292,7 @@
             mid[1, at : at + rows, :] = low
 
     def inner(high, low):
-        table_high = second_ref[:, : 2 * LANES]
-        table_low = second_ref[:, 2 * LANES :]
-        return dot(high, table_high) + dot(low, table_high) + dot(high, table_low)
+        return dot(jnp.concatenate([high, low, high], axis=1), second_ref[...])
 
     spec[...] = inner(mid[0], mid[1])
     for chan in range(chans):
@@ -314,12 +322,12 @@
         high, low = halves(turned)
         convolved = dot(last_ref[...], jnp.concatenate([high, low, high], axis=0))
         product = raw[0, chan * pitch : chan * pitch + rows, :]
-        final[chan * rows : (chan + 1) * rows, :] = convolved + skips[chan : chan + 1, :1] * product
+        final[chan * pitch : chan * pitch + rows, :] = convolved + skips[chan : chan + 1, :1] * product
     for mask in range(nodes):
         start = (place ^ mask) * per_node
         for tile in range(per_node):
             outs[mask][:, tile * LANES : (tile + 1) * LANES] = final[
-                pl.ds(start + tile, chans, stride=rows), :
+                pl.ds(start + tile, chans, stride=pitch), :
             ].astype(jnp.bfloat16)
 
 
@@ -340,57 +348,95 @@
             pltpu.VMEM((2, 2 * chans * rows, 2 * LANES), jnp.bfloat16),
             pltpu.VMEM((2 * chans * rows, 2 * LANES), jnp.float32),
             pltpu.VMEM((chans * rows, 2 * LANES), jnp.float32),
-            pltpu.VMEM((chans * rows, LANES), jnp.float32),
+            pltpu.VMEM((chans * (rows + PAD), LANES), jnp.float32),
         ],
         compiler_params=pltpu.CompilerParams(vmem_limit_bytes=24 << 20),
         name="long_mix",
     )(taps, *tables, *pieces)
 
 
-def project_kernel(nodes, weight_ref, *refs):
-    stacks = (len(refs) - 4) // 2
-    blocks = refs[: 2 * stacks]
-    out_ref, gathered, held, sems = refs[2 * stacks :]
+def gather_blocks(depths, blocks, gathered):
     place = lax.axis_index("ctx")
     spot = lax.axis_index("ch")
-    chans = blocks[0].shape[1]
-    for index in range(2 * stacks):
-        owner = spot ^ (2 * (index % stacks) + index // stacks)
+    level, core = spot // 2, spot % 2
+    for index, block in enumerate(blocks):
+        nodes, chans, _ = block.shape
+        side = core ^ (index % 2)
         for mask in range(nodes):
-            row = (owner * nodes + (place ^ mask)) * chans
-            gathered[pl.ds(pl.multiple_of(row, chans), chans), :] = blocks[index][mask]
-
-    parts = held.shape[0]
-    rows = held.shape[1]
+            row = ((2 * (index // 2) + side) * nodes + (place ^ mask)) * chans
+            gathered[pl.ds(pl.multiple_of(row, chans), chans), :] = block[mask]
+    width = 2 * nodes * chans
+    return [pl.ds(pl.multiple_of((level ^ depth) * width, width), width) for depth in depths]
+
+
+def partial_kernel(depths, rows, weight_ref, *refs):
+    blocks = refs[: 2 * len(depths)]
+    out_ref, gathered = refs[2 * len(depths) :]
+    columns = gather_blocks(depths, blocks, gathered)
+    for begin in range(0, out_ref.shape[0], rows):
+        weight = jnp.concatenate([weight_ref[begin : begin + rows, at] for at in columns], axis=1)
+        out_ref[begin : begin + rows, :] = dot(weight, gathered[...])
+
+
+def final_kernel(depths, cuts, weight_ref, partial_ref, *refs):
+    blocks = refs[: 2 * len(depths)]
+    out_ref, gathered, held, sems = refs[2 * len(depths) :]
+    columns = gather_blocks(depths, blocks, gathered)
     copies = []
-    for part in range(parts):
-        span = slice(part * rows, (part + 1) * rows)
-        held[part] = dot(weight_ref[span, :], gathered[...]).astype(jnp.bfloat16)
+    for part, (begin, end) in enumerate(zip(cuts, cuts[1:])):
+        weight = jnp.concatenate([weight_ref[begin:end, at] for at in columns], axis=1)
+        total = partial_ref[begin:end, :] + dot(weight, gathered[...])
+        held[begin:end, :] = total.astype(jnp.bfloat16)
+        rows = pl.ds(begin, end - begin)
         copies.append(
-            pltpu.make_async_copy(held.at[part], out_ref.at[pl.ds(part * rows, rows), :], sems.at[part])
+            pltpu.make_async_copy(held.at[rows, :], out_ref.at[rows, :], sems.at[part])
         )
         copies[-1].start()
     for copy in copies:
         copy.wait()
 
 
-def project(blocks, out_weight, parts):
-    nodes, _, block = blocks[0].shape
-    features, channels = out_weight.shape
-    whole = pl.BlockSpec(memory_space=pltpu.VMEM)
+def project_early(early, out_weight):
+    features, _ = out_weight.shape
+    near = pl.BlockSpec(memory_space=pltpu.VMEM)
+    blocks = [block for pair in early.values() for block in pair]
+    nodes, chans, block = blocks[0].shape
+    depth = nodes * chans * len(blocks)
+    cost = pl.CostEstimate(
+        flops=0, bytes_accessed=0, transcendentals=0
+    )
     return pl.pallas_call(
-        lambda *refs: project_kernel(nodes, *refs),
+        lambda *refs: partial_kernel(tuple(early), features // 4, *refs),
+        out_shape=jax.ShapeDtypeStruct((features, block), jnp.float32),
+        in_specs=[near] * (1 + len(blocks)),
+        out_specs=near,
+        scratch_shapes=[pltpu.VMEM((depth, block), jnp.bfloat16)],
+        compiler_params=pltpu.CompilerParams(vmem_limit_bytes=16 << 20),
+        cost_estimate=cost,
+        name="project_early",
+    )(out_weight, *blocks)
+
+
+def project_late(partial, late, out_weight):
+    features, _ = out_weight.shape
+    near = pl.BlockSpec(memory_space=pltpu.VMEM)
+    blocks = [block for pair in late.values() for block in pair]
+    nodes, chans, block = blocks[0].shape
+    depth = nodes * chans * len(blocks)
+    cuts = tuple(range(0, features + 1, features // 8))
+    return pl.pallas_call(
+        lambda *refs: final_kernel(tuple(late), cuts, *refs),
         out_shape=jax.ShapeDtypeStruct((features, block), jnp.bfloat16),
-        in_specs=[whole] * (1 + len(blocks)),
+        in_specs=[near] * (2 + len(blocks)),
         out_specs=pl.BlockSpec(memory_space=pl.ANY),
         scratch_shapes=[
-            pltpu.VMEM((channels, block), jnp.bfloat16),
-            pltpu.VMEM((parts, features // parts, block), jnp.bfloat16),
-            pltpu.SemaphoreType.DMA((parts,)),
+            pltpu.VMEM((depth, block), jnp.bfloat16),
+            pltpu.VMEM((features, block), jnp.bfloat16),
+            pltpu.SemaphoreType.DMA((len(cuts) - 1,)),
         ],
         compiler_params=pltpu.CompilerParams(vmem_limit_bytes=16 << 20),
-        name="project",
-    )(out_weight, *blocks)
+        name="project_late",
+    )(out_weight, partial, *blocks)
 
 
 def project_plain(blocks, out_weight):
@@ -449,7 +495,9 @@
         both = both.reshape(nodes, chans, 2 * block)
         pieces = [lax.dynamic_index_in_dim(both, place ^ mask, 0, False) for mask in range(nodes)]
     pieces = [swapped(pieces[mask], mask, "ctx") for mask in range(nodes)]
-    tables = near_tables(nodes * block // LANES, skip_gain, pieces[0])
+    out_weight, *tables = near_tables(
+        nodes * block // LANES, skip_gain, out_weight, pieces[0]
+    )
     mixed = long_mix(pieces, taps, tables, block)
 
     if fits:
@@ -461,10 +509,12 @@
     gated = (featured * mixed.astype(jnp.float32)).astype(jnp.bfloat16)
 
     column = [swapped(gated, 2 * depth, "ch") for depth in range(stacks)]
-    blocks = column + [swapped(part, 1, "ch") for part in column]
-    if fits:
-        return project(blocks, out_weight, 4)
-    return project_plain(blocks, out_weight)
+    if not fits:
+        return project_plain(column + [swapped(part, 1, "ch") for part in column], out_weight)
+    early = {depth: (column[depth], swapped(column[depth], 1, "ch")) for depth in (0, stacks - 1)}
+    partial = project_early(early, out_weight)
+    late = {depth: (column[depth], swapped(column[depth], 1, "ch")) for depth in range(1, stacks - 1)}
+    return project_late(partial, late, out_weight)
 
 
 def solution(mesh):

time: 36 us -> 35.3 us (0.981)
  waiting for transfers between devices: 14.4 us -> 13.3 us
  Pallas kernels: 8.24 us -> 8.7 us
    ppermute x13, waiting for transfers between devices: 14.4 us -> 13.3 us  [swapped(): lax.ppermute(block, axis, [(i, i ^ mask) for i in range(lax.axis_size(axi...]
    pallas_call x1, Pallas kernels: 1.03 us -> 1.4 us  [near_tables(): pl.pallas_call(lambda *refs: tables_kernel(count, *refs), out_shape=[jax....]
    pallas_call x1 -> x2, Pallas kernels: 2.17 us -> 2.43 us  [the longest x1 1.66 us: project_late(): pl.pallas_call(lambda *refs: final_kernel(tuple(late), cuts, *refs), out_...]
  transfers between devices with their start and end apart: 13 -> 13, of which waited for: 8 -> 8; matrix products, arithmetic and copies ran while one was open for 0% -> 0% of each run, Pallas kernels for 4% -> 7%
where the time goes in v3:
time: 35.3 us; the launch traced here: 35.2 us
  waiting for transfers between devices  13.3 us (38%)
  starting transfers between devices  13.1 us (37%)
  Pallas kernels  8.7 us (25%)
    ppermute x13, waiting for transfers between devices, swapped(): lax.ppermute(block, axis, [(i, i ^ mask) for i in range(lax.axis_size(axi...  13.3 us
    ppermute x13, starting transfers between devices, swapped(): lax.ppermute(block, axis, [(i, i ^ mask) for i in range(lax.axis_size(axi...  13.1 us
    pallas_call x1, Pallas kernels, long_mix(): pl.pallas_call(lambda *refs: long_kernel(nodes, chans, per_node, width >...  2.42 us
    pallas_call x1, Pallas kernels, pack(): pl.pallas_call(lambda *refs: pack_kernel(nodes, chans, *refs), out_shape=...  1.98 us
    pallas_call x1, Pallas kernels, project_late(): pl.pallas_call(lambda *refs: final_kernel(tuple(late), cuts, *refs), out_...  1.66 us
    pallas_call x1, Pallas kernels, near_tables(): pl.pallas_call(lambda *refs: tables_kernel(count, *refs), out_shape=[jax....  1.4 us
    pallas_call x1, Pallas kernels, project_early(): pl.pallas_call(lambda *refs: partial_kernel(tuple(early), features // 4,...  0.77 us
  transfers between devices with their start and end apart: 13, of which 8 were waited for; matrix products, arithmetic and copies ran while one was open for 0% of the time, Pallas kernels for 7%

profile of v3, /device:TPU:0, one launch (start us, length us, event | category | flops | bytes accessed | tf_op | source)
XLA Modules:
  0.0 35.2 jit_solution(2077088270773468840)
XLA Ops:
  0.0 2.0 %pack.1 = (bf16[16,2176]{1,0:T(8,128)(2,1)S(1)}, bf16[16,2176]{1,0:T(8,128)(2,1)S(1)}, bf16[16,2176]{1,0:T(8,128)(2,1)S(1)}, bf16[16,2176]{1,0:T(8,128)(2,1)S(1)...) custom-call(bf16[3,64,1024]{2,1,0:T(8,128)(2,1)} %refs_0_.2, f32[64,1024]{1,0:T(8,128)} %refs_1_.2, ...), custom_call_target="tpu_custom_call" | custom-call | tf_op jit(solution)/shard_map/pack/pallas_call | solution.py:173
  2.0 3.0 %collective-permute-start = (bf16[16,2176]{1,0:T(8,128)(2,1)S(1)}, bf16[16,2176]{1,0:T(8,128)(2,1)S(1)}, u32[]{:S(2)}, u32[]{:S(2)}) collective-permute-start(bf16[16,2176]{1,0:T(8,128)(2,1)S(1)} %get-tuple-element.29), channel_id=1, source_target_pairs={{0,8},{8,0},{16,24},{24,16},{1,9},{9,1},{17,25},{25,17},{2,10},{10... | collective-permute-start | bytes 208904 | tf_op jit(solution)/shard_map/ppermute | solution.py:477
  5.0 1.5 %collective-permute-start.1 = (bf16[16,2176]{1,0:T(8,128)(2,1)S(1)}, bf16[16,2176]{1,0:T(8,128)(2,1)S(1)}, u32[]{:S(2)}, u32[]{:S(2)}) collective-permute-start(bf16[16,2176]{1,0:T(8,128)(2,1)S(1)} %get-tuple-element.30), channel_id=1, source_target_pairs={{0,16},{8,24},{16,0},{24,8},{1,17},{9,25},{17,1},{25,9},{2,18},{10... | collective-permute-start | bytes 208904 | tf_op jit(solution)/shard_map/ppermute | solution.py:477
  6.5 0.0 collective-permute-start.2
  6.5 1.4 %near_tables.1 = (bf16[1024,512]{1,0:T(8,128)(2,1)S(1)}, bf16[64,64]{1,0:T(8,128)(2,1)S(1)}, f32[32,256]{1,0:T(8,128)S(1)}, bf16[768,256]{1,0:T(8,128)(2,1)S(1)}...) custom-call(bf16[1024,512]{1,0:T(8,128)(2,1)} %refs_0_.3, bf16[64,64]{1,0:T(8,128)(2,1)} %constant.8.clone.refs_1_, ...), custom_call_target="tpu_custom_call" | custom-call | tf_op jit(solution)/shard_map/near_tables/pallas_call | solution.py:90
  7.9 0.0 collective-permute-done.refs_7_.refs_3_
  7.9 1.4 %collective-permute-done.1.refs_8_.refs_4_ = bf16[16,2176]{1,0:T(8,128)(2,1)S(1)} collective-permute-done((bf16[16,2176]{1,0:T(8,128)(2,1)S(1)}, bf16[16,2176]{1,0:T(8,128)(2,1)S(1)}, u32[]{:S(2)}, u32[]{:S(2)}) %collective-permute-start.1) | collective-permute-done | bytes 69664 | tf_op jit(solution)/shard_map/ppermute | solution.py:477
  9.3 2.4 %collective-permute-done.2.refs_9_.refs_5_ = bf16[16,2176]{1,0:T(8,128)(2,1)S(1)} collective-permute-done((bf16[16,2176]{1,0:T(8,128)(2,1)S(1)}, bf16[16,2176]{1,0:T(8,128)(2,1)S(1)}, u32[]{:S(2)}, u32[]{:S(2)}) %collective-permute-start.2) | collective-permute-done | bytes 69664 | tf_op jit(solution)/shard_map/ppermute | solution.py:477
  11.7 2.4 %long_mix.1 = (bf16[16,1024]{1,0:T(8,128)(2,1)S(1)}, bf16[16,1024]{1,0:T(8,128)(2,1)S(1)}, bf16[16,1024]{1,0:T(8,128)(2,1)S(1)}, bf16[16,1024]{1,0:T(8,128)(2,1)S(1)}) custom-call(f32[3,64,7]{2,1,0:T(8,128)S(1)} %get-tuple-element.28.refs_0_.refs_1_, bf16[64,64]{1,0:T(8,128)(2,1)S(1)} %get-tuple-element.32.refs_1_, f32[32,256]{1,0:T(8,128)S(1)} %get-tuple-element.33.refs_2_, ...), custom_call_target="tpu_custom_call" | custom-call | tf_op jit(solution)/shard_map/long_mix/pallas_call | solution.py:340
  14.2 0.6 %collective-permute-start.3 = (bf16[16,1024]{1,0:T(8,128)(2,1)S(1)}, bf16[16,1024]{1,0:T(8,128)(2,1)S(1)}, u32[]{:S(2)}, u32[]{:S(2)}) collective-permute-start(bf16[16,1024]{1,0:T(8,128)(2,1)S(1)} %get-tuple-element.42), channel_id=1, source_target_pairs={{0,8},{8,0},{16,24},{24,16},{1,9},{9,1},{17,25},{25,17},{2,10},{10... | collective-permute-start | bytes 98312 | tf_op jit(solution)/shard_map/ppermute | solution.py:477
  14.8 0.4 %collective-permute-start.4 = (bf16[16,1024]{1,0:T(8,128)(2,1)S(1)}, bf16[16,1024]{1,0:T(8,128)(2,1)S(1)}, u32[]{:S(2)}, u32[]{:S(2)}) collective-permute-start(bf16[16,1024]{1,0:T(8,128)(2,1)S(1)} %get-tuple-element.43), channel_id=1, source_target_pairs={{0,16},{8,24},{16,0},{24,8},{1,17},{9,25},{17,1},{25,9},{2,18},{10... | collective-permute-start | bytes 98312 | tf_op jit(solution)/shard_map/ppermute | solution.py:477
  15.1 2.6 %collective-permute-start.5 = (bf16[16,1024]{1,0:T(8,128)(2,1)S(1)}, bf16[16,1024]{1,0:T(8,128)(2,1)S(1)}, u32[]{:S(2)}, u32[]{:S(2)}) collective-permute-start(bf16[16,1024]{1,0:T(8,128)(2,1)S(1)} %get-tuple-element.44), channel_id=1, source_target_pairs={{0,24},{8,16},{16,8},{24,0},{1,25},{9,17},{17,9},{25,1},{2,26},{10... | collective-permute-start | bytes 98312 | tf_op jit(solution)/shard_map/ppermute | solution.py:477
  17.7 0.5 %query_features.1 = f32[4,16,1024]{2,1,0:T(8,128)S(1)} custom-call(bf16[64,1024]{1,0:T(8,128)(2,1)S(1)} %get-tuple-element.27.refs_0_, f32[3,64,7]{2,1,0:T(8,128)S(1)} %get-tuple-element.28.refs_0_.refs_1_, bf16[16,2176]{1,0:T(8,128)(2,1)S(1)} %get-tuple-element.38.refs_6_.refs_2_, bf16[16,2176]{1,0:T(8,128)(2,1)S(1)} %collective-permute-done.refs_7_.refs_3_, ...), custom_call_target="tpu_custom_call" | custom-call | tf_op jit(solution)/shard_map/query_features/pallas_call | solution.py:222
  18.2 0.0 collective-permute-done.3
  18.2 0.5 %collective-permute-done.4 = bf16[16,1024]{1,0:T(8,128)(2,1)S(1)} collective-permute-done((bf16[16,1024]{1,0:T(8,128)(2,1)S(1)}, bf16[16,1024]{1,0:T(8,128)(2,1)S(1)}, u32[]{:S(2)}, u32[]{:S(2)}) %collective-permute-start.4) | collective-permute-done | bytes 32800 | tf_op jit(solution)/shard_map/ppermute | solution.py:477
  18.7 1.3 %collective-permute-done.5 = bf16[16,1024]{1,0:T(8,128)(2,1)S(1)} collective-permute-done((bf16[16,1024]{1,0:T(8,128)(2,1)S(1)}, bf16[16,1024]{1,0:T(8,128)(2,1)S(1)}, u32[]{:S(2)}, u32[]{:S(2)}) %collective-permute-start.5) | collective-permute-done | bytes 32800 | tf_op jit(solution)/shard_map/ppermute | solution.py:477
  20.0 3.8 %collective-permute-start.7 = (bf16[4,16,1024]{2,1,0:T(8,128)(2,1)S(1)}, bf16[4,16,1024]{2,1,0:T(8,128)(2,1)S(1)}, u32[]{:S(2)}, u32[]{:S(2)}) collective-permute-start(bf16[4,16,1024]{2,1,0:T(8,128)(2,1)S(1)} %multiply_convert_fusion.refs_1_), channel_id=1, source_target_pairs={{0,6},{1,7},{2,4},{3,5},{4,2},{5,3},{6,0},{7,1},{8,14},{9,15},{10,... | collective-permute-start | bytes 393224 | tf_op jit(solution)/shard_map/ppermute | solution.py:477
  23.8 0.0 collective-permute-start.11
  23.8 0.6 %collective-permute-start.9 = (bf16[4,16,1024]{2,1,0:T(8,128)(2,1)S(1)}, bf16[4,16,1024]{2,1,0:T(8,128)(2,1)S(1)}, u32[]{:S(2)}, u32[]{:S(2)}) collective-permute-start(bf16[4,16,1024]{2,1,0:T(8,128)(2,1)S(1)} %multiply_convert_fusion.refs_1_), channel_id=1, source_target_pairs={{0,2},{1,3},{2,0},{3,1},{4,6},{5,7},{6,4},{7,5},{8,10},{9,11},{10,... | collective-permute-start | bytes 393224 | tf_op jit(solution)/shard_map/ppermute | solution.py:477
  24.4 0.0 collective-permute-start.6
  24.4 3.7 %collective-permute-done.7.refs_3_ = bf16[4,16,1024]{2,1,0:T(8,128)(2,1)S(1)} collective-permute-done((bf16[4,16,1024]{2,1,0:T(8,128)(2,1)S(1)}, bf16[4,16,1024]{2,1,0:T(8,128)(2,1)S(1)}, u32[]{:S(2)}, u32[]{:S(2)}) %collective-permute-start.7) | collective-permute-done | bytes 131104 | tf_op jit(solution)/shard_map/ppermute | solution.py:477
  28.1 0.0 collective-permute-start.8
  28.1 3.9 %collective-permute-done.11.refs_4_ = bf16[4,16,1024]{2,1,0:T(8,128)(2,1)S(1)} collective-permute-done((bf16[4,16,1024]{2,1,0:T(8,128)(2,1)S(1)}, bf16[4,16,1024]{2,1,0:T(8,128)(2,1)S(1)}, u32[]{:S(2)}, u32[]{:S(2)}) %collective-permute-start.11) | collective-permute-done | bytes 131104 | tf_op jit(solution)/shard_map/ppermute | solution.py:477
  32.0 0.0 collective-permute-start.12
  32.0 0.0 collective-permute-done.9.refs_2_
  32.0 0.5 %collective-permute-start.10 = (bf16[4,16,1024]{2,1,0:T(8,128)(2,1)S(1)}, bf16[4,16,1024]{2,1,0:T(8,128)(2,1)S(1)}, u32[]{:S(2)}, u32[]{:S(2)}) collective-permute-start(bf16[4,16,1024]{2,1,0:T(8,128)(2,1)S(1)} %collective-permute-done.9.refs_2_), channel_id=1, source_target_pairs={{0,1},{1,0},{2,3},{3,2},{4,5},{5,4},{6,7},{7,6},{8,9},{9,8},{10,11... | collective-permute-start | bytes 393224 | tf_op jit(solution)/shard_map/ppermute | solution.py:477
  32.5 0.0 collective-permute-done.6.refs_2_
  32.5 0.0 collective-permute-done.8.refs_4_
  32.5 0.8 %project_early.1.refs_1_ = f32[1024,1024]{1,0:T(8,128)S(1)} custom-call(bf16[1024,512]{1,0:T(8,128)(2,1)S(1)} %get-tuple-element.26.refs_0_, bf16[4,16,1024]{2,1,0:T(8,128)(2,1)S(1)} %multiply_convert_fusion.refs_1_, bf16[4,16,1024]{2,1,0:T(8,128)(2,1)S(1)} %collective-permute-done.6.refs_2_, bf16[4,16,1024]{2,1,0:T(8,128)(2,1)S(1)} %collective-permute-done.7.refs_3_, ...), custom_call_target="tpu_custom_call" | custom-call | tf_op jit(solution)/shard_map/project_early/pallas_call | solution.py:408
  33.3 0.1 collective-permute-done.12.refs_5_
  33.3 0.2 collective-permute-done.10.refs_3_
  33.5 1.7 %project_late.1 = bf16[1024,1024]{1,0:T(8,128)(2,1)} custom-call(bf16[1024,512]{1,0:T(8,128)(2,1)S(1)} %get-tuple-element.26.refs_0_, f32[1024,1024]{1,0:T(8,128)S(1)} %project_early.1.refs_1_, bf16[4,16,1024]{2,1,0:T(8,128)(2,1)S(1)} %collective-permute-done.9.refs_2_, bf16[4,16,1024]{2,1,0:T(8,128)(2,1)S(1)} %collective-permute-done.10.refs_3_, ...), custom_call_target="tpu_custom_call" | custom-call | tf_op jit(solution)/shard_map/project_late/pallas_call | solution.py:427
  (1 shorter events, 0.0 us)
Async XLA Ops:
  2.0 6.0 %collective-permute-start = (bf16[16,2176]{1,0:T(8,128)(2,1)S(1)}, bf16[16,2176]{1,0:T(8,128)(2,1)S(1)}, u32[]{:S(2)}, u32[]{:S(2)}) collective-permute-start(bf16[16,2176]{1,0:T(8,128)(2,1)S(1)} %get-tuple-element.29), channel_id=1, source_target_pairs={{0,8},{8,0},{16,24},{24,16},{1,9},{9,1},{17,25},{25,17},{2,10},{10... | collective-permute-start | bytes 208904 | tf_op jit(solution)/shard_map/ppermute | solution.py:477
  5.0 4.3 %collective-permute-start.1 = (bf16[16,2176]{1,0:T(8,128)(2,1)S(1)}, bf16[16,2176]{1,0:T(8,128)(2,1)S(1)}, u32[]{:S(2)}, u32[]{:S(2)}) collective-permute-start(bf16[16,2176]{1,0:T(8,128)(2,1)S(1)} %get-tuple-element.30), channel_id=1, source_target_pairs={{0,16},{8,24},{16,0},{24,8},{1,17},{9,25},{17,1},{25,9},{2,18},{10... | collective-permute-start | bytes 208904 | tf_op jit(solution)/shard_map/ppermute | solution.py:477
  6.5 5.2 %collective-permute-start.2 = (bf16[16,2176]{1,0:T(8,128)(2,1)S(1)}, bf16[16,2176]{1,0:T(8,128)(2,1)S(1)}, u32[]{:S(2)}, u32[]{:S(2)}) collective-permute-start(bf16[16,2176]{1,0:T(8,128)(2,1)S(1)} %get-tuple-element.31), channel_id=1, source_target_pairs={{0,24},{8,16},{16,8},{24,0},{1,25},{9,17},{17,9},{25,1},{2,26},{10... | collective-permute-start | bytes 208904 | tf_op jit(solution)/shard_map/ppermute | solution.py:477
  14.2 4.0 %collective-permute-start.3 = (bf16[16,1024]{1,0:T(8,128)(2,1)S(1)}, bf16[16,1024]{1,0:T(8,128)(2,1)S(1)}, u32[]{:S(2)}, u32[]{:S(2)}) collective-permute-start(bf16[16,1024]{1,0:T(8,128)(2,1)S(1)} %get-tuple-element.42), channel_id=1, source_target_pairs={{0,8},{8,0},{16,24},{24,16},{1,9},{9,1},{17,25},{25,17},{2,10},{10... | collective-permute-start | bytes 98312 | tf_op jit(solution)/shard_map/ppermute | solution.py:477
  14.8 3.9 %collective-permute-start.4 = (bf16[16,1024]{1,0:T(8,128)(2,1)S(1)}, bf16[16,1024]{1,0:T(8,128)(2,1)S(1)}, u32[]{:S(2)}, u32[]{:S(2)}) collective-permute-start(bf16[16,1024]{1,0:T(8,128)(2,1)S(1)} %get-tuple-element.43), channel_id=1, source_target_pairs={{0,16},{8,24},{16,0},{24,8},{1,17},{9,25},{17,1},{25,9},{2,18},{10... | collective-permute-start | bytes 98312 | tf_op jit(solution)/shard_map/ppermute | solution.py:477
  15.1 4.8 %collective-permute-start.5 = (bf16[16,1024]{1,0:T(8,128)(2,1)S(1)}, bf16[16,1024]{1,0:T(8,128)(2,1)S(1)}, u32[]{:S(2)}, u32[]{:S(2)}) collective-permute-start(bf16[16,1024]{1,0:T(8,128)(2,1)S(1)} %get-tuple-element.44), channel_id=1, source_target_pairs={{0,24},{8,16},{16,8},{24,0},{1,25},{9,17},{17,9},{25,1},{2,26},{10... | collective-permute-start | bytes 98312 | tf_op jit(solution)/shard_map/ppermute | solution.py:477
  20.0 8.1 %collective-permute-start.7 = (bf16[4,16,1024]{2,1,0:T(8,128)(2,1)S(1)}, bf16[4,16,1024]{2,1,0:T(8,128)(2,1)S(1)}, u32[]{:S(2)}, u32[]{:S(2)}) collective-permute-start(bf16[4,16,1024]{2,1,0:T(8,128)(2,1)S(1)} %multiply_convert_fusion.refs_1_), channel_id=1, source_target_pairs={{0,6},{1,7},{2,4},{3,5},{4,2},{5,3},{6,0},{7,1},{8,14},{9,15},{10,... | collective-permute-start | bytes 393224 | tf_op jit(solution)/shard_map/ppermute | solution.py:477
  23.8 8.2 %collective-permute-start.11 = (bf16[4,16,1024]{2,1,0:T(8,128)(2,1)S(1)}, bf16[4,16,1024]{2,1,0:T(8,128)(2,1)S(1)}, u32[]{:S(2)}, u32[]{:S(2)}) collective-permute-start(bf16[4,16,1024]{2,1,0:T(8,128)(2,1)S(1)} %multiply_convert_fusion.refs_1_), channel_id=1, source_target_pairs={{0,4},{1,5},{2,6},{3,7},{4,0},{5,1},{6,2},{7,3},{8,12},{9,13},{10,... | collective-permute-start | bytes 393224 | tf_op jit(solution)/shard_map/ppermute | solution.py:477
  23.8 8.2 %collective-permute-start.9 = (bf16[4,16,1024]{2,1,0:T(8,128)(2,1)S(1)}, bf16[4,16,1024]{2,1,0:T(8,128)(2,1)S(1)}, u32[]{:S(2)}, u32[]{:S(2)}) collective-permute-start(bf16[4,16,1024]{2,1,0:T(8,128)(2,1)S(1)} %multiply_convert_fusion.refs_1_), channel_id=1, source_target_pairs={{0,2},{1,3},{2,0},{3,1},{4,6},{5,7},{6,4},{7,5},{8,10},{9,11},{10,... | collective-permute-start | bytes 393224 | tf_op jit(solution)/shard_map/ppermute | solution.py:477
  24.4 8.1 %collective-permute-start.6 = (bf16[4,16,1024]{2,1,0:T(8,128)(2,1)S(1)}, bf16[4,16,1024]{2,1,0:T(8,128)(2,1)S(1)}, u32[]{:S(2)}, u32[]{:S(2)}) collective-permute-start(bf16[4,16,1024]{2,1,0:T(8,128)(2,1)S(1)} %multiply_convert_fusion.refs_1_), channel_id=1, source_target_pairs={{0,1},{1,0},{2,3},{3,2},{4,5},{5,4},{6,7},{7,6},{8,9},{9,8},{10,11... | collective-permute-start | bytes 393224 | tf_op jit(solution)/shard_map/ppermute | solution.py:477
  28.1 4.4 %collective-permute-start.8 = (bf16[4,16,1024]{2,1,0:T(8,128)(2,1)S(1)}, bf16[4,16,1024]{2,1,0:T(8,128)(2,1)S(1)}, u32[]{:S(2)}, u32[]{:S(2)}) collective-permute-start(bf16[4,16,1024]{2,1,0:T(8,128)(2,1)S(1)} %collective-permute-done.7.refs_3_), channel_id=1, source_target_pairs={{0,1},{1,0},{2,3},{3,2},{4,5},{5,4},{6,7},{7,6},{8,9},{9,8},{10,11... | collective-permute-start | bytes 393224 | tf_op jit(solution)/shard_map/ppermute | solution.py:477
  32.0 1.3 %collective-permute-start.12 = (bf16[4,16,1024]{2,1,0:T(8,128)(2,1)S(1)}, bf16[4,16,1024]{2,1,0:T(8,128)(2,1)S(1)}, u32[]{:S(2)}, u32[]{:S(2)}) collective-permute-start(bf16[4,16,1024]{2,1,0:T(8,128)(2,1)S(1)} %collective-permute-done.11.refs_4_), channel_id=1, source_target_pairs={{0,1},{1,0},{2,3},{3,2},{4,5},{5,4},{6,7},{7,6},{8,9},{9,8},{10,11... | collective-permute-start | bytes 393224 | tf_op jit(solution)/shard_map/ppermute | solution.py:477
  32.0 1.5 %collective-permute-start.10 = (bf16[4,16,1024]{2,1,0:T(8,128)(2,1)S(1)}, bf16[4,16,1024]{2,1,0:T(8,128)(2,1)S(1)}, u32[]{:S(2)}, u32[]{:S(2)}) collective-permute-start(bf16[4,16,1024]{2,1,0:T(8,128)(2,1)S(1)} %collective-permute-done.9.refs_2_), channel_id=1, source_target_pairs={{0,1},{1,0},{2,3},{3,2},{4,5},{5,4},{6,7},{7,6},{8,9},{9,8},{10,11... | collective-permute-start | bytes 393224 | tf_op jit(solution)/shard_map/ppermute | solution.py:477

commit v4 on v3

--- a/solution.py
+++ b/solution.py
@@ -213,8 +213,8 @@
         for shift in range(1, rim + 1):
             joined = jnp.where(lane >= LANES - shift, history, values[:, :LANES])
             first = first + taps[:, shift : shift + 1] * pltpu.roll(joined, shift, 1)
-        out_ref[mask] = rolled_taps(values, taps)
-        out_ref[mask, :, :LANES] = first
+        out_ref[nodes - 1 - mask] = rolled_taps(values, taps)
+        out_ref[nodes - 1 - mask, :, :LANES] = first
 
 
 def query_features(query, short_taps, pieces, nodes, chans):
@@ -230,99 +230,99 @@
 
 
 def long_kernel(
-    nodes, chans, per_node, repair, taps_ref, first_ref, twist_ref, second_ref, last_ref, skip_ref, *refs
+    nodes, chans, per_node, rim, taps_ref, first_ref, twist_ref, second_ref, last_ref, skip_ref, *refs
 ):
-    pieces = refs[:nodes]
+    pieces = refs[:nodes][::-1]
     outs = refs[nodes : 2 * nodes]
-    raw, edges, mid, spec, unturned, final = refs[2 * nodes :]
+    raw, edges, final = refs[2 * nodes :]
     rows = nodes * per_node
     pitch = rows + PAD
     place = lax.axis_index("ctx")
     base = place * chans
     block = per_node * LANES
 
-    for mask in range(nodes):
-        start = (place ^ mask) * per_node
-        for part in range(2):
-            for tile in range(per_node):
-                at = part * block + tile * LANES
-                raw[part, pl.ds(start + tile, chans, stride=pitch), :] = pieces[mask][
-                    :, at : at + LANES
-                ].astype(jnp.float32)
-        if repair:
-            edges[(place ^ mask) + 1] = pieces[mask][:, 2 * block :].astype(jnp.float32)
-    if repair:
-        rim = taps_ref.shape[2] - 1
+    if rim:
         lane = lax.broadcasted_iota(jnp.int32, (chans, LANES), 1)
         own = pl.ds(pl.multiple_of(base, chans), chans)
         edges[0] = jnp.zeros((chans, LANES), jnp.float32)
-        for node in range(nodes):
-            before, now = edges[node], edges[node + 1]
-            product = None
-            for stream in range(2):
-                back = (LANES - stream * LANE_V) % LANES
-                joined = jnp.where(lane < stream * LANE_V + rim, before, now)
-                if back:
-                    joined = pltpu.roll(joined, back, 1)
-                featured = rolled_taps(joined, taps_ref[1 + stream, own, :])
-                product = featured if product is None else product * featured
-            product = pltpu.roll(product, LANES - rim, 1).astype(jnp.bfloat16).astype(jnp.float32)
-            spot = pl.ds(node * per_node, chans, stride=pitch)
-            raw[0, spot, :] = jnp.where(lane < rim, product, raw[0, spot, :])
+        for mask in range(nodes):
+            edges[(place ^ mask) + 1] = pieces[mask][:, 2 * block :].astype(jnp.float32)
+
+    def repaired(mask, tile):
+        before, now = edges[place ^ mask], pieces[mask][:, 2 * block :].astype(jnp.float32)
+        product = None
+        for stream in range(2):
+            back = (LANES - stream * LANE_V) % LANES
+            joined = jnp.where(lane < stream * LANE_V + rim, before, now)
+            if back:
+                joined = pltpu.roll(joined, back, 1)
+            featured = rolled_taps(joined, taps_ref[1 + stream, own, :])
+            product = featured if product is None else product * featured
+        product = pltpu.roll(product, LANES - rim, 1).astype(jnp.bfloat16).astype(jnp.float32)
+        return jnp.where(lane < rim, product, tile)
+
+    for part in reversed(range(2)):
+        for mask in range(nodes):
+            start = (place ^ mask) * per_node
+            for tile in range(per_node):
+                at = part * block + tile * LANES
+                values = pieces[mask][:, at : at + LANES].astype(jnp.float32)
+                if rim and at == 0:
+                    values = repaired(mask, values)
+                raw[part, pl.ds(start + tile, chans, stride=pitch), :] = values
 
     cos_twist = twist_ref[:, :LANES]
     sin_twist = twist_ref[:, LANES:]
+    skips = skip_ref[pl.ds(pl.multiple_of(base, chans), chans), :]
+
+    def inner(parts):
+        high, low = halves(jnp.concatenate(parts, axis=0))
+        return dot(jnp.concatenate([high, low, high], axis=1), second_ref[...])
+
+    def turn(real, imag, axis):
+        return jnp.concatenate(
+            [real * cos_twist + imag * sin_twist, imag * cos_twist - real * sin_twist], axis=axis
+        )
+
+    spectra = [[], []]
     for chan in range(chans):
         span = slice(chan * pitch, chan * pitch + rows)
         both = jnp.concatenate([raw[0, span, :], raw[1, span, :]], axis=1).astype(jnp.bfloat16)
         section = dot(first_ref[...], jnp.concatenate([both, both], axis=0))
         for part in range(2):
-            real = section[:rows, part * LANES : (part + 1) * LANES]
-            imag = section[rows:, part * LANES : (part + 1) * LANES]
-            turned = jnp.concatenate(
-                [
-                    real * cos_twist + imag * sin_twist,
-                    imag * cos_twist - real * sin_twist,
-                ],
-                axis=1,
-            )
-            high, low = halves(turned)
-            at = (part * chans + chan) * rows
-            mid[0, at : at + rows, :] = high
-            mid[1, at : at + rows, :] = low
-
-    def inner(high, low):
-        return dot(jnp.concatenate([high, low, high], axis=1), second_ref[...])
-
-    spec[...] = inner(mid[0], mid[1])
+            cols = slice(part * LANES, (part + 1) * LANES)
+            spectra[part].append(turn(section[:rows, cols], section[rows:, cols], 1))
+    spectra = spectra[0] + spectra[1]
+    spec = inner(spectra)
+    joined = []
     for chan in range(chans):
         sig = spec[chan * rows : (chan + 1) * rows, :]
         fil = spec[(chans + chan) * rows : (chans + chan + 1) * rows, :]
         sig_real, sig_imag = sig[:, :LANES], sig[:, LANES:]
         fil_real, fil_imag = fil[:, :LANES], fil[:, LANES:]
-        joined = jnp.concatenate(
-            [
-                sig_real * fil_real - sig_imag * fil_imag,
-                -(sig_real * fil_imag + sig_imag * fil_real),
-            ],
-            axis=1,
-        )
-        high, low = halves(joined)
-        mid[0, chan * rows : (chan + 1) * rows, :] = high
-        mid[1, chan * rows : (chan + 1) * rows, :] = low
-    skips = skip_ref[pl.ds(pl.multiple_of(base, chans), chans), :]
-    half = chans * rows
-    unturned[...] = inner(mid[0, :half, :], mid[1, :half, :])
+        joined.append(
+            jnp.concatenate(
+                [
+                    sig_real * fil_real - sig_imag * fil_imag,
+                    -(sig_real * fil_imag + sig_imag * fil_real),
+                ],
+                axis=1,
+            )
+        )
+    back = inner(joined)
+    turned = []
     for chan in range(chans):
-        back = unturned[chan * rows : (chan + 1) * rows, :]
-        real, imag = back[:, :LANES], back[:, LANES:]
-        turned = jnp.concatenate(
-            [real * cos_twist + imag * sin_twist, imag * cos_twist - real * sin_twist], axis=0
-        )
-        high, low = halves(turned)
-        convolved = dot(last_ref[...], jnp.concatenate([high, low, high], axis=0))
-        product = raw[0, chan * pitch : chan * pitch + rows, :]
-        final[chan * pitch : chan * pitch + rows, :] = convolved + skips[chan : chan + 1, :1] * product
+        real = back[chan * rows : (chan + 1) * rows, :LANES]
+        imag = back[chan * rows : (chan + 1) * rows, LANES:]
+        turned.append(turn(real, imag, 0))
+    high, low = halves(jnp.concatenate(turned, axis=1))
+    convolved = dot(last_ref[...], jnp.concatenate([high, low, high], axis=0))
+    for chan in range(chans):
+        span = slice(chan * pitch, chan * pitch + rows)
+        final[span, :] = (
+            convolved[:, chan * LANES : (chan + 1) * LANES]
+            + skips[chan : chan + 1, :1] * raw[0, span, :]
+        )
     for mask in range(nodes):
         start = (place ^ mask) * per_node
         for tile in range(per_node):
@@ -336,23 +336,21 @@
     chans, width = pieces[0].shape
     per_node = block // LANES
     rows = nodes * per_node
+    rim = taps.shape[2] - 1 if width > 2 * block else 0
     near = pl.BlockSpec(memory_space=pltpu.VMEM)
     return pl.pallas_call(
-        lambda *refs: long_kernel(nodes, chans, per_node, width > 2 * block, *refs),
+        lambda *refs: long_kernel(nodes, chans, per_node, rim, *refs),
         out_shape=[jax.ShapeDtypeStruct((chans, block), jnp.bfloat16)] * nodes,
         in_specs=[near] * (1 + len(tables) + nodes),
         out_specs=[near] * nodes,
         scratch_shapes=[
             pltpu.VMEM((2, chans * (rows + PAD), LANES), jnp.float32),
             pltpu.VMEM((nodes + 1, chans, LANES), jnp.float32),
-            pltpu.VMEM((2, 2 * chans * rows, 2 * LANES), jnp.bfloat16),
-            pltpu.VMEM((2 * chans * rows, 2 * LANES), jnp.float32),
-            pltpu.VMEM((chans * rows, 2 * LANES), jnp.float32),
             pltpu.VMEM((chans * (rows + PAD), LANES), jnp.float32),
         ],
         compiler_params=pltpu.CompilerParams(vmem_limit_bytes=24 << 20),
         name="long_mix",
-    )(taps, *tables, *pieces)
+    )(taps, *tables, *pieces[::-1])
 
 
 def gather_blocks(depths, blocks, gathered):
@@ -364,7 +362,7 @@
         side = core ^ (index % 2)
         for mask in range(nodes):
             row = ((2 * (index // 2) + side) * nodes + (place ^ mask)) * chans
-            gathered[pl.ds(pl.multiple_of(row, chans), chans), :] = block[mask]
+            gathered[pl.ds(pl.multiple_of(row, chans), chans), :] = block[nodes - 1 - mask]
     width = 2 * nodes * chans
     return [pl.ds(pl.multiple_of((level ^ depth) * width, width), width) for depth in depths]
 
@@ -447,7 +445,7 @@
     found = jnp.stack(blocks).reshape(2, stacks, nodes, chans, block)
     index = jnp.arange(2 * stacks, dtype=jnp.int32) ^ spot
     found = found[index % 2, index // 2]
-    found = found[:, jnp.arange(nodes, dtype=jnp.int32) ^ place]
+    found = found[:, nodes - 1 - (jnp.arange(nodes, dtype=jnp.int32) ^ place)]
     summed = jnp.dot(
         out_weight, found.reshape(-1, block), preferred_element_type=jnp.float32
     )
@@ -501,20 +499,20 @@
     mixed = long_mix(pieces, taps, tables, block)
 
     if fits:
-        tied = lax.optimization_barrier((pieces, mixed[0]))[0]
+        tied = lax.optimization_barrier((mixed[0], *pieces[::-1]))[:0:-1]
         featured = query_features(query, taps, tied, nodes, chans)
     else:
-        featured = query.reshape(nodes, chans, block)[jnp.arange(nodes, dtype=jnp.int32) ^ place]
-    mixed = jnp.stack([swapped(mixed[mask], mask, "ctx") for mask in range(nodes)])
+        featured = query.reshape(nodes, chans, block)[jnp.arange(nodes, dtype=jnp.int32) ^ place][::-1]
+    mixed = [swapped(mixed[mask], mask, "ctx") for mask in range(nodes)]
+    mixed = jnp.stack(mixed[::-1])
     gated = (featured * mixed.astype(jnp.float32)).astype(jnp.bfloat16)
 
     column = [swapped(gated, 2 * depth, "ch") for depth in range(stacks)]
     if not fits:
         return project_plain(column + [swapped(part, 1, "ch") for part in column], out_weight)
-    early = {depth: (column[depth], swapped(column[depth], 1, "ch")) for depth in (0, stacks - 1)}
-    partial = project_early(early, out_weight)
-    late = {depth: (column[depth], swapped(column[depth], 1, "ch")) for depth in range(1, stacks - 1)}
-    return project_late(partial, late, out_weight)
+    pairs = {depth: (part, swapped(part, 1, "ch")) for depth, part in enumerate(column)}
+    late = {depth: pairs.pop(depth) for depth in (3, 1)}
+    return project_late(project_early(pairs, out_weight), late, out_weight)
 
 
 def solution(mesh):

time: 35.3 us -> 33.6 us (0.952)
  waiting for transfers between devices: 13.3 us -> 11.7 us
    ppermute x13, waiting for transfers between devices: 13.3 us -> 11.7 us  [swapped(): lax.ppermute(block, axis, [(i, i ^ mask) for i in range(lax.axis_size(axi...]
  transfers between devices with their start and end apart: 13 -> 13, of which waited for: 8 -> 9; matrix products, arithmetic and copies ran while one was open for 0% -> 0% of each run, Pallas kernels for 7% -> 8%
where the time goes in v4:
time: 33.6 us; the launch traced here: 33.3 us
  starting transfers between devices  13.1 us (39%)
  waiting for transfers between devices  11.7 us (35%)
  Pallas kernels  8.43 us (25%)
    ppermute x13, starting transfers between devices, swapped(): lax.ppermute(block, axis, [(i, i ^ mask) for i in range(lax.axis_size(axi...  13.1 us
    ppermute x13, waiting for transfers between devices, swapped(): lax.ppermute(block, axis, [(i, i ^ mask) for i in range(lax.axis_size(axi...  11.7 us
    pallas_call x1, Pallas kernels, long_mix(): pl.pallas_call(lambda *refs: long_kernel(nodes, chans, per_node, rim, *re...  2.14 us
    pallas_call x1, Pallas kernels, pack(): pl.pallas_call(lambda *refs: pack_kernel(nodes, chans, *refs), out_shape=...  1.98 us
    pallas_call x1, Pallas kernels, project_late(): pl.pallas_call(lambda *refs: final_kernel(tuple(late), cuts, *refs), out_...  1.67 us
    pallas_call x1, Pallas kernels, near_tables(): pl.pallas_call(lambda *refs: tables_kernel(count, *refs), out_shape=[jax....  1.4 us
    pallas_call x1, Pallas kernels, project_early(): pl.pallas_call(lambda *refs: partial_kernel(tuple(early), features // 4,...  0.77 us
  transfers between devices with their start and end apart: 13, of which 9 were waited for; matrix products, arithmetic and copies ran while one was open for 0% of the time, Pallas kernels for 8%

profile of v4, /device:TPU:0, one launch (start us, length us, event | category | flops | bytes accessed | tf_op | source)
XLA Modules:
  0.0 33.3 jit_solution(6846897247893811250)
XLA Ops:
  0.0 2.0 %pack.1 = (bf16[16,2176]{1,0:T(8,128)(2,1)S(1)}, bf16[16,2176]{1,0:T(8,128)(2,1)S(1)}, bf16[16,2176]{1,0:T(8,128)(2,1)S(1)}, bf16[16,2176]{1,0:T(8,128)(2,1)S(1)...) custom-call(bf16[3,64,1024]{2,1,0:T(8,128)(2,1)} %refs_0_.2, f32[64,1024]{1,0:T(8,128)} %refs_1_.2, ...), custom_call_target="tpu_custom_call" | custom-call | tf_op jit(solution)/shard_map/pack/pallas_call | solution.py:173
  2.0 4.0 %collective-permute-start = (bf16[16,2176]{1,0:T(8,128)(2,1)S(1)}, bf16[16,2176]{1,0:T(8,128)(2,1)S(1)}, u32[]{:S(2)}, u32[]{:S(2)}) collective-permute-start(bf16[16,2176]{1,0:T(8,128)(2,1)S(1)} %get-tuple-element.34), channel_id=1, source_target_pairs={{0,24},{8,16},{16,8},{24,0},{1,25},{9,17},{17,9},{25,1},{2,26},{10... | collective-permute-start | bytes 208904 | tf_op jit(solution)/shard_map/ppermute | solution.py:475
  5.9 0.5 %collective-permute-start.1 = (bf16[16,2176]{1,0:T(8,128)(2,1)S(1)}, bf16[16,2176]{1,0:T(8,128)(2,1)S(1)}, u32[]{:S(2)}, u32[]{:S(2)}) collective-permute-start(bf16[16,2176]{1,0:T(8,128)(2,1)S(1)} %get-tuple-element.35), channel_id=1, source_target_pairs={{0,16},{8,24},{16,0},{24,8},{1,17},{9,25},{17,1},{25,9},{2,18},{10... | collective-permute-start | bytes 208904 | tf_op jit(solution)/shard_map/ppermute | solution.py:475
  6.5 0.1 collective-permute-start.2
  6.6 1.4 %near_tables.1 = (bf16[1024,512]{1,0:T(8,128)(2,1)S(1)}, bf16[64,64]{1,0:T(8,128)(2,1)S(1)}, f32[32,256]{1,0:T(8,128)S(1)}, bf16[768,256]{1,0:T(8,128)(2,1)S(1)}...) custom-call(bf16[1024,512]{1,0:T(8,128)(2,1)} %refs_0_.3, bf16[64,64]{1,0:T(8,128)(2,1)} %constant.8.clone.refs_1_, ...), custom_call_target="tpu_custom_call" | custom-call | tf_op jit(solution)/shard_map/near_tables/pallas_call | solution.py:90
  8.0 0.3 collective-permute-done.refs_6_.refs_5_
  8.2 2.0 %collective-permute-done.1.refs_7_.refs_4_ = bf16[16,2176]{1,0:T(8,128)(2,1)S(1)} collective-permute-done((bf16[16,2176]{1,0:T(8,128)(2,1)S(1)}, bf16[16,2176]{1,0:T(8,128)(2,1)S(1)}, u32[]{:S(2)}, u32[]{:S(2)}) %collective-permute-start.1) | collective-permute-done | bytes 69664 | tf_op jit(solution)/shard_map/ppermute | solution.py:475
  10.3 0.5 %collective-permute-done.2.refs_8_.refs_3_ = bf16[16,2176]{1,0:T(8,128)(2,1)S(1)} collective-permute-done((bf16[16,2176]{1,0:T(8,128)(2,1)S(1)}, bf16[16,2176]{1,0:T(8,128)(2,1)S(1)}, u32[]{:S(2)}, u32[]{:S(2)}) %collective-permute-start.2) | collective-permute-done | bytes 69664 | tf_op jit(solution)/shard_map/ppermute | solution.py:475
  10.8 2.1 %long_mix.1 = (bf16[16,1024]{1,0:T(8,128)(2,1)S(1)}, bf16[16,1024]{1,0:T(8,128)(2,1)S(1)}, bf16[16,1024]{1,0:T(8,128)(2,1)S(1)}, bf16[16,1024]{1,0:T(8,128)(2,1)S(1)}) custom-call(f32[3,64,7]{2,1,0:T(8,128)S(1)} %get-tuple-element.28.refs_0_.refs_1_, bf16[64,64]{1,0:T(8,128)(2,1)S(1)} %get-tuple-element.29.refs_1_, f32[32,256]{1,0:T(8,128)S(1)} %get-tuple-element.30.refs_2_, ...), custom_call_target="tpu_custom_call" | custom-call | tf_op jit(solution)/shard_map/long_mix/pallas_call | solution.py:341
  12.9 1.6 %collective-permute-start.3 = (bf16[16,1024]{1,0:T(8,128)(2,1)S(1)}, bf16[16,1024]{1,0:T(8,128)(2,1)S(1)}, u32[]{:S(2)}, u32[]{:S(2)}) collective-permute-start(bf16[16,1024]{1,0:T(8,128)(2,1)S(1)} %get-tuple-element.42), channel_id=1, source_target_pairs={{0,24},{8,16},{16,8},{24,0},{1,25},{9,17},{17,9},{25,1},{2,26},{10... | collective-permute-start | bytes 98312 | tf_op jit(solution)/shard_map/ppermute | solution.py:475
  14.5 0.6 %collective-permute-start.4 = (bf16[16,1024]{1,0:T(8,128)(2,1)S(1)}, bf16[16,1024]{1,0:T(8,128)(2,1)S(1)}, u32[]{:S(2)}, u32[]{:S(2)}) collective-permute-start(bf16[16,1024]{1,0:T(8,128)(2,1)S(1)} %get-tuple-element.43), channel_id=1, source_target_pairs={{0,16},{8,24},{16,0},{24,8},{1,17},{9,25},{17,1},{25,9},{2,18},{10... | collective-permute-start | bytes 98312 | tf_op jit(solution)/shard_map/ppermute | solution.py:475
  15.0 1.4 %collective-permute-start.5 = (bf16[16,1024]{1,0:T(8,128)(2,1)S(1)}, bf16[16,1024]{1,0:T(8,128)(2,1)S(1)}, u32[]{:S(2)}, u32[]{:S(2)}) collective-permute-start(bf16[16,1024]{1,0:T(8,128)(2,1)S(1)} %get-tuple-element.44), channel_id=1, source_target_pairs={{0,8},{8,0},{16,24},{24,16},{1,9},{9,1},{17,25},{25,17},{2,10},{10... | collective-permute-start | bytes 98312 | tf_op jit(solution)/shard_map/ppermute | solution.py:475
  16.5 0.5 %query_features.1 = f32[4,16,1024]{2,1,0:T(8,128)S(1)} custom-call(bf16[64,1024]{1,0:T(8,128)(2,1)S(1)} %get-tuple-element.27.refs_0_, f32[3,64,7]{2,1,0:T(8,128)S(1)} %get-tuple-element.28.refs_0_.refs_1_, bf16[16,2176]{1,0:T(8,128)(2,1)S(1)} %get-tuple-element.38.refs_6_.refs_9_.refs_2_, bf16[16,2176]{1,0:T(8,128)(2,1)S(1)} %collective-permute-done.2.refs_8_.refs_3_, ...), custom_call_target="tpu_custom_call" | custom-call | tf_op jit(solution)/shard_map/query_features/pallas_call | solution.py:222
  16.9 0.8 %collective-permute-done.3 = bf16[16,1024]{1,0:T(8,128)(2,1)S(1)} collective-permute-done((bf16[16,1024]{1,0:T(8,128)(2,1)S(1)}, bf16[16,1024]{1,0:T(8,128)(2,1)S(1)}, u32[]{:S(2)}, u32[]{:S(2)}) %collective-permute-start.3) | collective-permute-done | bytes 32800 | tf_op jit(solution)/shard_map/ppermute | solution.py:475
  17.8 0.6 %collective-permute-done.4 = bf16[16,1024]{1,0:T(8,128)(2,1)S(1)} collective-permute-done((bf16[16,1024]{1,0:T(8,128)(2,1)S(1)}, bf16[16,1024]{1,0:T(8,128)(2,1)S(1)}, u32[]{:S(2)}, u32[]{:S(2)}) %collective-permute-start.4) | collective-permute-done | bytes 32800 | tf_op jit(solution)/shard_map/ppermute | solution.py:475
  18.4 0.6 %collective-permute-done.5 = bf16[16,1024]{1,0:T(8,128)(2,1)S(1)} collective-permute-done((bf16[16,1024]{1,0:T(8,128)(2,1)S(1)}, bf16[16,1024]{1,0:T(8,128)(2,1)S(1)}, u32[]{:S(2)}, u32[]{:S(2)}) %collective-permute-start.5) | collective-permute-done | bytes 32800 | tf_op jit(solution)/shard_map/ppermute | solution.py:475
  19.0 2.6 %collective-permute-start.7 = (bf16[4,16,1024]{2,1,0:T(8,128)(2,1)S(1)}, bf16[4,16,1024]{2,1,0:T(8,128)(2,1)S(1)}, u32[]{:S(2)}, u32[]{:S(2)}) collective-permute-start(bf16[4,16,1024]{2,1,0:T(8,128)(2,1)S(1)} %multiply_convert_fusion.refs_1_), channel_id=1, source_target_pairs={{0,4},{1,5},{2,6},{3,7},{4,0},{5,1},{6,2},{7,3},{8,12},{9,13},{10,... | collective-permute-start | bytes 393224 | tf_op jit(solution)/shard_map/ppermute | solution.py:475
  21.6 1.6 %collective-permute-start.11 = (bf16[4,16,1024]{2,1,0:T(8,128)(2,1)S(1)}, bf16[4,16,1024]{2,1,0:T(8,128)(2,1)S(1)}, u32[]{:S(2)}, u32[]{:S(2)}) collective-permute-start(bf16[4,16,1024]{2,1,0:T(8,128)(2,1)S(1)} %multiply_convert_fusion.refs_1_), channel_id=1, source_target_pairs={{0,2},{1,3},{2,0},{3,1},{4,6},{5,7},{6,4},{7,5},{8,10},{9,11},{10,... | collective-permute-start | bytes 393224 | tf_op jit(solution)/shard_map/ppermute | solution.py:475
  23.2 0.2 collective-permute-start.9
  23.4 0.0 collective-permute-start.6
  23.5 5.3 %collective-permute-done.7.refs_3_ = bf16[4,16,1024]{2,1,0:T(8,128)(2,1)S(1)} collective-permute-done((bf16[4,16,1024]{2,1,0:T(8,128)(2,1)S(1)}, bf16[4,16,1024]{2,1,0:T(8,128)(2,1)S(1)}, u32[]{:S(2)}, u32[]{:S(2)}) %collective-permute-start.7) | collective-permute-done | bytes 131104 | tf_op jit(solution)/shard_map/ppermute | solution.py:475
  28.7 0.0 collective-permute-start.8
  28.8 0.0 collective-permute-done.11.refs_4_
  28.8 0.5 %collective-permute-start.12 = (bf16[4,16,1024]{2,1,0:T(8,128)(2,1)S(1)}, bf16[4,16,1024]{2,1,0:T(8,128)(2,1)S(1)}, u32[]{:S(2)}, u32[]{:S(2)}) collective-permute-start(bf16[4,16,1024]{2,1,0:T(8,128)(2,1)S(1)} %collective-permute-done.11.refs_4_), channel_id=1, source_target_pairs={{0,1},{1,0},{2,3},{3,2},{4,5},{5,4},{6,7},{7,6},{8,9},{9,8},{10,11... | collective-permute-start | bytes 393224 | tf_op jit(solution)/shard_map/ppermute | solution.py:475
  29.3 1.0 %collective-permute-done.9.refs_2_ = bf16[4,16,1024]{2,1,0:T(8,128)(2,1)S(1)} collective-permute-done((bf16[4,16,1024]{2,1,0:T(8,128)(2,1)S(1)}, bf16[4,16,1024]{2,1,0:T(8,128)(2,1)S(1)}, u32[]{:S(2)}, u32[]{:S(2)}) %collective-permute-start.9) | collective-permute-done | bytes 131104 | tf_op jit(solution)/shard_map/ppermute | solution.py:475
  30.3 0.0 collective-permute-start.10
  30.3 0.0 collective-permute-done.6.refs_2_
  30.3 0.0 collective-permute-done.8.refs_4_
  30.3 0.8 %project_early.1.refs_1_ = f32[1024,1024]{1,0:T(8,128)S(1)} custom-call(bf16[1024,512]{1,0:T(8,128)(2,1)S(1)} %get-tuple-element.26.refs_0_, bf16[4,16,1024]{2,1,0:T(8,128)(2,1)S(1)} %multiply_convert_fusion.refs_1_, bf16[4,16,1024]{2,1,0:T(8,128)(2,1)S(1)} %collective-permute-done.6.refs_2_, bf16[4,16,1024]{2,1,0:T(8,128)(2,1)S(1)} %collective-permute-done.7.refs_3_, ...), custom_call_target="tpu_custom_call" | custom-call | tf_op jit(solution)/shard_map/project_early/pallas_call | solution.py:406
  31.1 0.0 collective-permute-done.12.refs_5_
  31.1 0.6 %collective-permute-done.10.refs_3_ = bf16[4,16,1024]{2,1,0:T(8,128)(2,1)S(1)} collective-permute-done((bf16[4,16,1024]{2,1,0:T(8,128)(2,1)S(1)}, bf16[4,16,1024]{2,1,0:T(8,128)(2,1)S(1)}, u32[]{:S(2)}, u32[]{:S(2)}) %collective-permute-start.10) | collective-permute-done | bytes 131104 | tf_op jit(solution)/shard_map/ppermute | solution.py:475
  31.6 1.7 %project_late.1 = bf16[1024,1024]{1,0:T(8,128)(2,1)} custom-call(bf16[1024,512]{1,0:T(8,128)(2,1)S(1)} %get-tuple-element.26.refs_0_, f32[1024,1024]{1,0:T(8,128)S(1)} %project_early.1.refs_1_, bf16[4,16,1024]{2,1,0:T(8,128)(2,1)S(1)} %collective-permute-done.9.refs_2_, bf16[4,16,1024]{2,1,0:T(8,128)(2,1)S(1)} %collective-permute-done.10.refs_3_, ...), custom_call_target="tpu_custom_call" | custom-call | tf_op jit(solution)/shard_map/project_late/pallas_call | solution.py:425
  (1 shorter events, 0.0 us)
Async XLA Ops:
  2.0 6.3 %collective-permute-start = (bf16[16,2176]{1,0:T(8,128)(2,1)S(1)}, bf16[16,2176]{1,0:T(8,128)(2,1)S(1)}, u32[]{:S(2)}, u32[]{:S(2)}) collective-permute-start(bf16[16,2176]{1,0:T(8,128)(2,1)S(1)} %get-tuple-element.34), channel_id=1, source_target_pairs={{0,24},{8,16},{16,8},{24,0},{1,25},{9,17},{17,9},{25,1},{2,26},{10... | collective-permute-start | bytes 208904 | tf_op jit(solution)/shard_map/ppermute | solution.py:475
  5.9 4.3 %collective-permute-start.1 = (bf16[16,2176]{1,0:T(8,128)(2,1)S(1)}, bf16[16,2176]{1,0:T(8,128)(2,1)S(1)}, u32[]{:S(2)}, u32[]{:S(2)}) collective-permute-start(bf16[16,2176]{1,0:T(8,128)(2,1)S(1)} %get-tuple-element.35), channel_id=1, source_target_pairs={{0,16},{8,24},{16,0},{24,8},{1,17},{9,25},{17,1},{25,9},{2,18},{10... | collective-permute-start | bytes 208904 | tf_op jit(solution)/shard_map/ppermute | solution.py:475
  6.5 4.3 %collective-permute-start.2 = (bf16[16,2176]{1,0:T(8,128)(2,1)S(1)}, bf16[16,2176]{1,0:T(8,128)(2,1)S(1)}, u32[]{:S(2)}, u32[]{:S(2)}) collective-permute-start(bf16[16,2176]{1,0:T(8,128)(2,1)S(1)} %get-tuple-element.36), channel_id=1, source_target_pairs={{0,8},{8,0},{16,24},{24,16},{1,9},{9,1},{17,25},{25,17},{2,10},{10... | collective-permute-start | bytes 208904 | tf_op jit(solution)/shard_map/ppermute | solution.py:475
  12.9 4.9 %collective-permute-start.3 = (bf16[16,1024]{1,0:T(8,128)(2,1)S(1)}, bf16[16,1024]{1,0:T(8,128)(2,1)S(1)}, u32[]{:S(2)}, u32[]{:S(2)}) collective-permute-start(bf16[16,1024]{1,0:T(8,128)(2,1)S(1)} %get-tuple-element.42), channel_id=1, source_target_pairs={{0,24},{8,16},{16,8},{24,0},{1,25},{9,17},{17,9},{25,1},{2,26},{10... | collective-permute-start | bytes 98312 | tf_op jit(solution)/shard_map/ppermute | solution.py:475
  14.5 3.9 %collective-permute-start.4 = (bf16[16,1024]{1,0:T(8,128)(2,1)S(1)}, bf16[16,1024]{1,0:T(8,128)(2,1)S(1)}, u32[]{:S(2)}, u32[]{:S(2)}) collective-permute-start(bf16[16,1024]{1,0:T(8,128)(2,1)S(1)} %get-tuple-element.43), channel_id=1, source_target_pairs={{0,16},{8,24},{16,0},{24,8},{1,17},{9,25},{17,1},{25,9},{2,18},{10... | collective-permute-start | bytes 98312 | tf_op jit(solution)/shard_map/ppermute | solution.py:475
  15.0 3.9 %collective-permute-start.5 = (bf16[16,1024]{1,0:T(8,128)(2,1)S(1)}, bf16[16,1024]{1,0:T(8,128)(2,1)S(1)}, u32[]{:S(2)}, u32[]{:S(2)}) collective-permute-start(bf16[16,1024]{1,0:T(8,128)(2,1)S(1)} %get-tuple-element.44), channel_id=1, source_target_pairs={{0,8},{8,0},{16,24},{24,16},{1,9},{9,1},{17,25},{25,17},{2,10},{10... | collective-permute-start | bytes 98312 | tf_op jit(solution)/shard_map/ppermute | solution.py:475
  19.0 9.8 %collective-permute-start.7 = (bf16[4,16,1024]{2,1,0:T(8,128)(2,1)S(1)}, bf16[4,16,1024]{2,1,0:T(8,128)(2,1)S(1)}, u32[]{:S(2)}, u32[]{:S(2)}) collective-permute-start(bf16[4,16,1024]{2,1,0:T(8,128)(2,1)S(1)} %multiply_convert_fusion.refs_1_), channel_id=1, source_target_pairs={{0,4},{1,5},{2,6},{3,7},{4,0},{5,1},{6,2},{7,3},{8,12},{9,13},{10,... | collective-permute-start | bytes 393224 | tf_op jit(solution)/shard_map/ppermute | solution.py:475
  21.6 7.1 %collective-permute-start.11 = (bf16[4,16,1024]{2,1,0:T(8,128)(2,1)S(1)}, bf16[4,16,1024]{2,1,0:T(8,128)(2,1)S(1)}, u32[]{:S(2)}, u32[]{:S(2)}) collective-permute-start(bf16[4,16,1024]{2,1,0:T(8,128)(2,1)S(1)} %multiply_convert_fusion.refs_1_), channel_id=1, source_target_pairs={{0,2},{1,3},{2,0},{3,1},{4,6},{5,7},{6,4},{7,5},{8,10},{9,11},{10,... | collective-permute-start | bytes 393224 | tf_op jit(solution)/shard_map/ppermute | solution.py:475
  23.2 7.1 %collective-permute-start.9 = (bf16[4,16,1024]{2,1,0:T(8,128)(2,1)S(1)}, bf16[4,16,1024]{2,1,0:T(8,128)(2,1)S(1)}, u32[]{:S(2)}, u32[]{:S(2)}) collective-permute-start(bf16[4,16,1024]{2,1,0:T(8,128)(2,1)S(1)} %multiply_convert_fusion.refs_1_), channel_id=1, source_target_pairs={{0,6},{1,7},{2,4},{3,5},{4,2},{5,3},{6,0},{7,1},{8,14},{9,15},{10,... | collective-permute-start | bytes 393224 | tf_op jit(solution)/shard_map/ppermute | solution.py:475
  23.4 6.9 %collective-permute-start.6 = (bf16[4,16,1024]{2,1,0:T(8,128)(2,1)S(1)}, bf16[4,16,1024]{2,1,0:T(8,128)(2,1)S(1)}, u32[]{:S(2)}, u32[]{:S(2)}) collective-permute-start(bf16[4,16,1024]{2,1,0:T(8,128)(2,1)S(1)} %multiply_convert_fusion.refs_1_), channel_id=1, source_target_pairs={{0,1},{1,0},{2,3},{3,2},{4,5},{5,4},{6,7},{7,6},{8,9},{9,8},{10,11... | collective-permute-start | bytes 393224 | tf_op jit(solution)/shard_map/ppermute | solution.py:475
  28.7 1.6 %collective-permute-start.8 = (bf16[4,16,1024]{2,1,0:T(8,128)(2,1)S(1)}, bf16[4,16,1024]{2,1,0:T(8,128)(2,1)S(1)}, u32[]{:S(2)}, u32[]{:S(2)}) collective-permute-start(bf16[4,16,1024]{2,1,0:T(8,128)(2,1)S(1)} %collective-permute-done.7.refs_3_), channel_id=1, source_target_pairs={{0,1},{1,0},{2,3},{3,2},{4,5},{5,4},{6,7},{7,6},{8,9},{9,8},{10,11... | collective-permute-start | bytes 393224 | tf_op jit(solution)/shard_map/ppermute | solution.py:475
  28.8 2.3 %collective-permute-start.12 = (bf16[4,16,1024]{2,1,0:T(8,128)(2,1)S(1)}, bf16[4,16,1024]{2,1,0:T(8,128)(2,1)S(1)}, u32[]{:S(2)}, u32[]{:S(2)}) collective-permute-start(bf16[4,16,1024]{2,1,0:T(8,128)(2,1)S(1)} %collective-permute-done.11.refs_4_), channel_id=1, source_target_pairs={{0,1},{1,0},{2,3},{3,2},{4,5},{5,4},{6,7},{7,6},{8,9},{9,8},{10,11... | collective-permute-start | bytes 393224 | tf_op jit(solution)/shard_map/ppermute | solution.py:475
  30.3 1.3 %collective-permute-start.10 = (bf16[4,16,1024]{2,1,0:T(8,128)(2,1)S(1)}, bf16[4,16,1024]{2,1,0:T(8,128)(2,1)S(1)}, u32[]{:S(2)}, u32[]{:S(2)}) collective-permute-start(bf16[4,16,1024]{2,1,0:T(8,128)(2,1)S(1)} %collective-permute-done.9.refs_2_), channel_id=1, source_target_pairs={{0,1},{1,0},{2,3},{3,2},{4,5},{5,4},{6,7},{7,6},{8,9},{9,8},{10,11... | collective-permute-start | bytes 393224 | tf_op jit(solution)/shard_map/ppermute | solution.py:475

commit v5 on v4

--- a/solution.py
+++ b/solution.py
@@ -109,59 +109,56 @@
     place = lax.axis_index("ctx")
     block = qkv_ref.shape[2]
     rim = taps_ref.shape[2] - 1
-    moves = [
-        pltpu.make_async_copy(flat_ref, flat, sems.at[0]),
-        pltpu.make_async_copy(qkv_ref.at[0], query_ref, sems.at[1]),
-        pltpu.make_async_copy(filter_ref, filters, sems.at[2]),
+    shares = [
+        pl.ds(pl.multiple_of((place ^ mask) * chans, chans), chans) for mask in range(nodes)
     ]
-    shares = [
-        pl.ds(pl.multiple_of((place ^ mask) * chans, chans), chans)
-        for mask in reversed(range(nodes))
-    ]
-    arrivals = [
-        pltpu.make_async_copy(
-            qkv_ref.at[pl.ds(1, 2), rows, :], streams.at[:, rows, :], sems.at[3 + index]
-        )
-        for index, rows in enumerate(shares)
-    ]
-    for move in moves[:1] + arrivals + moves[1:]:
+    flat_move = pltpu.make_async_copy(flat_ref, flat, sems.at[0])
+    query_move = pltpu.make_async_copy(qkv_ref.at[0], query_ref, sems.at[1])
+    filter_move = pltpu.make_async_copy(filter_ref, filters, sems.at[2])
+    stream_move = pltpu.make_async_copy(qkv_ref.at[pl.ds(1, 2)], streams, sems.at[3])
+    for move in (flat_move, stream_move, query_move, filter_move):
         move.start()
     lane = lax.broadcasted_iota(jnp.int32, (chans, LANES), 1)
 
-    def place_at(tile, source, target, size, under):
-        moved = pltpu.roll(tile, (target - source) % LANES, 1)
-        return jnp.where((lane >= target) & (lane < target + size), moved, under)
-
-    moves[0].wait()
+    flat_move.wait()
     for stream in range(3):
         taps_ref[stream] = flat[stream].T
-    for index, rows in enumerate(shares):
-        mask = nodes - 1 - index
-        arrivals[index].wait()
-        edge = jnp.zeros((chans, LANES), jnp.float32)
-        product = None
-        for stream in range(2):
-            values = streams[stream, rows, :].astype(jnp.float32)
-            at = stream * LANE_V
-            edge = place_at(values[:, block - LANES :], LANES - rim, at, rim, edge)
-            edge = place_at(values[:, :LANES], 0, at + rim, rim, edge)
-            featured = rolled_taps(values, taps_ref[1 + stream, rows, :])
-            product = featured if product is None else product * featured
-        outs[mask][:, :block] = product.astype(jnp.bfloat16)
-        outs[mask][:, 2 * block :] = edge.astype(jnp.bfloat16)
-    moves[1].wait()
-    queries = jnp.zeros((chans, LANES), jnp.float32)
+    query_move.wait()
+    edges = jnp.zeros((chans, LANES), jnp.float32)
     for share in range(nodes):
         tile = query_ref[share * chans : (share + 1) * chans, block - LANES :]
-        queries = place_at(
-            tile.astype(jnp.float32), LANES - rim, LANE_Q + share * rim, rim, queries
-        )
-    for mask in range(nodes):
-        edge = outs[mask][:, 2 * block :].astype(jnp.float32)
-        outs[mask][:, 2 * block :] = jnp.where(lane >= LANE_Q, queries, edge).astype(jnp.bfloat16)
-    moves[2].wait()
-    for index, rows in enumerate(shares):
-        mask = nodes - 1 - index
+        moved = pltpu.roll(tile.astype(jnp.float32), LANE_Q + (share + 1) * rim, 1)
+        edges = jnp.where(lane >= LANE_Q + share * rim, moved, edges)
+    stream_move.wait()
+    for mask, rows in reversed(list(enumerate(shares))):
+        edge = edges
+        features = []
+        for stream in reversed(range(2)):
+            values = streams[stream, rows, :].astype(jnp.float32)
+            ends = jnp.where(lane < rim, values[:, :LANES], values[:, block - LANES :])
+            at = stream * LANE_V
+            edge = jnp.where(lane < at + LANE_V, pltpu.roll(ends, at + rim, 1), edge)
+            taps = taps_ref[1 + stream, rows, :]
+            wide = [jnp.broadcast_to(taps[:, tap : tap + 1], (chans, LANES)) for tap in range(rim + 1)]
+            raw = streams[stream, rows, :]
+            totals = []
+            for index in range(block // LANES):
+                tile = raw[:, index * LANES : (index + 1) * LANES]
+                total = wide[0] * tile.astype(jnp.float32)
+                moved = [pltpu.roll(tile, shift, 1) for shift in range(1, rim + 1)]
+                if index == 0:
+                    before = moved
+                for shift in range(1, rim + 1):
+                    joined = jnp.where(lane < shift, before[shift - 1].astype(jnp.float32), moved[shift - 1].astype(jnp.float32))
+                    total = total + wide[shift] * joined
+                before = moved
+                totals.append(total)
+            features.append(totals)
+        for index, (left, right) in enumerate(zip(*features)):
+            outs[mask][:, index * LANES : (index + 1) * LANES] = (left * right).astype(jnp.bfloat16)
+        outs[mask][:, 2 * block :] = edge.astype(jnp.bfloat16)
+    filter_move.wait()
+    for mask, rows in enumerate(shares):
         outs[mask][:, block : 2 * block] = filters[rows, :].astype(jnp.bfloat16)
 
 
@@ -183,7 +180,7 @@
             pltpu.VMEM((every, block), jnp.float32),
             pltpu.VMEM((2, every, block), jnp.bfloat16),
             pltpu.VMEM(flat.shape, jnp.float32),
-            pltpu.SemaphoreType.DMA((3 + nodes,)),
+            pltpu.SemaphoreType.DMA((4,)),
         ],
         compiler_params=pltpu.CompilerParams(vmem_limit_bytes=16 << 20),
         name="pack",
@@ -293,36 +290,38 @@
             cols = slice(part * LANES, (part + 1) * LANES)
             spectra[part].append(turn(section[:rows, cols], section[rows:, cols], 1))
     spectra = spectra[0] + spectra[1]
-    spec = inner(spectra)
-    joined = []
-    for chan in range(chans):
-        sig = spec[chan * rows : (chan + 1) * rows, :]
-        fil = spec[(chans + chan) * rows : (chans + chan + 1) * rows, :]
+    fil_spec = inner(spectra[chans:])
+    sig_spec = inner(spectra[:chans])
+    def product(chan):
+        sig = sig_spec[chan * rows : (chan + 1) * rows, :]
+        fil = fil_spec[chan * rows : (chan + 1) * rows, :]
         sig_real, sig_imag = sig[:, :LANES], sig[:, LANES:]
         fil_real, fil_imag = fil[:, :LANES], fil[:, LANES:]
-        joined.append(
-            jnp.concatenate(
-                [
-                    sig_real * fil_real - sig_imag * fil_imag,
-                    -(sig_real * fil_imag + sig_imag * fil_real),
-                ],
-                axis=1,
+        return jnp.concatenate(
+            [
+                sig_real * fil_real - sig_imag * fil_imag,
+                -(sig_real * fil_imag + sig_imag * fil_real),
+            ],
+            axis=1,
+        )
+
+    group = max(chans // 2, 1)
+    groups = [range(begin, begin + group) for begin in range(0, chans, group)]
+    turned = []
+    for members in groups:
+        back = inner([product(chan) for chan in members])
+        for index in range(group):
+            at = slice(index * rows, (index + 1) * rows)
+            turned.append(turn(back[at, :LANES], back[at, LANES:], 0))
+    for members in groups:
+        high, low = halves(jnp.concatenate([turned[chan] for chan in members], axis=1))
+        convolved = dot(last_ref[...], jnp.concatenate([high, low, high], axis=0))
+        for index, chan in enumerate(members):
+            span = slice(chan * pitch, chan * pitch + rows)
+            final[span, :] = (
+                convolved[:, index * LANES : (index + 1) * LANES]
+                + skips[chan : chan + 1, :1] * raw[0, span, :]
             )
-        )
-    back = inner(joined)
-    turned = []
-    for chan in range(chans):
-        real = back[chan * rows : (chan + 1) * rows, :LANES]
-        imag = back[chan * rows : (chan + 1) * rows, LANES:]
-        turned.append(turn(real, imag, 0))
-    high, low = halves(jnp.concatenate(turned, axis=1))
-    convolved = dot(last_ref[...], jnp.concatenate([high, low, high], axis=0))
-    for chan in range(chans):
-        span = slice(chan * pitch, chan * pitch + rows)
-        final[span, :] = (
-            convolved[:, chan * LANES : (chan + 1) * LANES]
-            + skips[chan : chan + 1, :1] * raw[0, span, :]
-        )
     for mask in range(nodes):
         start = (place ^ mask) * per_node
         for tile in range(per_node):

time: 33.6 us -> 33 us (0.982)
  Pallas kernels: 8.43 us -> 7.86 us
    pallas_call x1, Pallas kernels: 2.14 us -> 1.65 us  [long_mix(): pl.pallas_call(lambda *refs: long_kernel(nodes, chans, per_node, rim, *re...]
where the time goes in v5:
time: 33 us; the launch traced here: 32.8 us
  starting transfers between devices  13.1 us (40%)
  waiting for transfers between devices  11.7 us (35%)
  Pallas kernels  7.86 us (24%)
    ppermute x13, starting transfers between devices, swapped(): lax.ppermute(block, axis, [(i, i ^ mask) for i in range(lax.axis_size(axi...  13.1 us
    ppermute x13, waiting for transfers between devices, swapped(): lax.ppermute(block, axis, [(i, i ^ mask) for i in range(lax.axis_size(axi...  11.7 us
    pallas_call x1, Pallas kernels, pack(): pl.pallas_call(lambda *refs: pack_kernel(nodes, chans, *refs), out_shape=...  1.88 us
    pallas_call x1, Pallas kernels, project_late(): pl.pallas_call(lambda *refs: final_kernel(tuple(late), cuts, *refs), out_...  1.68 us
    pallas_call x1, Pallas kernels, long_mix(): pl.pallas_call(lambda *refs: long_kernel(nodes, chans, per_node, rim, *re...  1.65 us
    pallas_call x1, Pallas kernels, near_tables(): pl.pallas_call(lambda *refs: tables_kernel(count, *refs), out_shape=[jax....  1.4 us
    pallas_call x1, Pallas kernels, project_early(): pl.pallas_call(lambda *refs: partial_kernel(tuple(early), features // 4,...  0.77 us
  transfers between devices with their start and end apart: 13, of which 9 were waited for; matrix products, arithmetic and copies ran while one was open for 0% of the time, Pallas kernels for 8%

profile of v5, /device:TPU:0, one launch (start us, length us, event | category | flops | bytes accessed | tf_op | source)
XLA Modules:
  0.0 32.8 jit_solution(16455787887158582992)
XLA Ops:
  0.0 1.9 %pack.1 = (bf16[16,2176]{1,0:T(8,128)(2,1)S(1)}, bf16[16,2176]{1,0:T(8,128)(2,1)S(1)}, bf16[16,2176]{1,0:T(8,128)(2,1)S(1)}, bf16[16,2176]{1,0:T(8,128)(2,1)S(1)...) custom-call(bf16[3,64,1024]{2,1,0:T(8,128)(2,1)} %refs_0_.2, f32[64,1024]{1,0:T(8,128)} %refs_1_.2, ...), custom_call_target="tpu_custom_call" | custom-call | tf_op jit(solution)/shard_map/pack/pallas_call | solution.py:170
  1.9 4.0 %collective-permute-start = (bf16[16,2176]{1,0:T(8,128)(2,1)S(1)}, bf16[16,2176]{1,0:T(8,128)(2,1)S(1)}, u32[]{:S(2)}, u32[]{:S(2)}) collective-permute-start(bf16[16,2176]{1,0:T(8,128)(2,1)S(1)} %get-tuple-element.34), channel_id=1, source_target_pairs={{0,24},{8,16},{16,8},{24,0},{1,25},{9,17},{17,9},{25,1},{2,26},{10... | collective-permute-start | bytes 208904 | tf_op jit(solution)/shard_map/ppermute | solution.py:474
  5.9 0.5 %collective-permute-start.1 = (bf16[16,2176]{1,0:T(8,128)(2,1)S(1)}, bf16[16,2176]{1,0:T(8,128)(2,1)S(1)}, u32[]{:S(2)}, u32[]{:S(2)}) collective-permute-start(bf16[16,2176]{1,0:T(8,128)(2,1)S(1)} %get-tuple-element.35), channel_id=1, source_target_pairs={{0,16},{8,24},{16,0},{24,8},{1,17},{9,25},{17,1},{25,9},{2,18},{10... | collective-permute-start | bytes 208904 | tf_op jit(solution)/shard_map/ppermute | solution.py:474
  6.4 0.1 collective-permute-start.2
  6.5 1.4 %near_tables.1 = (bf16[1024,512]{1,0:T(8,128)(2,1)S(1)}, bf16[64,64]{1,0:T(8,128)(2,1)S(1)}, f32[32,256]{1,0:T(8,128)S(1)}, bf16[768,256]{1,0:T(8,128)(2,1)S(1)}...) custom-call(bf16[1024,512]{1,0:T(8,128)(2,1)} %refs_0_.3, bf16[64,64]{1,0:T(8,128)(2,1)} %constant.8.clone.refs_1_, ...), custom_call_target="tpu_custom_call" | custom-call | tf_op jit(solution)/shard_map/near_tables/pallas_call | solution.py:90
  7.9 0.3 collective-permute-done.refs_6_.refs_5_
  8.2 2.0 %collective-permute-done.1.refs_7_.refs_4_ = bf16[16,2176]{1,0:T(8,128)(2,1)S(1)} collective-permute-done((bf16[16,2176]{1,0:T(8,128)(2,1)S(1)}, bf16[16,2176]{1,0:T(8,128)(2,1)S(1)}, u32[]{:S(2)}, u32[]{:S(2)}) %collective-permute-start.1) | collective-permute-done | bytes 69664 | tf_op jit(solution)/shard_map/ppermute | solution.py:474
  10.2 0.5 %collective-permute-done.2.refs_8_.refs_3_ = bf16[16,2176]{1,0:T(8,128)(2,1)S(1)} collective-permute-done((bf16[16,2176]{1,0:T(8,128)(2,1)S(1)}, bf16[16,2176]{1,0:T(8,128)(2,1)S(1)}, u32[]{:S(2)}, u32[]{:S(2)}) %collective-permute-start.2) | collective-permute-done | bytes 69664 | tf_op jit(solution)/shard_map/ppermute | solution.py:474
  10.7 1.6 %long_mix.1 = (bf16[16,1024]{1,0:T(8,128)(2,1)S(1)}, bf16[16,1024]{1,0:T(8,128)(2,1)S(1)}, bf16[16,1024]{1,0:T(8,128)(2,1)S(1)}, bf16[16,1024]{1,0:T(8,128)(2,1)S(1)}) custom-call(f32[3,64,7]{2,1,0:T(8,128)S(1)} %get-tuple-element.28.refs_0_.refs_1_, bf16[64,64]{1,0:T(8,128)(2,1)S(1)} %get-tuple-element.29.refs_1_, f32[32,256]{1,0:T(8,128)S(1)} %get-tuple-element.30.refs_2_, ...), custom_call_target="tpu_custom_call" | custom-call | tf_op jit(solution)/shard_map/long_mix/pallas_call | solution.py:340
  12.3 1.6 %collective-permute-start.3 = (bf16[16,1024]{1,0:T(8,128)(2,1)S(1)}, bf16[16,1024]{1,0:T(8,128)(2,1)S(1)}, u32[]{:S(2)}, u32[]{:S(2)}) collective-permute-start(bf16[16,1024]{1,0:T(8,128)(2,1)S(1)} %get-tuple-element.42), channel_id=1, source_target_pairs={{0,24},{8,16},{16,8},{24,0},{1,25},{9,17},{17,9},{25,1},{2,26},{10... | collective-permute-start | bytes 98312 | tf_op jit(solution)/shard_map/ppermute | solution.py:474
  13.9 0.6 %collective-permute-start.4 = (bf16[16,1024]{1,0:T(8,128)(2,1)S(1)}, bf16[16,1024]{1,0:T(8,128)(2,1)S(1)}, u32[]{:S(2)}, u32[]{:S(2)}) collective-permute-start(bf16[16,1024]{1,0:T(8,128)(2,1)S(1)} %get-tuple-element.43), channel_id=1, source_target_pairs={{0,16},{8,24},{16,0},{24,8},{1,17},{9,25},{17,1},{25,9},{2,18},{10... | collective-permute-start | bytes 98312 | tf_op jit(solution)/shard_map/ppermute | solution.py:474
  14.4 1.4 %collective-permute-start.5 = (bf16[16,1024]{1,0:T(8,128)(2,1)S(1)}, bf16[16,1024]{1,0:T(8,128)(2,1)S(1)}, u32[]{:S(2)}, u32[]{:S(2)}) collective-permute-start(bf16[16,1024]{1,0:T(8,128)(2,1)S(1)} %get-tuple-element.44), channel_id=1, source_target_pairs={{0,8},{8,0},{16,24},{24,16},{1,9},{9,1},{17,25},{25,17},{2,10},{10... | collective-permute-start | bytes 98312 | tf_op jit(solution)/shard_map/ppermute | solution.py:474
  15.9 0.5 %query_features.1 = f32[4,16,1024]{2,1,0:T(8,128)S(1)} custom-call(bf16[64,1024]{1,0:T(8,128)(2,1)S(1)} %get-tuple-element.27.refs_0_, f32[3,64,7]{2,1,0:T(8,128)S(1)} %get-tuple-element.28.refs_0_.refs_1_, bf16[16,2176]{1,0:T(8,128)(2,1)S(1)} %get-tuple-element.38.refs_6_.refs_9_.refs_2_, bf16[16,2176]{1,0:T(8,128)(2,1)S(1)} %collective-permute-done.2.refs_8_.refs_3_, ...), custom_call_target="tpu_custom_call" | custom-call | tf_op jit(solution)/shard_map/query_features/pallas_call | solution.py:219
  16.4 0.8 %collective-permute-done.3 = bf16[16,1024]{1,0:T(8,128)(2,1)S(1)} collective-permute-done((bf16[16,1024]{1,0:T(8,128)(2,1)S(1)}, bf16[16,1024]{1,0:T(8,128)(2,1)S(1)}, u32[]{:S(2)}, u32[]{:S(2)}) %collective-permute-start.3) | collective-permute-done | bytes 32800 | tf_op jit(solution)/shard_map/ppermute | solution.py:474
  17.2 0.6 %collective-permute-done.4 = bf16[16,1024]{1,0:T(8,128)(2,1)S(1)} collective-permute-done((bf16[16,1024]{1,0:T(8,128)(2,1)S(1)}, bf16[16,1024]{1,0:T(8,128)(2,1)S(1)}, u32[]{:S(2)}, u32[]{:S(2)}) %collective-permute-start.4) | collective-permute-done | bytes 32800 | tf_op jit(solution)/shard_map/ppermute | solution.py:474
  17.8 0.6 %collective-permute-done.5 = bf16[16,1024]{1,0:T(8,128)(2,1)S(1)} collective-permute-done((bf16[16,1024]{1,0:T(8,128)(2,1)S(1)}, bf16[16,1024]{1,0:T(8,128)(2,1)S(1)}, u32[]{:S(2)}, u32[]{:S(2)}) %collective-permute-start.5) | collective-permute-done | bytes 32800 | tf_op jit(solution)/shard_map/ppermute | solution.py:474
  18.4 2.7 %collective-permute-start.7 = (bf16[4,16,1024]{2,1,0:T(8,128)(2,1)S(1)}, bf16[4,16,1024]{2,1,0:T(8,128)(2,1)S(1)}, u32[]{:S(2)}, u32[]{:S(2)}) collective-permute-start(bf16[4,16,1024]{2,1,0:T(8,128)(2,1)S(1)} %multiply_convert_fusion.refs_1_), channel_id=1, source_target_pairs={{0,4},{1,5},{2,6},{3,7},{4,0},{5,1},{6,2},{7,3},{8,12},{9,13},{10,... | collective-permute-start | bytes 393224 | tf_op jit(solution)/shard_map/ppermute | solution.py:474
  21.1 1.6 %collective-permute-start.11 = (bf16[4,16,1024]{2,1,0:T(8,128)(2,1)S(1)}, bf16[4,16,1024]{2,1,0:T(8,128)(2,1)S(1)}, u32[]{:S(2)}, u32[]{:S(2)}) collective-permute-start(bf16[4,16,1024]{2,1,0:T(8,128)(2,1)S(1)} %multiply_convert_fusion.refs_1_), channel_id=1, source_target_pairs={{0,2},{1,3},{2,0},{3,1},{4,6},{5,7},{6,4},{7,5},{8,10},{9,11},{10,... | collective-permute-start | bytes 393224 | tf_op jit(solution)/shard_map/ppermute | solution.py:474
  22.7 0.2 collective-permute-start.9
  22.9 0.0 collective-permute-start.6
  22.9 5.3 %collective-permute-done.7.refs_3_ = bf16[4,16,1024]{2,1,0:T(8,128)(2,1)S(1)} collective-permute-done((bf16[4,16,1024]{2,1,0:T(8,128)(2,1)S(1)}, bf16[4,16,1024]{2,1,0:T(8,128)(2,1)S(1)}, u32[]{:S(2)}, u32[]{:S(2)}) %collective-permute-start.7) | collective-permute-done | bytes 131104 | tf_op jit(solution)/shard_map/ppermute | solution.py:474
  28.2 0.0 collective-permute-start.8
  28.2 0.0 collective-permute-done.11.refs_4_
  28.2 0.5 %collective-permute-start.12 = (bf16[4,16,1024]{2,1,0:T(8,128)(2,1)S(1)}, bf16[4,16,1024]{2,1,0:T(8,128)(2,1)S(1)}, u32[]{:S(2)}, u32[]{:S(2)}) collective-permute-start(bf16[4,16,1024]{2,1,0:T(8,128)(2,1)S(1)} %collective-permute-done.11.refs_4_), channel_id=1, source_target_pairs={{0,1},{1,0},{2,3},{3,2},{4,5},{5,4},{6,7},{7,6},{8,9},{9,8},{10,11... | collective-permute-start | bytes 393224 | tf_op jit(solution)/shard_map/ppermute | solution.py:474
  28.7 1.0 %collective-permute-done.9.refs_2_ = bf16[4,16,1024]{2,1,0:T(8,128)(2,1)S(1)} collective-permute-done((bf16[4,16,1024]{2,1,0:T(8,128)(2,1)S(1)}, bf16[4,16,1024]{2,1,0:T(8,128)(2,1)S(1)}, u32[]{:S(2)}, u32[]{:S(2)}) %collective-permute-start.9) | collective-permute-done | bytes 131104 | tf_op jit(solution)/shard_map/ppermute | solution.py:474
  29.7 0.0 collective-permute-start.10
  29.7 0.0 collective-permute-done.6.refs_2_
  29.7 0.0 collective-permute-done.8.refs_4_
  29.7 0.8 %project_early.1.refs_1_ = f32[1024,1024]{1,0:T(8,128)S(1)} custom-call(bf16[1024,512]{1,0:T(8,128)(2,1)S(1)} %get-tuple-element.26.refs_0_, bf16[4,16,1024]{2,1,0:T(8,128)(2,1)S(1)} %multiply_convert_fusion.refs_1_, bf16[4,16,1024]{2,1,0:T(8,128)(2,1)S(1)} %collective-permute-done.6.refs_2_, bf16[4,16,1024]{2,1,0:T(8,128)(2,1)S(1)} %collective-permute-done.7.refs_3_, ...), custom_call_target="tpu_custom_call" | custom-call | tf_op jit(solution)/shard_map/project_early/pallas_call | solution.py:405
  30.5 0.0 collective-permute-done.12.refs_5_
  30.5 0.6 %collective-permute-done.10.refs_3_ = bf16[4,16,1024]{2,1,0:T(8,128)(2,1)S(1)} collective-permute-done((bf16[4,16,1024]{2,1,0:T(8,128)(2,1)S(1)}, bf16[4,16,1024]{2,1,0:T(8,128)(2,1)S(1)}, u32[]{:S(2)}, u32[]{:S(2)}) %collective-permute-start.10) | collective-permute-done | bytes 131104 | tf_op jit(solution)/shard_map/ppermute | solution.py:474
  31.1 1.7 %project_late.1 = bf16[1024,1024]{1,0:T(8,128)(2,1)} custom-call(bf16[1024,512]{1,0:T(8,128)(2,1)S(1)} %get-tuple-element.26.refs_0_, f32[1024,1024]{1,0:T(8,128)S(1)} %project_early.1.refs_1_, bf16[4,16,1024]{2,1,0:T(8,128)(2,1)S(1)} %collective-permute-done.9.refs_2_, bf16[4,16,1024]{2,1,0:T(8,128)(2,1)S(1)} %collective-permute-done.10.refs_3_, ...), custom_call_target="tpu_custom_call" | custom-call | tf_op jit(solution)/shard_map/project_late/pallas_call | solution.py:424
  (1 shorter events, 0.0 us)
Async XLA Ops:
  1.9 6.3 %collective-permute-start = (bf16[16,2176]{1,0:T(8,128)(2,1)S(1)}, bf16[16,2176]{1,0:T(8,128)(2,1)S(1)}, u32[]{:S(2)}, u32[]{:S(2)}) collective-permute-start(bf16[16,2176]{1,0:T(8,128)(2,1)S(1)} %get-tuple-element.34), channel_id=1, source_target_pairs={{0,24},{8,16},{16,8},{24,0},{1,25},{9,17},{17,9},{25,1},{2,26},{10... | collective-permute-start | bytes 208904 | tf_op jit(solution)/shard_map/ppermute | solution.py:474
  5.9 4.3 %collective-permute-start.1 = (bf16[16,2176]{1,0:T(8,128)(2,1)S(1)}, bf16[16,2176]{1,0:T(8,128)(2,1)S(1)}, u32[]{:S(2)}, u32[]{:S(2)}) collective-permute-start(bf16[16,2176]{1,0:T(8,128)(2,1)S(1)} %get-tuple-element.35), channel_id=1, source_target_pairs={{0,16},{8,24},{16,0},{24,8},{1,17},{9,25},{17,1},{25,9},{2,18},{10... | collective-permute-start | bytes 208904 | tf_op jit(solution)/shard_map/ppermute | solution.py:474
  6.4 4.3 %collective-permute-start.2 = (bf16[16,2176]{1,0:T(8,128)(2,1)S(1)}, bf16[16,2176]{1,0:T(8,128)(2,1)S(1)}, u32[]{:S(2)}, u32[]{:S(2)}) collective-permute-start(bf16[16,2176]{1,0:T(8,128)(2,1)S(1)} %get-tuple-element.36), channel_id=1, source_target_pairs={{0,8},{8,0},{16,24},{24,16},{1,9},{9,1},{17,25},{25,17},{2,10},{10... | collective-permute-start | bytes 208904 | tf_op jit(solution)/shard_map/ppermute | solution.py:474
  12.3 4.9 %collective-permute-start.3 = (bf16[16,1024]{1,0:T(8,128)(2,1)S(1)}, bf16[16,1024]{1,0:T(8,128)(2,1)S(1)}, u32[]{:S(2)}, u32[]{:S(2)}) collective-permute-start(bf16[16,1024]{1,0:T(8,128)(2,1)S(1)} %get-tuple-element.42), channel_id=1, source_target_pairs={{0,24},{8,16},{16,8},{24,0},{1,25},{9,17},{17,9},{25,1},{2,26},{10... | collective-permute-start | bytes 98312 | tf_op jit(solution)/shard_map/ppermute | solution.py:474
  13.9 3.9 %collective-permute-start.4 = (bf16[16,1024]{1,0:T(8,128)(2,1)S(1)}, bf16[16,1024]{1,0:T(8,128)(2,1)S(1)}, u32[]{:S(2)}, u32[]{:S(2)}) collective-permute-start(bf16[16,1024]{1,0:T(8,128)(2,1)S(1)} %get-tuple-element.43), channel_id=1, source_target_pairs={{0,16},{8,24},{16,0},{24,8},{1,17},{9,25},{17,1},{25,9},{2,18},{10... | collective-permute-start | bytes 98312 | tf_op jit(solution)/shard_map/ppermute | solution.py:474
  14.4 3.9 %collective-permute-start.5 = (bf16[16,1024]{1,0:T(8,128)(2,1)S(1)}, bf16[16,1024]{1,0:T(8,128)(2,1)S(1)}, u32[]{:S(2)}, u32[]{:S(2)}) collective-permute-start(bf16[16,1024]{1,0:T(8,128)(2,1)S(1)} %get-tuple-element.44), channel_id=1, source_target_pairs={{0,8},{8,0},{16,24},{24,16},{1,9},{9,1},{17,25},{25,17},{2,10},{10... | collective-permute-start | bytes 98312 | tf_op jit(solution)/shard_map/ppermute | solution.py:474
  18.4 9.8 %collective-permute-start.7 = (bf16[4,16,1024]{2,1,0:T(8,128)(2,1)S(1)}, bf16[4,16,1024]{2,1,0:T(8,128)(2,1)S(1)}, u32[]{:S(2)}, u32[]{:S(2)}) collective-permute-start(bf16[4,16,1024]{2,1,0:T(8,128)(2,1)S(1)} %multiply_convert_fusion.refs_1_), channel_id=1, source_target_pairs={{0,4},{1,5},{2,6},{3,7},{4,0},{5,1},{6,2},{7,3},{8,12},{9,13},{10,... | collective-permute-start | bytes 393224 | tf_op jit(solution)/shard_map/ppermute | solution.py:474
  21.1 7.1 %collective-permute-start.11 = (bf16[4,16,1024]{2,1,0:T(8,128)(2,1)S(1)}, bf16[4,16,1024]{2,1,0:T(8,128)(2,1)S(1)}, u32[]{:S(2)}, u32[]{:S(2)}) collective-permute-start(bf16[4,16,1024]{2,1,0:T(8,128)(2,1)S(1)} %multiply_convert_fusion.refs_1_), channel_id=1, source_target_pairs={{0,2},{1,3},{2,0},{3,1},{4,6},{5,7},{6,4},{7,5},{8,10},{9,11},{10,... | collective-permute-start | bytes 393224 | tf_op jit(solution)/shard_map/ppermute | solution.py:474
  22.7 7.1 %collective-permute-start.9 = (bf16[4,16,1024]{2,1,0:T(8,128)(2,1)S(1)}, bf16[4,16,1024]{2,1,0:T(8,128)(2,1)S(1)}, u32[]{:S(2)}, u32[]{:S(2)}) collective-permute-start(bf16[4,16,1024]{2,1,0:T(8,128)(2,1)S(1)} %multiply_convert_fusion.refs_1_), channel_id=1, source_target_pairs={{0,6},{1,7},{2,4},{3,5},{4,2},{5,3},{6,0},{7,1},{8,14},{9,15},{10,... | collective-permute-start | bytes 393224 | tf_op jit(solution)/shard_map/ppermute | solution.py:474
  22.9 6.9 %collective-permute-start.6 = (bf16[4,16,1024]{2,1,0:T(8,128)(2,1)S(1)}, bf16[4,16,1024]{2,1,0:T(8,128)(2,1)S(1)}, u32[]{:S(2)}, u32[]{:S(2)}) collective-permute-start(bf16[4,16,1024]{2,1,0:T(8,128)(2,1)S(1)} %multiply_convert_fusion.refs_1_), channel_id=1, source_target_pairs={{0,1},{1,0},{2,3},{3,2},{4,5},{5,4},{6,7},{7,6},{8,9},{9,8},{10,11... | collective-permute-start | bytes 393224 | tf_op jit(solution)/shard_map/ppermute | solution.py:474
  28.2 1.6 %collective-permute-start.8 = (bf16[4,16,1024]{2,1,0:T(8,128)(2,1)S(1)}, bf16[4,16,1024]{2,1,0:T(8,128)(2,1)S(1)}, u32[]{:S(2)}, u32[]{:S(2)}) collective-permute-start(bf16[4,16,1024]{2,1,0:T(8,128)(2,1)S(1)} %collective-permute-done.7.refs_3_), channel_id=1, source_target_pairs={{0,1},{1,0},{2,3},{3,2},{4,5},{5,4},{6,7},{7,6},{8,9},{9,8},{10,11... | collective-permute-start | bytes 393224 | tf_op jit(solution)/shard_map/ppermute | solution.py:474
  28.2 2.3 %collective-permute-start.12 = (bf16[4,16,1024]{2,1,0:T(8,128)(2,1)S(1)}, bf16[4,16,1024]{2,1,0:T(8,128)(2,1)S(1)}, u32[]{:S(2)}, u32[]{:S(2)}) collective-permute-start(bf16[4,16,1024]{2,1,0:T(8,128)(2,1)S(1)} %collective-permute-done.11.refs_4_), channel_id=1, source_target_pairs={{0,1},{1,0},{2,3},{3,2},{4,5},{5,4},{6,7},{7,6},{8,9},{9,8},{10,11... | collective-permute-start | bytes 393224 | tf_op jit(solution)/shard_map/ppermute | solution.py:474
  29.7 1.3 %collective-permute-start.10 = (bf16[4,16,1024]{2,1,0:T(8,128)(2,1)S(1)}, bf16[4,16,1024]{2,1,0:T(8,128)(2,1)S(1)}, u32[]{:S(2)}, u32[]{:S(2)}) collective-permute-start(bf16[4,16,1024]{2,1,0:T(8,128)(2,1)S(1)} %collective-permute-done.9.refs_2_), channel_id=1, source_target_pairs={{0,1},{1,0},{2,3},{3,2},{4,5},{5,4},{6,7},{7,6},{8,9},{9,8},{10,11... | collective-permute-start | bytes 393224 | tf_op jit(solution)/shard_map/ppermute | solution.py:474

commit v6 on v5

--- a/solution.py
+++ b/solution.py
@@ -139,7 +139,9 @@
             at = stream * LANE_V
             edge = jnp.where(lane < at + LANE_V, pltpu.roll(ends, at + rim, 1), edge)
             taps = taps_ref[1 + stream, rows, :]
-            wide = [jnp.broadcast_to(taps[:, tap : tap + 1], (chans, LANES)) for tap in range(rim + 1)]
+            wide = [
+                jnp.broadcast_to(taps[:, tap : tap + 1], (chans, LANES)) for tap in range(rim + 1)
+            ]
             raw = streams[stream, rows, :]
             totals = []
             for index in range(block // LANES):
@@ -149,8 +151,8 @@
                 if index == 0:
                     before = moved
                 for shift in range(1, rim + 1):
-                    joined = jnp.where(lane < shift, before[shift - 1].astype(jnp.float32), moved[shift - 1].astype(jnp.float32))
-                    total = total + wide[shift] * joined
+                    joined = jnp.where(lane < shift, before[shift - 1], moved[shift - 1])
+                    total = total + wide[shift] * joined.astype(jnp.float32)
                 before = moved
                 totals.append(total)
             features.append(totals)
@@ -343,9 +345,9 @@
         in_specs=[near] * (1 + len(tables) + nodes),
         out_specs=[near] * nodes,
         scratch_shapes=[
-            pltpu.VMEM((2, chans * (rows + PAD), LANES), jnp.float32),
+            pltpu.VMEM((2, (chans + 1) * (rows + PAD), LANES), jnp.float32),
             pltpu.VMEM((nodes + 1, chans, LANES), jnp.float32),
-            pltpu.VMEM((chans * (rows + PAD), LANES), jnp.float32),
+            pltpu.VMEM(((chans + 1) * (rows + PAD), LANES), jnp.float32),
         ],
         compiler_params=pltpu.CompilerParams(vmem_limit_bytes=24 << 20),
         name="long_mix",

time: 33 us -> 33 us (level)
  no operation moved by 1% of the time
where the time goes in v6:
time: 33 us; the launch traced here: 32.7 us
  starting transfers between devices  13.1 us (40%)
  waiting for transfers between devices  11.7 us (35%)
  Pallas kernels  7.83 us (24%)
    ppermute x13, starting transfers between devices, swapped(): lax.ppermute(block, axis, [(i, i ^ mask) for i in range(lax.axis_size(axi...  13.1 us
    ppermute x13, waiting for transfers between devices, swapped(): lax.ppermute(block, axis, [(i, i ^ mask) for i in range(lax.axis_size(axi...  11.7 us
    pallas_call x1, Pallas kernels, pack(): pl.pallas_call(lambda *refs: pack_kernel(nodes, chans, *refs), out_shape=...  1.86 us
    pallas_call x1, Pallas kernels, project_late(): pl.pallas_call(lambda *refs: final_kernel(tuple(late), cuts, *refs), out_...  1.68 us
    pallas_call x1, Pallas kernels, long_mix(): pl.pallas_call(lambda *refs: long_kernel(nodes, chans, per_node, rim, *re...  1.65 us
    pallas_call x1, Pallas kernels, near_tables(): pl.pallas_call(lambda *refs: tables_kernel(count, *refs), out_shape=[jax....  1.4 us
    pallas_call x1, Pallas kernels, project_early(): pl.pallas_call(lambda *refs: partial_kernel(tuple(early), features // 4,...  0.77 us
  transfers between devices with their start and end apart: 13, of which 9 were waited for; matrix products, arithmetic and copies ran while one was open for 0% of the time, Pallas kernels for 8%

profile of v6, /device:TPU:0, one launch (start us, length us, event | category | flops | bytes accessed | tf_op | source)
XLA Modules:
  0.0 32.7 jit_solution(7578001445264662942)
XLA Ops:
  0.0 1.9 %pack.1 = (bf16[16,2176]{1,0:T(8,128)(2,1)S(1)}, bf16[16,2176]{1,0:T(8,128)(2,1)S(1)}, bf16[16,2176]{1,0:T(8,128)(2,1)S(1)}, bf16[16,2176]{1,0:T(8,128)(2,1)S(1)...) custom-call(bf16[3,64,1024]{2,1,0:T(8,128)(2,1)} %refs_0_.2, f32[64,1024]{1,0:T(8,128)} %refs_1_.2, ...), custom_call_target="tpu_custom_call" | custom-call | tf_op jit(solution)/shard_map/pack/pallas_call | solution.py:172
  1.9 4.0 %collective-permute-start = (bf16[16,2176]{1,0:T(8,128)(2,1)S(1)}, bf16[16,2176]{1,0:T(8,128)(2,1)S(1)}, u32[]{:S(2)}, u32[]{:S(2)}) collective-permute-start(bf16[16,2176]{1,0:T(8,128)(2,1)S(1)} %get-tuple-element.34), channel_id=1, source_target_pairs={{0,24},{8,16},{16,8},{24,0},{1,25},{9,17},{17,9},{25,1},{2,26},{10... | collective-permute-start | bytes 208904 | tf_op jit(solution)/shard_map/ppermute | solution.py:476
  5.8 0.5 %collective-permute-start.1 = (bf16[16,2176]{1,0:T(8,128)(2,1)S(1)}, bf16[16,2176]{1,0:T(8,128)(2,1)S(1)}, u32[]{:S(2)}, u32[]{:S(2)}) collective-permute-start(bf16[16,2176]{1,0:T(8,128)(2,1)S(1)} %get-tuple-element.35), channel_id=1, source_target_pairs={{0,16},{8,24},{16,0},{24,8},{1,17},{9,25},{17,1},{25,9},{2,18},{10... | collective-permute-start | bytes 208904 | tf_op jit(solution)/shard_map/ppermute | solution.py:476
  6.3 0.1 collective-permute-start.2
  6.5 1.4 %near_tables.1 = (bf16[1024,512]{1,0:T(8,128)(2,1)S(1)}, bf16[64,64]{1,0:T(8,128)(2,1)S(1)}, f32[32,256]{1,0:T(8,128)S(1)}, bf16[768,256]{1,0:T(8,128)(2,1)S(1)}...) custom-call(bf16[1024,512]{1,0:T(8,128)(2,1)} %refs_0_.3, bf16[64,64]{1,0:T(8,128)(2,1)} %constant.8.clone.refs_1_, ...), custom_call_target="tpu_custom_call" | custom-call | tf_op jit(solution)/shard_map/near_tables/pallas_call | solution.py:90
  7.9 0.3 collective-permute-done.refs_6_.refs_5_
  8.1 2.0 %collective-permute-done.1.refs_7_.refs_4_ = bf16[16,2176]{1,0:T(8,128)(2,1)S(1)} collective-permute-done((bf16[16,2176]{1,0:T(8,128)(2,1)S(1)}, bf16[16,2176]{1,0:T(8,128)(2,1)S(1)}, u32[]{:S(2)}, u32[]{:S(2)}) %collective-permute-start.1) | collective-permute-done | bytes 69664 | tf_op jit(solution)/shard_map/ppermute | solution.py:476
  10.1 0.5 %collective-permute-done.2.refs_8_.refs_3_ = bf16[16,2176]{1,0:T(8,128)(2,1)S(1)} collective-permute-done((bf16[16,2176]{1,0:T(8,128)(2,1)S(1)}, bf16[16,2176]{1,0:T(8,128)(2,1)S(1)}, u32[]{:S(2)}, u32[]{:S(2)}) %collective-permute-start.2) | collective-permute-done | bytes 69664 | tf_op jit(solution)/shard_map/ppermute | solution.py:476
  10.6 1.7 %long_mix.1 = (bf16[16,1024]{1,0:T(8,128)(2,1)S(1)}, bf16[16,1024]{1,0:T(8,128)(2,1)S(1)}, bf16[16,1024]{1,0:T(8,128)(2,1)S(1)}, bf16[16,1024]{1,0:T(8,128)(2,1)S(1)}) custom-call(f32[3,64,7]{2,1,0:T(8,128)S(1)} %get-tuple-element.28.refs_0_.refs_1_, bf16[64,64]{1,0:T(8,128)(2,1)S(1)} %get-tuple-element.29.refs_1_, f32[32,256]{1,0:T(8,128)S(1)} %get-tuple-element.30.refs_2_, ...), custom_call_target="tpu_custom_call" | custom-call | tf_op jit(solution)/shard_map/long_mix/pallas_call | solution.py:342
  12.3 1.6 %collective-permute-start.3 = (bf16[16,1024]{1,0:T(8,128)(2,1)S(1)}, bf16[16,1024]{1,0:T(8,128)(2,1)S(1)}, u32[]{:S(2)}, u32[]{:S(2)}) collective-permute-start(bf16[16,1024]{1,0:T(8,128)(2,1)S(1)} %get-tuple-element.42), channel_id=1, source_target_pairs={{0,24},{8,16},{16,8},{24,0},{1,25},{9,17},{17,9},{25,1},{2,26},{10... | collective-permute-start | bytes 98312 | tf_op jit(solution)/shard_map/ppermute | solution.py:476
  13.9 0.6 %collective-permute-start.4 = (bf16[16,1024]{1,0:T(8,128)(2,1)S(1)}, bf16[16,1024]{1,0:T(8,128)(2,1)S(1)}, u32[]{:S(2)}, u32[]{:S(2)}) collective-permute-start(bf16[16,1024]{1,0:T(8,128)(2,1)S(1)} %get-tuple-element.43), channel_id=1, source_target_pairs={{0,16},{8,24},{16,0},{24,8},{1,17},{9,25},{17,1},{25,9},{2,18},{10... | collective-permute-start | bytes 98312 | tf_op jit(solution)/shard_map/ppermute | solution.py:476
  14.4 1.4 %collective-permute-start.5 = (bf16[16,1024]{1,0:T(8,128)(2,1)S(1)}, bf16[16,1024]{1,0:T(8,128)(2,1)S(1)}, u32[]{:S(2)}, u32[]{:S(2)}) collective-permute-start(bf16[16,1024]{1,0:T(8,128)(2,1)S(1)} %get-tuple-element.44), channel_id=1, source_target_pairs={{0,8},{8,0},{16,24},{24,16},{1,9},{9,1},{17,25},{25,17},{2,10},{10... | collective-permute-start | bytes 98312 | tf_op jit(solution)/shard_map/ppermute | solution.py:476
  15.9 0.5 %query_features.1 = f32[4,16,1024]{2,1,0:T(8,128)S(1)} custom-call(bf16[64,1024]{1,0:T(8,128)(2,1)S(1)} %get-tuple-element.27.refs_0_, f32[3,64,7]{2,1,0:T(8,128)S(1)} %get-tuple-element.28.refs_0_.refs_1_, bf16[16,2176]{1,0:T(8,128)(2,1)S(1)} %get-tuple-element.38.refs_6_.refs_9_.refs_2_, bf16[16,2176]{1,0:T(8,128)(2,1)S(1)} %collective-permute-done.2.refs_8_.refs_3_, ...), custom_call_target="tpu_custom_call" | custom-call | tf_op jit(solution)/shard_map/query_features/pallas_call | solution.py:221
  16.3 0.8 %collective-permute-done.3 = bf16[16,1024]{1,0:T(8,128)(2,1)S(1)} collective-permute-done((bf16[16,1024]{1,0:T(8,128)(2,1)S(1)}, bf16[16,1024]{1,0:T(8,128)(2,1)S(1)}, u32[]{:S(2)}, u32[]{:S(2)}) %collective-permute-start.3) | collective-permute-done | bytes 32800 | tf_op jit(solution)/shard_map/ppermute | solution.py:476
  17.2 0.6 %collective-permute-done.4 = bf16[16,1024]{1,0:T(8,128)(2,1)S(1)} collective-permute-done((bf16[16,1024]{1,0:T(8,128)(2,1)S(1)}, bf16[16,1024]{1,0:T(8,128)(2,1)S(1)}, u32[]{:S(2)}, u32[]{:S(2)}) %collective-permute-start.4) | collective-permute-done | bytes 32800 | tf_op jit(solution)/shard_map/ppermute | solution.py:476
  17.8 0.6 %collective-permute-done.5 = bf16[16,1024]{1,0:T(8,128)(2,1)S(1)} collective-permute-done((bf16[16,1024]{1,0:T(8,128)(2,1)S(1)}, bf16[16,1024]{1,0:T(8,128)(2,1)S(1)}, u32[]{:S(2)}, u32[]{:S(2)}) %collective-permute-start.5) | collective-permute-done | bytes 32800 | tf_op jit(solution)/shard_map/ppermute | solution.py:476
  18.4 2.7 %collective-permute-start.7 = (bf16[4,16,1024]{2,1,0:T(8,128)(2,1)S(1)}, bf16[4,16,1024]{2,1,0:T(8,128)(2,1)S(1)}, u32[]{:S(2)}, u32[]{:S(2)}) collective-permute-start(bf16[4,16,1024]{2,1,0:T(8,128)(2,1)S(1)} %multiply_convert_fusion.refs_1_), channel_id=1, source_target_pairs={{0,4},{1,5},{2,6},{3,7},{4,0},{5,1},{6,2},{7,3},{8,12},{9,13},{10,... | collective-permute-start | bytes 393224 | tf_op jit(solution)/shard_map/ppermute | solution.py:476
  21.1 1.6 %collective-permute-start.11 = (bf16[4,16,1024]{2,1,0:T(8,128)(2,1)S(1)}, bf16[4,16,1024]{2,1,0:T(8,128)(2,1)S(1)}, u32[]{:S(2)}, u32[]{:S(2)}) collective-permute-start(bf16[4,16,1024]{2,1,0:T(8,128)(2,1)S(1)} %multiply_convert_fusion.refs_1_), channel_id=1, source_target_pairs={{0,2},{1,3},{2,0},{3,1},{4,6},{5,7},{6,4},{7,5},{8,10},{9,11},{10,... | collective-permute-start | bytes 393224 | tf_op jit(solution)/shard_map/ppermute | solution.py:476
  22.6 0.2 collective-permute-start.9
  22.8 0.0 collective-permute-start.6
  22.8 5.3 %collective-permute-done.7.refs_3_ = bf16[4,16,1024]{2,1,0:T(8,128)(2,1)S(1)} collective-permute-done((bf16[4,16,1024]{2,1,0:T(8,128)(2,1)S(1)}, bf16[4,16,1024]{2,1,0:T(8,128)(2,1)S(1)}, u32[]{:S(2)}, u32[]{:S(2)}) %collective-permute-start.7) | collective-permute-done | bytes 131104 | tf_op jit(solution)/shard_map/ppermute | solution.py:476
  28.2 0.0 collective-permute-start.8
  28.2 0.0 collective-permute-done.11.refs_4_
  28.2 0.5 %collective-permute-start.12 = (bf16[4,16,1024]{2,1,0:T(8,128)(2,1)S(1)}, bf16[4,16,1024]{2,1,0:T(8,128)(2,1)S(1)}, u32[]{:S(2)}, u32[]{:S(2)}) collective-permute-start(bf16[4,16,1024]{2,1,0:T(8,128)(2,1)S(1)} %collective-permute-done.11.refs_4_), channel_id=1, source_target_pairs={{0,1},{1,0},{2,3},{3,2},{4,5},{5,4},{6,7},{7,6},{8,9},{9,8},{10,11... | collective-permute-start | bytes 393224 | tf_op jit(solution)/shard_map/ppermute | solution.py:476
  28.7 1.0 %collective-permute-done.9.refs_2_ = bf16[4,16,1024]{2,1,0:T(8,128)(2,1)S(1)} collective-permute-done((bf16[4,16,1024]{2,1,0:T(8,128)(2,1)S(1)}, bf16[4,16,1024]{2,1,0:T(8,128)(2,1)S(1)}, u32[]{:S(2)}, u32[]{:S(2)}) %collective-permute-start.9) | collective-permute-done | bytes 131104 | tf_op jit(solution)/shard_map/ppermute | solution.py:476
  29.7 0.0 collective-permute-start.10
  29.7 0.0 collective-permute-done.6.refs_2_
  29.7 0.0 collective-permute-done.8.refs_4_
  29.7 0.8 %project_early.1.refs_1_ = f32[1024,1024]{1,0:T(8,128)S(1)} custom-call(bf16[1024,512]{1,0:T(8,128)(2,1)S(1)} %get-tuple-element.26.refs_0_, bf16[4,16,1024]{2,1,0:T(8,128)(2,1)S(1)} %multiply_convert_fusion.refs_1_, bf16[4,16,1024]{2,1,0:T(8,128)(2,1)S(1)} %collective-permute-done.6.refs_2_, bf16[4,16,1024]{2,1,0:T(8,128)(2,1)S(1)} %collective-permute-done.7.refs_3_, ...), custom_call_target="tpu_custom_call" | custom-call | tf_op jit(solution)/shard_map/project_early/pallas_call | solution.py:407
  30.5 0.0 collective-permute-done.12.refs_5_
  30.5 0.6 %collective-permute-done.10.refs_3_ = bf16[4,16,1024]{2,1,0:T(8,128)(2,1)S(1)} collective-permute-done((bf16[4,16,1024]{2,1,0:T(8,128)(2,1)S(1)}, bf16[4,16,1024]{2,1,0:T(8,128)(2,1)S(1)}, u32[]{:S(2)}, u32[]{:S(2)}) %collective-permute-start.10) | collective-permute-done | bytes 131104 | tf_op jit(solution)/shard_map/ppermute | solution.py:476
  31.0 1.7 %project_late.1 = bf16[1024,1024]{1,0:T(8,128)(2,1)} custom-call(bf16[1024,512]{1,0:T(8,128)(2,1)S(1)} %get-tuple-element.26.refs_0_, f32[1024,1024]{1,0:T(8,128)S(1)} %project_early.1.refs_1_, bf16[4,16,1024]{2,1,0:T(8,128)(2,1)S(1)} %collective-permute-done.9.refs_2_, bf16[4,16,1024]{2,1,0:T(8,128)(2,1)S(1)} %collective-permute-done.10.refs_3_, ...), custom_call_target="tpu_custom_call" | custom-call | tf_op jit(solution)/shard_map/project_late/pallas_call | solution.py:426
  (1 shorter events, 0.0 us)
Async XLA Ops:
  1.9 6.3 %collective-permute-start = (bf16[16,2176]{1,0:T(8,128)(2,1)S(1)}, bf16[16,2176]{1,0:T(8,128)(2,1)S(1)}, u32[]{:S(2)}, u32[]{:S(2)}) collective-permute-start(bf16[16,2176]{1,0:T(8,128)(2,1)S(1)} %get-tuple-element.34), channel_id=1, source_target_pairs={{0,24},{8,16},{16,8},{24,0},{1,25},{9,17},{17,9},{25,1},{2,26},{10... | collective-permute-start | bytes 208904 | tf_op jit(solution)/shard_map/ppermute | solution.py:476
  5.8 4.3 %collective-permute-start.1 = (bf16[16,2176]{1,0:T(8,128)(2,1)S(1)}, bf16[16,2176]{1,0:T(8,128)(2,1)S(1)}, u32[]{:S(2)}, u32[]{:S(2)}) collective-permute-start(bf16[16,2176]{1,0:T(8,128)(2,1)S(1)} %get-tuple-element.35), channel_id=1, source_target_pairs={{0,16},{8,24},{16,0},{24,8},{1,17},{9,25},{17,1},{25,9},{2,18},{10... | collective-permute-start | bytes 208904 | tf_op jit(solution)/shard_map/ppermute | solution.py:476
  6.3 4.3 %collective-permute-start.2 = (bf16[16,2176]{1,0:T(8,128)(2,1)S(1)}, bf16[16,2176]{1,0:T(8,128)(2,1)S(1)}, u32[]{:S(2)}, u32[]{:S(2)}) collective-permute-start(bf16[16,2176]{1,0:T(8,128)(2,1)S(1)} %get-tuple-element.36), channel_id=1, source_target_pairs={{0,8},{8,0},{16,24},{24,16},{1,9},{9,1},{17,25},{25,17},{2,10},{10... | collective-permute-start | bytes 208904 | tf_op jit(solution)/shard_map/ppermute | solution.py:476
  12.3 4.9 %collective-permute-start.3 = (bf16[16,1024]{1,0:T(8,128)(2,1)S(1)}, bf16[16,1024]{1,0:T(8,128)(2,1)S(1)}, u32[]{:S(2)}, u32[]{:S(2)}) collective-permute-start(bf16[16,1024]{1,0:T(8,128)(2,1)S(1)} %get-tuple-element.42), channel_id=1, source_target_pairs={{0,24},{8,16},{16,8},{24,0},{1,25},{9,17},{17,9},{25,1},{2,26},{10... | collective-permute-start | bytes 98312 | tf_op jit(solution)/shard_map/ppermute | solution.py:476
  13.9 3.9 %collective-permute-start.4 = (bf16[16,1024]{1,0:T(8,128)(2,1)S(1)}, bf16[16,1024]{1,0:T(8,128)(2,1)S(1)}, u32[]{:S(2)}, u32[]{:S(2)}) collective-permute-start(bf16[16,1024]{1,0:T(8,128)(2,1)S(1)} %get-tuple-element.43), channel_id=1, source_target_pairs={{0,16},{8,24},{16,0},{24,8},{1,17},{9,25},{17,1},{25,9},{2,18},{10... | collective-permute-start | bytes 98312 | tf_op jit(solution)/shard_map/ppermute | solution.py:476
  14.4 3.9 %collective-permute-start.5 = (bf16[16,1024]{1,0:T(8,128)(2,1)S(1)}, bf16[16,1024]{1,0:T(8,128)(2,1)S(1)}, u32[]{:S(2)}, u32[]{:S(2)}) collective-permute-start(bf16[16,1024]{1,0:T(8,128)(2,1)S(1)} %get-tuple-element.44), channel_id=1, source_target_pairs={{0,8},{8,0},{16,24},{24,16},{1,9},{9,1},{17,25},{25,17},{2,10},{10... | collective-permute-start | bytes 98312 | tf_op jit(solution)/shard_map/ppermute | solution.py:476
  18.4 9.8 %collective-permute-start.7 = (bf16[4,16,1024]{2,1,0:T(8,128)(2,1)S(1)}, bf16[4,16,1024]{2,1,0:T(8,128)(2,1)S(1)}, u32[]{:S(2)}, u32[]{:S(2)}) collective-permute-start(bf16[4,16,1024]{2,1,0:T(8,128)(2,1)S(1)} %multiply_convert_fusion.refs_1_), channel_id=1, source_target_pairs={{0,4},{1,5},{2,6},{3,7},{4,0},{5,1},{6,2},{7,3},{8,12},{9,13},{10,... | collective-permute-start | bytes 393224 | tf_op jit(solution)/shard_map/ppermute | solution.py:476
  21.1 7.1 %collective-permute-start.11 = (bf16[4,16,1024]{2,1,0:T(8,128)(2,1)S(1)}, bf16[4,16,1024]{2,1,0:T(8,128)(2,1)S(1)}, u32[]{:S(2)}, u32[]{:S(2)}) collective-permute-start(bf16[4,16,1024]{2,1,0:T(8,128)(2,1)S(1)} %multiply_convert_fusion.refs_1_), channel_id=1, source_target_pairs={{0,2},{1,3},{2,0},{3,1},{4,6},{5,7},{6,4},{7,5},{8,10},{9,11},{10,... | collective-permute-start | bytes 393224 | tf_op jit(solution)/shard_map/ppermute | solution.py:476
  22.6 7.1 %collective-permute-start.9 = (bf16[4,16,1024]{2,1,0:T(8,128)(2,1)S(1)}, bf16[4,16,1024]{2,1,0:T(8,128)(2,1)S(1)}, u32[]{:S(2)}, u32[]{:S(2)}) collective-permute-start(bf16[4,16,1024]{2,1,0:T(8,128)(2,1)S(1)} %multiply_convert_fusion.refs_1_), channel_id=1, source_target_pairs={{0,6},{1,7},{2,4},{3,5},{4,2},{5,3},{6,0},{7,1},{8,14},{9,15},{10,... | collective-permute-start | bytes 393224 | tf_op jit(solution)/shard_map/ppermute | solution.py:476
  22.8 6.9 %collective-permute-start.6 = (bf16[4,16,1024]{2,1,0:T(8,128)(2,1)S(1)}, bf16[4,16,1024]{2,1,0:T(8,128)(2,1)S(1)}, u32[]{:S(2)}, u32[]{:S(2)}) collective-permute-start(bf16[4,16,1024]{2,1,0:T(8,128)(2,1)S(1)} %multiply_convert_fusion.refs_1_), channel_id=1, source_target_pairs={{0,1},{1,0},{2,3},{3,2},{4,5},{5,4},{6,7},{7,6},{8,9},{9,8},{10,11... | collective-permute-start | bytes 393224 | tf_op jit(solution)/shard_map/ppermute | solution.py:476
  28.2 1.6 %collective-permute-start.8 = (bf16[4,16,1024]{2,1,0:T(8,128)(2,1)S(1)}, bf16[4,16,1024]{2,1,0:T(8,128)(2,1)S(1)}, u32[]{:S(2)}, u32[]{:S(2)}) collective-permute-start(bf16[4,16,1024]{2,1,0:T(8,128)(2,1)S(1)} %collective-permute-done.7.refs_3_), channel_id=1, source_target_pairs={{0,1},{1,0},{2,3},{3,2},{4,5},{5,4},{6,7},{7,6},{8,9},{9,8},{10,11... | collective-permute-start | bytes 393224 | tf_op jit(solution)/shard_map/ppermute | solution.py:476
  28.2 2.3 %collective-permute-start.12 = (bf16[4,16,1024]{2,1,0:T(8,128)(2,1)S(1)}, bf16[4,16,1024]{2,1,0:T(8,128)(2,1)S(1)}, u32[]{:S(2)}, u32[]{:S(2)}) collective-permute-start(bf16[4,16,1024]{2,1,0:T(8,128)(2,1)S(1)} %collective-permute-done.11.refs_4_), channel_id=1, source_target_pairs={{0,1},{1,0},{2,3},{3,2},{4,5},{5,4},{6,7},{7,6},{8,9},{9,8},{10,11... | collective-permute-start | bytes 393224 | tf_op jit(solution)/shard_map/ppermute | solution.py:476
  29.7 1.3 %collective-permute-start.10 = (bf16[4,16,1024]{2,1,0:T(8,128)(2,1)S(1)}, bf16[4,16,1024]{2,1,0:T(8,128)(2,1)S(1)}, u32[]{:S(2)}, u32[]{:S(2)}) collective-permute-start(bf16[4,16,1024]{2,1,0:T(8,128)(2,1)S(1)} %collective-permute-done.9.refs_2_), channel_id=1, source_target_pairs={{0,1},{1,0},{2,3},{3,2},{4,5},{5,4},{6,7},{7,6},{8,9},{9,8},{10,11... | collective-permute-start | bytes 393224 | tf_op jit(solution)/shard_map/ppermute | solution.py:476

commit v7 on v6

--- a/solution.py
+++ b/solution.py
@@ -243,19 +243,28 @@
     if rim:
         lane = lax.broadcasted_iota(jnp.int32, (chans, LANES), 1)
         own = pl.ds(pl.multiple_of(base, chans), chans)
-        edges[0] = jnp.zeros((chans, LANES), jnp.float32)
+        edges[0] = jnp.zeros((chans, LANES), jnp.bfloat16)
         for mask in range(nodes):
-            edges[(place ^ mask) + 1] = pieces[mask][:, 2 * block :].astype(jnp.float32)
+            edges[(place ^ mask) + 1] = pieces[mask][:, 2 * block :]
+        wide = []
+        for stream in range(2):
+            taps = taps_ref[1 + stream, own, :]
+            wide.append(
+                [jnp.broadcast_to(taps[:, tap : tap + 1], (chans, LANES)) for tap in range(rim + 1)]
+            )
 
     def repaired(mask, tile):
-        before, now = edges[place ^ mask], pieces[mask][:, 2 * block :].astype(jnp.float32)
+        before, now = edges[place ^ mask], pieces[mask][:, 2 * block :]
         product = None
         for stream in range(2):
             back = (LANES - stream * LANE_V) % LANES
             joined = jnp.where(lane < stream * LANE_V + rim, before, now)
             if back:
                 joined = pltpu.roll(joined, back, 1)
-            featured = rolled_taps(joined, taps_ref[1 + stream, own, :])
+            featured = wide[stream][0] * joined.astype(jnp.float32)
+            for shift in range(1, rim + 1):
+                moved = pltpu.roll(joined, shift, 1).astype(jnp.float32)
+                featured = featured + wide[stream][shift] * moved
             product = featured if product is None else product * featured
         product = pltpu.roll(product, LANES - rim, 1).astype(jnp.bfloat16).astype(jnp.float32)
         return jnp.where(lane < rim, product, tile)
@@ -346,7 +355,7 @@
         out_specs=[near] * nodes,
         scratch_shapes=[
             pltpu.VMEM((2, (chans + 1) * (rows + PAD), LANES), jnp.float32),
-            pltpu.VMEM((nodes + 1, chans, LANES), jnp.float32),
+            pltpu.VMEM((nodes + 1, chans, LANES), jnp.bfloat16),
             pltpu.VMEM(((chans + 1) * (rows + PAD), LANES), jnp.float32),
         ],
         compiler_params=pltpu.CompilerParams(vmem_limit_bytes=24 << 20),

time: 33 us -> 32.8 us (level)
  no operation moved by 1% of the time
where the time goes in v7:
time: 32.8 us; the launch traced here: 32.6 us
  starting transfers between devices  13.1 us (40%)
  waiting for transfers between devices  11.7 us (36%)
  Pallas kernels  7.66 us (23%)
    ppermute x13, starting transfers between devices, swapped(): lax.ppermute(block, axis, [(i, i ^ mask) for i in range(lax.axis_size(axi...  13.1 us
    ppermute x13, waiting for transfers between devices, swapped(): lax.ppermute(block, axis, [(i, i ^ mask) for i in range(lax.axis_size(axi...  11.7 us
    pallas_call x1, Pallas kernels, pack(): pl.pallas_call(lambda *refs: pack_kernel(nodes, chans, *refs), out_shape=...  1.86 us
    pallas_call x1, Pallas kernels, project_late(): pl.pallas_call(lambda *refs: final_kernel(tuple(late), cuts, *refs), out_...  1.67 us
    pallas_call x1, Pallas kernels, long_mix(): pl.pallas_call(lambda *refs: long_kernel(nodes, chans, per_node, rim, *re...  1.49 us
    pallas_call x1, Pallas kernels, near_tables(): pl.pallas_call(lambda *refs: tables_kernel(count, *refs), out_shape=[jax....  1.4 us
    pallas_call x1, Pallas kernels, project_early(): pl.pallas_call(lambda *refs: partial_kernel(tuple(early), features // 4,...  0.77 us
  transfers between devices with their start and end apart: 13, of which 9 were waited for; matrix products, arithmetic and copies ran while one was open for 0% of the time, Pallas kernels for 8%

profile of v7, /device:TPU:0, one launch (start us, length us, event | category | flops | bytes accessed | tf_op | source)
XLA Modules:
  0.0 32.6 jit_solution(13801917354462869967)
XLA Ops:
  0.0 1.9 %pack.1 = (bf16[16,2176]{1,0:T(8,128)(2,1)S(1)}, bf16[16,2176]{1,0:T(8,128)(2,1)S(1)}, bf16[16,2176]{1,0:T(8,128)(2,1)S(1)}, bf16[16,2176]{1,0:T(8,128)(2,1)S(1)...) custom-call(bf16[3,64,1024]{2,1,0:T(8,128)(2,1)} %refs_0_.2, f32[64,1024]{1,0:T(8,128)} %refs_1_.2, ...), custom_call_target="tpu_custom_call" | custom-call | tf_op jit(solution)/shard_map/pack/pallas_call | solution.py:172
  1.9 4.0 %collective-permute-start = (bf16[16,2176]{1,0:T(8,128)(2,1)S(1)}, bf16[16,2176]{1,0:T(8,128)(2,1)S(1)}, u32[]{:S(2)}, u32[]{:S(2)}) collective-permute-start(bf16[16,2176]{1,0:T(8,128)(2,1)S(1)} %get-tuple-element.34), channel_id=1, source_target_pairs={{0,24},{8,16},{16,8},{24,0},{1,25},{9,17},{17,9},{25,1},{2,26},{10... | collective-permute-start | bytes 208904 | tf_op jit(solution)/shard_map/ppermute | solution.py:485
  5.8 0.5 %collective-permute-start.1 = (bf16[16,2176]{1,0:T(8,128)(2,1)S(1)}, bf16[16,2176]{1,0:T(8,128)(2,1)S(1)}, u32[]{:S(2)}, u32[]{:S(2)}) collective-permute-start(bf16[16,2176]{1,0:T(8,128)(2,1)S(1)} %get-tuple-element.35), channel_id=1, source_target_pairs={{0,16},{8,24},{16,0},{24,8},{1,17},{9,25},{17,1},{25,9},{2,18},{10... | collective-permute-start | bytes 208904 | tf_op jit(solution)/shard_map/ppermute | solution.py:485
  6.3 0.1 collective-permute-start.2
  6.5 1.4 %near_tables.1 = (bf16[1024,512]{1,0:T(8,128)(2,1)S(1)}, bf16[64,64]{1,0:T(8,128)(2,1)S(1)}, f32[32,256]{1,0:T(8,128)S(1)}, bf16[768,256]{1,0:T(8,128)(2,1)S(1)}...) custom-call(bf16[1024,512]{1,0:T(8,128)(2,1)} %refs_0_.3, bf16[64,64]{1,0:T(8,128)(2,1)} %constant.8.clone.refs_1_, ...), custom_call_target="tpu_custom_call" | custom-call | tf_op jit(solution)/shard_map/near_tables/pallas_call | solution.py:90
  7.9 0.3 collective-permute-done.refs_6_.refs_5_
  8.1 2.0 %collective-permute-done.1.refs_7_.refs_4_ = bf16[16,2176]{1,0:T(8,128)(2,1)S(1)} collective-permute-done((bf16[16,2176]{1,0:T(8,128)(2,1)S(1)}, bf16[16,2176]{1,0:T(8,128)(2,1)S(1)}, u32[]{:S(2)}, u32[]{:S(2)}) %collective-permute-start.1) | collective-permute-done | bytes 69664 | tf_op jit(solution)/shard_map/ppermute | solution.py:485
  10.1 0.5 %collective-permute-done.2.refs_8_.refs_3_ = bf16[16,2176]{1,0:T(8,128)(2,1)S(1)} collective-permute-done((bf16[16,2176]{1,0:T(8,128)(2,1)S(1)}, bf16[16,2176]{1,0:T(8,128)(2,1)S(1)}, u32[]{:S(2)}, u32[]{:S(2)}) %collective-permute-start.2) | collective-permute-done | bytes 69664 | tf_op jit(solution)/shard_map/ppermute | solution.py:485
  10.6 1.5 %long_mix.1 = (bf16[16,1024]{1,0:T(8,128)(2,1)S(1)}, bf16[16,1024]{1,0:T(8,128)(2,1)S(1)}, bf16[16,1024]{1,0:T(8,128)(2,1)S(1)}, bf16[16,1024]{1,0:T(8,128)(2,1)S(1)}) custom-call(f32[3,64,7]{2,1,0:T(8,128)S(1)} %get-tuple-element.28.refs_0_.refs_1_, bf16[64,64]{1,0:T(8,128)(2,1)S(1)} %get-tuple-element.29.refs_1_, f32[32,256]{1,0:T(8,128)S(1)} %get-tuple-element.30.refs_2_, ...), custom_call_target="tpu_custom_call" | custom-call | tf_op jit(solution)/shard_map/long_mix/pallas_call | solution.py:351
  12.1 1.6 %collective-permute-start.3 = (bf16[16,1024]{1,0:T(8,128)(2,1)S(1)}, bf16[16,1024]{1,0:T(8,128)(2,1)S(1)}, u32[]{:S(2)}, u32[]{:S(2)}) collective-permute-start(bf16[16,1024]{1,0:T(8,128)(2,1)S(1)} %get-tuple-element.42), channel_id=1, source_target_pairs={{0,24},{8,16},{16,8},{24,0},{1,25},{9,17},{17,9},{25,1},{2,26},{10... | collective-permute-start | bytes 98312 | tf_op jit(solution)/shard_map/ppermute | solution.py:485
  13.7 0.6 %collective-permute-start.4 = (bf16[16,1024]{1,0:T(8,128)(2,1)S(1)}, bf16[16,1024]{1,0:T(8,128)(2,1)S(1)}, u32[]{:S(2)}, u32[]{:S(2)}) collective-permute-start(bf16[16,1024]{1,0:T(8,128)(2,1)S(1)} %get-tuple-element.43), channel_id=1, source_target_pairs={{0,16},{8,24},{16,0},{24,8},{1,17},{9,25},{17,1},{25,9},{2,18},{10... | collective-permute-start | bytes 98312 | tf_op jit(solution)/shard_map/ppermute | solution.py:485
  14.3 1.4 %collective-permute-start.5 = (bf16[16,1024]{1,0:T(8,128)(2,1)S(1)}, bf16[16,1024]{1,0:T(8,128)(2,1)S(1)}, u32[]{:S(2)}, u32[]{:S(2)}) collective-permute-start(bf16[16,1024]{1,0:T(8,128)(2,1)S(1)} %get-tuple-element.44), channel_id=1, source_target_pairs={{0,8},{8,0},{16,24},{24,16},{1,9},{9,1},{17,25},{25,17},{2,10},{10... | collective-permute-start | bytes 98312 | tf_op jit(solution)/shard_map/ppermute | solution.py:485
  15.7 0.5 %query_features.1 = f32[4,16,1024]{2,1,0:T(8,128)S(1)} custom-call(bf16[64,1024]{1,0:T(8,128)(2,1)S(1)} %get-tuple-element.27.refs_0_, f32[3,64,7]{2,1,0:T(8,128)S(1)} %get-tuple-element.28.refs_0_.refs_1_, bf16[16,2176]{1,0:T(8,128)(2,1)S(1)} %get-tuple-element.38.refs_6_.refs_9_.refs_2_, bf16[16,2176]{1,0:T(8,128)(2,1)S(1)} %collective-permute-done.2.refs_8_.refs_3_, ...), custom_call_target="tpu_custom_call" | custom-call | tf_op jit(solution)/shard_map/query_features/pallas_call | solution.py:221
  16.2 0.8 %collective-permute-done.3 = bf16[16,1024]{1,0:T(8,128)(2,1)S(1)} collective-permute-done((bf16[16,1024]{1,0:T(8,128)(2,1)S(1)}, bf16[16,1024]{1,0:T(8,128)(2,1)S(1)}, u32[]{:S(2)}, u32[]{:S(2)}) %collective-permute-start.3) | collective-permute-done | bytes 32800 | tf_op jit(solution)/shard_map/ppermute | solution.py:485
  17.0 0.6 %collective-permute-done.4 = bf16[16,1024]{1,0:T(8,128)(2,1)S(1)} collective-permute-done((bf16[16,1024]{1,0:T(8,128)(2,1)S(1)}, bf16[16,1024]{1,0:T(8,128)(2,1)S(1)}, u32[]{:S(2)}, u32[]{:S(2)}) %collective-permute-start.4) | collective-permute-done | bytes 32800 | tf_op jit(solution)/shard_map/ppermute | solution.py:485
  17.6 0.6 %collective-permute-done.5 = bf16[16,1024]{1,0:T(8,128)(2,1)S(1)} collective-permute-done((bf16[16,1024]{1,0:T(8,128)(2,1)S(1)}, bf16[16,1024]{1,0:T(8,128)(2,1)S(1)}, u32[]{:S(2)}, u32[]{:S(2)}) %collective-permute-start.5) | collective-permute-done | bytes 32800 | tf_op jit(solution)/shard_map/ppermute | solution.py:485
  18.2 2.6 %collective-permute-start.7 = (bf16[4,16,1024]{2,1,0:T(8,128)(2,1)S(1)}, bf16[4,16,1024]{2,1,0:T(8,128)(2,1)S(1)}, u32[]{:S(2)}, u32[]{:S(2)}) collective-permute-start(bf16[4,16,1024]{2,1,0:T(8,128)(2,1)S(1)} %multiply_convert_fusion.refs_1_), channel_id=1, source_target_pairs={{0,4},{1,5},{2,6},{3,7},{4,0},{5,1},{6,2},{7,3},{8,12},{9,13},{10,... | collective-permute-start | bytes 393224 | tf_op jit(solution)/shard_map/ppermute | solution.py:485
  20.9 1.6 %collective-permute-start.11 = (bf16[4,16,1024]{2,1,0:T(8,128)(2,1)S(1)}, bf16[4,16,1024]{2,1,0:T(8,128)(2,1)S(1)}, u32[]{:S(2)}, u32[]{:S(2)}) collective-permute-start(bf16[4,16,1024]{2,1,0:T(8,128)(2,1)S(1)} %multiply_convert_fusion.refs_1_), channel_id=1, source_target_pairs={{0,2},{1,3},{2,0},{3,1},{4,6},{5,7},{6,4},{7,5},{8,10},{9,11},{10,... | collective-permute-start | bytes 393224 | tf_op jit(solution)/shard_map/ppermute | solution.py:485
  22.5 0.2 collective-permute-start.9
  22.7 0.0 collective-permute-start.6
  22.7 5.3 %collective-permute-done.7.refs_3_ = bf16[4,16,1024]{2,1,0:T(8,128)(2,1)S(1)} collective-permute-done((bf16[4,16,1024]{2,1,0:T(8,128)(2,1)S(1)}, bf16[4,16,1024]{2,1,0:T(8,128)(2,1)S(1)}, u32[]{:S(2)}, u32[]{:S(2)}) %collective-permute-start.7) | collective-permute-done | bytes 131104 | tf_op jit(solution)/shard_map/ppermute | solution.py:485
  28.0 0.0 collective-permute-start.8
  28.0 0.0 collective-permute-done.11.refs_4_
  28.0 0.5 %collective-permute-start.12 = (bf16[4,16,1024]{2,1,0:T(8,128)(2,1)S(1)}, bf16[4,16,1024]{2,1,0:T(8,128)(2,1)S(1)}, u32[]{:S(2)}, u32[]{:S(2)}) collective-permute-start(bf16[4,16,1024]{2,1,0:T(8,128)(2,1)S(1)} %collective-permute-done.11.refs_4_), channel_id=1, source_target_pairs={{0,1},{1,0},{2,3},{3,2},{4,5},{5,4},{6,7},{7,6},{8,9},{9,8},{10,11... | collective-permute-start | bytes 393224 | tf_op jit(solution)/shard_map/ppermute | solution.py:485
  28.5 1.0 %collective-permute-done.9.refs_2_ = bf16[4,16,1024]{2,1,0:T(8,128)(2,1)S(1)} collective-permute-done((bf16[4,16,1024]{2,1,0:T(8,128)(2,1)S(1)}, bf16[4,16,1024]{2,1,0:T(8,128)(2,1)S(1)}, u32[]{:S(2)}, u32[]{:S(2)}) %collective-permute-start.9) | collective-permute-done | bytes 131104 | tf_op jit(solution)/shard_map/ppermute | solution.py:485
  29.5 0.0 collective-permute-start.10
  29.5 0.0 collective-permute-done.6.refs_2_
  29.5 0.0 collective-permute-done.8.refs_4_
  29.6 0.8 %project_early.1.refs_1_ = f32[1024,1024]{1,0:T(8,128)S(1)} custom-call(bf16[1024,512]{1,0:T(8,128)(2,1)S(1)} %get-tuple-element.26.refs_0_, bf16[4,16,1024]{2,1,0:T(8,128)(2,1)S(1)} %multiply_convert_fusion.refs_1_, bf16[4,16,1024]{2,1,0:T(8,128)(2,1)S(1)} %collective-permute-done.6.refs_2_, bf16[4,16,1024]{2,1,0:T(8,128)(2,1)S(1)} %collective-permute-done.7.refs_3_, ...), custom_call_target="tpu_custom_call" | custom-call | tf_op jit(solution)/shard_map/project_early/pallas_call | solution.py:416
  30.3 0.0 collective-permute-done.12.refs_5_
  30.3 0.6 %collective-permute-done.10.refs_3_ = bf16[4,16,1024]{2,1,0:T(8,128)(2,1)S(1)} collective-permute-done((bf16[4,16,1024]{2,1,0:T(8,128)(2,1)S(1)}, bf16[4,16,1024]{2,1,0:T(8,128)(2,1)S(1)}, u32[]{:S(2)}, u32[]{:S(2)}) %collective-permute-start.10) | collective-permute-done | bytes 131104 | tf_op jit(solution)/shard_map/ppermute | solution.py:485
  30.9 1.7 %project_late.1 = bf16[1024,1024]{1,0:T(8,128)(2,1)} custom-call(bf16[1024,512]{1,0:T(8,128)(2,1)S(1)} %get-tuple-element.26.refs_0_, f32[1024,1024]{1,0:T(8,128)S(1)} %project_early.1.refs_1_, bf16[4,16,1024]{2,1,0:T(8,128)(2,1)S(1)} %collective-permute-done.9.refs_2_, bf16[4,16,1024]{2,1,0:T(8,128)(2,1)S(1)} %collective-permute-done.10.refs_3_, ...), custom_call_target="tpu_custom_call" | custom-call | tf_op jit(solution)/shard_map/project_late/pallas_call | solution.py:435
  (1 shorter events, 0.0 us)
Async XLA Ops:
  1.9 6.3 %collective-permute-start = (bf16[16,2176]{1,0:T(8,128)(2,1)S(1)}, bf16[16,2176]{1,0:T(8,128)(2,1)S(1)}, u32[]{:S(2)}, u32[]{:S(2)}) collective-permute-start(bf16[16,2176]{1,0:T(8,128)(2,1)S(1)} %get-tuple-element.34), channel_id=1, source_target_pairs={{0,24},{8,16},{16,8},{24,0},{1,25},{9,17},{17,9},{25,1},{2,26},{10... | collective-permute-start | bytes 208904 | tf_op jit(solution)/shard_map/ppermute | solution.py:485
  5.8 4.3 %collective-permute-start.1 = (bf16[16,2176]{1,0:T(8,128)(2,1)S(1)}, bf16[16,2176]{1,0:T(8,128)(2,1)S(1)}, u32[]{:S(2)}, u32[]{:S(2)}) collective-permute-start(bf16[16,2176]{1,0:T(8,128)(2,1)S(1)} %get-tuple-element.35), channel_id=1, source_target_pairs={{0,16},{8,24},{16,0},{24,8},{1,17},{9,25},{17,1},{25,9},{2,18},{10... | collective-permute-start | bytes 208904 | tf_op jit(solution)/shard_map/ppermute | solution.py:485
  6.3 4.3 %collective-permute-start.2 = (bf16[16,2176]{1,0:T(8,128)(2,1)S(1)}, bf16[16,2176]{1,0:T(8,128)(2,1)S(1)}, u32[]{:S(2)}, u32[]{:S(2)}) collective-permute-start(bf16[16,2176]{1,0:T(8,128)(2,1)S(1)} %get-tuple-element.36), channel_id=1, source_target_pairs={{0,8},{8,0},{16,24},{24,16},{1,9},{9,1},{17,25},{25,17},{2,10},{10... | collective-permute-start | bytes 208904 | tf_op jit(solution)/shard_map/ppermute | solution.py:485
  12.1 4.9 %collective-permute-start.3 = (bf16[16,1024]{1,0:T(8,128)(2,1)S(1)}, bf16[16,1024]{1,0:T(8,128)(2,1)S(1)}, u32[]{:S(2)}, u32[]{:S(2)}) collective-permute-start(bf16[16,1024]{1,0:T(8,128)(2,1)S(1)} %get-tuple-element.42), channel_id=1, source_target_pairs={{0,24},{8,16},{16,8},{24,0},{1,25},{9,17},{17,9},{25,1},{2,26},{10... | collective-permute-start | bytes 98312 | tf_op jit(solution)/shard_map/ppermute | solution.py:485
  13.7 3.9 %collective-permute-start.4 = (bf16[16,1024]{1,0:T(8,128)(2,1)S(1)}, bf16[16,1024]{1,0:T(8,128)(2,1)S(1)}, u32[]{:S(2)}, u32[]{:S(2)}) collective-permute-start(bf16[16,1024]{1,0:T(8,128)(2,1)S(1)} %get-tuple-element.43), channel_id=1, source_target_pairs={{0,16},{8,24},{16,0},{24,8},{1,17},{9,25},{17,1},{25,9},{2,18},{10... | collective-permute-start | bytes 98312 | tf_op jit(solution)/shard_map/ppermute | solution.py:485
  14.3 3.9 %collective-permute-start.5 = (bf16[16,1024]{1,0:T(8,128)(2,1)S(1)}, bf16[16,1024]{1,0:T(8,128)(2,1)S(1)}, u32[]{:S(2)}, u32[]{:S(2)}) collective-permute-start(bf16[16,1024]{1,0:T(8,128)(2,1)S(1)} %get-tuple-element.44), channel_id=1, source_target_pairs={{0,8},{8,0},{16,24},{24,16},{1,9},{9,1},{17,25},{25,17},{2,10},{10... | collective-permute-start | bytes 98312 | tf_op jit(solution)/shard_map/ppermute | solution.py:485
  18.2 9.8 %collective-permute-start.7 = (bf16[4,16,1024]{2,1,0:T(8,128)(2,1)S(1)}, bf16[4,16,1024]{2,1,0:T(8,128)(2,1)S(1)}, u32[]{:S(2)}, u32[]{:S(2)}) collective-permute-start(bf16[4,16,1024]{2,1,0:T(8,128)(2,1)S(1)} %multiply_convert_fusion.refs_1_), channel_id=1, source_target_pairs={{0,4},{1,5},{2,6},{3,7},{4,0},{5,1},{6,2},{7,3},{8,12},{9,13},{10,... | collective-permute-start | bytes 393224 | tf_op jit(solution)/shard_map/ppermute | solution.py:485
  20.9 7.1 %collective-permute-start.11 = (bf16[4,16,1024]{2,1,0:T(8,128)(2,1)S(1)}, bf16[4,16,1024]{2,1,0:T(8,128)(2,1)S(1)}, u32[]{:S(2)}, u32[]{:S(2)}) collective-permute-start(bf16[4,16,1024]{2,1,0:T(8,128)(2,1)S(1)} %multiply_convert_fusion.refs_1_), channel_id=1, source_target_pairs={{0,2},{1,3},{2,0},{3,1},{4,6},{5,7},{6,4},{7,5},{8,10},{9,11},{10,... | collective-permute-start | bytes 393224 | tf_op jit(solution)/shard_map/ppermute | solution.py:485
  22.5 7.1 %collective-permute-start.9 = (bf16[4,16,1024]{2,1,0:T(8,128)(2,1)S(1)}, bf16[4,16,1024]{2,1,0:T(8,128)(2,1)S(1)}, u32[]{:S(2)}, u32[]{:S(2)}) collective-permute-start(bf16[4,16,1024]{2,1,0:T(8,128)(2,1)S(1)} %multiply_convert_fusion.refs_1_), channel_id=1, source_target_pairs={{0,6},{1,7},{2,4},{3,5},{4,2},{5,3},{6,0},{7,1},{8,14},{9,15},{10,... | collective-permute-start | bytes 393224 | tf_op jit(solution)/shard_map/ppermute | solution.py:485
  22.7 6.9 %collective-permute-start.6 = (bf16[4,16,1024]{2,1,0:T(8,128)(2,1)S(1)}, bf16[4,16,1024]{2,1,0:T(8,128)(2,1)S(1)}, u32[]{:S(2)}, u32[]{:S(2)}) collective-permute-start(bf16[4,16,1024]{2,1,0:T(8,128)(2,1)S(1)} %multiply_convert_fusion.refs_1_), channel_id=1, source_target_pairs={{0,1},{1,0},{2,3},{3,2},{4,5},{5,4},{6,7},{7,6},{8,9},{9,8},{10,11... | collective-permute-start | bytes 393224 | tf_op jit(solution)/shard_map/ppermute | solution.py:485
  28.0 1.6 %collective-permute-start.8 = (bf16[4,16,1024]{2,1,0:T(8,128)(2,1)S(1)}, bf16[4,16,1024]{2,1,0:T(8,128)(2,1)S(1)}, u32[]{:S(2)}, u32[]{:S(2)}) collective-permute-start(bf16[4,16,1024]{2,1,0:T(8,128)(2,1)S(1)} %collective-permute-done.7.refs_3_), channel_id=1, source_target_pairs={{0,1},{1,0},{2,3},{3,2},{4,5},{5,4},{6,7},{7,6},{8,9},{9,8},{10,11... | collective-permute-start | bytes 393224 | tf_op jit(solution)/shard_map/ppermute | solution.py:485
  28.0 2.3 %collective-permute-start.12 = (bf16[4,16,1024]{2,1,0:T(8,128)(2,1)S(1)}, bf16[4,16,1024]{2,1,0:T(8,128)(2,1)S(1)}, u32[]{:S(2)}, u32[]{:S(2)}) collective-permute-start(bf16[4,16,1024]{2,1,0:T(8,128)(2,1)S(1)} %collective-permute-done.11.refs_4_), channel_id=1, source_target_pairs={{0,1},{1,0},{2,3},{3,2},{4,5},{5,4},{6,7},{7,6},{8,9},{9,8},{10,11... | collective-permute-start | bytes 393224 | tf_op jit(solution)/shard_map/ppermute | solution.py:485
  29.5 1.3 %collective-permute-start.10 = (bf16[4,16,1024]{2,1,0:T(8,128)(2,1)S(1)}, bf16[4,16,1024]{2,1,0:T(8,128)(2,1)S(1)}, u32[]{:S(2)}, u32[]{:S(2)}) collective-permute-start(bf16[4,16,1024]{2,1,0:T(8,128)(2,1)S(1)} %collective-permute-done.9.refs_2_), channel_id=1, source_target_pairs={{0,1},{1,0},{2,3},{3,2},{4,5},{5,4},{6,7},{7,6},{8,9},{9,8},{10,11... | collective-permute-start | bytes 393224 | tf_op jit(solution)/shard_map/ppermute | solution.py:485

commit v8 on v7

--- a/solution.py
+++ b/solution.py
@@ -54,11 +54,31 @@
     return jnp.dot(left, right, preferred_element_type=jnp.float32)
 
 
-def rolled_taps(values, taps):
-    total = taps[:, :1] * values
-    for shift in range(1, taps.shape[1]):
-        total = total + taps[:, shift : shift + 1] * pltpu.roll(values, shift, 1)
+def rolled_taps(values, weights):
+    total = weights[0] * values
+    for shift, weight in enumerate(weights[1:], 1):
+        total = total + weight * pltpu.roll(values, shift, 1)
     return total
+
+
+def widened(flat):
+    count, every = flat.shape
+    rest = jnp.concatenate([flat, jnp.zeros((8 - count, every), jnp.float32)], axis=0)
+    parts = []
+    for _ in range(3):
+        part = rest.astype(jnp.bfloat16)
+        rest = rest - part.astype(jnp.float32)
+        parts.append(part.astype(jnp.float32))
+    shape = (8, count * LANES)
+    tap = lax.broadcasted_iota(jnp.int32, shape, 0) * LANES
+    lane = lax.broadcasted_iota(jnp.int32, shape, 1)
+    ones = jnp.where((lane >= tap) & (lane < tap + LANES), 1.0, 0.0)
+    left = jnp.concatenate(parts, axis=0).T.astype(jnp.bfloat16)
+    return dot(left, jnp.concatenate([ones] * 3, axis=0).astype(jnp.bfloat16))
+
+
+def tap_tiles(wide_ref, stream, rows):
+    return [wide_ref[stream, rows, at : at + LANES] for at in range(0, wide_ref.shape[2], LANES)]
 
 
 def in_hbm(*arrays):
@@ -104,11 +124,11 @@
 
 def pack_kernel(nodes, chans, qkv_ref, filter_ref, flat_ref, *refs):
     outs = refs[:nodes]
-    query_ref, taps_ref = refs[nodes : nodes + 2]
+    query_ref, wide_ref = refs[nodes : nodes + 2]
     filters, streams, flat, sems = refs[nodes + 2 :]
     place = lax.axis_index("ctx")
     block = qkv_ref.shape[2]
-    rim = taps_ref.shape[2] - 1
+    rim = flat_ref.shape[1] - 1
     shares = [
         pl.ds(pl.multiple_of((place ^ mask) * chans, chans), chans) for mask in range(nodes)
     ]
@@ -122,7 +142,7 @@
 
     flat_move.wait()
     for stream in range(3):
-        taps_ref[stream] = flat[stream].T
+        wide_ref[stream] = widened(flat[stream])
     query_move.wait()
     edges = jnp.zeros((chans, LANES), jnp.float32)
     for share in range(nodes):
@@ -138,10 +158,7 @@
             ends = jnp.where(lane < rim, values[:, :LANES], values[:, block - LANES :])
             at = stream * LANE_V
             edge = jnp.where(lane < at + LANE_V, pltpu.roll(ends, at + rim, 1), edge)
-            taps = taps_ref[1 + stream, rows, :]
-            wide = [
-                jnp.broadcast_to(taps[:, tap : tap + 1], (chans, LANES)) for tap in range(rim + 1)
-            ]
+            wide = tap_tiles(wide_ref, 1 + stream, rows)
             raw = streams[stream, rows, :]
             totals = []
             for index in range(block // LANES):
@@ -169,12 +186,12 @@
     far = pl.BlockSpec(memory_space=pltpu.HBM)
     near = pl.BlockSpec(memory_space=pltpu.VMEM)
     flat = jnp.swapaxes(short_taps, 1, 2)
-    *pieces, query, taps = pl.pallas_call(
+    *pieces, query, wide = pl.pallas_call(
         lambda *refs: pack_kernel(nodes, chans, *refs),
         out_shape=[jax.ShapeDtypeStruct((chans, 2 * block + LANES), jnp.bfloat16)] * nodes
         + [
             jax.ShapeDtypeStruct((every, block), jnp.bfloat16),
-            jax.ShapeDtypeStruct(short_taps.shape, jnp.float32),
+            jax.ShapeDtypeStruct((3, every, short_taps.shape[2] * LANES), jnp.float32),
         ],
         in_specs=[far] * 3,
         out_specs=[near] * (nodes + 2),
@@ -187,15 +204,15 @@
         compiler_params=pltpu.CompilerParams(vmem_limit_bytes=16 << 20),
         name="pack",
     )(*in_hbm(qkv, long_filter, flat))
-    return pieces, query, taps
-
-
-def query_kernel(nodes, query_ref, taps_ref, *refs):
+    return pieces, query, wide
+
+
+def query_kernel(nodes, query_ref, wide_ref, *refs):
     pieces = refs[:nodes]
     out_ref = refs[nodes]
     place = lax.axis_index("ctx")
     _, chans, block = out_ref.shape
-    rim = taps_ref.shape[2] - 1
+    rim = wide_ref.shape[2] // LANES - 1
     lane = lax.broadcasted_iota(jnp.int32, (chans, LANES), 1)
     edge = jnp.zeros((chans, LANES), jnp.float32)
     for mask in range(1, nodes):
@@ -205,18 +222,18 @@
     for mask in range(nodes):
         share = place ^ mask
         rows = pl.ds(pl.multiple_of(share * chans, chans), chans)
-        taps = taps_ref[0, rows, :]
+        weights = [tile[:, :1] for tile in tap_tiles(wide_ref, 0, rows)]
         values = query_ref[rows, :].astype(jnp.float32)
         history = pltpu.roll(edge, LANES - LANE_Q - (share + 1) * rim, 1)
-        first = taps[:, :1] * values[:, :LANES]
+        first = weights[0] * values[:, :LANES]
         for shift in range(1, rim + 1):
             joined = jnp.where(lane >= LANES - shift, history, values[:, :LANES])
-            first = first + taps[:, shift : shift + 1] * pltpu.roll(joined, shift, 1)
-        out_ref[nodes - 1 - mask] = rolled_taps(values, taps)
+            first = first + weights[shift] * pltpu.roll(joined, shift, 1)
+        out_ref[nodes - 1 - mask] = rolled_taps(values, weights)
         out_ref[nodes - 1 - mask, :, :LANES] = first
 
 
-def query_features(query, short_taps, pieces, nodes, chans):
+def query_features(query, wide, pieces, nodes, chans):
     near = pl.BlockSpec(memory_space=pltpu.VMEM)
     return pl.pallas_call(
         lambda *refs: query_kernel(nodes, *refs),
@@ -225,11 +242,11 @@
         out_specs=near,
         compiler_params=pltpu.CompilerParams(vmem_limit_bytes=16 << 20),
         name="query_features",
-    )(query, short_taps, *pieces)
+    )(query, wide, *pieces)
 
 
 def long_kernel(
-    nodes, chans, per_node, rim, taps_ref, first_ref, twist_ref, second_ref, last_ref, skip_ref, *refs
+    nodes, chans, per_node, rim, wide_ref, first_ref, twist_ref, second_ref, last_ref, skip_ref, *refs
 ):
     pieces = refs[:nodes][::-1]
     outs = refs[nodes : 2 * nodes]
@@ -246,12 +263,7 @@
         edges[0] = jnp.zeros((chans, LANES), jnp.bfloat16)
         for mask in range(nodes):
             edges[(place ^ mask) + 1] = pieces[mask][:, 2 * block :]
-        wide = []
-        for stream in range(2):
-            taps = taps_ref[1 + stream, own, :]
-            wide.append(
-                [jnp.broadcast_to(taps[:, tap : tap + 1], (chans, LANES)) for tap in range(rim + 1)]
-            )
+        wide = [tap_tiles(wide_ref, 1 + stream, own) for stream in range(2)]
 
     def repaired(mask, tile):
         before, now = edges[place ^ mask], pieces[mask][:, 2 * block :]
@@ -341,12 +353,12 @@
             ].astype(jnp.bfloat16)
 
 
-def long_mix(pieces, taps, tables, block):
+def long_mix(pieces, wide, tables, block):
     nodes = len(pieces)
     chans, width = pieces[0].shape
     per_node = block // LANES
     rows = nodes * per_node
-    rim = taps.shape[2] - 1 if width > 2 * block else 0
+    rim = wide.shape[2] // LANES - 1 if width > 2 * block else 0
     near = pl.BlockSpec(memory_space=pltpu.VMEM)
     return pl.pallas_call(
         lambda *refs: long_kernel(nodes, chans, per_node, rim, *refs),
@@ -360,7 +372,7 @@
         ],
         compiler_params=pltpu.CompilerParams(vmem_limit_bytes=24 << 20),
         name="long_mix",
-    )(taps, *tables, *pieces[::-1])
+    )(wide, *tables, *pieces[::-1])
 
 
 def gather_blocks(depths, blocks, gathered):
@@ -495,9 +507,9 @@
     fits = chans % 16 == 0
 
     if fits:
-        pieces, query, taps = pack(qkv, long_filter, short_taps, nodes, chans)
+        pieces, query, wide = pack(qkv, long_filter, short_taps, nodes, chans)
     else:
-        taps = short_taps
+        wide = short_taps
         query, key, value = features_plain(qkv, short_taps)
         both = jnp.concatenate([key * value, long_filter], axis=1).astype(jnp.bfloat16)
         both = both.reshape(nodes, chans, 2 * block)
@@ -506,11 +518,11 @@
     out_weight, *tables = near_tables(
         nodes * block // LANES, skip_gain, out_weight, pieces[0]
     )
-    mixed = long_mix(pieces, taps, tables, block)
+    mixed = long_mix(pieces, wide, tables, block)
 
     if fits:
         tied = lax.optimization_barrier((mixed[0], *pieces[::-1]))[:0:-1]
-        featured = query_features(query, taps, tied, nodes, chans)
+        featured = query_features(query, wide, tied, nodes, chans)
     else:
         featured = query.reshape(nodes, chans, block)[jnp.arange(nodes, dtype=jnp.int32) ^ place][::-1]
     mixed = [swapped(mixed[mask], mask, "ctx") for mask in range(nodes)]

time: 32.8 us -> 32.6 us (level)
  no operation moved by 1% of the time
where the time goes in v8:
time: 32.6 us; the launch traced here: 32.3 us
  starting transfers between devices  13.1 us (40%)
  waiting for transfers between devices  11.6 us (36%)
  Pallas kernels  7.53 us (23%)
    ppermute x13, starting transfers between devices, swapped(): lax.ppermute(block, axis, [(i, i ^ mask) for i in range(lax.axis_size(axi...  13.1 us
    ppermute x13, waiting for transfers between devices, swapped(): lax.ppermute(block, axis, [(i, i ^ mask) for i in range(lax.axis_size(axi...  11.6 us
    pallas_call x1, Pallas kernels, project_late(): pl.pallas_call(lambda *refs: final_kernel(tuple(late), cuts, *refs), out_...  1.68 us
    pallas_call x1, Pallas kernels, pack(): pl.pallas_call(lambda *refs: pack_kernel(nodes, chans, *refs), out_shape=...  1.63 us
    pallas_call x1, Pallas kernels, long_mix(): pl.pallas_call(lambda *refs: long_kernel(nodes, chans, per_node, rim, *re...  1.5 us
    pallas_call x1, Pallas kernels, near_tables(): pl.pallas_call(lambda *refs: tables_kernel(count, *refs), out_shape=[jax....  1.4 us
    pallas_call x1, Pallas kernels, project_early(): pl.pallas_call(lambda *refs: partial_kernel(tuple(early), features // 4,...  0.77 us
  transfers between devices with their start and end apart: 13, of which 9 were waited for; matrix products, arithmetic and copies ran while one was open for 0% of the time, Pallas kernels for 8%

profile of v8, /device:TPU:0, one launch (start us, length us, event | category | flops | bytes accessed | tf_op | source)
XLA Modules:
  0.0 32.3 jit_solution(13610459127205537441)
XLA Ops:
  0.0 1.6 %pack.1 = (bf16[16,2176]{1,0:T(8,128)(2,1)S(1)}, bf16[16,2176]{1,0:T(8,128)(2,1)S(1)}, bf16[16,2176]{1,0:T(8,128)(2,1)S(1)}, bf16[16,2176]{1,0:T(8,128)(2,1)S(1)...) custom-call(bf16[3,64,1024]{2,1,0:T(8,128)(2,1)} %refs_0_.2, f32[64,1024]{1,0:T(8,128)} %refs_1_.2, ...), custom_call_target="tpu_custom_call" | custom-call | tf_op jit(solution)/shard_map/pack/pallas_call | solution.py:189
  1.6 4.0 %collective-permute-start = (bf16[16,2176]{1,0:T(8,128)(2,1)S(1)}, bf16[16,2176]{1,0:T(8,128)(2,1)S(1)}, u32[]{:S(2)}, u32[]{:S(2)}) collective-permute-start(bf16[16,2176]{1,0:T(8,128)(2,1)S(1)} %get-tuple-element.34), channel_id=1, source_target_pairs={{0,24},{8,16},{16,8},{24,0},{1,25},{9,17},{17,9},{25,1},{2,26},{10... | collective-permute-start | bytes 208904 | tf_op jit(solution)/shard_map/ppermute | solution.py:497
  5.6 0.5 %collective-permute-start.1 = (bf16[16,2176]{1,0:T(8,128)(2,1)S(1)}, bf16[16,2176]{1,0:T(8,128)(2,1)S(1)}, u32[]{:S(2)}, u32[]{:S(2)}) collective-permute-start(bf16[16,2176]{1,0:T(8,128)(2,1)S(1)} %get-tuple-element.35), channel_id=1, source_target_pairs={{0,16},{8,24},{16,0},{24,8},{1,17},{9,25},{17,1},{25,9},{2,18},{10... | collective-permute-start | bytes 208904 | tf_op jit(solution)/shard_map/ppermute | solution.py:497
  6.1 0.1 collective-permute-start.2
  6.2 1.4 %near_tables.1 = (bf16[1024,512]{1,0:T(8,128)(2,1)S(1)}, bf16[64,64]{1,0:T(8,128)(2,1)S(1)}, f32[32,256]{1,0:T(8,128)S(1)}, bf16[768,256]{1,0:T(8,128)(2,1)S(1)}...) custom-call(bf16[1024,512]{1,0:T(8,128)(2,1)} %refs_0_.3, bf16[64,64]{1,0:T(8,128)(2,1)} %constant.8.clone.refs_1_, ...), custom_call_target="tpu_custom_call" | custom-call | tf_op jit(solution)/shard_map/near_tables/pallas_call | solution.py:110
  7.7 0.3 collective-permute-done.refs_6_.refs_5_
  7.9 2.0 %collective-permute-done.1.refs_7_.refs_4_ = bf16[16,2176]{1,0:T(8,128)(2,1)S(1)} collective-permute-done((bf16[16,2176]{1,0:T(8,128)(2,1)S(1)}, bf16[16,2176]{1,0:T(8,128)(2,1)S(1)}, u32[]{:S(2)}, u32[]{:S(2)}) %collective-permute-start.1) | collective-permute-done | bytes 69664 | tf_op jit(solution)/shard_map/ppermute | solution.py:497
  9.9 0.5 %collective-permute-done.2.refs_8_.refs_3_ = bf16[16,2176]{1,0:T(8,128)(2,1)S(1)} collective-permute-done((bf16[16,2176]{1,0:T(8,128)(2,1)S(1)}, bf16[16,2176]{1,0:T(8,128)(2,1)S(1)}, u32[]{:S(2)}, u32[]{:S(2)}) %collective-permute-start.2) | collective-permute-done | bytes 69664 | tf_op jit(solution)/shard_map/ppermute | solution.py:497
  10.4 1.5 %long_mix.1 = (bf16[16,1024]{1,0:T(8,128)(2,1)S(1)}, bf16[16,1024]{1,0:T(8,128)(2,1)S(1)}, bf16[16,1024]{1,0:T(8,128)(2,1)S(1)}, bf16[16,1024]{1,0:T(8,128)(2,1)S(1)}) custom-call(f32[3,64,896]{2,1,0:T(8,128)S(1)} %get-tuple-element.28.refs_0_.refs_1_, bf16[64,64]{1,0:T(8,128)(2,1)S(1)} %get-tuple-element.29.refs_1_, ...), custom_call_target="tpu_custom_call" | custom-call | tf_op jit(solution)/shard_map/long_mix/pallas_call | solution.py:363
  11.9 1.6 %collective-permute-start.3 = (bf16[16,1024]{1,0:T(8,128)(2,1)S(1)}, bf16[16,1024]{1,0:T(8,128)(2,1)S(1)}, u32[]{:S(2)}, u32[]{:S(2)}) collective-permute-start(bf16[16,1024]{1,0:T(8,128)(2,1)S(1)} %get-tuple-element.42), channel_id=1, source_target_pairs={{0,24},{8,16},{16,8},{24,0},{1,25},{9,17},{17,9},{25,1},{2,26},{10... | collective-permute-start | bytes 98312 | tf_op jit(solution)/shard_map/ppermute | solution.py:497
  13.5 0.6 %collective-permute-start.4 = (bf16[16,1024]{1,0:T(8,128)(2,1)S(1)}, bf16[16,1024]{1,0:T(8,128)(2,1)S(1)}, u32[]{:S(2)}, u32[]{:S(2)}) collective-permute-start(bf16[16,1024]{1,0:T(8,128)(2,1)S(1)} %get-tuple-element.43), channel_id=1, source_target_pairs={{0,16},{8,24},{16,0},{24,8},{1,17},{9,25},{17,1},{25,9},{2,18},{10... | collective-permute-start | bytes 98312 | tf_op jit(solution)/shard_map/ppermute | solution.py:497
  14.0 1.4 %collective-permute-start.5 = (bf16[16,1024]{1,0:T(8,128)(2,1)S(1)}, bf16[16,1024]{1,0:T(8,128)(2,1)S(1)}, u32[]{:S(2)}, u32[]{:S(2)}) collective-permute-start(bf16[16,1024]{1,0:T(8,128)(2,1)S(1)} %get-tuple-element.44), channel_id=1, source_target_pairs={{0,8},{8,0},{16,24},{24,16},{1,9},{9,1},{17,25},{25,17},{2,10},{10... | collective-permute-start | bytes 98312 | tf_op jit(solution)/shard_map/ppermute | solution.py:497
  15.5 0.6 %query_features.1 = f32[4,16,1024]{2,1,0:T(8,128)S(1)} custom-call(bf16[64,1024]{1,0:T(8,128)(2,1)S(1)} %get-tuple-element.27.refs_0_, f32[3,64,896]{2,1,0:T(8,128)S(1)} %get-tuple-element.28.refs_0_.refs_1_, bf16[16,2176]{1,0:T(8,128)(2,1)S(1)} %get-tuple-element.38.refs_6_.refs_9_.refs_2_, bf16[16,2176]{1,0:T(8,128)(2,1)S(1)} %collective-permute-done.2.refs_8_.refs_3_, ...), custom_call_target="tpu_custom_call" | custom-call | tf_op jit(solution)/shard_map/query_features/pallas_call | solution.py:238
  16.0 0.8 %collective-permute-done.3 = bf16[16,1024]{1,0:T(8,128)(2,1)S(1)} collective-permute-done((bf16[16,1024]{1,0:T(8,128)(2,1)S(1)}, bf16[16,1024]{1,0:T(8,128)(2,1)S(1)}, u32[]{:S(2)}, u32[]{:S(2)}) %collective-permute-start.3) | collective-permute-done | bytes 32800 | tf_op jit(solution)/shard_map/ppermute | solution.py:497
  16.8 0.6 %collective-permute-done.4 = bf16[16,1024]{1,0:T(8,128)(2,1)S(1)} collective-permute-done((bf16[16,1024]{1,0:T(8,128)(2,1)S(1)}, bf16[16,1024]{1,0:T(8,128)(2,1)S(1)}, u32[]{:S(2)}, u32[]{:S(2)}) %collective-permute-start.4) | collective-permute-done | bytes 32800 | tf_op jit(solution)/shard_map/ppermute | solution.py:497
  17.4 0.6 %collective-permute-done.5 = bf16[16,1024]{1,0:T(8,128)(2,1)S(1)} collective-permute-done((bf16[16,1024]{1,0:T(8,128)(2,1)S(1)}, bf16[16,1024]{1,0:T(8,128)(2,1)S(1)}, u32[]{:S(2)}, u32[]{:S(2)}) %collective-permute-start.5) | collective-permute-done | bytes 32800 | tf_op jit(solution)/shard_map/ppermute | solution.py:497
  18.0 2.7 %collective-permute-start.7 = (bf16[4,16,1024]{2,1,0:T(8,128)(2,1)S(1)}, bf16[4,16,1024]{2,1,0:T(8,128)(2,1)S(1)}, u32[]{:S(2)}, u32[]{:S(2)}) collective-permute-start(bf16[4,16,1024]{2,1,0:T(8,128)(2,1)S(1)} %multiply_convert_fusion.refs_1_), channel_id=1, source_target_pairs={{0,4},{1,5},{2,6},{3,7},{4,0},{5,1},{6,2},{7,3},{8,12},{9,13},{10,... | collective-permute-start | bytes 393224 | tf_op jit(solution)/shard_map/ppermute | solution.py:497
  20.7 1.6 %collective-permute-start.11 = (bf16[4,16,1024]{2,1,0:T(8,128)(2,1)S(1)}, bf16[4,16,1024]{2,1,0:T(8,128)(2,1)S(1)}, u32[]{:S(2)}, u32[]{:S(2)}) collective-permute-start(bf16[4,16,1024]{2,1,0:T(8,128)(2,1)S(1)} %multiply_convert_fusion.refs_1_), channel_id=1, source_target_pairs={{0,2},{1,3},{2,0},{3,1},{4,6},{5,7},{6,4},{7,5},{8,10},{9,11},{10,... | collective-permute-start | bytes 393224 | tf_op jit(solution)/shard_map/ppermute | solution.py:497
  22.2 0.2 collective-permute-start.9
  22.5 0.0 collective-permute-start.6
  22.5 5.3 %collective-permute-done.7.refs_3_ = bf16[4,16,1024]{2,1,0:T(8,128)(2,1)S(1)} collective-permute-done((bf16[4,16,1024]{2,1,0:T(8,128)(2,1)S(1)}, bf16[4,16,1024]{2,1,0:T(8,128)(2,1)S(1)}, u32[]{:S(2)}, u32[]{:S(2)}) %collective-permute-start.7) | collective-permute-done | bytes 131104 | tf_op jit(solution)/shard_map/ppermute | solution.py:497
  27.8 0.0 collective-permute-start.8
  27.8 0.0 collective-permute-done.11.refs_4_
  27.8 0.5 %collective-permute-start.12 = (bf16[4,16,1024]{2,1,0:T(8,128)(2,1)S(1)}, bf16[4,16,1024]{2,1,0:T(8,128)(2,1)S(1)}, u32[]{:S(2)}, u32[]{:S(2)}) collective-permute-start(bf16[4,16,1024]{2,1,0:T(8,128)(2,1)S(1)} %collective-permute-done.11.refs_4_), channel_id=1, source_target_pairs={{0,1},{1,0},{2,3},{3,2},{4,5},{5,4},{6,7},{7,6},{8,9},{9,8},{10,11... | collective-permute-start | bytes 393224 | tf_op jit(solution)/shard_map/ppermute | solution.py:497
  28.3 1.0 %collective-permute-done.9.refs_2_ = bf16[4,16,1024]{2,1,0:T(8,128)(2,1)S(1)} collective-permute-done((bf16[4,16,1024]{2,1,0:T(8,128)(2,1)S(1)}, bf16[4,16,1024]{2,1,0:T(8,128)(2,1)S(1)}, u32[]{:S(2)}, u32[]{:S(2)}) %collective-permute-start.9) | collective-permute-done | bytes 131104 | tf_op jit(solution)/shard_map/ppermute | solution.py:497
  29.3 0.0 collective-permute-start.10
  29.3 0.0 collective-permute-done.6.refs_2_
  29.3 0.0 collective-permute-done.8.refs_4_
  29.3 0.8 %project_early.1.refs_1_ = f32[1024,1024]{1,0:T(8,128)S(1)} custom-call(bf16[1024,512]{1,0:T(8,128)(2,1)S(1)} %get-tuple-element.26.refs_0_, bf16[4,16,1024]{2,1,0:T(8,128)(2,1)S(1)} %multiply_convert_fusion.refs_1_, bf16[4,16,1024]{2,1,0:T(8,128)(2,1)S(1)} %collective-permute-done.6.refs_2_, bf16[4,16,1024]{2,1,0:T(8,128)(2,1)S(1)} %collective-permute-done.7.refs_3_, ...), custom_call_target="tpu_custom_call" | custom-call | tf_op jit(solution)/shard_map/project_early/pallas_call | solution.py:428
  30.1 0.0 collective-permute-done.12.refs_5_
  30.1 0.6 %collective-permute-done.10.refs_3_ = bf16[4,16,1024]{2,1,0:T(8,128)(2,1)S(1)} collective-permute-done((bf16[4,16,1024]{2,1,0:T(8,128)(2,1)S(1)}, bf16[4,16,1024]{2,1,0:T(8,128)(2,1)S(1)}, u32[]{:S(2)}, u32[]{:S(2)}) %collective-permute-start.10) | collective-permute-done | bytes 131104 | tf_op jit(solution)/shard_map/ppermute | solution.py:497
  30.7 1.7 %project_late.1 = bf16[1024,1024]{1,0:T(8,128)(2,1)} custom-call(bf16[1024,512]{1,0:T(8,128)(2,1)S(1)} %get-tuple-element.26.refs_0_, f32[1024,1024]{1,0:T(8,128)S(1)} %project_early.1.refs_1_, bf16[4,16,1024]{2,1,0:T(8,128)(2,1)S(1)} %collective-permute-done.9.refs_2_, bf16[4,16,1024]{2,1,0:T(8,128)(2,1)S(1)} %collective-permute-done.10.refs_3_, ...), custom_call_target="tpu_custom_call" | custom-call | tf_op jit(solution)/shard_map/project_late/pallas_call | solution.py:447
  (1 shorter events, 0.0 us)
Async XLA Ops:
  1.6 6.3 %collective-permute-start = (bf16[16,2176]{1,0:T(8,128)(2,1)S(1)}, bf16[16,2176]{1,0:T(8,128)(2,1)S(1)}, u32[]{:S(2)}, u32[]{:S(2)}) collective-permute-start(bf16[16,2176]{1,0:T(8,128)(2,1)S(1)} %get-tuple-element.34), channel_id=1, source_target_pairs={{0,24},{8,16},{16,8},{24,0},{1,25},{9,17},{17,9},{25,1},{2,26},{10... | collective-permute-start | bytes 208904 | tf_op jit(solution)/shard_map/ppermute | solution.py:497
  5.6 4.3 %collective-permute-start.1 = (bf16[16,2176]{1,0:T(8,128)(2,1)S(1)}, bf16[16,2176]{1,0:T(8,128)(2,1)S(1)}, u32[]{:S(2)}, u32[]{:S(2)}) collective-permute-start(bf16[16,2176]{1,0:T(8,128)(2,1)S(1)} %get-tuple-element.35), channel_id=1, source_target_pairs={{0,16},{8,24},{16,0},{24,8},{1,17},{9,25},{17,1},{25,9},{2,18},{10... | collective-permute-start | bytes 208904 | tf_op jit(solution)/shard_map/ppermute | solution.py:497
  6.1 4.3 %collective-permute-start.2 = (bf16[16,2176]{1,0:T(8,128)(2,1)S(1)}, bf16[16,2176]{1,0:T(8,128)(2,1)S(1)}, u32[]{:S(2)}, u32[]{:S(2)}) collective-permute-start(bf16[16,2176]{1,0:T(8,128)(2,1)S(1)} %get-tuple-element.36), channel_id=1, source_target_pairs={{0,8},{8,0},{16,24},{24,16},{1,9},{9,1},{17,25},{25,17},{2,10},{10... | collective-permute-start | bytes 208904 | tf_op jit(solution)/shard_map/ppermute | solution.py:497
  11.9 4.9 %collective-permute-start.3 = (bf16[16,1024]{1,0:T(8,128)(2,1)S(1)}, bf16[16,1024]{1,0:T(8,128)(2,1)S(1)}, u32[]{:S(2)}, u32[]{:S(2)}) collective-permute-start(bf16[16,1024]{1,0:T(8,128)(2,1)S(1)} %get-tuple-element.42), channel_id=1, source_target_pairs={{0,24},{8,16},{16,8},{24,0},{1,25},{9,17},{17,9},{25,1},{2,26},{10... | collective-permute-start | bytes 98312 | tf_op jit(solution)/shard_map/ppermute | solution.py:497
  13.5 3.9 %collective-permute-start.4 = (bf16[16,1024]{1,0:T(8,128)(2,1)S(1)}, bf16[16,1024]{1,0:T(8,128)(2,1)S(1)}, u32[]{:S(2)}, u32[]{:S(2)}) collective-permute-start(bf16[16,1024]{1,0:T(8,128)(2,1)S(1)} %get-tuple-element.43), channel_id=1, source_target_pairs={{0,16},{8,24},{16,0},{24,8},{1,17},{9,25},{17,1},{25,9},{2,18},{10... | collective-permute-start | bytes 98312 | tf_op jit(solution)/shard_map/ppermute | solution.py:497
  14.0 3.9 %collective-permute-start.5 = (bf16[16,1024]{1,0:T(8,128)(2,1)S(1)}, bf16[16,1024]{1,0:T(8,128)(2,1)S(1)}, u32[]{:S(2)}, u32[]{:S(2)}) collective-permute-start(bf16[16,1024]{1,0:T(8,128)(2,1)S(1)} %get-tuple-element.44), channel_id=1, source_target_pairs={{0,8},{8,0},{16,24},{24,16},{1,9},{9,1},{17,25},{25,17},{2,10},{10... | collective-permute-start | bytes 98312 | tf_op jit(solution)/shard_map/ppermute | solution.py:497
  18.0 9.8 %collective-permute-start.7 = (bf16[4,16,1024]{2,1,0:T(8,128)(2,1)S(1)}, bf16[4,16,1024]{2,1,0:T(8,128)(2,1)S(1)}, u32[]{:S(2)}, u32[]{:S(2)}) collective-permute-start(bf16[4,16,1024]{2,1,0:T(8,128)(2,1)S(1)} %multiply_convert_fusion.refs_1_), channel_id=1, source_target_pairs={{0,4},{1,5},{2,6},{3,7},{4,0},{5,1},{6,2},{7,3},{8,12},{9,13},{10,... | collective-permute-start | bytes 393224 | tf_op jit(solution)/shard_map/ppermute | solution.py:497
  20.7 7.1 %collective-permute-start.11 = (bf16[4,16,1024]{2,1,0:T(8,128)(2,1)S(1)}, bf16[4,16,1024]{2,1,0:T(8,128)(2,1)S(1)}, u32[]{:S(2)}, u32[]{:S(2)}) collective-permute-start(bf16[4,16,1024]{2,1,0:T(8,128)(2,1)S(1)} %multiply_convert_fusion.refs_1_), channel_id=1, source_target_pairs={{0,2},{1,3},{2,0},{3,1},{4,6},{5,7},{6,4},{7,5},{8,10},{9,11},{10,... | collective-permute-start | bytes 393224 | tf_op jit(solution)/shard_map/ppermute | solution.py:497
  22.2 7.1 %collective-permute-start.9 = (bf16[4,16,1024]{2,1,0:T(8,128)(2,1)S(1)}, bf16[4,16,1024]{2,1,0:T(8,128)(2,1)S(1)}, u32[]{:S(2)}, u32[]{:S(2)}) collective-permute-start(bf16[4,16,1024]{2,1,0:T(8,128)(2,1)S(1)} %multiply_convert_fusion.refs_1_), channel_id=1, source_target_pairs={{0,6},{1,7},{2,4},{3,5},{4,2},{5,3},{6,0},{7,1},{8,14},{9,15},{10,... | collective-permute-start | bytes 393224 | tf_op jit(solution)/shard_map/ppermute | solution.py:497
  22.5 6.9 %collective-permute-start.6 = (bf16[4,16,1024]{2,1,0:T(8,128)(2,1)S(1)}, bf16[4,16,1024]{2,1,0:T(8,128)(2,1)S(1)}, u32[]{:S(2)}, u32[]{:S(2)}) collective-permute-start(bf16[4,16,1024]{2,1,0:T(8,128)(2,1)S(1)} %multiply_convert_fusion.refs_1_), channel_id=1, source_target_pairs={{0,1},{1,0},{2,3},{3,2},{4,5},{5,4},{6,7},{7,6},{8,9},{9,8},{10,11... | collective-permute-start | bytes 393224 | tf_op jit(solution)/shard_map/ppermute | solution.py:497
  27.8 1.6 %collective-permute-start.8 = (bf16[4,16,1024]{2,1,0:T(8,128)(2,1)S(1)}, bf16[4,16,1024]{2,1,0:T(8,128)(2,1)S(1)}, u32[]{:S(2)}, u32[]{:S(2)}) collective-permute-start(bf16[4,16,1024]{2,1,0:T(8,128)(2,1)S(1)} %collective-permute-done.7.refs_3_), channel_id=1, source_target_pairs={{0,1},{1,0},{2,3},{3,2},{4,5},{5,4},{6,7},{7,6},{8,9},{9,8},{10,11... | collective-permute-start | bytes 393224 | tf_op jit(solution)/shard_map/ppermute | solution.py:497
  27.8 2.3 %collective-permute-start.12 = (bf16[4,16,1024]{2,1,0:T(8,128)(2,1)S(1)}, bf16[4,16,1024]{2,1,0:T(8,128)(2,1)S(1)}, u32[]{:S(2)}, u32[]{:S(2)}) collective-permute-start(bf16[4,16,1024]{2,1,0:T(8,128)(2,1)S(1)} %collective-permute-done.11.refs_4_), channel_id=1, source_target_pairs={{0,1},{1,0},{2,3},{3,2},{4,5},{5,4},{6,7},{7,6},{8,9},{9,8},{10,11... | collective-permute-start | bytes 393224 | tf_op jit(solution)/shard_map/ppermute | solution.py:497
  29.3 1.3 %collective-permute-start.10 = (bf16[4,16,1024]{2,1,0:T(8,128)(2,1)S(1)}, bf16[4,16,1024]{2,1,0:T(8,128)(2,1)S(1)}, u32[]{:S(2)}, u32[]{:S(2)}) collective-permute-start(bf16[4,16,1024]{2,1,0:T(8,128)(2,1)S(1)} %collective-permute-done.9.refs_2_), channel_id=1, source_target_pairs={{0,1},{1,0},{2,3},{3,2},{4,5},{5,4},{6,7},{7,6},{8,9},{9,8},{10,11... | collective-permute-start | bytes 393224 | tf_op jit(solution)/shard_map/ppermute | solution.py:497

commit v9 on v8

--- a/solution.py
+++ b/solution.py
@@ -97,7 +97,7 @@
     for move in moves:
         move.start()
     moves[count].wait()
-    column_ref[...] = jnp.broadcast_to(skips[...].reshape(1, -1), (8, skips.shape[0])).T
+    column_ref[...] = jnp.broadcast_to(skips[...].reshape(1, -1), (LANES, skips.shape[0])).T
     for move in moves[:count]:
         move.wait()
 
@@ -110,7 +110,7 @@
     return pl.pallas_call(
         lambda *refs: tables_kernel(count, *refs),
         out_shape=[jax.ShapeDtypeStruct(table.shape, table.dtype) for table in tables]
-        + [jax.ShapeDtypeStruct((skip_gain.shape[0], 8), jnp.float32)],
+        + [jax.ShapeDtypeStruct((skip_gain.shape[0], LANES), jnp.float32)],
         in_specs=[far] * (count + 1) + [near],
         out_specs=[near] * (count + 1),
         scratch_shapes=[
@@ -152,30 +152,29 @@
     stream_move.wait()
     for mask, rows in reversed(list(enumerate(shares))):
         edge = edges
-        features = []
+        raws = [streams[stream, rows, :] for stream in range(2)]
+        wides = [tap_tiles(wide_ref, 1 + stream, rows) for stream in range(2)]
         for stream in reversed(range(2)):
-            values = streams[stream, rows, :].astype(jnp.float32)
-            ends = jnp.where(lane < rim, values[:, :LANES], values[:, block - LANES :])
+            ends = jnp.where(lane < rim, raws[stream][:, :LANES], raws[stream][:, block - LANES :])
             at = stream * LANE_V
-            edge = jnp.where(lane < at + LANE_V, pltpu.roll(ends, at + rim, 1), edge)
-            wide = tap_tiles(wide_ref, 1 + stream, rows)
-            raw = streams[stream, rows, :]
-            totals = []
-            for index in range(block // LANES):
-                tile = raw[:, index * LANES : (index + 1) * LANES]
+            moved = pltpu.roll(ends, at + rim, 1).astype(jnp.float32)
+            edge = jnp.where(lane < at + LANE_V, moved, edge)
+        outs[mask][:, 2 * block :] = edge.astype(jnp.bfloat16)
+        before = [None, None]
+        for index in range(block // LANES):
+            product = None
+            for stream in range(2):
+                tile = raws[stream][:, index * LANES : (index + 1) * LANES]
+                wide = wides[stream]
+                moved = [pltpu.roll(tile, shift, 1) for shift in range(1, rim + 1)]
+                behind = before[stream] or moved
                 total = wide[0] * tile.astype(jnp.float32)
-                moved = [pltpu.roll(tile, shift, 1) for shift in range(1, rim + 1)]
-                if index == 0:
-                    before = moved
                 for shift in range(1, rim + 1):
-                    joined = jnp.where(lane < shift, before[shift - 1], moved[shift - 1])
+                    joined = jnp.where(lane < shift, behind[shift - 1], moved[shift - 1])
                     total = total + wide[shift] * joined.astype(jnp.float32)
-                before = moved
-                totals.append(total)
-            features.append(totals)
-        for index, (left, right) in enumerate(zip(*features)):
-            outs[mask][:, index * LANES : (index + 1) * LANES] = (left * right).astype(jnp.bfloat16)
-        outs[mask][:, 2 * block :] = edge.astype(jnp.bfloat16)
+                before[stream] = moved
+                product = total if product is None else product * total
+            outs[mask][:, index * LANES : (index + 1) * LANES] = product.astype(jnp.bfloat16)
     filter_move.wait()
     for mask, rows in enumerate(shares):
         outs[mask][:, block : 2 * block] = filters[rows, :].astype(jnp.bfloat16)
@@ -328,7 +327,7 @@
             axis=1,
         )
 
-    group = max(chans // 2, 1)
+    group = max(chans // 4, 1)
     groups = [range(begin, begin + group) for begin in range(0, chans, group)]
     turned = []
     for members in groups:
@@ -343,7 +342,7 @@
             span = slice(chan * pitch, chan * pitch + rows)
             final[span, :] = (
                 convolved[:, index * LANES : (index + 1) * LANES]
-                + skips[chan : chan + 1, :1] * raw[0, span, :]
+                + skips[chan : chan + 1, :] * raw[0, span, :]
             )
     for mask in range(nodes):
         start = (place ^ mask) * per_node

time: 32.6 us -> 32.6 us (level)
  no operation moved by 1% of the time
where the time goes in v9:
time: 32.6 us; the launch traced here: 32.3 us
  starting transfers between devices  13.1 us (40%)
  waiting for transfers between devices  11.6 us (36%)
  Pallas kernels  7.51 us (23%)
    ppermute x13, starting transfers between devices, swapped(): lax.ppermute(block, axis, [(i, i ^ mask) for i in range(lax.axis_size(axi...  13.1 us
    ppermute x13, waiting for transfers between devices, swapped(): lax.ppermute(block, axis, [(i, i ^ mask) for i in range(lax.axis_size(axi...  11.6 us
    pallas_call x1, Pallas kernels, project_late(): pl.pallas_call(lambda *refs: final_kernel(tuple(late), cuts, *refs), out_...  1.67 us
    pallas_call x1, Pallas kernels, pack(): pl.pallas_call(lambda *refs: pack_kernel(nodes, chans, *refs), out_shape=...  1.64 us
    pallas_call x1, Pallas kernels, long_mix(): pl.pallas_call(lambda *refs: long_kernel(nodes, chans, per_node, rim, *re...  1.48 us
    pallas_call x1, Pallas kernels, near_tables(): pl.pallas_call(lambda *refs: tables_kernel(count, *refs), out_shape=[jax....  1.4 us
    pallas_call x1, Pallas kernels, project_early(): pl.pallas_call(lambda *refs: partial_kernel(tuple(early), features // 4,...  0.77 us
  transfers between devices with their start and end apart: 13, of which 9 were waited for; matrix products, arithmetic and copies ran while one was open for 0% of the time, Pallas kernels for 8%

profile of v9, /device:TPU:0, one launch (start us, length us, event | category | flops | bytes accessed | tf_op | source)
XLA Modules:
  0.0 32.3 jit_solution(8291752772749212904)
XLA Ops:
  0.0 1.6 %pack.1 = (bf16[16,2176]{1,0:T(8,128)(2,1)S(1)}, bf16[16,2176]{1,0:T(8,128)(2,1)S(1)}, bf16[16,2176]{1,0:T(8,128)(2,1)S(1)}, bf16[16,2176]{1,0:T(8,128)(2,1)S(1)...) custom-call(bf16[3,64,1024]{2,1,0:T(8,128)(2,1)} %refs_0_.2, f32[64,1024]{1,0:T(8,128)} %refs_1_.2, ...), custom_call_target="tpu_custom_call" | custom-call | tf_op jit(solution)/shard_map/pack/pallas_call | solution.py:188
  1.6 4.0 %collective-permute-start = (bf16[16,2176]{1,0:T(8,128)(2,1)S(1)}, bf16[16,2176]{1,0:T(8,128)(2,1)S(1)}, u32[]{:S(2)}, u32[]{:S(2)}) collective-permute-start(bf16[16,2176]{1,0:T(8,128)(2,1)S(1)} %get-tuple-element.34), channel_id=1, source_target_pairs={{0,24},{8,16},{16,8},{24,0},{1,25},{9,17},{17,9},{25,1},{2,26},{10... | collective-permute-start | bytes 208904 | tf_op jit(solution)/shard_map/ppermute | solution.py:496
  5.6 0.5 %collective-permute-start.1 = (bf16[16,2176]{1,0:T(8,128)(2,1)S(1)}, bf16[16,2176]{1,0:T(8,128)(2,1)S(1)}, u32[]{:S(2)}, u32[]{:S(2)}) collective-permute-start(bf16[16,2176]{1,0:T(8,128)(2,1)S(1)} %get-tuple-element.35), channel_id=1, source_target_pairs={{0,16},{8,24},{16,0},{24,8},{1,17},{9,25},{17,1},{25,9},{2,18},{10... | collective-permute-start | bytes 208904 | tf_op jit(solution)/shard_map/ppermute | solution.py:496
  6.1 0.1 collective-permute-start.2
  6.2 1.4 %near_tables.1 = (bf16[1024,512]{1,0:T(8,128)(2,1)S(1)}, bf16[64,64]{1,0:T(8,128)(2,1)S(1)}, f32[32,256]{1,0:T(8,128)S(1)}, bf16[768,256]{1,0:T(8,128)(2,1)S(1)}...) custom-call(bf16[1024,512]{1,0:T(8,128)(2,1)} %refs_0_.3, bf16[64,64]{1,0:T(8,128)(2,1)} %constant.8.clone.refs_1_, ...), custom_call_target="tpu_custom_call" | custom-call | tf_op jit(solution)/shard_map/near_tables/pallas_call | solution.py:110
  7.6 0.3 collective-permute-done.refs_6_.refs_5_
  7.9 2.0 %collective-permute-done.1.refs_7_.refs_4_ = bf16[16,2176]{1,0:T(8,128)(2,1)S(1)} collective-permute-done((bf16[16,2176]{1,0:T(8,128)(2,1)S(1)}, bf16[16,2176]{1,0:T(8,128)(2,1)S(1)}, u32[]{:S(2)}, u32[]{:S(2)}) %collective-permute-start.1) | collective-permute-done | bytes 69664 | tf_op jit(solution)/shard_map/ppermute | solution.py:496
  9.9 0.5 %collective-permute-done.2.refs_8_.refs_3_ = bf16[16,2176]{1,0:T(8,128)(2,1)S(1)} collective-permute-done((bf16[16,2176]{1,0:T(8,128)(2,1)S(1)}, bf16[16,2176]{1,0:T(8,128)(2,1)S(1)}, u32[]{:S(2)}, u32[]{:S(2)}) %collective-permute-start.2) | collective-permute-done | bytes 69664 | tf_op jit(solution)/shard_map/ppermute | solution.py:496
  10.4 1.5 %long_mix.1 = (bf16[16,1024]{1,0:T(8,128)(2,1)S(1)}, bf16[16,1024]{1,0:T(8,128)(2,1)S(1)}, bf16[16,1024]{1,0:T(8,128)(2,1)S(1)}, bf16[16,1024]{1,0:T(8,128)(2,1)S(1)}) custom-call(f32[3,64,896]{2,1,0:T(8,128)S(1)} %get-tuple-element.28.refs_0_.refs_1_, bf16[64,64]{1,0:T(8,128)(2,1)S(1)} %get-tuple-element.29.refs_1_, ...), custom_call_target="tpu_custom_call" | custom-call | tf_op jit(solution)/shard_map/long_mix/pallas_call | solution.py:362
  11.9 1.6 %collective-permute-start.3 = (bf16[16,1024]{1,0:T(8,128)(2,1)S(1)}, bf16[16,1024]{1,0:T(8,128)(2,1)S(1)}, u32[]{:S(2)}, u32[]{:S(2)}) collective-permute-start(bf16[16,1024]{1,0:T(8,128)(2,1)S(1)} %get-tuple-element.42), channel_id=1, source_target_pairs={{0,24},{8,16},{16,8},{24,0},{1,25},{9,17},{17,9},{25,1},{2,26},{10... | collective-permute-start | bytes 98312 | tf_op jit(solution)/shard_map/ppermute | solution.py:496
  13.5 0.6 %collective-permute-start.4 = (bf16[16,1024]{1,0:T(8,128)(2,1)S(1)}, bf16[16,1024]{1,0:T(8,128)(2,1)S(1)}, u32[]{:S(2)}, u32[]{:S(2)}) collective-permute-start(bf16[16,1024]{1,0:T(8,128)(2,1)S(1)} %get-tuple-element.43), channel_id=1, source_target_pairs={{0,16},{8,24},{16,0},{24,8},{1,17},{9,25},{17,1},{25,9},{2,18},{10... | collective-permute-start | bytes 98312 | tf_op jit(solution)/shard_map/ppermute | solution.py:496
  14.0 1.4 %collective-permute-start.5 = (bf16[16,1024]{1,0:T(8,128)(2,1)S(1)}, bf16[16,1024]{1,0:T(8,128)(2,1)S(1)}, u32[]{:S(2)}, u32[]{:S(2)}) collective-permute-start(bf16[16,1024]{1,0:T(8,128)(2,1)S(1)} %get-tuple-element.44), channel_id=1, source_target_pairs={{0,8},{8,0},{16,24},{24,16},{1,9},{9,1},{17,25},{25,17},{2,10},{10... | collective-permute-start | bytes 98312 | tf_op jit(solution)/shard_map/ppermute | solution.py:496
  15.5 0.6 %query_features.1 = f32[4,16,1024]{2,1,0:T(8,128)S(1)} custom-call(bf16[64,1024]{1,0:T(8,128)(2,1)S(1)} %get-tuple-element.27.refs_0_, f32[3,64,896]{2,1,0:T(8,128)S(1)} %get-tuple-element.28.refs_0_.refs_1_, bf16[16,2176]{1,0:T(8,128)(2,1)S(1)} %get-tuple-element.38.refs_6_.refs_9_.refs_2_, bf16[16,2176]{1,0:T(8,128)(2,1)S(1)} %collective-permute-done.2.refs_8_.refs_3_, ...), custom_call_target="tpu_custom_call" | custom-call | tf_op jit(solution)/shard_map/query_features/pallas_call | solution.py:237
  16.0 0.8 %collective-permute-done.3 = bf16[16,1024]{1,0:T(8,128)(2,1)S(1)} collective-permute-done((bf16[16,1024]{1,0:T(8,128)(2,1)S(1)}, bf16[16,1024]{1,0:T(8,128)(2,1)S(1)}, u32[]{:S(2)}, u32[]{:S(2)}) %collective-permute-start.3) | collective-permute-done | bytes 32800 | tf_op jit(solution)/shard_map/ppermute | solution.py:496
  16.8 0.6 %collective-permute-done.4 = bf16[16,1024]{1,0:T(8,128)(2,1)S(1)} collective-permute-done((bf16[16,1024]{1,0:T(8,128)(2,1)S(1)}, bf16[16,1024]{1,0:T(8,128)(2,1)S(1)}, u32[]{:S(2)}, u32[]{:S(2)}) %collective-permute-start.4) | collective-permute-done | bytes 32800 | tf_op jit(solution)/shard_map/ppermute | solution.py:496
  17.4 0.6 %collective-permute-done.5 = bf16[16,1024]{1,0:T(8,128)(2,1)S(1)} collective-permute-done((bf16[16,1024]{1,0:T(8,128)(2,1)S(1)}, bf16[16,1024]{1,0:T(8,128)(2,1)S(1)}, u32[]{:S(2)}, u32[]{:S(2)}) %collective-permute-start.5) | collective-permute-done | bytes 32800 | tf_op jit(solution)/shard_map/ppermute | solution.py:496
  18.0 2.7 %collective-permute-start.7 = (bf16[4,16,1024]{2,1,0:T(8,128)(2,1)S(1)}, bf16[4,16,1024]{2,1,0:T(8,128)(2,1)S(1)}, u32[]{:S(2)}, u32[]{:S(2)}) collective-permute-start(bf16[4,16,1024]{2,1,0:T(8,128)(2,1)S(1)} %multiply_convert_fusion.refs_1_), channel_id=1, source_target_pairs={{0,4},{1,5},{2,6},{3,7},{4,0},{5,1},{6,2},{7,3},{8,12},{9,13},{10,... | collective-permute-start | bytes 393224 | tf_op jit(solution)/shard_map/ppermute | solution.py:496
  20.6 1.6 %collective-permute-start.11 = (bf16[4,16,1024]{2,1,0:T(8,128)(2,1)S(1)}, bf16[4,16,1024]{2,1,0:T(8,128)(2,1)S(1)}, u32[]{:S(2)}, u32[]{:S(2)}) collective-permute-start(bf16[4,16,1024]{2,1,0:T(8,128)(2,1)S(1)} %multiply_convert_fusion.refs_1_), channel_id=1, source_target_pairs={{0,2},{1,3},{2,0},{3,1},{4,6},{5,7},{6,4},{7,5},{8,10},{9,11},{10,... | collective-permute-start | bytes 393224 | tf_op jit(solution)/shard_map/ppermute | solution.py:496
  22.2 0.2 collective-permute-start.9
  22.4 0.0 collective-permute-start.6
  22.4 5.3 %collective-permute-done.7.refs_3_ = bf16[4,16,1024]{2,1,0:T(8,128)(2,1)S(1)} collective-permute-done((bf16[4,16,1024]{2,1,0:T(8,128)(2,1)S(1)}, bf16[4,16,1024]{2,1,0:T(8,128)(2,1)S(1)}, u32[]{:S(2)}, u32[]{:S(2)}) %collective-permute-start.7) | collective-permute-done | bytes 131104 | tf_op jit(solution)/shard_map/ppermute | solution.py:496
  27.7 0.0 collective-permute-start.8
  27.7 0.0 collective-permute-done.11.refs_4_
  27.7 0.5 %collective-permute-start.12 = (bf16[4,16,1024]{2,1,0:T(8,128)(2,1)S(1)}, bf16[4,16,1024]{2,1,0:T(8,128)(2,1)S(1)}, u32[]{:S(2)}, u32[]{:S(2)}) collective-permute-start(bf16[4,16,1024]{2,1,0:T(8,128)(2,1)S(1)} %collective-permute-done.11.refs_4_), channel_id=1, source_target_pairs={{0,1},{1,0},{2,3},{3,2},{4,5},{5,4},{6,7},{7,6},{8,9},{9,8},{10,11... | collective-permute-start | bytes 393224 | tf_op jit(solution)/shard_map/ppermute | solution.py:496
  28.3 1.0 %collective-permute-done.9.refs_2_ = bf16[4,16,1024]{2,1,0:T(8,128)(2,1)S(1)} collective-permute-done((bf16[4,16,1024]{2,1,0:T(8,128)(2,1)S(1)}, bf16[4,16,1024]{2,1,0:T(8,128)(2,1)S(1)}, u32[]{:S(2)}, u32[]{:S(2)}) %collective-permute-start.9) | collective-permute-done | bytes 131104 | tf_op jit(solution)/shard_map/ppermute | solution.py:496
  29.3 0.0 collective-permute-start.10
  29.3 0.0 collective-permute-done.6.refs_2_
  29.3 0.0 collective-permute-done.8.refs_4_
  29.3 0.8 %project_early.1.refs_1_ = f32[1024,1024]{1,0:T(8,128)S(1)} custom-call(bf16[1024,512]{1,0:T(8,128)(2,1)S(1)} %get-tuple-element.26.refs_0_, bf16[4,16,1024]{2,1,0:T(8,128)(2,1)S(1)} %multiply_convert_fusion.refs_1_, bf16[4,16,1024]{2,1,0:T(8,128)(2,1)S(1)} %collective-permute-done.6.refs_2_, bf16[4,16,1024]{2,1,0:T(8,128)(2,1)S(1)} %collective-permute-done.7.refs_3_, ...), custom_call_target="tpu_custom_call" | custom-call | tf_op jit(solution)/shard_map/project_early/pallas_call | solution.py:427
  30.1 0.0 collective-permute-done.12.refs_5_
  30.1 0.6 %collective-permute-done.10.refs_3_ = bf16[4,16,1024]{2,1,0:T(8,128)(2,1)S(1)} collective-permute-done((bf16[4,16,1024]{2,1,0:T(8,128)(2,1)S(1)}, bf16[4,16,1024]{2,1,0:T(8,128)(2,1)S(1)}, u32[]{:S(2)}, u32[]{:S(2)}) %collective-permute-start.10) | collective-permute-done | bytes 131104 | tf_op jit(solution)/shard_map/ppermute | solution.py:496
  30.6 1.7 %project_late.1 = bf16[1024,1024]{1,0:T(8,128)(2,1)} custom-call(bf16[1024,512]{1,0:T(8,128)(2,1)S(1)} %get-tuple-element.26.refs_0_, f32[1024,1024]{1,0:T(8,128)S(1)} %project_early.1.refs_1_, bf16[4,16,1024]{2,1,0:T(8,128)(2,1)S(1)} %collective-permute-done.9.refs_2_, bf16[4,16,1024]{2,1,0:T(8,128)(2,1)S(1)} %collective-permute-done.10.refs_3_, ...), custom_call_target="tpu_custom_call" | custom-call | tf_op jit(solution)/shard_map/project_late/pallas_call | solution.py:446
  (1 shorter events, 0.0 us)
Async XLA Ops:
  1.6 6.3 %collective-permute-start = (bf16[16,2176]{1,0:T(8,128)(2,1)S(1)}, bf16[16,2176]{1,0:T(8,128)(2,1)S(1)}, u32[]{:S(2)}, u32[]{:S(2)}) collective-permute-start(bf16[16,2176]{1,0:T(8,128)(2,1)S(1)} %get-tuple-element.34), channel_id=1, source_target_pairs={{0,24},{8,16},{16,8},{24,0},{1,25},{9,17},{17,9},{25,1},{2,26},{10... | collective-permute-start | bytes 208904 | tf_op jit(solution)/shard_map/ppermute | solution.py:496
  5.6 4.3 %collective-permute-start.1 = (bf16[16,2176]{1,0:T(8,128)(2,1)S(1)}, bf16[16,2176]{1,0:T(8,128)(2,1)S(1)}, u32[]{:S(2)}, u32[]{:S(2)}) collective-permute-start(bf16[16,2176]{1,0:T(8,128)(2,1)S(1)} %get-tuple-element.35), channel_id=1, source_target_pairs={{0,16},{8,24},{16,0},{24,8},{1,17},{9,25},{17,1},{25,9},{2,18},{10... | collective-permute-start | bytes 208904 | tf_op jit(solution)/shard_map/ppermute | solution.py:496
  6.1 4.3 %collective-permute-start.2 = (bf16[16,2176]{1,0:T(8,128)(2,1)S(1)}, bf16[16,2176]{1,0:T(8,128)(2,1)S(1)}, u32[]{:S(2)}, u32[]{:S(2)}) collective-permute-start(bf16[16,2176]{1,0:T(8,128)(2,1)S(1)} %get-tuple-element.36), channel_id=1, source_target_pairs={{0,8},{8,0},{16,24},{24,16},{1,9},{9,1},{17,25},{25,17},{2,10},{10... | collective-permute-start | bytes 208904 | tf_op jit(solution)/shard_map/ppermute | solution.py:496
  11.9 4.9 %collective-permute-start.3 = (bf16[16,1024]{1,0:T(8,128)(2,1)S(1)}, bf16[16,1024]{1,0:T(8,128)(2,1)S(1)}, u32[]{:S(2)}, u32[]{:S(2)}) collective-permute-start(bf16[16,1024]{1,0:T(8,128)(2,1)S(1)} %get-tuple-element.42), channel_id=1, source_target_pairs={{0,24},{8,16},{16,8},{24,0},{1,25},{9,17},{17,9},{25,1},{2,26},{10... | collective-permute-start | bytes 98312 | tf_op jit(solution)/shard_map/ppermute | solution.py:496
  13.5 3.9 %collective-permute-start.4 = (bf16[16,1024]{1,0:T(8,128)(2,1)S(1)}, bf16[16,1024]{1,0:T(8,128)(2,1)S(1)}, u32[]{:S(2)}, u32[]{:S(2)}) collective-permute-start(bf16[16,1024]{1,0:T(8,128)(2,1)S(1)} %get-tuple-element.43), channel_id=1, source_target_pairs={{0,16},{8,24},{16,0},{24,8},{1,17},{9,25},{17,1},{25,9},{2,18},{10... | collective-permute-start | bytes 98312 | tf_op jit(solution)/shard_map/ppermute | solution.py:496
  14.0 3.9 %collective-permute-start.5 = (bf16[16,1024]{1,0:T(8,128)(2,1)S(1)}, bf16[16,1024]{1,0:T(8,128)(2,1)S(1)}, u32[]{:S(2)}, u32[]{:S(2)}) collective-permute-start(bf16[16,1024]{1,0:T(8,128)(2,1)S(1)} %get-tuple-element.44), channel_id=1, source_target_pairs={{0,8},{8,0},{16,24},{24,16},{1,9},{9,1},{17,25},{25,17},{2,10},{10... | collective-permute-start | bytes 98312 | tf_op jit(solution)/shard_map/ppermute | solution.py:496
  18.0 9.8 %collective-permute-start.7 = (bf16[4,16,1024]{2,1,0:T(8,128)(2,1)S(1)}, bf16[4,16,1024]{2,1,0:T(8,128)(2,1)S(1)}, u32[]{:S(2)}, u32[]{:S(2)}) collective-permute-start(bf16[4,16,1024]{2,1,0:T(8,128)(2,1)S(1)} %multiply_convert_fusion.refs_1_), channel_id=1, source_target_pairs={{0,4},{1,5},{2,6},{3,7},{4,0},{5,1},{6,2},{7,3},{8,12},{9,13},{10,... | collective-permute-start | bytes 393224 | tf_op jit(solution)/shard_map/ppermute | solution.py:496
  20.6 7.1 %collective-permute-start.11 = (bf16[4,16,1024]{2,1,0:T(8,128)(2,1)S(1)}, bf16[4,16,1024]{2,1,0:T(8,128)(2,1)S(1)}, u32[]{:S(2)}, u32[]{:S(2)}) collective-permute-start(bf16[4,16,1024]{2,1,0:T(8,128)(2,1)S(1)} %multiply_convert_fusion.refs_1_), channel_id=1, source_target_pairs={{0,2},{1,3},{2,0},{3,1},{4,6},{5,7},{6,4},{7,5},{8,10},{9,11},{10,... | collective-permute-start | bytes 393224 | tf_op jit(solution)/shard_map/ppermute | solution.py:496
  22.2 7.1 %collective-permute-start.9 = (bf16[4,16,1024]{2,1,0:T(8,128)(2,1)S(1)}, bf16[4,16,1024]{2,1,0:T(8,128)(2,1)S(1)}, u32[]{:S(2)}, u32[]{:S(2)}) collective-permute-start(bf16[4,16,1024]{2,1,0:T(8,128)(2,1)S(1)} %multiply_convert_fusion.refs_1_), channel_id=1, source_target_pairs={{0,6},{1,7},{2,4},{3,5},{4,2},{5,3},{6,0},{7,1},{8,14},{9,15},{10,... | collective-permute-start | bytes 393224 | tf_op jit(solution)/shard_map/ppermute | solution.py:496
  22.4 6.9 %collective-permute-start.6 = (bf16[4,16,1024]{2,1,0:T(8,128)(2,1)S(1)}, bf16[4,16,1024]{2,1,0:T(8,128)(2,1)S(1)}, u32[]{:S(2)}, u32[]{:S(2)}) collective-permute-start(bf16[4,16,1024]{2,1,0:T(8,128)(2,1)S(1)} %multiply_convert_fusion.refs_1_), channel_id=1, source_target_pairs={{0,1},{1,0},{2,3},{3,2},{4,5},{5,4},{6,7},{7,6},{8,9},{9,8},{10,11... | collective-permute-start | bytes 393224 | tf_op jit(solution)/shard_map/ppermute | solution.py:496
  27.7 1.6 %collective-permute-start.8 = (bf16[4,16,1024]{2,1,0:T(8,128)(2,1)S(1)}, bf16[4,16,1024]{2,1,0:T(8,128)(2,1)S(1)}, u32[]{:S(2)}, u32[]{:S(2)}) collective-permute-start(bf16[4,16,1024]{2,1,0:T(8,128)(2,1)S(1)} %collective-permute-done.7.refs_3_), channel_id=1, source_target_pairs={{0,1},{1,0},{2,3},{3,2},{4,5},{5,4},{6,7},{7,6},{8,9},{9,8},{10,11... | collective-permute-start | bytes 393224 | tf_op jit(solution)/shard_map/ppermute | solution.py:496
  27.7 2.3 %collective-permute-start.12 = (bf16[4,16,1024]{2,1,0:T(8,128)(2,1)S(1)}, bf16[4,16,1024]{2,1,0:T(8,128)(2,1)S(1)}, u32[]{:S(2)}, u32[]{:S(2)}) collective-permute-start(bf16[4,16,1024]{2,1,0:T(8,128)(2,1)S(1)} %collective-permute-done.11.refs_4_), channel_id=1, source_target_pairs={{0,1},{1,0},{2,3},{3,2},{4,5},{5,4},{6,7},{7,6},{8,9},{9,8},{10,11... | collective-permute-start | bytes 393224 | tf_op jit(solution)/shard_map/ppermute | solution.py:496
  29.3 1.3 %collective-permute-start.10 = (bf16[4,16,1024]{2,1,0:T(8,128)(2,1)S(1)}, bf16[4,16,1024]{2,1,0:T(8,128)(2,1)S(1)}, u32[]{:S(2)}, u32[]{:S(2)}) collective-permute-start(bf16[4,16,1024]{2,1,0:T(8,128)(2,1)S(1)} %collective-permute-done.9.refs_2_), channel_id=1, source_target_pairs={{0,1},{1,0},{2,3},{3,2},{4,5},{5,4},{6,7},{7,6},{8,9},{9,8},{10,11... | collective-permute-start | bytes 393224 | tf_op jit(solution)/shard_map/ppermute | solution.py:496

commit v10 on v9

--- a/solution.py
+++ b/solution.py
@@ -124,8 +124,8 @@
 
 def pack_kernel(nodes, chans, qkv_ref, filter_ref, flat_ref, *refs):
     outs = refs[:nodes]
-    query_ref, wide_ref = refs[nodes : nodes + 2]
-    filters, streams, flat, sems = refs[nodes + 2 :]
+    query_ref, first_ref, wide_ref = refs[nodes : nodes + 3]
+    filters, streams, flat, sems = refs[nodes + 3 :]
     place = lax.axis_index("ctx")
     block = qkv_ref.shape[2]
     rim = flat_ref.shape[1] - 1
@@ -141,8 +141,9 @@
     lane = lax.broadcasted_iota(jnp.int32, (chans, LANES), 1)
 
     flat_move.wait()
-    for stream in range(3):
-        wide_ref[stream] = widened(flat[stream])
+    for stream in range(2):
+        wide_ref[stream] = widened(flat[1 + stream])
+    first_ref[...] = flat[0]
     query_move.wait()
     edges = jnp.zeros((chans, LANES), jnp.float32)
     for share in range(nodes):
@@ -153,7 +154,7 @@
     for mask, rows in reversed(list(enumerate(shares))):
         edge = edges
         raws = [streams[stream, rows, :] for stream in range(2)]
-        wides = [tap_tiles(wide_ref, 1 + stream, rows) for stream in range(2)]
+        wides = [tap_tiles(wide_ref, stream, rows) for stream in range(2)]
         for stream in reversed(range(2)):
             ends = jnp.where(lane < rim, raws[stream][:, :LANES], raws[stream][:, block - LANES :])
             at = stream * LANE_V
@@ -185,15 +186,16 @@
     far = pl.BlockSpec(memory_space=pltpu.HBM)
     near = pl.BlockSpec(memory_space=pltpu.VMEM)
     flat = jnp.swapaxes(short_taps, 1, 2)
-    *pieces, query, wide = pl.pallas_call(
+    *pieces, query, first, wide = pl.pallas_call(
         lambda *refs: pack_kernel(nodes, chans, *refs),
         out_shape=[jax.ShapeDtypeStruct((chans, 2 * block + LANES), jnp.bfloat16)] * nodes
         + [
             jax.ShapeDtypeStruct((every, block), jnp.bfloat16),
-            jax.ShapeDtypeStruct((3, every, short_taps.shape[2] * LANES), jnp.float32),
+            jax.ShapeDtypeStruct(flat.shape[1:], jnp.float32),
+            jax.ShapeDtypeStruct((2, every, short_taps.shape[2] * LANES), jnp.float32),
         ],
         in_specs=[far] * 3,
-        out_specs=[near] * (nodes + 2),
+        out_specs=[near] * (nodes + 3),
         scratch_shapes=[
             pltpu.VMEM((every, block), jnp.float32),
             pltpu.VMEM((2, every, block), jnp.bfloat16),
@@ -203,12 +205,13 @@
         compiler_params=pltpu.CompilerParams(vmem_limit_bytes=16 << 20),
         name="pack",
     )(*in_hbm(qkv, long_filter, flat))
-    return pieces, query, wide
-
-
-def query_kernel(nodes, query_ref, wide_ref, *refs):
+    return pieces, (query, first), wide
+
+
+def query_kernel(nodes, query_ref, flat_ref, *refs):
     pieces = refs[:nodes]
-    out_ref = refs[nodes]
+    out_ref, wide_ref = refs[nodes:]
+    wide_ref[0] = widened(flat_ref[...])
     place = lax.axis_index("ctx")
     _, chans, block = out_ref.shape
     rim = wide_ref.shape[2] // LANES - 1
@@ -232,16 +235,17 @@
         out_ref[nodes - 1 - mask, :, :LANES] = first
 
 
-def query_features(query, wide, pieces, nodes, chans):
+def query_features(query, flat, pieces, nodes, chans):
     near = pl.BlockSpec(memory_space=pltpu.VMEM)
     return pl.pallas_call(
         lambda *refs: query_kernel(nodes, *refs),
         out_shape=jax.ShapeDtypeStruct((nodes, chans, query.shape[1]), jnp.float32),
         in_specs=[near] * (2 + nodes),
         out_specs=near,
+        scratch_shapes=[pltpu.VMEM((1, flat.shape[1], flat.shape[0] * LANES), jnp.float32)],
         compiler_params=pltpu.CompilerParams(vmem_limit_bytes=16 << 20),
         name="query_features",
-    )(query, wide, *pieces)
+    )(query, flat, *pieces)
 
 
 def long_kernel(
@@ -262,7 +266,7 @@
         edges[0] = jnp.zeros((chans, LANES), jnp.bfloat16)
         for mask in range(nodes):
             edges[(place ^ mask) + 1] = pieces[mask][:, 2 * block :]
-        wide = [tap_tiles(wide_ref, 1 + stream, own) for stream in range(2)]
+        wide = [tap_tiles(wide_ref, stream, own) for stream in range(2)]
 
     def repaired(mask, tile):
         before, now = edges[place ^ mask], pieces[mask][:, 2 * block :]
@@ -521,7 +525,7 @@
 
     if fits:
         tied = lax.optimization_barrier((mixed[0], *pieces[::-1]))[:0:-1]
-        featured = query_features(query, wide, tied, nodes, chans)
+        featured = query_features(*query, tied, nodes, chans)
     else:
         featured = query.reshape(nodes, chans, block)[jnp.arange(nodes, dtype=jnp.int32) ^ place][::-1]
     mixed = [swapped(mixed[mask], mask, "ctx") for mask in range(nodes)]

time: 32.6 us -> 32.5 us (level)
  transfers between devices with their start and end apart: 13 -> 13, of which waited for: 9 -> 9; matrix products, arithmetic and copies ran while one was open for 0% -> 0% of each run, Pallas kernels for 8% -> 9%
where the time goes in v10:
time: 32.5 us; the launch traced here: 32.3 us
  starting transfers between devices  13.1 us (40%)
  waiting for transfers between devices  11.5 us (35%)
  Pallas kernels  7.58 us (23%)
    ppermute x13, starting transfers between devices, swapped(): lax.ppermute(block, axis, [(i, i ^ mask) for i in range(lax.axis_size(axi...  13.1 us
    ppermute x13, waiting for transfers between devices, swapped(): lax.ppermute(block, axis, [(i, i ^ mask) for i in range(lax.axis_size(axi...  11.5 us
    pallas_call x1, Pallas kernels, project_late(): pl.pallas_call(lambda *refs: final_kernel(tuple(late), cuts, *refs), out_...  1.67 us
    pallas_call x1, Pallas kernels, pack(): pl.pallas_call(lambda *refs: pack_kernel(nodes, chans, *refs), out_shape=...  1.63 us
    pallas_call x1, Pallas kernels, long_mix(): pl.pallas_call(lambda *refs: long_kernel(nodes, chans, per_node, rim, *re...  1.47 us
    pallas_call x1, Pallas kernels, near_tables(): pl.pallas_call(lambda *refs: tables_kernel(count, *refs), out_shape=[jax....  1.4 us
    pallas_call x1, Pallas kernels, project_early(): pl.pallas_call(lambda *refs: partial_kernel(tuple(early), features // 4,...  0.77 us
    pallas_call x1, Pallas kernels, query_features(): pl.pallas_call(lambda *refs: query_kernel(nodes, *refs), out_shape=jax.Sh...  0.65 us
  transfers between devices with their start and end apart: 13, of which 9 were waited for; matrix products, arithmetic and copies ran while one was open for 0% of the time, Pallas kernels for 9%

profile of v10, /device:TPU:0, one launch (start us, length us, event | category | flops | bytes accessed | tf_op | source)
XLA Modules:
  0.0 32.3 jit_solution(4745552255632471647)
XLA Ops:
  0.0 1.6 %pack.1 = (bf16[16,2176]{1,0:T(8,128)(2,1)S(1)}, bf16[16,2176]{1,0:T(8,128)(2,1)S(1)}, bf16[16,2176]{1,0:T(8,128)(2,1)S(1)}, bf16[16,2176]{1,0:T(8,128)(2,1)S(1)...) custom-call(bf16[3,64,1024]{2,1,0:T(8,128)(2,1)} %refs_0_.2, f32[64,1024]{1,0:T(8,128)} %refs_1_.2, ...), custom_call_target="tpu_custom_call" | custom-call | tf_op jit(solution)/shard_map/pack/pallas_call | solution.py:189
  1.6 4.0 %collective-permute-start = (bf16[16,2176]{1,0:T(8,128)(2,1)S(1)}, bf16[16,2176]{1,0:T(8,128)(2,1)S(1)}, u32[]{:S(2)}, u32[]{:S(2)}) collective-permute-start(bf16[16,2176]{1,0:T(8,128)(2,1)S(1)} %get-tuple-element.36), channel_id=1, source_target_pairs={{0,24},{8,16},{16,8},{24,0},{1,25},{9,17},{17,9},{25,1},{2,26},{10... | collective-permute-start | bytes 208904 | tf_op jit(solution)/shard_map/ppermute | solution.py:500
  5.6 0.5 %collective-permute-start.1 = (bf16[16,2176]{1,0:T(8,128)(2,1)S(1)}, bf16[16,2176]{1,0:T(8,128)(2,1)S(1)}, u32[]{:S(2)}, u32[]{:S(2)}) collective-permute-start(bf16[16,2176]{1,0:T(8,128)(2,1)S(1)} %get-tuple-element.37), channel_id=1, source_target_pairs={{0,16},{8,24},{16,0},{24,8},{1,17},{9,25},{17,1},{25,9},{2,18},{10... | collective-permute-start | bytes 208904 | tf_op jit(solution)/shard_map/ppermute | solution.py:500
  6.1 0.1 collective-permute-start.2
  6.2 1.4 %near_tables.1 = (bf16[1024,512]{1,0:T(8,128)(2,1)S(1)}, bf16[64,64]{1,0:T(8,128)(2,1)S(1)}, f32[32,256]{1,0:T(8,128)S(1)}, bf16[768,256]{1,0:T(8,128)(2,1)S(1)}...) custom-call(bf16[1024,512]{1,0:T(8,128)(2,1)} %refs_0_.3, bf16[64,64]{1,0:T(8,128)(2,1)} %constant.8.clone.refs_1_, ...), custom_call_target="tpu_custom_call" | custom-call | tf_op jit(solution)/shard_map/near_tables/pallas_call | solution.py:110
  7.6 0.3 collective-permute-done.refs_6_.refs_5_
  7.9 2.0 %collective-permute-done.1.refs_7_.refs_4_ = bf16[16,2176]{1,0:T(8,128)(2,1)S(1)} collective-permute-done((bf16[16,2176]{1,0:T(8,128)(2,1)S(1)}, bf16[16,2176]{1,0:T(8,128)(2,1)S(1)}, u32[]{:S(2)}, u32[]{:S(2)}) %collective-permute-start.1) | collective-permute-done | bytes 69664 | tf_op jit(solution)/shard_map/ppermute | solution.py:500
  9.9 0.5 %collective-permute-done.2.refs_8_.refs_3_ = bf16[16,2176]{1,0:T(8,128)(2,1)S(1)} collective-permute-done((bf16[16,2176]{1,0:T(8,128)(2,1)S(1)}, bf16[16,2176]{1,0:T(8,128)(2,1)S(1)}, u32[]{:S(2)}, u32[]{:S(2)}) %collective-permute-start.2) | collective-permute-done | bytes 69664 | tf_op jit(solution)/shard_map/ppermute | solution.py:500
  10.4 1.5 %long_mix.1 = (bf16[16,1024]{1,0:T(8,128)(2,1)S(1)}, bf16[16,1024]{1,0:T(8,128)(2,1)S(1)}, bf16[16,1024]{1,0:T(8,128)(2,1)S(1)}, bf16[16,1024]{1,0:T(8,128)(2,1)S(1)}) custom-call(f32[2,64,896]{2,1,0:T(8,128)S(1)} %get-tuple-element.30.refs_0_, bf16[64,64]{1,0:T(8,128)(2,1)S(1)} %get-tuple-element.31.refs_1_, f32[32,256]{1,0:T(8,128)S(1)} %get-tuple-element.32.refs_2_, ...), custom_call_target="tpu_custom_call" | custom-call | tf_op jit(solution)/shard_map/long_mix/pallas_call | solution.py:366
  11.9 1.6 %collective-permute-start.3 = (bf16[16,1024]{1,0:T(8,128)(2,1)S(1)}, bf16[16,1024]{1,0:T(8,128)(2,1)S(1)}, u32[]{:S(2)}, u32[]{:S(2)}) collective-permute-start(bf16[16,1024]{1,0:T(8,128)(2,1)S(1)} %get-tuple-element.44), channel_id=1, source_target_pairs={{0,24},{8,16},{16,8},{24,0},{1,25},{9,17},{17,9},{25,1},{2,26},{10... | collective-permute-start | bytes 98312 | tf_op jit(solution)/shard_map/ppermute | solution.py:500
  13.5 0.6 %collective-permute-start.4 = (bf16[16,1024]{1,0:T(8,128)(2,1)S(1)}, bf16[16,1024]{1,0:T(8,128)(2,1)S(1)}, u32[]{:S(2)}, u32[]{:S(2)}) collective-permute-start(bf16[16,1024]{1,0:T(8,128)(2,1)S(1)} %get-tuple-element.45), channel_id=1, source_target_pairs={{0,16},{8,24},{16,0},{24,8},{1,17},{9,25},{17,1},{25,9},{2,18},{10... | collective-permute-start | bytes 98312 | tf_op jit(solution)/shard_map/ppermute | solution.py:500
  14.0 1.4 %collective-permute-start.5 = (bf16[16,1024]{1,0:T(8,128)(2,1)S(1)}, bf16[16,1024]{1,0:T(8,128)(2,1)S(1)}, u32[]{:S(2)}, u32[]{:S(2)}) collective-permute-start(bf16[16,1024]{1,0:T(8,128)(2,1)S(1)} %get-tuple-element.46), channel_id=1, source_target_pairs={{0,8},{8,0},{16,24},{24,16},{1,9},{9,1},{17,25},{25,17},{2,10},{10... | collective-permute-start | bytes 98312 | tf_op jit(solution)/shard_map/ppermute | solution.py:500
  15.4 0.7 %query_features.1 = f32[4,16,1024]{2,1,0:T(8,128)S(1)} custom-call(bf16[64,1024]{1,0:T(8,128)(2,1)S(1)} %get-tuple-element.28.refs_0_, f32[7,64]{1,0:T(8,128)S(1)} %get-tuple-element.29.refs_1_, bf16[16,2176]{1,0:T(8,128)(2,1)S(1)} %get-tuple-element.40.refs_6_.refs_9_.refs_2_, bf16[16,2176]{1,0:T(8,128)(2,1)S(1)} %collective-permute-done.2.refs_8_.refs_3_, ...), custom_call_target="tpu_custom_call" | custom-call | tf_op jit(solution)/shard_map/query_features/pallas_call | solution.py:240
  16.1 0.7 %collective-permute-done.3 = bf16[16,1024]{1,0:T(8,128)(2,1)S(1)} collective-permute-done((bf16[16,1024]{1,0:T(8,128)(2,1)S(1)}, bf16[16,1024]{1,0:T(8,128)(2,1)S(1)}, u32[]{:S(2)}, u32[]{:S(2)}) %collective-permute-start.3) | collective-permute-done | bytes 32800 | tf_op jit(solution)/shard_map/ppermute | solution.py:500
  16.8 0.6 %collective-permute-done.4 = bf16[16,1024]{1,0:T(8,128)(2,1)S(1)} collective-permute-done((bf16[16,1024]{1,0:T(8,128)(2,1)S(1)}, bf16[16,1024]{1,0:T(8,128)(2,1)S(1)}, u32[]{:S(2)}, u32[]{:S(2)}) %collective-permute-start.4) | collective-permute-done | bytes 32800 | tf_op jit(solution)/shard_map/ppermute | solution.py:500
  17.4 0.6 %collective-permute-done.5 = bf16[16,1024]{1,0:T(8,128)(2,1)S(1)} collective-permute-done((bf16[16,1024]{1,0:T(8,128)(2,1)S(1)}, bf16[16,1024]{1,0:T(8,128)(2,1)S(1)}, u32[]{:S(2)}, u32[]{:S(2)}) %collective-permute-start.5) | collective-permute-done | bytes 32800 | tf_op jit(solution)/shard_map/ppermute | solution.py:500
  18.0 2.7 %collective-permute-start.7 = (bf16[4,16,1024]{2,1,0:T(8,128)(2,1)S(1)}, bf16[4,16,1024]{2,1,0:T(8,128)(2,1)S(1)}, u32[]{:S(2)}, u32[]{:S(2)}) collective-permute-start(bf16[4,16,1024]{2,1,0:T(8,128)(2,1)S(1)} %multiply_convert_fusion.refs_1_), channel_id=1, source_target_pairs={{0,4},{1,5},{2,6},{3,7},{4,0},{5,1},{6,2},{7,3},{8,12},{9,13},{10,... | collective-permute-start | bytes 393224 | tf_op jit(solution)/shard_map/ppermute | solution.py:500
  20.6 1.6 %collective-permute-start.11 = (bf16[4,16,1024]{2,1,0:T(8,128)(2,1)S(1)}, bf16[4,16,1024]{2,1,0:T(8,128)(2,1)S(1)}, u32[]{:S(2)}, u32[]{:S(2)}) collective-permute-start(bf16[4,16,1024]{2,1,0:T(8,128)(2,1)S(1)} %multiply_convert_fusion.refs_1_), channel_id=1, source_target_pairs={{0,2},{1,3},{2,0},{3,1},{4,6},{5,7},{6,4},{7,5},{8,10},{9,11},{10,... | collective-permute-start | bytes 393224 | tf_op jit(solution)/shard_map/ppermute | solution.py:500
  22.2 0.2 collective-permute-start.9
  22.4 0.0 collective-permute-start.6
  22.4 5.3 %collective-permute-done.7.refs_3_ = bf16[4,16,1024]{2,1,0:T(8,128)(2,1)S(1)} collective-permute-done((bf16[4,16,1024]{2,1,0:T(8,128)(2,1)S(1)}, bf16[4,16,1024]{2,1,0:T(8,128)(2,1)S(1)}, u32[]{:S(2)}, u32[]{:S(2)}) %collective-permute-start.7) | collective-permute-done | bytes 131104 | tf_op jit(solution)/shard_map/ppermute | solution.py:500
  27.7 0.0 collective-permute-start.8
  27.7 0.0 collective-permute-done.11.refs_4_
  27.7 0.5 %collective-permute-start.12 = (bf16[4,16,1024]{2,1,0:T(8,128)(2,1)S(1)}, bf16[4,16,1024]{2,1,0:T(8,128)(2,1)S(1)}, u32[]{:S(2)}, u32[]{:S(2)}) collective-permute-start(bf16[4,16,1024]{2,1,0:T(8,128)(2,1)S(1)} %collective-permute-done.11.refs_4_), channel_id=1, source_target_pairs={{0,1},{1,0},{2,3},{3,2},{4,5},{5,4},{6,7},{7,6},{8,9},{9,8},{10,11... | collective-permute-start | bytes 393224 | tf_op jit(solution)/shard_map/ppermute | solution.py:500
  28.2 1.1 %collective-permute-done.9.refs_2_ = bf16[4,16,1024]{2,1,0:T(8,128)(2,1)S(1)} collective-permute-done((bf16[4,16,1024]{2,1,0:T(8,128)(2,1)S(1)}, bf16[4,16,1024]{2,1,0:T(8,128)(2,1)S(1)}, u32[]{:S(2)}, u32[]{:S(2)}) %collective-permute-start.9) | collective-permute-done | bytes 131104 | tf_op jit(solution)/shard_map/ppermute | solution.py:500
  29.3 0.0 collective-permute-start.10
  29.3 0.0 collective-permute-done.6.refs_2_
  29.3 0.0 collective-permute-done.8.refs_4_
  29.3 0.8 %project_early.1.refs_1_ = f32[1024,1024]{1,0:T(8,128)S(1)} custom-call(bf16[1024,512]{1,0:T(8,128)(2,1)S(1)} %get-tuple-element.27.refs_0_, bf16[4,16,1024]{2,1,0:T(8,128)(2,1)S(1)} %multiply_convert_fusion.refs_1_, bf16[4,16,1024]{2,1,0:T(8,128)(2,1)S(1)} %collective-permute-done.6.refs_2_, bf16[4,16,1024]{2,1,0:T(8,128)(2,1)S(1)} %collective-permute-done.7.refs_3_, ...), custom_call_target="tpu_custom_call" | custom-call | tf_op jit(solution)/shard_map/project_early/pallas_call | solution.py:431
  30.1 0.0 collective-permute-done.12.refs_5_
  30.1 0.6 %collective-permute-done.10.refs_3_ = bf16[4,16,1024]{2,1,0:T(8,128)(2,1)S(1)} collective-permute-done((bf16[4,16,1024]{2,1,0:T(8,128)(2,1)S(1)}, bf16[4,16,1024]{2,1,0:T(8,128)(2,1)S(1)}, u32[]{:S(2)}, u32[]{:S(2)}) %collective-permute-start.10) | collective-permute-done | bytes 131104 | tf_op jit(solution)/shard_map/ppermute | solution.py:500
  30.6 1.7 %project_late.1 = bf16[1024,1024]{1,0:T(8,128)(2,1)} custom-call(bf16[1024,512]{1,0:T(8,128)(2,1)S(1)} %get-tuple-element.27.refs_0_, f32[1024,1024]{1,0:T(8,128)S(1)} %project_early.1.refs_1_, bf16[4,16,1024]{2,1,0:T(8,128)(2,1)S(1)} %collective-permute-done.9.refs_2_, bf16[4,16,1024]{2,1,0:T(8,128)(2,1)S(1)} %collective-permute-done.10.refs_3_, ...), custom_call_target="tpu_custom_call" | custom-call | tf_op jit(solution)/shard_map/project_late/pallas_call | solution.py:450
  (1 shorter events, 0.0 us)
Async XLA Ops:
  1.6 6.3 %collective-permute-start = (bf16[16,2176]{1,0:T(8,128)(2,1)S(1)}, bf16[16,2176]{1,0:T(8,128)(2,1)S(1)}, u32[]{:S(2)}, u32[]{:S(2)}) collective-permute-start(bf16[16,2176]{1,0:T(8,128)(2,1)S(1)} %get-tuple-element.36), channel_id=1, source_target_pairs={{0,24},{8,16},{16,8},{24,0},{1,25},{9,17},{17,9},{25,1},{2,26},{10... | collective-permute-start | bytes 208904 | tf_op jit(solution)/shard_map/ppermute | solution.py:500
  5.6 4.3 %collective-permute-start.1 = (bf16[16,2176]{1,0:T(8,128)(2,1)S(1)}, bf16[16,2176]{1,0:T(8,128)(2,1)S(1)}, u32[]{:S(2)}, u32[]{:S(2)}) collective-permute-start(bf16[16,2176]{1,0:T(8,128)(2,1)S(1)} %get-tuple-element.37), channel_id=1, source_target_pairs={{0,16},{8,24},{16,0},{24,8},{1,17},{9,25},{17,1},{25,9},{2,18},{10... | collective-permute-start | bytes 208904 | tf_op jit(solution)/shard_map/ppermute | solution.py:500
  6.1 4.3 %collective-permute-start.2 = (bf16[16,2176]{1,0:T(8,128)(2,1)S(1)}, bf16[16,2176]{1,0:T(8,128)(2,1)S(1)}, u32[]{:S(2)}, u32[]{:S(2)}) collective-permute-start(bf16[16,2176]{1,0:T(8,128)(2,1)S(1)} %get-tuple-element.38), channel_id=1, source_target_pairs={{0,8},{8,0},{16,24},{24,16},{1,9},{9,1},{17,25},{25,17},{2,10},{10... | collective-permute-start | bytes 208904 | tf_op jit(solution)/shard_map/ppermute | solution.py:500
  11.9 4.9 %collective-permute-start.3 = (bf16[16,1024]{1,0:T(8,128)(2,1)S(1)}, bf16[16,1024]{1,0:T(8,128)(2,1)S(1)}, u32[]{:S(2)}, u32[]{:S(2)}) collective-permute-start(bf16[16,1024]{1,0:T(8,128)(2,1)S(1)} %get-tuple-element.44), channel_id=1, source_target_pairs={{0,24},{8,16},{16,8},{24,0},{1,25},{9,17},{17,9},{25,1},{2,26},{10... | collective-permute-start | bytes 98312 | tf_op jit(solution)/shard_map/ppermute | solution.py:500
  13.5 3.9 %collective-permute-start.4 = (bf16[16,1024]{1,0:T(8,128)(2,1)S(1)}, bf16[16,1024]{1,0:T(8,128)(2,1)S(1)}, u32[]{:S(2)}, u32[]{:S(2)}) collective-permute-start(bf16[16,1024]{1,0:T(8,128)(2,1)S(1)} %get-tuple-element.45), channel_id=1, source_target_pairs={{0,16},{8,24},{16,0},{24,8},{1,17},{9,25},{17,1},{25,9},{2,18},{10... | collective-permute-start | bytes 98312 | tf_op jit(solution)/shard_map/ppermute | solution.py:500
  14.0 3.9 %collective-permute-start.5 = (bf16[16,1024]{1,0:T(8,128)(2,1)S(1)}, bf16[16,1024]{1,0:T(8,128)(2,1)S(1)}, u32[]{:S(2)}, u32[]{:S(2)}) collective-permute-start(bf16[16,1024]{1,0:T(8,128)(2,1)S(1)} %get-tuple-element.46), channel_id=1, source_target_pairs={{0,8},{8,0},{16,24},{24,16},{1,9},{9,1},{17,25},{25,17},{2,10},{10... | collective-permute-start | bytes 98312 | tf_op jit(solution)/shard_map/ppermute | solution.py:500
  18.0 9.8 %collective-permute-start.7 = (bf16[4,16,1024]{2,1,0:T(8,128)(2,1)S(1)}, bf16[4,16,1024]{2,1,0:T(8,128)(2,1)S(1)}, u32[]{:S(2)}, u32[]{:S(2)}) collective-permute-start(bf16[4,16,1024]{2,1,0:T(8,128)(2,1)S(1)} %multiply_convert_fusion.refs_1_), channel_id=1, source_target_pairs={{0,4},{1,5},{2,6},{3,7},{4,0},{5,1},{6,2},{7,3},{8,12},{9,13},{10,... | collective-permute-start | bytes 393224 | tf_op jit(solution)/shard_map/ppermute | solution.py:500
  20.6 7.1 %collective-permute-start.11 = (bf16[4,16,1024]{2,1,0:T(8,128)(2,1)S(1)}, bf16[4,16,1024]{2,1,0:T(8,128)(2,1)S(1)}, u32[]{:S(2)}, u32[]{:S(2)}) collective-permute-start(bf16[4,16,1024]{2,1,0:T(8,128)(2,1)S(1)} %multiply_convert_fusion.refs_1_), channel_id=1, source_target_pairs={{0,2},{1,3},{2,0},{3,1},{4,6},{5,7},{6,4},{7,5},{8,10},{9,11},{10,... | collective-permute-start | bytes 393224 | tf_op jit(solution)/shard_map/ppermute | solution.py:500
  22.2 7.1 %collective-permute-start.9 = (bf16[4,16,1024]{2,1,0:T(8,128)(2,1)S(1)}, bf16[4,16,1024]{2,1,0:T(8,128)(2,1)S(1)}, u32[]{:S(2)}, u32[]{:S(2)}) collective-permute-start(bf16[4,16,1024]{2,1,0:T(8,128)(2,1)S(1)} %multiply_convert_fusion.refs_1_), channel_id=1, source_target_pairs={{0,6},{1,7},{2,4},{3,5},{4,2},{5,3},{6,0},{7,1},{8,14},{9,15},{10,... | collective-permute-start | bytes 393224 | tf_op jit(solution)/shard_map/ppermute | solution.py:500
  22.4 6.9 %collective-permute-start.6 = (bf16[4,16,1024]{2,1,0:T(8,128)(2,1)S(1)}, bf16[4,16,1024]{2,1,0:T(8,128)(2,1)S(1)}, u32[]{:S(2)}, u32[]{:S(2)}) collective-permute-start(bf16[4,16,1024]{2,1,0:T(8,128)(2,1)S(1)} %multiply_convert_fusion.refs_1_), channel_id=1, source_target_pairs={{0,1},{1,0},{2,3},{3,2},{4,5},{5,4},{6,7},{7,6},{8,9},{9,8},{10,11... | collective-permute-start | bytes 393224 | tf_op jit(solution)/shard_map/ppermute | solution.py:500
  27.7 1.6 %collective-permute-start.8 = (bf16[4,16,1024]{2,1,0:T(8,128)(2,1)S(1)}, bf16[4,16,1024]{2,1,0:T(8,128)(2,1)S(1)}, u32[]{:S(2)}, u32[]{:S(2)}) collective-permute-start(bf16[4,16,1024]{2,1,0:T(8,128)(2,1)S(1)} %collective-permute-done.7.refs_3_), channel_id=1, source_target_pairs={{0,1},{1,0},{2,3},{3,2},{4,5},{5,4},{6,7},{7,6},{8,9},{9,8},{10,11... | collective-permute-start | bytes 393224 | tf_op jit(solution)/shard_map/ppermute | solution.py:500
  27.7 2.3 %collective-permute-start.12 = (bf16[4,16,1024]{2,1,0:T(8,128)(2,1)S(1)}, bf16[4,16,1024]{2,1,0:T(8,128)(2,1)S(1)}, u32[]{:S(2)}, u32[]{:S(2)}) collective-permute-start(bf16[4,16,1024]{2,1,0:T(8,128)(2,1)S(1)} %collective-permute-done.11.refs_4_), channel_id=1, source_target_pairs={{0,1},{1,0},{2,3},{3,2},{4,5},{5,4},{6,7},{7,6},{8,9},{9,8},{10,11... | collective-permute-start | bytes 393224 | tf_op jit(solution)/shard_map/ppermute | solution.py:500
  29.3 1.3 %collective-permute-start.10 = (bf16[4,16,1024]{2,1,0:T(8,128)(2,1)S(1)}, bf16[4,16,1024]{2,1,0:T(8,128)(2,1)S(1)}, u32[]{:S(2)}, u32[]{:S(2)}) collective-permute-start(bf16[4,16,1024]{2,1,0:T(8,128)(2,1)S(1)} %collective-permute-done.9.refs_2_), channel_id=1, source_target_pairs={{0,1},{1,0},{2,3},{3,2},{4,5},{5,4},{6,7},{7,6},{8,9},{9,8},{10,11... | collective-permute-start | bytes 393224 | tf_op jit(solution)/shard_map/ppermute | solution.py:500

commit v11 on v10

--- a/solution.py
+++ b/solution.py
@@ -141,8 +141,9 @@
     lane = lax.broadcasted_iota(jnp.int32, (chans, LANES), 1)
 
     flat_move.wait()
+    both = widened(jnp.concatenate([flat[1], flat[2]], axis=1))
     for stream in range(2):
-        wide_ref[stream] = widened(flat[1 + stream])
+        wide_ref[stream] = both[stream * flat.shape[2] : (stream + 1) * flat.shape[2]]
     first_ref[...] = flat[0]
     query_move.wait()
     edges = jnp.zeros((chans, LANES), jnp.float32)

time: 32.5 us -> 32.6 us (level)
  no operation moved by 1% of the time
where the time goes in v11:
time: 32.6 us; the launch traced here: 32.4 us
  starting transfers between devices  13.1 us (40%)
  waiting for transfers between devices  11.5 us (35%)
  Pallas kernels  7.65 us (23%)
    ppermute x13, starting transfers between devices, swapped(): lax.ppermute(block, axis, [(i, i ^ mask) for i in range(lax.axis_size(axi...  13.1 us
    ppermute x13, waiting for transfers between devices, swapped(): lax.ppermute(block, axis, [(i, i ^ mask) for i in range(lax.axis_size(axi...  11.5 us
    pallas_call x1, Pallas kernels, project_late(): pl.pallas_call(lambda *refs: final_kernel(tuple(late), cuts, *refs), out_...  1.68 us
    pallas_call x1, Pallas kernels, pack(): pl.pallas_call(lambda *refs: pack_kernel(nodes, chans, *refs), out_shape=...  1.68 us
    pallas_call x1, Pallas kernels, long_mix(): pl.pallas_call(lambda *refs: long_kernel(nodes, chans, per_node, rim, *re...  1.48 us
    pallas_call x1, Pallas kernels, near_tables(): pl.pallas_call(lambda *refs: tables_kernel(count, *refs), out_shape=[jax....  1.4 us
    pallas_call x1, Pallas kernels, project_early(): pl.pallas_call(lambda *refs: partial_kernel(tuple(early), features // 4,...  0.77 us
    pallas_call x1, Pallas kernels, query_features(): pl.pallas_call(lambda *refs: query_kernel(nodes, *refs), out_shape=jax.Sh...  0.65 us
  transfers between devices with their start and end apart: 13, of which 9 were waited for; matrix products, arithmetic and copies ran while one was open for 0% of the time, Pallas kernels for 9%

profile of v11, /device:TPU:0, one launch (start us, length us, event | category | flops | bytes accessed | tf_op | source)
XLA Modules:
  0.0 32.4 jit_solution(13571667134388114556)
XLA Ops:
  0.0 1.7 %pack.1 = (bf16[16,2176]{1,0:T(8,128)(2,1)S(1)}, bf16[16,2176]{1,0:T(8,128)(2,1)S(1)}, bf16[16,2176]{1,0:T(8,128)(2,1)S(1)}, bf16[16,2176]{1,0:T(8,128)(2,1)S(1)...) custom-call(bf16[3,64,1024]{2,1,0:T(8,128)(2,1)} %refs_0_.2, f32[64,1024]{1,0:T(8,128)} %refs_1_.2, ...), custom_call_target="tpu_custom_call" | custom-call | tf_op jit(solution)/shard_map/pack/pallas_call | solution.py:190
  1.7 4.0 %collective-permute-start = (bf16[16,2176]{1,0:T(8,128)(2,1)S(1)}, bf16[16,2176]{1,0:T(8,128)(2,1)S(1)}, u32[]{:S(2)}, u32[]{:S(2)}) collective-permute-start(bf16[16,2176]{1,0:T(8,128)(2,1)S(1)} %get-tuple-element.36), channel_id=1, source_target_pairs={{0,24},{8,16},{16,8},{24,0},{1,25},{9,17},{17,9},{25,1},{2,26},{10... | collective-permute-start | bytes 208904 | tf_op jit(solution)/shard_map/ppermute | solution.py:501
  5.6 0.5 %collective-permute-start.1 = (bf16[16,2176]{1,0:T(8,128)(2,1)S(1)}, bf16[16,2176]{1,0:T(8,128)(2,1)S(1)}, u32[]{:S(2)}, u32[]{:S(2)}) collective-permute-start(bf16[16,2176]{1,0:T(8,128)(2,1)S(1)} %get-tuple-element.37), channel_id=1, source_target_pairs={{0,16},{8,24},{16,0},{24,8},{1,17},{9,25},{17,1},{25,9},{2,18},{10... | collective-permute-start | bytes 208904 | tf_op jit(solution)/shard_map/ppermute | solution.py:501
  6.2 0.1 collective-permute-start.2
  6.3 1.4 %near_tables.1 = (bf16[1024,512]{1,0:T(8,128)(2,1)S(1)}, bf16[64,64]{1,0:T(8,128)(2,1)S(1)}, f32[32,256]{1,0:T(8,128)S(1)}, bf16[768,256]{1,0:T(8,128)(2,1)S(1)}...) custom-call(bf16[1024,512]{1,0:T(8,128)(2,1)} %refs_0_.3, bf16[64,64]{1,0:T(8,128)(2,1)} %constant.8.clone.refs_1_, ...), custom_call_target="tpu_custom_call" | custom-call | tf_op jit(solution)/shard_map/near_tables/pallas_call | solution.py:110
  7.7 0.3 collective-permute-done.refs_6_.refs_5_
  8.0 2.0 %collective-permute-done.1.refs_7_.refs_4_ = bf16[16,2176]{1,0:T(8,128)(2,1)S(1)} collective-permute-done((bf16[16,2176]{1,0:T(8,128)(2,1)S(1)}, bf16[16,2176]{1,0:T(8,128)(2,1)S(1)}, u32[]{:S(2)}, u32[]{:S(2)}) %collective-permute-start.1) | collective-permute-done | bytes 69664 | tf_op jit(solution)/shard_map/ppermute | solution.py:501
  10.0 0.5 %collective-permute-done.2.refs_8_.refs_3_ = bf16[16,2176]{1,0:T(8,128)(2,1)S(1)} collective-permute-done((bf16[16,2176]{1,0:T(8,128)(2,1)S(1)}, bf16[16,2176]{1,0:T(8,128)(2,1)S(1)}, u32[]{:S(2)}, u32[]{:S(2)}) %collective-permute-start.2) | collective-permute-done | bytes 69664 | tf_op jit(solution)/shard_map/ppermute | solution.py:501
  10.5 1.5 %long_mix.1 = (bf16[16,1024]{1,0:T(8,128)(2,1)S(1)}, bf16[16,1024]{1,0:T(8,128)(2,1)S(1)}, bf16[16,1024]{1,0:T(8,128)(2,1)S(1)}, bf16[16,1024]{1,0:T(8,128)(2,1)S(1)}) custom-call(f32[2,64,896]{2,1,0:T(8,128)S(1)} %get-tuple-element.30.refs_0_, bf16[64,64]{1,0:T(8,128)(2,1)S(1)} %get-tuple-element.31.refs_1_, f32[32,256]{1,0:T(8,128)S(1)} %get-tuple-element.32.refs_2_, ...), custom_call_target="tpu_custom_call" | custom-call | tf_op jit(solution)/shard_map/long_mix/pallas_call | solution.py:367
  11.9 1.6 %collective-permute-start.3 = (bf16[16,1024]{1,0:T(8,128)(2,1)S(1)}, bf16[16,1024]{1,0:T(8,128)(2,1)S(1)}, u32[]{:S(2)}, u32[]{:S(2)}) collective-permute-start(bf16[16,1024]{1,0:T(8,128)(2,1)S(1)} %get-tuple-element.44), channel_id=1, source_target_pairs={{0,24},{8,16},{16,8},{24,0},{1,25},{9,17},{17,9},{25,1},{2,26},{10... | collective-permute-start | bytes 98312 | tf_op jit(solution)/shard_map/ppermute | solution.py:501
  13.5 0.6 %collective-permute-start.4 = (bf16[16,1024]{1,0:T(8,128)(2,1)S(1)}, bf16[16,1024]{1,0:T(8,128)(2,1)S(1)}, u32[]{:S(2)}, u32[]{:S(2)}) collective-permute-start(bf16[16,1024]{1,0:T(8,128)(2,1)S(1)} %get-tuple-element.45), channel_id=1, source_target_pairs={{0,16},{8,24},{16,0},{24,8},{1,17},{9,25},{17,1},{25,9},{2,18},{10... | collective-permute-start | bytes 98312 | tf_op jit(solution)/shard_map/ppermute | solution.py:501
  14.1 1.4 %collective-permute-start.5 = (bf16[16,1024]{1,0:T(8,128)(2,1)S(1)}, bf16[16,1024]{1,0:T(8,128)(2,1)S(1)}, u32[]{:S(2)}, u32[]{:S(2)}) collective-permute-start(bf16[16,1024]{1,0:T(8,128)(2,1)S(1)} %get-tuple-element.46), channel_id=1, source_target_pairs={{0,8},{8,0},{16,24},{24,16},{1,9},{9,1},{17,25},{25,17},{2,10},{10... | collective-permute-start | bytes 98312 | tf_op jit(solution)/shard_map/ppermute | solution.py:501
  15.5 0.7 %query_features.1 = f32[4,16,1024]{2,1,0:T(8,128)S(1)} custom-call(bf16[64,1024]{1,0:T(8,128)(2,1)S(1)} %get-tuple-element.28.refs_0_, f32[7,64]{1,0:T(8,128)S(1)} %get-tuple-element.29.refs_1_, bf16[16,2176]{1,0:T(8,128)(2,1)S(1)} %get-tuple-element.40.refs_6_.refs_9_.refs_2_, bf16[16,2176]{1,0:T(8,128)(2,1)S(1)} %collective-permute-done.2.refs_8_.refs_3_, ...), custom_call_target="tpu_custom_call" | custom-call | tf_op jit(solution)/shard_map/query_features/pallas_call | solution.py:241
  16.2 0.7 %collective-permute-done.3 = bf16[16,1024]{1,0:T(8,128)(2,1)S(1)} collective-permute-done((bf16[16,1024]{1,0:T(8,128)(2,1)S(1)}, bf16[16,1024]{1,0:T(8,128)(2,1)S(1)}, u32[]{:S(2)}, u32[]{:S(2)}) %collective-permute-start.3) | collective-permute-done | bytes 32800 | tf_op jit(solution)/shard_map/ppermute | solution.py:501
  16.8 0.6 %collective-permute-done.4 = bf16[16,1024]{1,0:T(8,128)(2,1)S(1)} collective-permute-done((bf16[16,1024]{1,0:T(8,128)(2,1)S(1)}, bf16[16,1024]{1,0:T(8,128)(2,1)S(1)}, u32[]{:S(2)}, u32[]{:S(2)}) %collective-permute-start.4) | collective-permute-done | bytes 32800 | tf_op jit(solution)/shard_map/ppermute | solution.py:501
  17.4 0.6 %collective-permute-done.5 = bf16[16,1024]{1,0:T(8,128)(2,1)S(1)} collective-permute-done((bf16[16,1024]{1,0:T(8,128)(2,1)S(1)}, bf16[16,1024]{1,0:T(8,128)(2,1)S(1)}, u32[]{:S(2)}, u32[]{:S(2)}) %collective-permute-start.5) | collective-permute-done | bytes 32800 | tf_op jit(solution)/shard_map/ppermute | solution.py:501
  18.0 2.7 %collective-permute-start.7 = (bf16[4,16,1024]{2,1,0:T(8,128)(2,1)S(1)}, bf16[4,16,1024]{2,1,0:T(8,128)(2,1)S(1)}, u32[]{:S(2)}, u32[]{:S(2)}) collective-permute-start(bf16[4,16,1024]{2,1,0:T(8,128)(2,1)S(1)} %multiply_convert_fusion.refs_1_), channel_id=1, source_target_pairs={{0,4},{1,5},{2,6},{3,7},{4,0},{5,1},{6,2},{7,3},{8,12},{9,13},{10,... | collective-permute-start | bytes 393224 | tf_op jit(solution)/shard_map/ppermute | solution.py:501
  20.7 1.6 %collective-permute-start.11 = (bf16[4,16,1024]{2,1,0:T(8,128)(2,1)S(1)}, bf16[4,16,1024]{2,1,0:T(8,128)(2,1)S(1)}, u32[]{:S(2)}, u32[]{:S(2)}) collective-permute-start(bf16[4,16,1024]{2,1,0:T(8,128)(2,1)S(1)} %multiply_convert_fusion.refs_1_), channel_id=1, source_target_pairs={{0,2},{1,3},{2,0},{3,1},{4,6},{5,7},{6,4},{7,5},{8,10},{9,11},{10,... | collective-permute-start | bytes 393224 | tf_op jit(solution)/shard_map/ppermute | solution.py:501
  22.3 0.2 collective-permute-start.9
  22.5 0.0 collective-permute-start.6
  22.5 5.3 %collective-permute-done.7.refs_3_ = bf16[4,16,1024]{2,1,0:T(8,128)(2,1)S(1)} collective-permute-done((bf16[4,16,1024]{2,1,0:T(8,128)(2,1)S(1)}, bf16[4,16,1024]{2,1,0:T(8,128)(2,1)S(1)}, u32[]{:S(2)}, u32[]{:S(2)}) %collective-permute-start.7) | collective-permute-done | bytes 131104 | tf_op jit(solution)/shard_map/ppermute | solution.py:501
  27.8 0.0 collective-permute-start.8
  27.8 0.0 collective-permute-done.11.refs_4_
  27.8 0.5 %collective-permute-start.12 = (bf16[4,16,1024]{2,1,0:T(8,128)(2,1)S(1)}, bf16[4,16,1024]{2,1,0:T(8,128)(2,1)S(1)}, u32[]{:S(2)}, u32[]{:S(2)}) collective-permute-start(bf16[4,16,1024]{2,1,0:T(8,128)(2,1)S(1)} %collective-permute-done.11.refs_4_), channel_id=1, source_target_pairs={{0,1},{1,0},{2,3},{3,2},{4,5},{5,4},{6,7},{7,6},{8,9},{9,8},{10,11... | collective-permute-start | bytes 393224 | tf_op jit(solution)/shard_map/ppermute | solution.py:501
  28.3 1.0 %collective-permute-done.9.refs_2_ = bf16[4,16,1024]{2,1,0:T(8,128)(2,1)S(1)} collective-permute-done((bf16[4,16,1024]{2,1,0:T(8,128)(2,1)S(1)}, bf16[4,16,1024]{2,1,0:T(8,128)(2,1)S(1)}, u32[]{:S(2)}, u32[]{:S(2)}) %collective-permute-start.9) | collective-permute-done | bytes 131104 | tf_op jit(solution)/shard_map/ppermute | solution.py:501
  29.3 0.0 collective-permute-start.10
  29.3 0.0 collective-permute-done.6.refs_2_
  29.3 0.0 collective-permute-done.8.refs_4_
  29.3 0.8 %project_early.1.refs_1_ = f32[1024,1024]{1,0:T(8,128)S(1)} custom-call(bf16[1024,512]{1,0:T(8,128)(2,1)S(1)} %get-tuple-element.27.refs_0_, bf16[4,16,1024]{2,1,0:T(8,128)(2,1)S(1)} %multiply_convert_fusion.refs_1_, bf16[4,16,1024]{2,1,0:T(8,128)(2,1)S(1)} %collective-permute-done.6.refs_2_, bf16[4,16,1024]{2,1,0:T(8,128)(2,1)S(1)} %collective-permute-done.7.refs_3_, ...), custom_call_target="tpu_custom_call" | custom-call | tf_op jit(solution)/shard_map/project_early/pallas_call | solution.py:432
  30.1 0.0 collective-permute-done.12.refs_5_
  30.1 0.6 %collective-permute-done.10.refs_3_ = bf16[4,16,1024]{2,1,0:T(8,128)(2,1)S(1)} collective-permute-done((bf16[4,16,1024]{2,1,0:T(8,128)(2,1)S(1)}, bf16[4,16,1024]{2,1,0:T(8,128)(2,1)S(1)}, u32[]{:S(2)}, u32[]{:S(2)}) %collective-permute-start.10) | collective-permute-done | bytes 131104 | tf_op jit(solution)/shard_map/ppermute | solution.py:501
  30.7 1.7 %project_late.1 = bf16[1024,1024]{1,0:T(8,128)(2,1)} custom-call(bf16[1024,512]{1,0:T(8,128)(2,1)S(1)} %get-tuple-element.27.refs_0_, f32[1024,1024]{1,0:T(8,128)S(1)} %project_early.1.refs_1_, bf16[4,16,1024]{2,1,0:T(8,128)(2,1)S(1)} %collective-permute-done.9.refs_2_, bf16[4,16,1024]{2,1,0:T(8,128)(2,1)S(1)} %collective-permute-done.10.refs_3_, ...), custom_call_target="tpu_custom_call" | custom-call | tf_op jit(solution)/shard_map/project_late/pallas_call | solution.py:451
  (1 shorter events, 0.0 us)
Async XLA Ops:
  1.7 6.3 %collective-permute-start = (bf16[16,2176]{1,0:T(8,128)(2,1)S(1)}, bf16[16,2176]{1,0:T(8,128)(2,1)S(1)}, u32[]{:S(2)}, u32[]{:S(2)}) collective-permute-start(bf16[16,2176]{1,0:T(8,128)(2,1)S(1)} %get-tuple-element.36), channel_id=1, source_target_pairs={{0,24},{8,16},{16,8},{24,0},{1,25},{9,17},{17,9},{25,1},{2,26},{10... | collective-permute-start | bytes 208904 | tf_op jit(solution)/shard_map/ppermute | solution.py:501
  5.6 4.3 %collective-permute-start.1 = (bf16[16,2176]{1,0:T(8,128)(2,1)S(1)}, bf16[16,2176]{1,0:T(8,128)(2,1)S(1)}, u32[]{:S(2)}, u32[]{:S(2)}) collective-permute-start(bf16[16,2176]{1,0:T(8,128)(2,1)S(1)} %get-tuple-element.37), channel_id=1, source_target_pairs={{0,16},{8,24},{16,0},{24,8},{1,17},{9,25},{17,1},{25,9},{2,18},{10... | collective-permute-start | bytes 208904 | tf_op jit(solution)/shard_map/ppermute | solution.py:501
  6.2 4.3 %collective-permute-start.2 = (bf16[16,2176]{1,0:T(8,128)(2,1)S(1)}, bf16[16,2176]{1,0:T(8,128)(2,1)S(1)}, u32[]{:S(2)}, u32[]{:S(2)}) collective-permute-start(bf16[16,2176]{1,0:T(8,128)(2,1)S(1)} %get-tuple-element.38), channel_id=1, source_target_pairs={{0,8},{8,0},{16,24},{24,16},{1,9},{9,1},{17,25},{25,17},{2,10},{10... | collective-permute-start | bytes 208904 | tf_op jit(solution)/shard_map/ppermute | solution.py:501
  11.9 4.9 %collective-permute-start.3 = (bf16[16,1024]{1,0:T(8,128)(2,1)S(1)}, bf16[16,1024]{1,0:T(8,128)(2,1)S(1)}, u32[]{:S(2)}, u32[]{:S(2)}) collective-permute-start(bf16[16,1024]{1,0:T(8,128)(2,1)S(1)} %get-tuple-element.44), channel_id=1, source_target_pairs={{0,24},{8,16},{16,8},{24,0},{1,25},{9,17},{17,9},{25,1},{2,26},{10... | collective-permute-start | bytes 98312 | tf_op jit(solution)/shard_map/ppermute | solution.py:501
  13.5 3.9 %collective-permute-start.4 = (bf16[16,1024]{1,0:T(8,128)(2,1)S(1)}, bf16[16,1024]{1,0:T(8,128)(2,1)S(1)}, u32[]{:S(2)}, u32[]{:S(2)}) collective-permute-start(bf16[16,1024]{1,0:T(8,128)(2,1)S(1)} %get-tuple-element.45), channel_id=1, source_target_pairs={{0,16},{8,24},{16,0},{24,8},{1,17},{9,25},{17,1},{25,9},{2,18},{10... | collective-permute-start | bytes 98312 | tf_op jit(solution)/shard_map/ppermute | solution.py:501
  14.1 3.9 %collective-permute-start.5 = (bf16[16,1024]{1,0:T(8,128)(2,1)S(1)}, bf16[16,1024]{1,0:T(8,128)(2,1)S(1)}, u32[]{:S(2)}, u32[]{:S(2)}) collective-permute-start(bf16[16,1024]{1,0:T(8,128)(2,1)S(1)} %get-tuple-element.46), channel_id=1, source_target_pairs={{0,8},{8,0},{16,24},{24,16},{1,9},{9,1},{17,25},{25,17},{2,10},{10... | collective-permute-start | bytes 98312 | tf_op jit(solution)/shard_map/ppermute | solution.py:501
  18.0 9.8 %collective-permute-start.7 = (bf16[4,16,1024]{2,1,0:T(8,128)(2,1)S(1)}, bf16[4,16,1024]{2,1,0:T(8,128)(2,1)S(1)}, u32[]{:S(2)}, u32[]{:S(2)}) collective-permute-start(bf16[4,16,1024]{2,1,0:T(8,128)(2,1)S(1)} %multiply_convert_fusion.refs_1_), channel_id=1, source_target_pairs={{0,4},{1,5},{2,6},{3,7},{4,0},{5,1},{6,2},{7,3},{8,12},{9,13},{10,... | collective-permute-start | bytes 393224 | tf_op jit(solution)/shard_map/ppermute | solution.py:501
  20.7 7.1 %collective-permute-start.11 = (bf16[4,16,1024]{2,1,0:T(8,128)(2,1)S(1)}, bf16[4,16,1024]{2,1,0:T(8,128)(2,1)S(1)}, u32[]{:S(2)}, u32[]{:S(2)}) collective-permute-start(bf16[4,16,1024]{2,1,0:T(8,128)(2,1)S(1)} %multiply_convert_fusion.refs_1_), channel_id=1, source_target_pairs={{0,2},{1,3},{2,0},{3,1},{4,6},{5,7},{6,4},{7,5},{8,10},{9,11},{10,... | collective-permute-start | bytes 393224 | tf_op jit(solution)/shard_map/ppermute | solution.py:501
  22.3 7.1 %collective-permute-start.9 = (bf16[4,16,1024]{2,1,0:T(8,128)(2,1)S(1)}, bf16[4,16,1024]{2,1,0:T(8,128)(2,1)S(1)}, u32[]{:S(2)}, u32[]{:S(2)}) collective-permute-start(bf16[4,16,1024]{2,1,0:T(8,128)(2,1)S(1)} %multiply_convert_fusion.refs_1_), channel_id=1, source_target_pairs={{0,6},{1,7},{2,4},{3,5},{4,2},{5,3},{6,0},{7,1},{8,14},{9,15},{10,... | collective-permute-start | bytes 393224 | tf_op jit(solution)/shard_map/ppermute | solution.py:501
  22.5 6.9 %collective-permute-start.6 = (bf16[4,16,1024]{2,1,0:T(8,128)(2,1)S(1)}, bf16[4,16,1024]{2,1,0:T(8,128)(2,1)S(1)}, u32[]{:S(2)}, u32[]{:S(2)}) collective-permute-start(bf16[4,16,1024]{2,1,0:T(8,128)(2,1)S(1)} %multiply_convert_fusion.refs_1_), channel_id=1, source_target_pairs={{0,1},{1,0},{2,3},{3,2},{4,5},{5,4},{6,7},{7,6},{8,9},{9,8},{10,11... | collective-permute-start | bytes 393224 | tf_op jit(solution)/shard_map/ppermute | solution.py:501
  27.8 1.6 %collective-permute-start.8 = (bf16[4,16,1024]{2,1,0:T(8,128)(2,1)S(1)}, bf16[4,16,1024]{2,1,0:T(8,128)(2,1)S(1)}, u32[]{:S(2)}, u32[]{:S(2)}) collective-permute-start(bf16[4,16,1024]{2,1,0:T(8,128)(2,1)S(1)} %collective-permute-done.7.refs_3_), channel_id=1, source_target_pairs={{0,1},{1,0},{2,3},{3,2},{4,5},{5,4},{6,7},{7,6},{8,9},{9,8},{10,11... | collective-permute-start | bytes 393224 | tf_op jit(solution)/shard_map/ppermute | solution.py:501
  27.8 2.3 %collective-permute-start.12 = (bf16[4,16,1024]{2,1,0:T(8,128)(2,1)S(1)}, bf16[4,16,1024]{2,1,0:T(8,128)(2,1)S(1)}, u32[]{:S(2)}, u32[]{:S(2)}) collective-permute-start(bf16[4,16,1024]{2,1,0:T(8,128)(2,1)S(1)} %collective-permute-done.11.refs_4_), channel_id=1, source_target_pairs={{0,1},{1,0},{2,3},{3,2},{4,5},{5,4},{6,7},{7,6},{8,9},{9,8},{10,11... | collective-permute-start | bytes 393224 | tf_op jit(solution)/shard_map/ppermute | solution.py:501
  29.3 1.3 %collective-permute-start.10 = (bf16[4,16,1024]{2,1,0:T(8,128)(2,1)S(1)}, bf16[4,16,1024]{2,1,0:T(8,128)(2,1)S(1)}, u32[]{:S(2)}, u32[]{:S(2)}) collective-permute-start(bf16[4,16,1024]{2,1,0:T(8,128)(2,1)S(1)} %collective-permute-done.9.refs_2_), channel_id=1, source_target_pairs={{0,1},{1,0},{2,3},{3,2},{4,5},{5,4},{6,7},{7,6},{8,9},{9,8},{10,11... | collective-permute-start | bytes 393224 | tf_op jit(solution)/shard_map/ppermute | solution.py:501

commit v12 on v10

--- a/solution.py
+++ b/solution.py
@@ -145,10 +145,10 @@
         wide_ref[stream] = widened(flat[1 + stream])
     first_ref[...] = flat[0]
     query_move.wait()
-    edges = jnp.zeros((chans, LANES), jnp.float32)
+    edges = jnp.zeros((chans, LANES), jnp.bfloat16)
     for share in range(nodes):
         tile = query_ref[share * chans : (share + 1) * chans, block - LANES :]
-        moved = pltpu.roll(tile.astype(jnp.float32), LANE_Q + (share + 1) * rim, 1)
+        moved = pltpu.roll(tile, LANE_Q + (share + 1) * rim, 1)
         edges = jnp.where(lane >= LANE_Q + share * rim, moved, edges)
     stream_move.wait()
     for mask, rows in reversed(list(enumerate(shares))):
@@ -158,9 +158,9 @@
         for stream in reversed(range(2)):
             ends = jnp.where(lane < rim, raws[stream][:, :LANES], raws[stream][:, block - LANES :])
             at = stream * LANE_V
-            moved = pltpu.roll(ends, at + rim, 1).astype(jnp.float32)
+            moved = pltpu.roll(ends, at + rim, 1)
             edge = jnp.where(lane < at + LANE_V, moved, edge)
-        outs[mask][:, 2 * block :] = edge.astype(jnp.bfloat16)
+        outs[mask][:, 2 * block :] = edge
         before = [None, None]
         for index in range(block // LANES):
             product = None

time: 32.5 us -> 32.5 us (level)
  no operation moved by 1% of the time
where the time goes in v12:
time: 32.5 us; the launch traced here: 32.3 us
  starting transfers between devices  13.1 us (40%)
  waiting for transfers between devices  11.5 us (35%)
  Pallas kernels  7.6 us (23%)
    ppermute x13, starting transfers between devices, swapped(): lax.ppermute(block, axis, [(i, i ^ mask) for i in range(lax.axis_size(axi...  13.1 us
    ppermute x13, waiting for transfers between devices, swapped(): lax.ppermute(block, axis, [(i, i ^ mask) for i in range(lax.axis_size(axi...  11.5 us
    pallas_call x1, Pallas kernels, project_late(): pl.pallas_call(lambda *refs: final_kernel(tuple(late), cuts, *refs), out_...  1.68 us
    pallas_call x1, Pallas kernels, pack(): pl.pallas_call(lambda *refs: pack_kernel(nodes, chans, *refs), out_shape=...  1.63 us
    pallas_call x1, Pallas kernels, long_mix(): pl.pallas_call(lambda *refs: long_kernel(nodes, chans, per_node, rim, *re...  1.48 us
    pallas_call x1, Pallas kernels, near_tables(): pl.pallas_call(lambda *refs: tables_kernel(count, *refs), out_shape=[jax....  1.4 us
    pallas_call x1, Pallas kernels, project_early(): pl.pallas_call(lambda *refs: partial_kernel(tuple(early), features // 4,...  0.77 us
    pallas_call x1, Pallas kernels, query_features(): pl.pallas_call(lambda *refs: query_kernel(nodes, *refs), out_shape=jax.Sh...  0.65 us
  transfers between devices with their start and end apart: 13, of which 9 were waited for; matrix products, arithmetic and copies ran while one was open for 0% of the time, Pallas kernels for 9%

profile of v12, /device:TPU:0, one launch (start us, length us, event | category | flops | bytes accessed | tf_op | source)
XLA Modules:
  0.0 32.3 jit_solution(2403850556492926478)
XLA Ops:
  0.0 1.6 %pack.1 = (bf16[16,2176]{1,0:T(8,128)(2,1)S(1)}, bf16[16,2176]{1,0:T(8,128)(2,1)S(1)}, bf16[16,2176]{1,0:T(8,128)(2,1)S(1)}, bf16[16,2176]{1,0:T(8,128)(2,1)S(1)...) custom-call(bf16[3,64,1024]{2,1,0:T(8,128)(2,1)} %refs_0_.2, f32[64,1024]{1,0:T(8,128)} %refs_1_.2, ...), custom_call_target="tpu_custom_call" | custom-call | tf_op jit(solution)/shard_map/pack/pallas_call | solution.py:189
  1.6 4.0 %collective-permute-start = (bf16[16,2176]{1,0:T(8,128)(2,1)S(1)}, bf16[16,2176]{1,0:T(8,128)(2,1)S(1)}, u32[]{:S(2)}, u32[]{:S(2)}) collective-permute-start(bf16[16,2176]{1,0:T(8,128)(2,1)S(1)} %get-tuple-element.36), channel_id=1, source_target_pairs={{0,24},{8,16},{16,8},{24,0},{1,25},{9,17},{17,9},{25,1},{2,26},{10... | collective-permute-start | bytes 208904 | tf_op jit(solution)/shard_map/ppermute | solution.py:500
  5.6 0.5 %collective-permute-start.1 = (bf16[16,2176]{1,0:T(8,128)(2,1)S(1)}, bf16[16,2176]{1,0:T(8,128)(2,1)S(1)}, u32[]{:S(2)}, u32[]{:S(2)}) collective-permute-start(bf16[16,2176]{1,0:T(8,128)(2,1)S(1)} %get-tuple-element.37), channel_id=1, source_target_pairs={{0,16},{8,24},{16,0},{24,8},{1,17},{9,25},{17,1},{25,9},{2,18},{10... | collective-permute-start | bytes 208904 | tf_op jit(solution)/shard_map/ppermute | solution.py:500
  6.1 0.1 collective-permute-start.2
  6.2 1.4 %near_tables.1 = (bf16[1024,512]{1,0:T(8,128)(2,1)S(1)}, bf16[64,64]{1,0:T(8,128)(2,1)S(1)}, f32[32,256]{1,0:T(8,128)S(1)}, bf16[768,256]{1,0:T(8,128)(2,1)S(1)}...) custom-call(bf16[1024,512]{1,0:T(8,128)(2,1)} %refs_0_.3, bf16[64,64]{1,0:T(8,128)(2,1)} %constant.8.clone.refs_1_, ...), custom_call_target="tpu_custom_call" | custom-call | tf_op jit(solution)/shard_map/near_tables/pallas_call | solution.py:110
  7.6 0.3 collective-permute-done.refs_6_.refs_5_
  7.9 2.0 %collective-permute-done.1.refs_7_.refs_4_ = bf16[16,2176]{1,0:T(8,128)(2,1)S(1)} collective-permute-done((bf16[16,2176]{1,0:T(8,128)(2,1)S(1)}, bf16[16,2176]{1,0:T(8,128)(2,1)S(1)}, u32[]{:S(2)}, u32[]{:S(2)}) %collective-permute-start.1) | collective-permute-done | bytes 69664 | tf_op jit(solution)/shard_map/ppermute | solution.py:500
  9.9 0.5 %collective-permute-done.2.refs_8_.refs_3_ = bf16[16,2176]{1,0:T(8,128)(2,1)S(1)} collective-permute-done((bf16[16,2176]{1,0:T(8,128)(2,1)S(1)}, bf16[16,2176]{1,0:T(8,128)(2,1)S(1)}, u32[]{:S(2)}, u32[]{:S(2)}) %collective-permute-start.2) | collective-permute-done | bytes 69664 | tf_op jit(solution)/shard_map/ppermute | solution.py:500
  10.4 1.5 %long_mix.1 = (bf16[16,1024]{1,0:T(8,128)(2,1)S(1)}, bf16[16,1024]{1,0:T(8,128)(2,1)S(1)}, bf16[16,1024]{1,0:T(8,128)(2,1)S(1)}, bf16[16,1024]{1,0:T(8,128)(2,1)S(1)}) custom-call(f32[2,64,896]{2,1,0:T(8,128)S(1)} %get-tuple-element.30.refs_0_, bf16[64,64]{1,0:T(8,128)(2,1)S(1)} %get-tuple-element.31.refs_1_, f32[32,256]{1,0:T(8,128)S(1)} %get-tuple-element.32.refs_2_, ...), custom_call_target="tpu_custom_call" | custom-call | tf_op jit(solution)/shard_map/long_mix/pallas_call | solution.py:366
  11.9 1.6 %collective-permute-start.3 = (bf16[16,1024]{1,0:T(8,128)(2,1)S(1)}, bf16[16,1024]{1,0:T(8,128)(2,1)S(1)}, u32[]{:S(2)}, u32[]{:S(2)}) collective-permute-start(bf16[16,1024]{1,0:T(8,128)(2,1)S(1)} %get-tuple-element.44), channel_id=1, source_target_pairs={{0,24},{8,16},{16,8},{24,0},{1,25},{9,17},{17,9},{25,1},{2,26},{10... | collective-permute-start | bytes 98312 | tf_op jit(solution)/shard_map/ppermute | solution.py:500
  13.5 0.6 %collective-permute-start.4 = (bf16[16,1024]{1,0:T(8,128)(2,1)S(1)}, bf16[16,1024]{1,0:T(8,128)(2,1)S(1)}, u32[]{:S(2)}, u32[]{:S(2)}) collective-permute-start(bf16[16,1024]{1,0:T(8,128)(2,1)S(1)} %get-tuple-element.45), channel_id=1, source_target_pairs={{0,16},{8,24},{16,0},{24,8},{1,17},{9,25},{17,1},{25,9},{2,18},{10... | collective-permute-start | bytes 98312 | tf_op jit(solution)/shard_map/ppermute | solution.py:500
  14.0 1.4 %collective-permute-start.5 = (bf16[16,1024]{1,0:T(8,128)(2,1)S(1)}, bf16[16,1024]{1,0:T(8,128)(2,1)S(1)}, u32[]{:S(2)}, u32[]{:S(2)}) collective-permute-start(bf16[16,1024]{1,0:T(8,128)(2,1)S(1)} %get-tuple-element.46), channel_id=1, source_target_pairs={{0,8},{8,0},{16,24},{24,16},{1,9},{9,1},{17,25},{25,17},{2,10},{10... | collective-permute-start | bytes 98312 | tf_op jit(solution)/shard_map/ppermute | solution.py:500
  15.4 0.7 %query_features.1 = f32[4,16,1024]{2,1,0:T(8,128)S(1)} custom-call(bf16[64,1024]{1,0:T(8,128)(2,1)S(1)} %get-tuple-element.28.refs_0_, f32[7,64]{1,0:T(8,128)S(1)} %get-tuple-element.29.refs_1_, bf16[16,2176]{1,0:T(8,128)(2,1)S(1)} %get-tuple-element.40.refs_6_.refs_9_.refs_2_, bf16[16,2176]{1,0:T(8,128)(2,1)S(1)} %collective-permute-done.2.refs_8_.refs_3_, ...), custom_call_target="tpu_custom_call" | custom-call | tf_op jit(solution)/shard_map/query_features/pallas_call | solution.py:240
  16.1 0.7 %collective-permute-done.3 = bf16[16,1024]{1,0:T(8,128)(2,1)S(1)} collective-permute-done((bf16[16,1024]{1,0:T(8,128)(2,1)S(1)}, bf16[16,1024]{1,0:T(8,128)(2,1)S(1)}, u32[]{:S(2)}, u32[]{:S(2)}) %collective-permute-start.3) | collective-permute-done | bytes 32800 | tf_op jit(solution)/shard_map/ppermute | solution.py:500
  16.8 0.6 %collective-permute-done.4 = bf16[16,1024]{1,0:T(8,128)(2,1)S(1)} collective-permute-done((bf16[16,1024]{1,0:T(8,128)(2,1)S(1)}, bf16[16,1024]{1,0:T(8,128)(2,1)S(1)}, u32[]{:S(2)}, u32[]{:S(2)}) %collective-permute-start.4) | collective-permute-done | bytes 32800 | tf_op jit(solution)/shard_map/ppermute | solution.py:500
  17.4 0.6 %collective-permute-done.5 = bf16[16,1024]{1,0:T(8,128)(2,1)S(1)} collective-permute-done((bf16[16,1024]{1,0:T(8,128)(2,1)S(1)}, bf16[16,1024]{1,0:T(8,128)(2,1)S(1)}, u32[]{:S(2)}, u32[]{:S(2)}) %collective-permute-start.5) | collective-permute-done | bytes 32800 | tf_op jit(solution)/shard_map/ppermute | solution.py:500
  18.0 2.6 %collective-permute-start.7 = (bf16[4,16,1024]{2,1,0:T(8,128)(2,1)S(1)}, bf16[4,16,1024]{2,1,0:T(8,128)(2,1)S(1)}, u32[]{:S(2)}, u32[]{:S(2)}) collective-permute-start(bf16[4,16,1024]{2,1,0:T(8,128)(2,1)S(1)} %multiply_convert_fusion.refs_1_), channel_id=1, source_target_pairs={{0,4},{1,5},{2,6},{3,7},{4,0},{5,1},{6,2},{7,3},{8,12},{9,13},{10,... | collective-permute-start | bytes 393224 | tf_op jit(solution)/shard_map/ppermute | solution.py:500
  20.6 1.6 %collective-permute-start.11 = (bf16[4,16,1024]{2,1,0:T(8,128)(2,1)S(1)}, bf16[4,16,1024]{2,1,0:T(8,128)(2,1)S(1)}, u32[]{:S(2)}, u32[]{:S(2)}) collective-permute-start(bf16[4,16,1024]{2,1,0:T(8,128)(2,1)S(1)} %multiply_convert_fusion.refs_1_), channel_id=1, source_target_pairs={{0,2},{1,3},{2,0},{3,1},{4,6},{5,7},{6,4},{7,5},{8,10},{9,11},{10,... | collective-permute-start | bytes 393224 | tf_op jit(solution)/shard_map/ppermute | solution.py:500
  22.2 0.2 collective-permute-start.9
  22.4 0.0 collective-permute-start.6
  22.4 5.3 %collective-permute-done.7.refs_3_ = bf16[4,16,1024]{2,1,0:T(8,128)(2,1)S(1)} collective-permute-done((bf16[4,16,1024]{2,1,0:T(8,128)(2,1)S(1)}, bf16[4,16,1024]{2,1,0:T(8,128)(2,1)S(1)}, u32[]{:S(2)}, u32[]{:S(2)}) %collective-permute-start.7) | collective-permute-done | bytes 131104 | tf_op jit(solution)/shard_map/ppermute | solution.py:500
  27.7 0.0 collective-permute-start.8
  27.7 0.0 collective-permute-done.11.refs_4_
  27.7 0.5 %collective-permute-start.12 = (bf16[4,16,1024]{2,1,0:T(8,128)(2,1)S(1)}, bf16[4,16,1024]{2,1,0:T(8,128)(2,1)S(1)}, u32[]{:S(2)}, u32[]{:S(2)}) collective-permute-start(bf16[4,16,1024]{2,1,0:T(8,128)(2,1)S(1)} %collective-permute-done.11.refs_4_), channel_id=1, source_target_pairs={{0,1},{1,0},{2,3},{3,2},{4,5},{5,4},{6,7},{7,6},{8,9},{9,8},{10,11... | collective-permute-start | bytes 393224 | tf_op jit(solution)/shard_map/ppermute | solution.py:500
  28.2 1.0 %collective-permute-done.9.refs_2_ = bf16[4,16,1024]{2,1,0:T(8,128)(2,1)S(1)} collective-permute-done((bf16[4,16,1024]{2,1,0:T(8,128)(2,1)S(1)}, bf16[4,16,1024]{2,1,0:T(8,128)(2,1)S(1)}, u32[]{:S(2)}, u32[]{:S(2)}) %collective-permute-start.9) | collective-permute-done | bytes 131104 | tf_op jit(solution)/shard_map/ppermute | solution.py:500
  29.3 0.0 collective-permute-start.10
  29.3 0.0 collective-permute-done.6.refs_2_
  29.3 0.0 collective-permute-done.8.refs_4_
  29.3 0.8 %project_early.1.refs_1_ = f32[1024,1024]{1,0:T(8,128)S(1)} custom-call(bf16[1024,512]{1,0:T(8,128)(2,1)S(1)} %get-tuple-element.27.refs_0_, bf16[4,16,1024]{2,1,0:T(8,128)(2,1)S(1)} %multiply_convert_fusion.refs_1_, bf16[4,16,1024]{2,1,0:T(8,128)(2,1)S(1)} %collective-permute-done.6.refs_2_, bf16[4,16,1024]{2,1,0:T(8,128)(2,1)S(1)} %collective-permute-done.7.refs_3_, ...), custom_call_target="tpu_custom_call" | custom-call | tf_op jit(solution)/shard_map/project_early/pallas_call | solution.py:431
  30.1 0.0 collective-permute-done.12.refs_5_
  30.1 0.6 %collective-permute-done.10.refs_3_ = bf16[4,16,1024]{2,1,0:T(8,128)(2,1)S(1)} collective-permute-done((bf16[4,16,1024]{2,1,0:T(8,128)(2,1)S(1)}, bf16[4,16,1024]{2,1,0:T(8,128)(2,1)S(1)}, u32[]{:S(2)}, u32[]{:S(2)}) %collective-permute-start.10) | collective-permute-done | bytes 131104 | tf_op jit(solution)/shard_map/ppermute | solution.py:500
  30.6 1.7 %project_late.1 = bf16[1024,1024]{1,0:T(8,128)(2,1)} custom-call(bf16[1024,512]{1,0:T(8,128)(2,1)S(1)} %get-tuple-element.27.refs_0_, f32[1024,1024]{1,0:T(8,128)S(1)} %project_early.1.refs_1_, bf16[4,16,1024]{2,1,0:T(8,128)(2,1)S(1)} %collective-permute-done.9.refs_2_, bf16[4,16,1024]{2,1,0:T(8,128)(2,1)S(1)} %collective-permute-done.10.refs_3_, ...), custom_call_target="tpu_custom_call" | custom-call | tf_op jit(solution)/shard_map/project_late/pallas_call | solution.py:450
  (1 shorter events, 0.0 us)
Async XLA Ops:
  1.6 6.3 %collective-permute-start = (bf16[16,2176]{1,0:T(8,128)(2,1)S(1)}, bf16[16,2176]{1,0:T(8,128)(2,1)S(1)}, u32[]{:S(2)}, u32[]{:S(2)}) collective-permute-start(bf16[16,2176]{1,0:T(8,128)(2,1)S(1)} %get-tuple-element.36), channel_id=1, source_target_pairs={{0,24},{8,16},{16,8},{24,0},{1,25},{9,17},{17,9},{25,1},{2,26},{10... | collective-permute-start | bytes 208904 | tf_op jit(solution)/shard_map/ppermute | solution.py:500
  5.6 4.3 %collective-permute-start.1 = (bf16[16,2176]{1,0:T(8,128)(2,1)S(1)}, bf16[16,2176]{1,0:T(8,128)(2,1)S(1)}, u32[]{:S(2)}, u32[]{:S(2)}) collective-permute-start(bf16[16,2176]{1,0:T(8,128)(2,1)S(1)} %get-tuple-element.37), channel_id=1, source_target_pairs={{0,16},{8,24},{16,0},{24,8},{1,17},{9,25},{17,1},{25,9},{2,18},{10... | collective-permute-start | bytes 208904 | tf_op jit(solution)/shard_map/ppermute | solution.py:500
  6.1 4.3 %collective-permute-start.2 = (bf16[16,2176]{1,0:T(8,128)(2,1)S(1)}, bf16[16,2176]{1,0:T(8,128)(2,1)S(1)}, u32[]{:S(2)}, u32[]{:S(2)}) collective-permute-start(bf16[16,2176]{1,0:T(8,128)(2,1)S(1)} %get-tuple-element.38), channel_id=1, source_target_pairs={{0,8},{8,0},{16,24},{24,16},{1,9},{9,1},{17,25},{25,17},{2,10},{10... | collective-permute-start | bytes 208904 | tf_op jit(solution)/shard_map/ppermute | solution.py:500
  11.9 4.9 %collective-permute-start.3 = (bf16[16,1024]{1,0:T(8,128)(2,1)S(1)}, bf16[16,1024]{1,0:T(8,128)(2,1)S(1)}, u32[]{:S(2)}, u32[]{:S(2)}) collective-permute-start(bf16[16,1024]{1,0:T(8,128)(2,1)S(1)} %get-tuple-element.44), channel_id=1, source_target_pairs={{0,24},{8,16},{16,8},{24,0},{1,25},{9,17},{17,9},{25,1},{2,26},{10... | collective-permute-start | bytes 98312 | tf_op jit(solution)/shard_map/ppermute | solution.py:500
  13.5 3.9 %collective-permute-start.4 = (bf16[16,1024]{1,0:T(8,128)(2,1)S(1)}, bf16[16,1024]{1,0:T(8,128)(2,1)S(1)}, u32[]{:S(2)}, u32[]{:S(2)}) collective-permute-start(bf16[16,1024]{1,0:T(8,128)(2,1)S(1)} %get-tuple-element.45), channel_id=1, source_target_pairs={{0,16},{8,24},{16,0},{24,8},{1,17},{9,25},{17,1},{25,9},{2,18},{10... | collective-permute-start | bytes 98312 | tf_op jit(solution)/shard_map/ppermute | solution.py:500
  14.0 3.9 %collective-permute-start.5 = (bf16[16,1024]{1,0:T(8,128)(2,1)S(1)}, bf16[16,1024]{1,0:T(8,128)(2,1)S(1)}, u32[]{:S(2)}, u32[]{:S(2)}) collective-permute-start(bf16[16,1024]{1,0:T(8,128)(2,1)S(1)} %get-tuple-element.46), channel_id=1, source_target_pairs={{0,8},{8,0},{16,24},{24,16},{1,9},{9,1},{17,25},{25,17},{2,10},{10... | collective-permute-start | bytes 98312 | tf_op jit(solution)/shard_map/ppermute | solution.py:500
  18.0 9.8 %collective-permute-start.7 = (bf16[4,16,1024]{2,1,0:T(8,128)(2,1)S(1)}, bf16[4,16,1024]{2,1,0:T(8,128)(2,1)S(1)}, u32[]{:S(2)}, u32[]{:S(2)}) collective-permute-start(bf16[4,16,1024]{2,1,0:T(8,128)(2,1)S(1)} %multiply_convert_fusion.refs_1_), channel_id=1, source_target_pairs={{0,4},{1,5},{2,6},{3,7},{4,0},{5,1},{6,2},{7,3},{8,12},{9,13},{10,... | collective-permute-start | bytes 393224 | tf_op jit(solution)/shard_map/ppermute | solution.py:500
  20.6 7.1 %collective-permute-start.11 = (bf16[4,16,1024]{2,1,0:T(8,128)(2,1)S(1)}, bf16[4,16,1024]{2,1,0:T(8,128)(2,1)S(1)}, u32[]{:S(2)}, u32[]{:S(2)}) collective-permute-start(bf16[4,16,1024]{2,1,0:T(8,128)(2,1)S(1)} %multiply_convert_fusion.refs_1_), channel_id=1, source_target_pairs={{0,2},{1,3},{2,0},{3,1},{4,6},{5,7},{6,4},{7,5},{8,10},{9,11},{10,... | collective-permute-start | bytes 393224 | tf_op jit(solution)/shard_map/ppermute | solution.py:500
  22.2 7.1 %collective-permute-start.9 = (bf16[4,16,1024]{2,1,0:T(8,128)(2,1)S(1)}, bf16[4,16,1024]{2,1,0:T(8,128)(2,1)S(1)}, u32[]{:S(2)}, u32[]{:S(2)}) collective-permute-start(bf16[4,16,1024]{2,1,0:T(8,128)(2,1)S(1)} %multiply_convert_fusion.refs_1_), channel_id=1, source_target_pairs={{0,6},{1,7},{2,4},{3,5},{4,2},{5,3},{6,0},{7,1},{8,14},{9,15},{10,... | collective-permute-start | bytes 393224 | tf_op jit(solution)/shard_map/ppermute | solution.py:500
  22.4 6.8 %collective-permute-start.6 = (bf16[4,16,1024]{2,1,0:T(8,128)(2,1)S(1)}, bf16[4,16,1024]{2,1,0:T(8,128)(2,1)S(1)}, u32[]{:S(2)}, u32[]{:S(2)}) collective-permute-start(bf16[4,16,1024]{2,1,0:T(8,128)(2,1)S(1)} %multiply_convert_fusion.refs_1_), channel_id=1, source_target_pairs={{0,1},{1,0},{2,3},{3,2},{4,5},{5,4},{6,7},{7,6},{8,9},{9,8},{10,11... | collective-permute-start | bytes 393224 | tf_op jit(solution)/shard_map/ppermute | solution.py:500
  27.7 1.6 %collective-permute-start.8 = (bf16[4,16,1024]{2,1,0:T(8,128)(2,1)S(1)}, bf16[4,16,1024]{2,1,0:T(8,128)(2,1)S(1)}, u32[]{:S(2)}, u32[]{:S(2)}) collective-permute-start(bf16[4,16,1024]{2,1,0:T(8,128)(2,1)S(1)} %collective-permute-done.7.refs_3_), channel_id=1, source_target_pairs={{0,1},{1,0},{2,3},{3,2},{4,5},{5,4},{6,7},{7,6},{8,9},{9,8},{10,11... | collective-permute-start | bytes 393224 | tf_op jit(solution)/shard_map/ppermute | solution.py:500
  27.7 2.3 %collective-permute-start.12 = (bf16[4,16,1024]{2,1,0:T(8,128)(2,1)S(1)}, bf16[4,16,1024]{2,1,0:T(8,128)(2,1)S(1)}, u32[]{:S(2)}, u32[]{:S(2)}) collective-permute-start(bf16[4,16,1024]{2,1,0:T(8,128)(2,1)S(1)} %collective-permute-done.11.refs_4_), channel_id=1, source_target_pairs={{0,1},{1,0},{2,3},{3,2},{4,5},{5,4},{6,7},{7,6},{8,9},{9,8},{10,11... | collective-permute-start | bytes 393224 | tf_op jit(solution)/shard_map/ppermute | solution.py:500
  29.3 1.3 %collective-permute-start.10 = (bf16[4,16,1024]{2,1,0:T(8,128)(2,1)S(1)}, bf16[4,16,1024]{2,1,0:T(8,128)(2,1)S(1)}, u32[]{:S(2)}, u32[]{:S(2)}) collective-permute-start(bf16[4,16,1024]{2,1,0:T(8,128)(2,1)S(1)} %collective-permute-done.9.refs_2_), channel_id=1, source_target_pairs={{0,1},{1,0},{2,3},{3,2},{4,5},{5,4},{6,7},{7,6},{8,9},{9,8},{10,11... | collective-permute-start | bytes 393224 | tf_op jit(solution)/shard_map/ppermute | solution.py:500
